TPU v7x, 32 devices: a whole 2x2x4 slice. The times are simulated.
32 devices in a mesh: scan: 4 (over y, x), blk: 8 (over z, core).
Axes of the slice: x: 2, y: 2, z: 4, core: 2. Of those that a mesh axis runs over, the one named last changes fastest.
Arguments:
- ref_feats: bfloat16 [4, 4096, 256], P('scan', 'blk'), may hold values from -120 to 120
- src_feats: bfloat16 [4, 1024, 256], P('scan', 'blk'), may hold values from -120 to 120
- grad_out: bfloat16 [4, 4096, 256], P('scan', 'blk'), may hold values from -6 to 6
- w_query: bfloat16 [256, 256], replicated, may hold values from -1 to 1
- w_key: bfloat16 [256, 256], replicated, may hold values from -1 to 1
- w_value: bfloat16 [256, 256], replicated, may hold values from -0.375 to 0.375
- w_out: bfloat16 [256, 256], replicated, may hold values from -0.375 to 0.375
- intersection: int32 [4, 32, 8], P('scan', 'blk'), may hold values from 0 to 1, as said below
Outputs:
- matched: bfloat16 [4, 4096, 256], P('scan', 'blk')
- grad_ref: bfloat16 [4, 4096, 256], P('scan', 'blk')
- grad_src: bfloat16 [4, 1024, 256], P('scan', 'blk')
- grad_w_query: float32 [256, 256], replicated
- grad_w_key: float32 [256, 256], replicated
- grad_w_value: float32 [256, 256], replicated
- grad_w_out: float32 [256, 256], replicated
Inputs may be any that keep to these rules, and one draw needn't show every extreme that they name: intersection[p, b, c] is 1 for c = b * 8 // 32, so every reference block and every source block of a pair has a listed partner.
All inputs are finite; a program needn't handle non-finite values.
Results may differ from a plain program's by a relative error of at most 0.035.
Values may be sent and summed in bfloat16 or wider, within the bound.
No kernel may reach another device: no remote copies, remote signals or barrier semaphores. Data moves between devices by JAX's collectives and lax.ppermute only.
A program may use at most 64 MiB of HBM per device.

v0:
```python
import math

import jax
import jax.numpy as jnp
from jax import lax
from jax.sharding import PartitionSpec as P

HEADS = 4
BLOCK = 128


NEG = -1e30


def combined_all(part, axis, combine):
    gathered = jax.tree.map(lambda a: lax.all_gather(a, axis), part)

    def take(source):
        return jax.tree.map(lambda a: lax.dynamic_index_in_dim(a, source, 0, False), gathered)

    return lax.fori_loop(
        1, lax.axis_size(axis), lambda source, state: combine(state, take(source)), take(0)
    )


def combine_stats(first_stats, second_stats):
    peak_now = jnp.maximum(first_stats[0], second_stats[0])
    total_now = first_stats[1] * jnp.exp(first_stats[0] - peak_now) + second_stats[1] * jnp.exp(
        second_stats[0] - peak_now
    )
    return (peak_now, total_now)


def exact_dot(left, right):
    return jnp.dot(left, right, precision=lax.Precision.HIGHEST)


def on_device(ref_feats, src_feats, grad_out, w_query, w_key, w_value, w_out, intersection):
    ref_rows = ref_feats[0]
    src_rows = src_feats[0]
    out_grad = grad_out[0]
    blocks = intersection[0] == 1
    query_count = ref_rows.shape[0]
    model_width = ref_rows.shape[1]
    head_count = HEADS
    head_dim = model_width // head_count
    score_scale = head_dim ** (-0.5)
    queries = jnp.dot(ref_rows, w_query, preferred_element_type=jnp.float32).astype(jnp.bfloat16)
    query_heads = queries.reshape(query_count, head_count, head_dim)
    grad_att = jnp.dot(out_grad, w_out.T, preferred_element_type=jnp.float32).astype(jnp.bfloat16)
    grad_heads = grad_att.reshape(query_count, head_count, head_dim)
    source_all = lax.all_gather(src_rows, "blk", axis=0, tiled=True)
    keys_all = jnp.dot(source_all, w_key, preferred_element_type=jnp.float32).astype(jnp.bfloat16)
    values_all = jnp.dot(source_all, w_value, preferred_element_type=jnp.float32).astype(
        jnp.bfloat16
    )
    key_total = keys_all.shape[0]

    def mask_blocks(first_row, tile_rows):
        return lax.dynamic_slice_in_dim(blocks, first_row // BLOCK, tile_rows // BLOCK, 1)

    def allowed_at(first_row, tile_rows):
        mask_piece = mask_blocks(first_row, tile_rows)
        mask_wide = jnp.broadcast_to(
            mask_piece[:, None, :, None], (mask_piece.shape[0], BLOCK, mask_piece.shape[1], BLOCK)
        )
        return mask_wide.reshape(query_count, tile_rows)[None]

    def key_heads(first_row, tile_rows):
        return lax.dynamic_slice_in_dim(keys_all, first_row, tile_rows, 0).reshape(
            tile_rows, head_count, head_dim
        )

    def value_heads(first_row, tile_rows):
        return lax.dynamic_slice_in_dim(values_all, first_row, tile_rows, 0).reshape(
            tile_rows, head_count, head_dim
        )

    def raw_scores(first_row, tile_rows):
        return (
            jnp.einsum(
                "ihc,jhc->hij",
                query_heads,
                key_heads(first_row, tile_rows),
                preferred_element_type=jnp.float32,
            )
            * score_scale
        )

    def sweep(update, carried, first_row, row_count):
        tile_rows = math.gcd(4 * BLOCK, row_count)

        def visit_tile(tile_index, state_now):
            tile_first = first_row + tile_index * tile_rows
            return update(state_now, tile_first, tile_rows)

        return lax.fori_loop(0, row_count // tile_rows, visit_tile, carried)

    def stats_update(state_now, first_row, tile_rows):
        row_peak, row_total, col_peak, col_total = state_now
        allowed = allowed_at(first_row, tile_rows)
        scores = raw_scores(first_row, tile_rows)
        masked = jnp.where(allowed, scores, NEG)
        peak_next = jnp.maximum(row_peak, masked.max(axis=2))
        row_total = row_total * jnp.exp(row_peak - peak_next) + jnp.where(
            allowed, jnp.exp(scores - peak_next[:, :, None]), 0.0
        ).sum(axis=2)
        tile_peak = masked.max(axis=1)
        tile_total = jnp.where(allowed, jnp.exp(scores - tile_peak[:, None, :]), 0.0).sum(axis=1)
        col_peak = lax.dynamic_update_slice_in_dim(col_peak, tile_peak, first_row, 1)
        col_total = lax.dynamic_update_slice_in_dim(col_total, tile_total, first_row, 1)
        return (peak_next, row_total, col_peak, col_total)

    row_start = jnp.full((head_count, query_count), NEG, jnp.float32)
    col_start = jnp.full((head_count, key_total), NEG, jnp.float32)
    row_peak, row_total, col_peak, col_total = sweep(
        stats_update,
        (row_start, jnp.zeros_like(row_start), col_start, jnp.zeros_like(col_start)),
        0,
        key_total,
    )
    col_peak, col_total = combined_all((col_peak, col_total), "blk", combine_stats)

    def probabilities(first_row, tile_rows):
        allowed = allowed_at(first_row, tile_rows)
        scores = raw_scores(first_row, tile_rows)
        peak_piece = lax.dynamic_slice_in_dim(col_peak, first_row, tile_rows, 1)
        total_piece = lax.dynamic_slice_in_dim(col_total, first_row, tile_rows, 1)
        row_prob = (
            jnp.where(allowed, jnp.exp(scores - row_peak[:, :, None]), 0.0) / row_total[:, :, None]
        )
        col_prob = (
            jnp.where(allowed, jnp.exp(scores - peak_piece[:, None, :]), 0.0)
            / total_piece[:, None, :]
        )
        return (row_prob, col_prob, (row_prob * col_prob).astype(jnp.bfloat16))

    def forward_update(state_now, first_row, tile_rows):
        attended, row_dot, col_dot = state_now
        row_prob, col_prob, match_prob = probabilities(first_row, tile_rows)
        value_piece = value_heads(first_row, tile_rows)
        attended = attended + jnp.einsum(
            "hij,jhc->ihc", match_prob, value_piece, preferred_element_type=jnp.float32
        )
        grad_prob = jnp.einsum(
            "ihc,jhc->hij", grad_heads, value_piece, preferred_element_type=jnp.float32
        )
        product = match_prob.astype(jnp.float32) * grad_prob
        row_dot = row_dot + product.sum(axis=2)
        col_dot = lax.dynamic_update_slice_in_dim(col_dot, product.sum(axis=1), first_row, 1)
        return (attended, row_dot, col_dot)

    attended, row_dot, col_dot = sweep(
        forward_update,
        (
            jnp.zeros((query_count, head_count, head_dim), jnp.float32),
            jnp.zeros((head_count, query_count), jnp.float32),
            jnp.zeros((head_count, key_total), jnp.float32),
        ),
        0,
        key_total,
    )
    attended_rows = attended.reshape(query_count, model_width).astype(jnp.bfloat16)
    matched = (
        ref_rows.astype(jnp.float32)
        + jnp.dot(attended_rows, w_out, preferred_element_type=jnp.float32)
    ).astype(jnp.bfloat16)
    col_dot = lax.psum(col_dot, "blk")

    def score_grads(first_row, tile_rows):
        row_prob, col_prob, match_prob = probabilities(first_row, tile_rows)
        grad_prob = jnp.einsum(
            "ihc,jhc->hij",
            grad_heads,
            value_heads(first_row, tile_rows),
            preferred_element_type=jnp.float32,
        )
        column_share = lax.dynamic_slice_in_dim(col_dot, first_row, tile_rows, 1)
        grad_score = score_scale * (
            2.0 * match_prob.astype(jnp.float32) * grad_prob
            - row_prob * row_dot[:, :, None]
            - col_prob * column_share[:, None, :]
        )
        return (match_prob, grad_score.astype(jnp.bfloat16))

    def tile_grads(grad_acc, first_row, tile_rows):
        match_prob, grad_score = score_grads(first_row, tile_rows)
        grad_acc = grad_acc + jnp.einsum(
            "hij,jhc->ihc",
            grad_score,
            key_heads(first_row, tile_rows),
            preferred_element_type=jnp.float32,
        )
        grad_keys = jnp.einsum(
            "hij,ihc->jhc", grad_score, query_heads, preferred_element_type=jnp.float32
        )
        grad_values = jnp.einsum(
            "hij,ihc->jhc", match_prob, grad_heads, preferred_element_type=jnp.float32
        )
        return (
            grad_acc,
            grad_keys.reshape(tile_rows, model_width),
            grad_values.reshape(tile_rows, model_width),
        )

    query_start = jnp.zeros((query_count, head_count, head_dim), jnp.float32)

    def buffer_update(state_now, first_row, tile_rows):
        grad_acc, grad_keys, grad_values = tile_grads(state_now[0], first_row, tile_rows)
        buffer_now = lax.dynamic_update_slice_in_dim(
            state_now[1], jnp.concatenate([grad_keys, grad_values], axis=1), first_row, 0
        )
        return (grad_acc, buffer_now)

    grad_query, key_buffer = sweep(
        buffer_update,
        (query_start, jnp.zeros((key_total, 2 * model_width), jnp.float32)),
        0,
        key_total,
    )
    summed = lax.psum_scatter(
        key_buffer.astype(jnp.bfloat16), "blk", scatter_dimension=0, tiled=True
    ).astype(jnp.float32)
    grad_keys = summed[:, :model_width]
    grad_values = summed[:, model_width:]
    grad_src = (
        exact_dot(grad_keys, w_key.T.astype(jnp.float32))
        + exact_dot(grad_values, w_value.T.astype(jnp.float32))
    ).astype(jnp.bfloat16)
    source_wide = src_rows.astype(jnp.float32)
    weight_key = exact_dot(source_wide.T, grad_keys)
    weight_value = exact_dot(source_wide.T, grad_values)
    grad_query = grad_query.reshape(query_count, model_width).astype(jnp.bfloat16)
    grad_ref = (
        out_grad.astype(jnp.float32)
        + jnp.dot(grad_query, w_query.T, preferred_element_type=jnp.float32)
    ).astype(jnp.bfloat16)
    weight_query = jnp.einsum("ic,id->cd", ref_rows, grad_query, preferred_element_type=jnp.float32)
    weight_out = jnp.einsum(
        "ic,id->cd", attended_rows, out_grad, preferred_element_type=jnp.float32
    )
    weight_totals = lax.psum((weight_query, weight_key, weight_value, weight_out), ("scan", "blk"))
    return (
        matched[None],
        grad_ref[None],
        grad_src[None],
        weight_totals[0],
        weight_totals[1],
        weight_totals[2],
        weight_totals[3],
    )


def solution(mesh):
    in_specs = (
        P("scan", "blk", None),
        P("scan", "blk", None),
        P("scan", "blk", None),
        P(),
        P(),
        P(),
        P(),
        P("scan", "blk", None),
    )
    out_specs = (
        P("scan", "blk", None),
        P("scan", "blk", None),
        P("scan", "blk", None),
        P(),
        P(),
        P(),
        P(),
    )
    return jax.shard_map(
        on_device, mesh=mesh, in_specs=in_specs, out_specs=out_specs, check_vma=False
    )
```

profile of v0, /device:TPU:0, one launch (start us, length us, event | category | flops | bytes accessed | tf_op | source)
XLA Modules:
  0.0 324.4 jit_solution(7546900038711364008)
XLA Ops:
  7.3 16.8 %all-gather = bf16[1,1024,256]{2,1,0:T(8,128)(2,1)S(1)} all-gather(bf16[1,128,256]{2,1,0:T(8,128)(2,1)} %param.17), channel_id=2, replica_groups=mesh['scan'=4,'blk'=8] {'blk'}, dimensions={1}, use_global_device_ids=true | all-gather | bytes 589824 | tf_op jit(solution)/shard_map/all_gather | solution.py:52
  26.7 14.4 %while.78 = (s32[]{:T(128)}, f32[4,512]{1,0:T(4,128)S(1)}, f32[4,512]{1,0:T(4,128)S(1)}, f32[4,1024]{1,0:T(4,128)S(1)}, f32[4,1024]{1,0:T(4,128)S(1)}, /*index=5...) while((s32[]{:T(128)}, f32[4,512]{1,0:T(4,128)S(1)}, ...), condition=%wide.region_5.6_spmd.clone, body=%wide.region_0.5_spmd.clone.sunk | while | flops 145758224 | bytes 10912189 | solution.py:97
  27.1 2.9 fusion.113
  30.1 3.8 %fusion.114 = (f32[4,512]{1,0:T(4,128)S(1)}, f32[4,512]{1,0:T(4,128)S(1)}) fusion(f32[4,512,512]{2,1,0:T(8,128)} %get-tuple-element.1532, f32[4,512]{1,0:T(4,128)S(1)} %get-tuple-element.1533, pred[512,512]{0,1:T(8,128)(4,1)S(1)} %bitcast.288, f32[4,512]{1,0:T(4,128)S(1)} %select_maximum_fusion.2), kind=kLoop, calls=%fused_computation.13.clone.1 | loop fusion | flops 7335936 | bytes 4489216 | tf_op jit(solution)/shard_map/while/body/eval_jaxpr/reduce_sum | solution.py:109
  34.3 2.9 fusion.113
  37.3 3.8 %fusion.114 = (f32[4,512]{1,0:T(4,128)S(1)}, f32[4,512]{1,0:T(4,128)S(1)}) fusion(f32[4,512,512]{2,1,0:T(8,128)} %get-tuple-element.1532, f32[4,512]{1,0:T(4,128)S(1)} %get-tuple-element.1533, pred[512,512]{0,1:T(8,128)(4,1)S(1)} %bitcast.288, f32[4,512]{1,0:T(4,128)S(1)} %select_maximum_fusion.2), kind=kLoop, calls=%fused_computation.13.clone.1 | loop fusion | flops 7335936 | bytes 4489216 | tf_op jit(solution)/shard_map/while/body/eval_jaxpr/reduce_sum | solution.py:109
  41.1 14.0 %all-gather.4 = f32[8,4,1024]{2,1,0:T(4,128)S(1)} all-gather(f32[1,4,1024]{2,1,0:T(4,128)S(1)} %bitcast.305), channel_id=4, replica_groups=mesh['scan'=4,'blk'=8] {'blk'}, dimensions={0}, use_global_device_ids=true | all-gather | bytes 147456 | tf_op jit(solution)/shard_map/all_gather | solution.py:16
  55.1 14.0 %all-gather.3 = f32[8,4,1024]{2,1,0:T(4,128)S(1)} all-gather(f32[1,4,1024]{2,1,0:T(4,128)S(1)} %bitcast.306), channel_id=3, replica_groups=mesh['scan'=4,'blk'=8] {'blk'}, dimensions={0}, use_global_device_ids=true | all-gather | bytes 147456 | tf_op jit(solution)/shard_map/all_gather | solution.py:16
  71.8 11.5 %while.79 = (s32[]{:T(128)}, f32[512,4,64]{0,2,1:T(8,128)}, f32[4,512]{1,0:T(4,128)S(1)}, f32[4,1024]{1,0:T(4,128)S(1)}, bf16[1024,256]{0,1:T(8,128)(2,1)}, /*in...) while((s32[]{:T(128)}, f32[512,4,64]{0,2,1:T(8,128)}, ...), condition=%wide.region_11.12_spmd.clone, body=%wide.region_8.11_spmd.clone.sunk | while | flops 416546816 | bytes 14017061 | solution.py:97
  72.3 2.5 fusion.122
  77.5 2.5 fusion.122
  81.0 2.3 fusion.123
  83.3 29.6 %psum.35 = f32[4,1024]{1,0:T(4,128)} all-reduce(f32[4,1024]{1,0:T(4,128)S(1)} %get-tuple-element.993), channel_id=1, replica_groups=mesh['scan'=4,'blk'=8] {'blk'}, use_global_device_ids=true, to_apply=%region_12.13 | all-reduce | flops 4096 | bytes 32768 | tf_op jit(solution)/shard_map/psum | solution.py:168
  114.0 28.2 %while.80 = (s32[]{:T(128)}, f32[512,4,64]{0,2,1:T(8,128)}, bf16[1024,512]{0,1:T(8,128)(2,1)}, bf16[1024,256]{0,1:T(8,128)(2,1)S(1)}, pred[4,8]{0,1:T(8,128)(4,1...) while((s32[]{:T(128)}, f32[512,4,64]{0,2,1:T(8,128)}, ...), condition=%wide.region_14.15_spmd.clone, body=%wide.region_13.14_spmd.clone.sunk | while | flops 700710912 | bytes 27198500 | solution.py:97
  117.3 4.2 %fusion.135 = bf16[4,512,512]{1,2,0:T(8,128)(2,1)S(1)} fusion(bf16[512,4,64]{0,2,1:T(8,128)(2,1)S(1)} %bitcast.298, bf16[512,4,64]{0,2,1:T(8,128)(2,1)S(1)} %copy-done.17, f32[4,512]{1,0:T(4,128)S(1)} %get-tuple-element.1571, f32[4,512]{1,0:T(4,128)} %copy-done.20, f32[4,512]{1,0:T(4,128)} %copy-done.18, f32[4,512]{1,0:T(4,128)} %copy-done.8, ...), kind=kOutput, calls=%fused_computation.47.clone.1 | convolution fusion | flops 153092096 | bytes 7127040 | tf_op jit(solution)/shard_map/while/body/eval_jaxpr/ihc,jhc->hij/dot_general | solution.py:172
  122.3 3.0 fusion.137
  130.9 4.2 %fusion.135 = bf16[4,512,512]{1,2,0:T(8,128)(2,1)S(1)} fusion(bf16[512,4,64]{0,2,1:T(8,128)(2,1)S(1)} %bitcast.298, bf16[512,4,64]{0,2,1:T(8,128)(2,1)S(1)} %copy-done.17, f32[4,512]{1,0:T(4,128)S(1)} %get-tuple-element.1571, f32[4,512]{1,0:T(4,128)} %copy-done.20, f32[4,512]{1,0:T(4,128)} %copy-done.18, f32[4,512]{1,0:T(4,128)} %copy-done.8, ...), kind=kOutput, calls=%fused_computation.47.clone.1 | convolution fusion | flops 153092096 | bytes 7127040 | tf_op jit(solution)/shard_map/while/body/eval_jaxpr/ihc,jhc->hij/dot_general | solution.py:172
  135.9 3.0 fusion.137
  139.9 2.3 fusion.136
  142.3 2.4 copy.51
  147.8 27.5 %reduce-scatter.4.cloned.1.call-done = bf16[128,512]{1,0:T(8,128)(2,1)} async-done(((bf16[1024,512]{1,0:T(8,128)(2,1)}), bf16[128,512]{1,0:T(8,128)(2,1)}) %reduce-scatter.4.cloned.1.call-update) | async-done | bytes 131088
  183.5 127.0 %all-reduce.3.cloned.1.call-done = (f32[256,256]{0,1:T(8,128)}, f32[256,256]{0,1:T(8,128)}, f32[256,256]{0,1:T(8,128)}, f32[256,256]{1,0:T(8,128)}) async-done(((f32[256,256]{0,1:T(8,128)}, f32[256,256]{0,1:T(8,128)}, f32[256,256]{0,1:T(8,128)}, f32[256,256]{1,0:T(8,128)}), (f32[256,256]{0,1:T(8,128)}, f32[256,256]{0,1:T(8,128)}, f32[256,256]{0,1:T(8,128)}, ...) | async-done | bytes 1048592 | tf_op jit(solution)/shard_map/psum | solution.py:242
  310.5 1.8 copy.44
  312.3 1.8 copy.45
  (171 shorter events, 37.3 us)
Async XLA Ops:
  7.2 16.9 %copy-start = (bf16[256,256]{1,0:T(8,128)(2,1)S(1)}, bf16[256,256]{1,0:T(8,128)(2,1)}, u32[]{:S(2)}) copy-start(bf16[256,256]{1,0:T(8,128)(2,1)} %param.20) | copy-start | bytes 393220
  7.2 168.1 %reduce-scatter.4.cloned.1.call-start = ((), (), s32[]{:S(2)}) async-start(), calls=%async_computation.1 | async-start | bytes 1179648
  26.6 42.8 %copy-start.14 = (bf16[256,256]{1,0:T(8,128)(2,1)S(1)}, bf16[256,256]{1,0:T(8,128)(2,1)}, u32[]{:S(2)}) copy-start(bf16[256,256]{1,0:T(8,128)(2,1)} %param.21) | copy-start | bytes 393220
  26.7 44.2 %copy-start.3 = (bf16[1,512,256]{2,1,0:T(8,128)(2,1)S(1)}, bf16[1,512,256]{2,1,0:T(8,128)(2,1)}, u32[]{:S(2)}) copy-start(bf16[1,512,256]{2,1,0:T(8,128)(2,1)} %param.18) | copy-start | bytes 786436
  26.7 44.2 %copy-start.12 = (bf16[256,256]{1,0:T(8,128)(2,1)S(1)}, bf16[256,256]{1,0:T(8,128)(2,1)}, u32[]{:S(2)}) copy-start(bf16[256,256]{1,0:T(8,128)(2,1)} %param.22) | copy-start | bytes 393220
  72.2 2.5 copy-start.1
  72.3 2.5 copy-start.16
  77.5 2.5 copy-start.1
  77.5 2.5 copy-start.16
  114.8 2.5 copy-start.17
  128.4 2.5 copy-start.17
  138.9 3.3 %copy-start.7 = (f32[4,1024]{1,0:T(4,128)S(1)}, f32[4,1024]{1,0:T(4,128)}, u32[]{:S(2)}) copy-start(f32[4,1024]{1,0:T(4,128)} %copy-done.6) | copy-start | bytes 49156 | tf_op jit(solution)/shard_map/while
  138.9 3.3 %copy-start.9 = (f32[4,512]{1,0:T(4,128)S(1)}, f32[4,512]{1,0:T(4,128)}, u32[]{:S(2)}) copy-start(f32[4,512]{1,0:T(4,128)} %copy-done.8) | copy-start | bytes 24580 | tf_op jit(solution)/shard_map/while
  139.0 3.3 %copy-start.19 = (f32[4,512]{1,0:T(4,128)S(1)}, f32[4,512]{1,0:T(4,128)}, u32[]{:S(2)}) copy-start(f32[4,512]{1,0:T(4,128)} %copy-done.18) | copy-start | bytes 24580 | tf_op jit(solution)/shard_map/while
  139.0 3.2 %copy-start.21 = (f32[4,512]{1,0:T(4,128)S(1)}, f32[4,512]{1,0:T(4,128)}, u32[]{:S(2)}) copy-start(f32[4,512]{1,0:T(4,128)} %copy-done.20) | copy-start | bytes 24580 | tf_op jit(solution)/shard_map/while
  139.0 3.2 copy-start.23
  142.2 3.6 %copy-start.2 = (f32[512,4,64]{0,2,1:T(8,128)S(1)}, f32[512,4,64]{0,2,1:T(8,128)}, u32[]{:S(2)}) copy-start(f32[512,4,64]{0,2,1:T(8,128)} %get-tuple-element.991) | copy-start | bytes 1572868
  142.2 3.7 %copy-start.5 = (bf16[1,512,256]{2,1,0:T(8,128)(2,1)S(1)}, bf16[1,512,256]{2,1,0:T(8,128)(2,1)}, u32[]{:S(2)}) copy-start(bf16[1,512,256]{2,1,0:T(8,128)(2,1)} %param.16) | copy-start | bytes 786436
  142.3 4.6 %copy-start.4 = (bf16[1,512,256]{2,1,0:T(8,128)(2,1)S(1)}, bf16[1,512,256]{2,1,0:T(8,128)(2,1)}, u32[]{:S(2)}) copy-start(bf16[1,512,256]{2,1,0:T(8,128)(2,1)} %param.18) | copy-start | bytes 786436
  142.3 33.1 %copy-start.10 = (bf16[1,128,256]{2,1,0:T(8,128)(2,1)S(1)}, bf16[1,128,256]{2,1,0:T(8,128)(2,1)}, u32[]{:S(2)}) copy-start(bf16[1,128,256]{2,1,0:T(8,128)(2,1)} %param.17) | copy-start | bytes 196612
  142.3 36.6 %copy-start.11 = (bf16[256,256]{1,0:T(8,128)(2,1)S(1)}, bf16[256,256]{1,0:T(8,128)(2,1)}, u32[]{:S(2)}) copy-start(bf16[256,256]{1,0:T(8,128)(2,1)} %param.19) | copy-start | bytes 393220
  142.3 37.5 %copy-start.13 = (bf16[256,256]{1,0:T(8,128)(2,1)S(1)}, bf16[256,256]{1,0:T(8,128)(2,1)}, u32[]{:S(2)}) copy-start(bf16[256,256]{1,0:T(8,128)(2,1)} %param.22) | copy-start | bytes 393220
  144.7 37.1 %copy-start.15 = (bf16[256,256]{1,0:T(8,128)(2,1)S(1)}, bf16[256,256]{1,0:T(8,128)(2,1)}, u32[]{:S(2)}) copy-start(bf16[256,256]{1,0:T(8,128)(2,1)} %param.21) | copy-start | bytes 393220
  144.7 165.8 %all-reduce.3.cloned.1.call-start = ((), (), s32[]{:S(2)}) async-start(), calls=%async_computation.2 | async-start | bytes 2097152 | tf_op jit(solution)/shard_map/psum | solution.py:242
  (15 other events, 17.1 us)
Sparse Core Ops, SparseCore 0:
  144.9 30.4 reduce-scatter.3
  181.4 129.0 all-reduce.2
where the time goes:
time: 325 us; the launch traced here: 324 us
  waiting for transfers between devices  155 us (48%)
  blocking collectives  74.4 us (23%)
  matrix products  50.1 us (15%)
  local copies, waits for them, and re-layouts  18.6 us (6%)
  between operations  14.3 us (4%)
  other arithmetic  11.5 us (4%)
    psum x1, waiting for transfers between devices, on_device(): lax.psum((weight_query, weight_key, weight_value, weight_out), ('scan', '...  127 us
    psum x1, blocking collectives, on_device(): col_dot = lax.psum(col_dot, 'blk')  29.6 us
    all_gather x2, blocking collectives, combined_all(): gathered = jax.tree.map(lambda a: lax.all_gather(a, axis), part)  28 us
    unnamed x3, waiting for transfers between devices  27.6 us
    all_gather x1, blocking collectives, on_device(): source_all = lax.all_gather(src_rows, 'blk', axis=0, tiled=True)  16.8 us
    dot_general x6, matrix products, raw_scores(): jnp.einsum('ihc,jhc->hij', query_heads, key_heads(first_row, tile_rows),...  12.3 us
    unnamed x30, local copies, waits for them, and re-layouts  10.8 us
    dot_general x2, matrix products, score_grads(): jnp.einsum('ihc,jhc->hij', grad_heads, value_heads(first_row, tile_rows),...  8.48 us
  transfers between devices with their start and end apart: 2, of which 2 were waited for; matrix products, arithmetic and copies ran while one was open for 2% of the time, Pallas kernels for 0%

commit v1 on v0

v1 whole, which is shorter than its diff:
```python
import functools

import jax
import jax.numpy as jnp
from jax import lax
from jax.experimental import pallas as pl
from jax.experimental.pallas import tpu as pltpu
from jax.sharding import PartitionSpec as P

HEADS = 4
BLOCK = 128
NEG = -1e30
FLOOR = -1e29
VMEM_LIMIT = 56 * 1024 * 1024

NT = (((1,), (1,)), ((), ()))
TN = (((0,), (0,)), ((), ()))
TT = (((0,), (1,)), ((), ()))


def mm(left, right):
    return jnp.dot(left, right, preferred_element_type=jnp.float32)


def mm_general(left, right, dims):
    return lax.dot_general(left, right, dims, preferred_element_type=jnp.float32)


def bf(x):
    return x.astype(jnp.bfloat16)


def lane_head(shape, head_dim):
    return lax.broadcasted_iota(jnp.int32, shape, 1) // head_dim


def fill_bias(inter_ref, bias_ref, head_dim):
    query_blocks, key_blocks = inter_ref.shape
    width = bias_ref.shape[1]
    lane = lax.broadcasted_iota(jnp.int32, (1, width), 1) % head_dim
    for key_block in range(key_blocks):
        row = jnp.zeros((1, width), jnp.float32)
        for query_block in range(query_blocks):
            listed = inter_ref[query_block, key_block] == 1
            row = jnp.where(lane == query_block, jnp.where(listed, 0.0, NEG), row)
        bias_ref[pl.ds(key_block * BLOCK, BLOCK), :] = bf(
            jnp.broadcast_to(row, (BLOCK, width))
        )


def masked_query(head, queries, head_dim):
    rows, width = queries.shape
    heads = width // head_dim
    lanes = lane_head((rows, width), head_dim)
    lane = lax.broadcasted_iota(jnp.int32, (rows, width), 1)
    block = lax.broadcasted_iota(jnp.int32, (rows, width), 0) // BLOCK
    other = (head + 1) % heads
    hot = jnp.where((lanes == other) & (lane - other * head_dim == block), 1.0, 0.0)
    return bf(jnp.where(lanes == head, queries.astype(jnp.float32), hot))


def masked_key(head, keys, bias, head_dim):
    heads = keys.shape[1] // head_dim
    lanes = lane_head(keys.shape, head_dim)
    other = jnp.where(lanes == (head + 1) % heads, bias.astype(jnp.float32), 0.0)
    return bf(jnp.where(lanes == head, keys.astype(jnp.float32), other))


def only_head(head, values, head_dim):
    lanes = lane_head(values.shape, head_dim)
    return bf(jnp.where(lanes == head, values.astype(jnp.float32), 0.0))


def fill_scores(head, query_ref, key_ref, bias_ref, grad_ref, value_ref, score_ref, prob_ref, head_dim):
    left = masked_query(head, query_ref[...], head_dim)
    left_grad = only_head(head, grad_ref[...], head_dim)
    key_total = key_ref.shape[0]
    step = min(256, key_total)
    for first in range(0, key_total, step):
        span = pl.ds(first, step)
        right = masked_key(head, key_ref[span, :], bias_ref[span, :], head_dim)
        score_ref[:, span] = mm_general(left, right, NT)
        prob_ref[:, span] = mm_general(left_grad, value_ref[span, :], NT)


def stats_kernel(
    head_count, inter_ref, ref_ref, gout_ref, src_ref, wq_ref, wk_ref, wv_ref, wo_ref,
    row_ref, col_ref, query_ref, grad_ref, key_ref, value_ref, bias_ref, score_ref, prob_ref,
):
    rows, width = ref_ref.shape
    key_total = src_ref.shape[0]
    head_dim = width // head_count
    scale = head_dim ** -0.5
    query_ref[...] = bf(bf(mm(ref_ref[...], wq_ref[...])).astype(jnp.float32) * scale)
    grad_ref[...] = bf(mm_general(gout_ref[...], wo_ref[...], NT))
    key_ref[...] = bf(mm(src_ref[...], wk_ref[...]))
    value_ref[...] = bf(mm(src_ref[...], wv_ref[...]))
    fill_bias(inter_ref, bias_ref, head_dim)
    for head in range(head_count):
        fill_scores(
            head, query_ref, key_ref, bias_ref, grad_ref, value_ref, score_ref, prob_ref, head_dim
        )

        def peaks(step, col_peak):
            span = pl.ds(step * 8, 8)
            scores = score_ref[span, :]
            row_ref[span, head : head + 1] = scores.max(axis=1, keepdims=True)
            return jnp.maximum(col_peak, scores)

        col_peak = lax.fori_loop(
            0, rows // 8, peaks, jnp.full((8, key_total), FLOOR, jnp.float32), unroll=4
        )
        col_peak = jnp.broadcast_to(col_peak.max(axis=0, keepdims=True), (8, key_total))
        col_ref[head : head + 1, :] = col_peak[:1]

        def totals(step, col_total):
            span = pl.ds(step * 8, 8)
            scores = score_ref[span, :]
            row_exp = jnp.exp(scores - row_ref[span, head : head + 1])
            row_total = row_exp.sum(axis=1, keepdims=True)
            at = head_count + head
            row_ref[span, at : at + 1] = 1.0 / row_total
            col_exp = jnp.exp(scores - col_peak)
            prob_ref[span, :] = row_exp * col_exp * prob_ref[span, :]
            return col_total + col_exp

        zero = jnp.zeros((8, key_total), jnp.float32)
        col_total = lax.fori_loop(0, rows // 8, totals, zero, unroll=2)
        at = head_count + head
        col_ref[at : at + 1, :] = col_total.sum(axis=0, keepdims=True)

        def dots(step, col_dot):
            span = pl.ds(step * 8, 8)
            at = head_count + head
            return col_dot + prob_ref[span, :] * row_ref[span, at : at + 1]

        col_dot = lax.fori_loop(0, rows // 8, dots, zero, unroll=4)
        at = 2 * head_count + head
        col_ref[at : at + 1, :] = col_dot.sum(axis=0, keepdims=True)


def grads_kernel(
    head_count, inter_ref, ref_ref, gout_ref, src_ref, wq_ref, wk_ref, wv_ref, wo_ref, row_ref, all_ref,
    matched_ref, gref_ref, gsrc_ref, weight_ref,
    query_ref, grad_ref, key_ref, value_ref, bias_ref, score_ref, prob_ref,
    match_ref, gscore_ref, query_t_ref, grad_t_ref, gkey_ref, gvalue_ref, att_ref, gquery_ref, col_ref,
):
    rows, width = ref_ref.shape
    key_total = src_ref.shape[0]
    head_dim = width // head_count
    scale = head_dim ** -0.5
    queries = bf(mm(ref_ref[...], wq_ref[...])).astype(jnp.float32)
    query_ref[...] = bf(queries * scale)
    grad_ref[...] = bf(mm_general(gout_ref[...], wo_ref[...], NT))
    queries_t = bf(mm_general(wq_ref[...], ref_ref[...], TT)).astype(jnp.float32)
    query_t_ref[...] = bf(queries_t * (2.0 * scale))
    grad_t_ref[...] = bf(mm_general(wo_ref[...], gout_ref[...], NT))
    key_ref[...] = bf(mm(src_ref[...], wk_ref[...]))
    value_ref[...] = bf(mm(src_ref[...], wv_ref[...]))
    fill_bias(inter_ref, bias_ref, head_dim)

    devices = all_ref.shape[0]
    peak = all_ref[0, :head_count, :]
    for device in range(1, devices):
        peak = jnp.maximum(peak, all_ref[device, :head_count, :])
    total = jnp.zeros_like(peak)
    dots = jnp.zeros_like(peak)
    for device in range(devices):
        factor = jnp.exp(all_ref[device, :head_count, :] - peak)
        total = total + factor * all_ref[device, head_count : 2 * head_count, :]
        dots = dots + factor * all_ref[device, 2 * head_count : 3 * head_count, :]
    inverse = 1.0 / total
    col_ref[:head_count, :] = peak
    col_ref[head_count : 2 * head_count, :] = inverse
    col_ref[2 * head_count : 3 * head_count, :] = dots * inverse * 0.5

    for head in range(head_count):
        fill_scores(
            head, query_ref, key_ref, bias_ref, grad_ref, value_ref, score_ref, prob_ref, head_dim
        )
        strip = 16

        def col_row(kind):
            at = kind * head_count + head
            return jnp.broadcast_to(col_ref[at : at + 1, :], (8, key_total))

        col_peak, col_inverse, col_half = col_row(0), col_row(1), col_row(2)

        def tile(step, carry):
            matches, grads = [], []
            for part in range(strip // 8):
                span = pl.ds(step * strip + part * 8, 8)
                scores = score_ref[span, :]
                row_inverse = row_ref[span, head_count + head : head_count + head + 1]
                row_prob = jnp.exp(scores - row_ref[span, head : head + 1]) * row_inverse
                col_prob = jnp.exp(scores - col_peak) * col_inverse
                match = row_prob * col_prob
                product = match * prob_ref[span, :]
                row_half = product.sum(axis=1, keepdims=True) * 0.5
                grads.append(product - row_prob * row_half - col_prob * col_half)
                matches.append(match)
            span = pl.ds(step * strip, strip)
            match_ref[span, :] = bf(jnp.concatenate(matches, axis=0))
            gscore_ref[span, :] = bf(jnp.concatenate(grads, axis=0))
            return carry

        lax.fori_loop(0, rows // strip, tile, 0)

        values = only_head(head, value_ref[...], head_dim)
        keys = only_head(head, key_ref[...].astype(jnp.float32) * (2.0 * scale), head_dim)
        attended = mm(match_ref[...], values)
        gquery = mm(gscore_ref[...], keys)
        if head == 0:
            att_ref[...] = attended
            gquery_ref[...] = gquery
        else:
            att_ref[...] += attended
            gquery_ref[...] += gquery
        span = pl.ds(head * head_dim, head_dim)
        gkey_ref[span, :] = bf(mm(query_t_ref[span, :], gscore_ref[...]))
        gvalue_ref[span, :] = bf(mm(grad_t_ref[span, :], match_ref[...]))

    attended = bf(att_ref[...])
    gquery = bf(gquery_ref[...])
    matched_ref[...] = bf(ref_ref[...].astype(jnp.float32) + mm(attended, wo_ref[...]))
    gref_ref[...] = bf(
        gout_ref[...].astype(jnp.float32) + mm_general(gquery, wq_ref[...], NT)
    )
    gsrc_t = mm(wk_ref[...], gkey_ref[...]) + mm(wv_ref[...], gvalue_ref[...])
    gsrc_ref[...] = bf(gsrc_t.T)
    weight_ref[0] = bf(mm_general(ref_ref[...], gquery, TN))
    weight_ref[1] = bf(mm(gkey_ref[...], src_ref[...]).T)
    weight_ref[2] = bf(mm(gvalue_ref[...], src_ref[...]).T)
    weight_ref[3] = bf(mm_general(attended, gout_ref[...], TN))


def vmem_call(kernel, name, out_shape, scratch, flops, moved, args):
    specs = [pl.BlockSpec(memory_space=pltpu.SMEM)]
    specs += [pl.BlockSpec(memory_space=pltpu.VMEM)] * (len(args) - 1)
    return pl.pallas_call(
        kernel,
        name=name,
        out_shape=out_shape,
        in_specs=specs,
        out_specs=[pl.BlockSpec(memory_space=pltpu.VMEM)] * len(out_shape),
        scratch_shapes=scratch,
        compiler_params=pltpu.CompilerParams(vmem_limit_bytes=VMEM_LIMIT),
        cost_estimate=pl.CostEstimate(flops=flops, bytes_accessed=moved, transcendentals=0),
    )(*args)


def on_device(ref_feats, src_feats, grad_out, w_query, w_key, w_value, w_out, intersection):
    ref_rows = ref_feats[0]
    src_rows = src_feats[0]
    out_grad = grad_out[0]
    listed = intersection[0]
    rows, width = ref_rows.shape
    blk = lax.axis_size("blk")
    everyone = lax.axis_size("scan") * blk
    key_rows = src_rows.shape[0]
    key_total = key_rows * blk
    source_all = lax.all_gather(src_rows, "blk", axis=0, tiled=True)

    f32, b16 = jnp.float32, jnp.bfloat16
    shape = jax.ShapeDtypeStruct
    common = [
        pltpu.VMEM((rows, width), b16),
        pltpu.VMEM((rows, width), b16),
        pltpu.VMEM((key_total, width), b16),
        pltpu.VMEM((key_total, width), b16),
        pltpu.VMEM((key_total, width), b16),
        pltpu.VMEM((rows, key_total), f32),
        pltpu.VMEM((rows, key_total), f32),
    ]
    base = (listed, ref_rows, out_grad, source_all, w_query, w_key, w_value, w_out)
    tile_flops = 2 * rows * key_total * width
    row_stats, col_stats = vmem_call(
        functools.partial(stats_kernel, HEADS),
        "match_stats",
        [shape((rows, 2 * HEADS), f32), shape((3 * HEADS, key_total), f32)],
        common,
        2 * tile_flops,
        2 << 20,
        base,
    )
    all_stats = lax.all_gather(col_stats, "blk", axis=0)
    matched, grad_ref, source_part, weight_part = vmem_call(
        functools.partial(grads_kernel, HEADS),
        "match_grads",
        [
            shape((rows, width), b16),
            shape((rows, width), b16),
            shape((key_total, width), b16),
            shape((4, width, width), b16),
        ],
        common
        + [
            pltpu.VMEM((rows, key_total), b16),
            pltpu.VMEM((rows, key_total), b16),
            pltpu.VMEM((width, rows), b16),
            pltpu.VMEM((width, rows), b16),
            pltpu.VMEM((width, key_total), b16),
            pltpu.VMEM((width, key_total), b16),
            pltpu.VMEM((rows, width), f32),
            pltpu.VMEM((rows, width), f32),
            pltpu.VMEM((3 * HEADS, key_total), f32),
        ],
        6 * tile_flops,
        4 << 20,
        base + (row_stats, all_stats),
    )

    source_parts = lax.all_to_all(
        source_part.reshape(blk, key_rows, width), "blk", split_axis=0, concat_axis=0
    )
    grad_src = source_parts.astype(f32).sum(axis=0).astype(b16)

    weight_rows = 4 * width // everyone
    weight_parts = lax.all_to_all(
        weight_part.reshape(everyone, weight_rows, width), ("scan", "blk"), split_axis=0, concat_axis=0
    )
    weight_sum = weight_parts.astype(f32).sum(axis=0).astype(b16)
    weights = lax.all_gather(weight_sum, ("scan", "blk"), axis=0, tiled=True)
    weights = weights.astype(f32).reshape(4, width, width)
    return (
        matched[None],
        grad_ref[None],
        grad_src[None],
        weights[0],
        weights[1],
        weights[2],
        weights[3],
    )


def solution(mesh):
    split = P("scan", "blk", None)
    whole = P()
    return jax.shard_map(
        on_device,
        mesh=mesh,
        in_specs=(split, split, split, whole, whole, whole, whole, split),
        out_specs=(split, split, split, whole, whole, whole, whole),
        check_vma=False,
    )
```

time: 325 us -> 187 us (0.58)
  waiting for transfers between devices: 155 us -> 15.6 us
  Pallas kernels: 0 us -> 70.8 us
  matrix products: 50.1 us -> 0 us
  blocking collectives: 74.4 us -> 94.3 us
  local copies, waits for them, and re-layouts: 18.6 us -> 0.98 us
  between operations: 14.3 us -> 0.65 us
  other arithmetic: 11.5 us -> 0.79 us
  starting transfers between devices: 0.08 us -> 3.49 us
    psum x1 -> x0, waiting for transfers between devices: 127 us -> none  [on_device(): lax.psum((weight_query, weight_key, weight_value, weight_out), ('scan', '...]
    pallas_call x0 -> x2, Pallas kernels: none -> 70.8 us  [vmem_call(): pl.pallas_call(kernel, name=name, out_shape=out_shape, in_specs=specs, ou...]
    dot_general x30 -> x0, matrix products: 50.1 us -> none  [the longest x6 12.3 us: raw_scores(): jnp.einsum('ihc,jhc->hij', query_heads, key_heads(first_row, tile_rows),...]
    psum x1 -> x0, blocking collectives: 29.6 us -> none  [on_device(): col_dot = lax.psum(col_dot, 'blk')]
    all_gather x2, blocking collectives: 28 us -> 56.5 us  [the longest x1 40.3 us: on_device(): weights = lax.all_gather(weight_sum, ('scan', 'blk'), axis=0, tiled=True)]
    unnamed x3 -> x0, waiting for transfers between devices: 27.6 us -> none
    all_to_all x0 -> x1, blocking collectives: none -> 20.1 us  [on_device(): lax.all_to_all(source_part.reshape(blk, key_rows, width), 'blk', split_ax...]
    all_to_all x0 -> x1, waiting for transfers between devices: none -> 15.6 us  [on_device(): lax.all_to_all(weight_part.reshape(everyone, weight_rows, width), ('scan'...]
  transfers between devices with their start and end apart: 2 -> 1, of which waited for: 2 -> 1; matrix products, arithmetic and copies ran while one was open for 2% -> 0% of each run, Pallas kernels for 0% -> 0%
where the time goes in v1:
time: 187 us
  blocking collectives  94.3 us (50%)
  Pallas kernels  70.8 us (38%)
  waiting for transfers between devices  15.6 us (8%)
  starting transfers between devices  3.49 us (2%)
    pallas_call x2, Pallas kernels, vmem_call(): pl.pallas_call(kernel, name=name, out_shape=out_shape, in_specs=specs, ou...  70.8 us
    all_gather x1, blocking collectives, on_device(): weights = lax.all_gather(weight_sum, ('scan', 'blk'), axis=0, tiled=True)  40.3 us
    all_to_all x1, blocking collectives, on_device(): lax.all_to_all(source_part.reshape(blk, key_rows, width), 'blk', split_ax...  20.1 us
    all_gather x1, blocking collectives, on_device(): source_all = lax.all_gather(src_rows, 'blk', axis=0, tiled=True)  17.8 us
    all_gather x1, blocking collectives, on_device(): all_stats = lax.all_gather(col_stats, 'blk', axis=0)  16.2 us
    all_to_all x1, waiting for transfers between devices, on_device(): lax.all_to_all(weight_part.reshape(everyone, weight_rows, width), ('scan'...  15.6 us
  transfers between devices with their start and end apart: 1, of which 1 were waited for; matrix products, arithmetic and copies ran while one was open for 0% of the time, Pallas kernels for 0%

profile of v1, /device:TPU:0, one launch (start us, length us, event | category | flops | bytes accessed | tf_op | source)
XLA Modules:
  0.0 186.7 jit_solution(18069427886968164854)
XLA Ops:
  0.6 17.8 %all-gather = bf16[1,1024,256]{2,1,0:T(8,128)(2,1)} all-gather(bf16[1,128,256]{2,1,0:T(8,128)(2,1)} %param.9), channel_id=2, replica_groups=mesh['scan'=4,'blk'=8] {'blk'}, dimensions={1}, use_global_device_ids=true | all-gather | bytes 589824 | tf_op jit(solution)/shard_map/all_gather | solution.py:262
  18.4 37.8 %match_stats.1 = (f32[512,8]{1,0:T(8,128)}, f32[12,1024]{1,0:T(8,128)}) custom-call(s32[4,8]{1,0:T(4,128)} %bitcast.19, bf16[512,256]{1,0:T(8,128)(2,1)} %bitcast.15, bf16[512,256]{1,0:T(8,128)(2,1)} %bitcast.17, bf16[1024,256]{1,0:T(8,128)(2,1)} %bitcast.10, bf16[256,256]{1,0:T(8,128)(2,1)} %wq_ref.3, bf16[256,256]{1,0:T(8,128)(2,1)} %wk_ref.3, ...), custom_call_target="tpu_custom_call" | custom-call | flops 536870912 | bytes 2097152 | tf_op jit(solution)/shard_map/match_stats/pallas_call | solution.py:240
  56.2 16.2 %all-gather.2.all_ref = f32[8,12,1024]{2,1,0:T(8,128)} all-gather(f32[1,12,1024]{2,1,0:T(8,128)} %bitcast.13), channel_id=3, replica_groups=mesh['scan'=4,'blk'=8] {'blk'}, dimensions={0}, use_global_device_ids=true | all-gather | bytes 442368 | tf_op jit(solution)/shard_map/all_gather | solution.py:286
  72.4 33.0 %match_grads.1 = (bf16[512,256]{1,0:T(8,128)(2,1)}, bf16[512,256]{1,0:T(8,128)(2,1)}, bf16[1024,256]{1,0:T(8,128)(2,1)}, bf16[4,256,256]{2,1,0:T(8,128)(2,1)}) custom-call(s32[4,8]{1,0:T(4,128)} %bitcast.20, bf16[512,256]{1,0:T(8,128)(2,1)} %bitcast.16, bf16[512,256]{1,0:T(8,128)(2,1)} %bitcast.18, bf16[1024,256]{1,0:T(8,128)(2,1)} %bitcast.11, ...), custom_call_target="tpu_custom_call" | custom-call | flops 1610612736 | bytes 4194304 | tf_op jit(solution)/shard_map/match_grads/pallas_call | solution.py:240
  105.4 20.1 %all_to_all.10 = bf16[8,128,256]{2,1,0:T(8,128)(2,1)S(1)} all-to-all(bf16[8,128,256]{2,1,0:T(8,128)(2,1)} %bitcast.12), channel_id=1, replica_groups=mesh['scan'=4,'blk'=8] {'blk'}, dimensions={0} | all-to-all | bytes 1048576 | tf_op jit(solution)/shard_map/all_to_all | solution.py:313
  125.5 3.5 %all-to-all-start.1 = ((bf16[32,32,256]{2,1,0:T(8,128)(2,1)}), bf16[32,32,256]{2,1,0:T(8,128)(2,1)S(1)}, u32[]{:S(2)}, u32[]{:S(2)}) async-start(bf16[32,32,256]{2,1,0:T(8,128)(2,1)} %bitcast.9), calls=%async_computation.1 | async-start | bytes 1048576 | tf_op jit(solution)/shard_map/all_to_all | solution.py:319
  129.0 0.7 reduce_sum.24
  129.7 15.6 %all-to-all-done.1 = bf16[32,32,256]{2,1,0:T(8,128)(2,1)S(1)} async-done(((bf16[32,32,256]{2,1,0:T(8,128)(2,1)}), bf16[32,32,256]{2,1,0:T(8,128)(2,1)S(1)}, u32[]{:S(2)}, u32[]{:S(2)}) %all-to-all-start.1) | async-done | bytes 524320 | tf_op jit(solution)/shard_map/all_to_all | solution.py:319
  145.3 0.1 reduce_sum.25
  145.4 40.3 %all_gather.15 = bf16[1024,256]{1,0:T(8,128)(2,1)S(1)} all-gather(bf16[32,256]{1,0:T(8,128)(2,1)S(1)} %reduce_sum.25), channel_id=1, replica_groups=mesh['scan'=4,'blk'=8] {'scan','blk'}, dimensions={0}, use_global_device_ids=true | all-gather | bytes 540672 | tf_op jit(solution)/shard_map/all_gather | solution.py:323
  185.7 1.0 fusion
Async XLA Ops:
  125.5 19.8 %all-to-all-start.1 = ((bf16[32,32,256]{2,1,0:T(8,128)(2,1)}), bf16[32,32,256]{2,1,0:T(8,128)(2,1)S(1)}, u32[]{:S(2)}, u32[]{:S(2)}) async-start(bf16[32,32,256]{2,1,0:T(8,128)(2,1)} %bitcast.9), calls=%async_computation.1 | async-start | bytes 1048576 | tf_op jit(solution)/shard_map/all_to_all | solution.py:319

commit v2 on v1

v2 whole, which is shorter than its diff:
```python
import functools

import jax
import jax.numpy as jnp
from jax import lax
from jax.experimental import pallas as pl
from jax.experimental.pallas import tpu as pltpu
from jax.sharding import PartitionSpec as P

HEADS = 4
BLOCK = 128
NEG = -1e30
FLOOR = -1e29
VMEM_LIMIT = 56 * 1024 * 1024

NT = (((1,), (1,)), ((), ()))
TN = (((0,), (0,)), ((), ()))
TT = (((0,), (1,)), ((), ()))


def mm(left, right):
    return jnp.dot(left, right, preferred_element_type=jnp.float32)


def mm_general(left, right, dims):
    return lax.dot_general(left, right, dims, preferred_element_type=jnp.float32)


def bf(x):
    return x.astype(jnp.bfloat16)


def lane_row(width, head, head_dim):
    lanes = lax.broadcasted_iota(jnp.int32, (1, width), 1) // head_dim
    return bf(jnp.where(lanes == head, 1.0, 0.0))


def fill_bias(inter_ref, bias_ref, head_dim):
    query_blocks, key_blocks = inter_ref.shape
    width = bias_ref.shape[1]
    lane = lax.broadcasted_iota(jnp.int32, (1, width), 1) % head_dim
    for key_block in range(key_blocks):
        row = jnp.zeros((1, width), jnp.float32)
        for query_block in range(query_blocks):
            listed = inter_ref[query_block, key_block] == 1
            row = jnp.where(lane == query_block, jnp.where(listed, 0.0, NEG), row)
        bias_ref[pl.ds(key_block * BLOCK, BLOCK), :] = bf(
            jnp.broadcast_to(row, (BLOCK, width))
        )


def fill_hot(hot_ref, head_dim):
    rows, width = hot_ref.shape
    lane = lax.broadcasted_iota(jnp.int32, (1, width), 1) % head_dim
    for block in range(rows // BLOCK):
        row = bf(jnp.where(lane == block, 1.0, 0.0))
        hot_ref[pl.ds(block * BLOCK, BLOCK), :] = jnp.broadcast_to(row, (BLOCK, width))


def fill_scores(
    head, heads, query_ref, hot_ref, key_ref, bias_ref, grad_ref, value_ref, score_ref, prob_ref,
    peak_ref=None,
):
    rows, width = query_ref.shape
    own = lane_row(width, head, width // heads)
    other = lane_row(width, (head + 1) % heads, width // heads)
    left = query_ref[...] * own + hot_ref[...] * other
    left_grad = grad_ref[...] * own
    key_total = key_ref.shape[0]
    step = min(256, key_total)
    row_peak = None
    col_peaks = []
    for first in range(0, key_total, step):
        span = pl.ds(first, step)
        right = key_ref[span, :] * own + bias_ref[span, :] * other
        scores = mm_general(left, right, NT)
        score_ref[:, span] = scores
        if peak_ref is not None:
            for at in range(0, step, 128):
                piece = scores[:, at : at + 128]
                row_peak = piece if row_peak is None else jnp.maximum(row_peak, piece)
            col_peaks.append(scores.max(axis=0, keepdims=True))
        prob_ref[:, span] = mm_general(left_grad, value_ref[span, :], NT)
    if peak_ref is not None:
        peak_ref[...] = row_peak
        return jnp.concatenate(col_peaks, axis=1)


def spread(reduced, like):
    return jnp.broadcast_to(reduced, like.shape)


def fold8(x):
    return x.reshape(x.shape[0] // 8, 8, x.shape[1]).sum(axis=0)


STRIP = 32


def stats_kernel(
    head_count, inter_ref, ref_ref, gout_ref, src_ref, wq_ref, wk_ref, wv_ref, wo_ref,
    row_ref, col_ref, query_ref, grad_ref, key_ref, value_ref, bias_ref, hot_ref, score_ref, prob_ref,
    part_ref,
):
    rows, width = ref_ref.shape
    key_total = src_ref.shape[0]
    tiles = key_total // 128
    head_dim = width // head_count
    scale = head_dim ** -0.5
    query_ref[...] = bf(bf(mm(ref_ref[...], wq_ref[...])).astype(jnp.float32) * scale)
    grad_ref[...] = bf(mm_general(gout_ref[...], wo_ref[...], NT))
    key_ref[...] = bf(mm(src_ref[...], wk_ref[...]))
    value_ref[...] = bf(mm(src_ref[...], wv_ref[...]))
    fill_bias(inter_ref, bias_ref, head_dim)
    fill_hot(hot_ref, head_dim)
    for head in range(head_count):
        peak_at, total_at, dot_at = head, head_count + head, 2 * head_count + head
        col_peak = fill_scores(
            head, head_count, query_ref, hot_ref, key_ref, bias_ref, grad_ref, value_ref,
            score_ref, prob_ref, part_ref,
        )
        col_ref[peak_at : peak_at + 1, :] = jnp.maximum(col_peak, FLOOR)
        row_ref[head] = spread(part_ref[...].max(axis=1, keepdims=True), part_ref)

        def totals(step, col_totals):
            span = pl.ds(step * STRIP, STRIP)
            row_peak = row_ref[head, span, :]
            row_total = jnp.zeros((STRIP, 128), jnp.float32)
            out = []
            for tile in range(tiles):
                lanes = slice(tile * 128, tile * 128 + 128)
                scores = score_ref[span, lanes]
                row_exp = jnp.exp(scores - row_peak)
                col_exp = jnp.exp(scores - col_ref[peak_at : peak_at + 1, lanes])
                row_total = row_total + row_exp
                prob_ref[span, lanes] = row_exp * col_exp * prob_ref[span, lanes]
                out.append(col_totals[tile] + fold8(col_exp))
            part_ref[span, :] = row_total
            return tuple(out)

        zeros = tuple(jnp.zeros((8, 128), jnp.float32) for _ in range(tiles))
        col_totals = lax.fori_loop(0, rows // STRIP, totals, zeros)
        row_total = part_ref[...].sum(axis=1, keepdims=True)
        row_ref[head_count + head] = spread(1.0 / row_total, part_ref)

        def dots(step, col_dots):
            span = pl.ds(step * STRIP, STRIP)
            row_inverse = row_ref[head_count + head, span, :]
            return tuple(
                col_dots[tile]
                + fold8(prob_ref[span, tile * 128 : tile * 128 + 128] * row_inverse)
                for tile in range(tiles)
            )

        col_dots = lax.fori_loop(0, rows // STRIP, dots, zeros)
        for tile in range(tiles):
            lanes = slice(tile * 128, tile * 128 + 128)
            col_ref[total_at : total_at + 1, lanes] = col_totals[tile].sum(axis=0, keepdims=True)
            col_ref[dot_at : dot_at + 1, lanes] = col_dots[tile].sum(axis=0, keepdims=True)


def grads_kernel(
    head_count, inter_ref, ref_ref, gout_ref, src_ref, wq_ref, wk_ref, wv_ref, wo_ref, row_ref, all_ref,
    matched_ref, gref_ref, gsrc_ref, weight_ref,
    query_ref, grad_ref, key_ref, value_ref, bias_ref, hot_ref, score_ref, prob_ref, part_ref,
    match_ref, gscore_ref, query_t_ref, grad_t_ref, gkey_ref, gvalue_ref, att_ref, gquery_ref,
    col_ref,
):
    rows, width = ref_ref.shape
    key_total = src_ref.shape[0]
    tiles = key_total // 128
    head_dim = width // head_count
    scale = head_dim ** -0.5
    queries = bf(mm(ref_ref[...], wq_ref[...])).astype(jnp.float32)
    query_ref[...] = bf(queries * scale)
    grad_ref[...] = bf(mm_general(gout_ref[...], wo_ref[...], NT))
    queries_t = bf(mm_general(wq_ref[...], ref_ref[...], TT)).astype(jnp.float32)
    query_t_ref[...] = bf(queries_t * (2.0 * scale))
    grad_t_ref[...] = bf(mm_general(wo_ref[...], gout_ref[...], NT))
    key_ref[...] = bf(mm(src_ref[...], wk_ref[...]))
    value_ref[...] = bf(mm(src_ref[...], wv_ref[...]))
    fill_bias(inter_ref, bias_ref, head_dim)
    fill_hot(hot_ref, head_dim)

    devices = all_ref.shape[0]
    peak = all_ref[0, :head_count, :]
    for device in range(1, devices):
        peak = jnp.maximum(peak, all_ref[device, :head_count, :])
    total = jnp.zeros_like(peak)
    dots = jnp.zeros_like(peak)
    for device in range(devices):
        factor = jnp.exp(all_ref[device, :head_count, :] - peak)
        total = total + factor * all_ref[device, head_count : 2 * head_count, :]
        dots = dots + factor * all_ref[device, 2 * head_count : 3 * head_count, :]
    inverse = 1.0 / total
    col_ref[:head_count, :] = peak
    col_ref[head_count : 2 * head_count, :] = inverse
    col_ref[2 * head_count : 3 * head_count, :] = dots * inverse * 0.5

    for head in range(head_count):
        peak_at, inverse_at, half_at = head, head_count + head, 2 * head_count + head
        fill_scores(
            head, head_count, query_ref, hot_ref, key_ref, bias_ref, grad_ref, value_ref,
            score_ref, prob_ref,
        )

        def products(step, carry):
            span = pl.ds(step * STRIP, STRIP)
            row_peak = row_ref[head, span, :]
            row_inverse = row_ref[head_count + head, span, :]
            row_dot = jnp.zeros((STRIP, 128), jnp.float32)
            for tile in range(tiles):
                lanes = slice(tile * 128, tile * 128 + 128)
                scores = score_ref[span, lanes]
                row_prob = jnp.exp(scores - row_peak) * row_inverse
                col_prob = (
                    jnp.exp(scores - col_ref[peak_at : peak_at + 1, lanes])
                    * col_ref[inverse_at : inverse_at + 1, lanes]
                )
                match = row_prob * col_prob
                product = match * prob_ref[span, lanes]
                row_dot = row_dot + product
                match_ref[span, lanes] = bf(match)
                score_ref[span, lanes] = row_prob
                prob_ref[span, lanes] = product - col_prob * col_ref[half_at : half_at + 1, lanes]
            part_ref[span, :] = row_dot
            return carry

        lax.fori_loop(0, rows // STRIP, products, 0)
        part_ref[...] = spread(part_ref[...].sum(axis=1, keepdims=True) * 0.5, part_ref)

        def score_grads(step, carry):
            span = pl.ds(step * STRIP, STRIP)
            row_half = part_ref[span, :]
            for tile in range(tiles):
                lanes = slice(tile * 128, tile * 128 + 128)
                gscore_ref[span, lanes] = bf(
                    prob_ref[span, lanes] - score_ref[span, lanes] * row_half
                )
            return carry

        lax.fori_loop(0, rows // STRIP, score_grads, 0)

        own = lane_row(width, head, head_dim)
        attended = mm(match_ref[...], value_ref[...] * own)
        gquery = mm(gscore_ref[...], key_ref[...] * bf(own.astype(jnp.float32) * (2.0 * scale)))
        if head == 0:
            att_ref[...] = attended
            gquery_ref[...] = gquery
        else:
            att_ref[...] += attended
            gquery_ref[...] += gquery
        span = pl.ds(head * head_dim, head_dim)
        gkey_ref[span, :] = bf(mm(query_t_ref[span, :], gscore_ref[...]))
        gvalue_ref[span, :] = bf(mm(grad_t_ref[span, :], match_ref[...]))

    attended = bf(att_ref[...])
    gquery = bf(gquery_ref[...])
    matched_ref[...] = bf(ref_ref[...].astype(jnp.float32) + mm(attended, wo_ref[...]))
    gref_ref[...] = bf(
        gout_ref[...].astype(jnp.float32) + mm_general(gquery, wq_ref[...], NT)
    )
    gsrc_t = mm(wk_ref[...], gkey_ref[...]) + mm(wv_ref[...], gvalue_ref[...])
    gsrc_ref[...] = bf(gsrc_t.T)
    weight_ref[0] = bf(mm_general(ref_ref[...], gquery, TN))
    weight_ref[1] = bf(mm(gkey_ref[...], src_ref[...]).T)
    weight_ref[2] = bf(mm(gvalue_ref[...], src_ref[...]).T)
    weight_ref[3] = bf(mm_general(attended, gout_ref[...], TN))


def unshuffle_kernel(bits, me_ref, piece_ref, *out_refs):
    pieces, piece_rows, _ = piece_ref.shape
    per_out = pieces // len(out_refs)
    for chunk in range(pieces):
        apart = me_ref[0] ^ chunk
        place = 0
        for at, bit in enumerate(bits):
            place = place + ((apart // bit) % 2) * (1 << at)
        rows = pl.ds((chunk % per_out) * piece_rows, piece_rows)
        out_refs[chunk // per_out][rows, :] = piece_ref[place].astype(jnp.float32)


def gather_by_doubling(chunk, steps):
    held = chunk[None]
    for axis, bit in steps:
        pairs = [(i, i ^ bit) for i in range(lax.axis_size(axis))]
        held = jnp.concatenate([held, lax.ppermute(held, axis, pairs)], axis=0)
    return held


def axis_bits(axis):
    return [1 << at for at in range(lax.axis_size(axis).bit_length() - 1)]


def vmem_call(kernel, name, out_shape, scratch, flops, moved, args):
    specs = [pl.BlockSpec(memory_space=pltpu.SMEM)]
    specs += [pl.BlockSpec(memory_space=pltpu.VMEM)] * (len(args) - 1)
    return pl.pallas_call(
        kernel,
        name=name,
        out_shape=out_shape,
        in_specs=specs,
        out_specs=[pl.BlockSpec(memory_space=pltpu.VMEM)] * len(out_shape),
        scratch_shapes=scratch,
        compiler_params=pltpu.CompilerParams(vmem_limit_bytes=VMEM_LIMIT),
        cost_estimate=pl.CostEstimate(flops=flops, bytes_accessed=moved, transcendentals=0),
    )(*args)


def on_device(ref_feats, src_feats, grad_out, w_query, w_key, w_value, w_out, intersection):
    ref_rows = ref_feats[0]
    src_rows = src_feats[0]
    out_grad = grad_out[0]
    listed = intersection[0]
    rows, width = ref_rows.shape
    blk = lax.axis_size("blk")
    everyone = lax.axis_size("scan") * blk
    key_rows = src_rows.shape[0]
    key_total = key_rows * blk
    source_all = lax.all_gather(src_rows, "blk", axis=0, tiled=True)

    f32, b16 = jnp.float32, jnp.bfloat16
    shape = jax.ShapeDtypeStruct
    common = [
        pltpu.VMEM((rows, width), b16),
        pltpu.VMEM((rows, width), b16),
        pltpu.VMEM((key_total, width), b16),
        pltpu.VMEM((key_total, width), b16),
        pltpu.VMEM((key_total, width), b16),
        pltpu.VMEM((rows, width), b16),
        pltpu.VMEM((rows, key_total), f32),
        pltpu.VMEM((rows, key_total), f32),
        pltpu.VMEM((rows, 128), f32),
    ]
    base = (listed, ref_rows, out_grad, source_all, w_query, w_key, w_value, w_out)
    tile_flops = 2 * rows * key_total * width
    row_stats, col_stats = vmem_call(
        functools.partial(stats_kernel, HEADS),
        "match_stats",
        [shape((2 * HEADS, rows, 128), f32), shape((3 * HEADS, key_total), f32)],
        common,
        2 * tile_flops,
        2 << 20,
        base,
    )
    all_stats = lax.all_gather(col_stats, "blk", axis=0)
    matched, grad_ref, source_part, weight_part = vmem_call(
        functools.partial(grads_kernel, HEADS),
        "match_grads",
        [
            shape((rows, width), b16),
            shape((rows, width), b16),
            shape((key_total, width), b16),
            shape((4, width, width), b16),
        ],
        common
        + [
            pltpu.VMEM((rows, key_total), b16),
            pltpu.VMEM((rows, key_total), b16),
            pltpu.VMEM((width, rows), b16),
            pltpu.VMEM((width, rows), b16),
            pltpu.VMEM((width, key_total), b16),
            pltpu.VMEM((width, key_total), b16),
            pltpu.VMEM((rows, width), f32),
            pltpu.VMEM((rows, width), f32),
            pltpu.VMEM((3 * HEADS, key_total), f32),
        ],
        6 * tile_flops,
        4 << 20,
        base + (row_stats, all_stats),
    )

    weight_rows = 4 * width // everyone
    weight_parts = lax.all_to_all(
        weight_part.reshape(everyone, weight_rows, width), ("scan", "blk"), split_axis=0, concat_axis=0
    )
    weight_sum = weight_parts.astype(f32).sum(axis=0).astype(b16)
    blk_bits, scan_bits = axis_bits("blk"), axis_bits("scan")
    steps = [("blk", bit) for bit in blk_bits[1:]]
    steps += [("scan", bit) for bit in reversed(scan_bits)]
    steps += [("blk", bit) for bit in blk_bits[:1]]
    pieces = gather_by_doubling(weight_sum, steps)
    me = lax.axis_index("scan") * blk + lax.axis_index("blk")
    weights = vmem_call(
        functools.partial(
            unshuffle_kernel, [bit * (blk if axis == "scan" else 1) for axis, bit in steps]
        ),
        "unshuffle_weights",
        [shape((width, width), f32)] * 4,
        [],
        0,
        3 << 20,
        (me.astype(jnp.int32)[None], pieces),
    )

    source_part, weight_parts = lax.optimization_barrier((source_part, weight_parts))
    source_parts = lax.all_to_all(
        source_part.reshape(blk, key_rows, width), "blk", split_axis=0, concat_axis=0
    )
    grad_src = source_parts.astype(f32).sum(axis=0).astype(b16)
    return (matched[None], grad_ref[None], grad_src[None], *weights)


def solution(mesh):
    split = P("scan", "blk", None)
    whole = P()
    return jax.shard_map(
        on_device,
        mesh=mesh,
        in_specs=(split, split, split, whole, whole, whole, whole, split),
        out_specs=(split, split, split, whole, whole, whole, whole),
        check_vma=False,
    )
```

time: 187 us -> 110 us (0.59)
  Pallas kernels: 70.8 us -> 31.5 us
  blocking collectives: 94.3 us -> 56 us
    all_gather x1 -> x0, blocking collectives: 40.3 us -> none  [on_device(): weights = lax.all_gather(weight_sum, ('scan', 'blk'), axis=0, tiled=True)]
    pallas_call x2 -> x3, Pallas kernels: 70.8 us -> 31.5 us  [vmem_call(): pl.pallas_call(kernel, name=name, out_shape=out_shape, in_specs=specs, ou...]
    all_to_all x1, waiting for transfers between devices: 15.6 us -> 0.17 us  [on_device(): lax.all_to_all(source_part.reshape(blk, key_rows, width), 'blk', split_ax...]
    ppermute x0 -> x5, waiting for transfers between devices: none -> 14.5 us  [gather_by_doubling(): held = jnp.concatenate([held, lax.ppermute(held, axis, pairs)], axis=0)]
    all_to_all x1, blocking collectives: 20.1 us -> 22 us  [on_device(): lax.all_to_all(weight_part.reshape(everyone, weight_rows, width), ('scan'...]
  transfers between devices with their start and end apart: 1 -> 6, of which waited for: 1 -> 6; matrix products, arithmetic and copies ran while one was open for 0% -> 0% of each run, Pallas kernels for 0% -> 2%
where the time goes in v2:
time: 110 us
  blocking collectives  56 us (51%)
  Pallas kernels  31.5 us (29%)
  waiting for transfers between devices  14.6 us (13%)
  starting transfers between devices  5.03 us (5%)
    pallas_call x3, Pallas kernels, vmem_call(): pl.pallas_call(kernel, name=name, out_shape=out_shape, in_specs=specs, ou...  31.5 us
    all_to_all x1, blocking collectives, on_device(): lax.all_to_all(weight_part.reshape(everyone, weight_rows, width), ('scan'...  22 us
    all_gather x1, blocking collectives, on_device(): source_all = lax.all_gather(src_rows, 'blk', axis=0, tiled=True)  17.8 us
    all_gather x1, blocking collectives, on_device(): all_stats = lax.all_gather(col_stats, 'blk', axis=0)  16.2 us
    ppermute x5, waiting for transfers between devices, gather_by_doubling(): held = jnp.concatenate([held, lax.ppermute(held, axis, pairs)], axis=0)  14.5 us
    all_to_all x1, starting transfers between devices, on_device(): lax.all_to_all(source_part.reshape(blk, key_rows, width), 'blk', split_ax...  4.19 us
  transfers between devices with their start and end apart: 6, of which 6 were waited for; matrix products, arithmetic and copies ran while one was open for 0% of the time, Pallas kernels for 2%

profile of v2, /device:TPU:0, one launch (start us, length us, event | category | flops | bytes accessed | tf_op | source)
XLA Modules:
  0.0 109.6 jit_solution(17220238141616223734)
XLA Ops:
  0.6 17.8 %all-gather = bf16[1,1024,256]{2,1,0:T(8,128)(2,1)} all-gather(bf16[1,128,256]{2,1,0:T(8,128)(2,1)} %param.9), channel_id=2, replica_groups=mesh['scan'=4,'blk'=8] {'blk'}, dimensions={1}, use_global_device_ids=true | all-gather | bytes 589824 | tf_op jit(solution)/shard_map/all_gather | solution.py:320
  18.4 11.3 %match_stats.1 = (f32[8,512,128]{2,1,0:T(8,128)}, f32[12,1024]{1,0:T(8,128)}) custom-call(s32[4,8]{1,0:T(4,128)} %bitcast.28, bf16[512,256]{1,0:T(8,128)(2,1)} %bitcast.24, bf16[512,256]{1,0:T(8,128)(2,1)} %bitcast.26, bf16[1024,256]{1,0:T(8,128)(2,1)} %bitcast.14, bf16[256,256]{1,0:T(8,128)(2,1)} %wq_ref.3, bf16[256,256]{1,0:T(8,128)(2,1)} %wk_ref.3, ...), custom_call_target="tpu_custom_call" | custom-call | flops 536870912 | bytes 2097152 | tf_op jit(solution)/shard_map/match_stats/pallas_call | solution.py:298
  29.7 16.2 %all-gather.2.all_ref = f32[8,12,1024]{2,1,0:T(8,128)} all-gather(f32[1,12,1024]{2,1,0:T(8,128)} %bitcast.22), channel_id=3, replica_groups=mesh['scan'=4,'blk'=8] {'blk'}, dimensions={0}, use_global_device_ids=true | all-gather | bytes 442368 | tf_op jit(solution)/shard_map/all_gather | solution.py:346
  45.9 17.5 %match_grads.1 = (bf16[512,256]{1,0:T(8,128)(2,1)}, bf16[512,256]{1,0:T(8,128)(2,1)}, bf16[1024,256]{1,0:T(8,128)(2,1)}, bf16[4,256,256]{2,1,0:T(8,128)(2,1)}) custom-call(s32[4,8]{1,0:T(4,128)} %bitcast.29, bf16[512,256]{1,0:T(8,128)(2,1)} %bitcast.25, bf16[512,256]{1,0:T(8,128)(2,1)} %bitcast.27, bf16[1024,256]{1,0:T(8,128)(2,1)} %bitcast.15, ...), custom_call_target="tpu_custom_call" | custom-call | flops 1610612736 | bytes 4194304 | tf_op jit(solution)/shard_map/match_grads/pallas_call | solution.py:298
  63.4 22.0 %all_to_all.10 = bf16[32,32,256]{2,1,0:T(8,128)(2,1)S(1)} all-to-all(bf16[32,32,256]{2,1,0:T(8,128)(2,1)} %bitcast.17), channel_id=1, replica_groups=mesh['scan'=4,'blk'=8] {'scan','blk'}, dimensions={0} | all-to-all | bytes 1048576 | tf_op jit(solution)/shard_map/all_to_all | solution.py:374
  85.4 0.1 reduce_sum.25
  85.5 0.1 collective-permute-start
  85.6 3.7 %collective-permute-done = bf16[1,32,256]{2,1,0:T(8,128)(2,1)S(1)} collective-permute-done((bf16[1,32,256]{2,1,0:T(8,128)(2,1)S(1)}, bf16[1,32,256]{2,1,0:T(8,128)(2,1)S(1)}, u32[]{:S(2)}, u32[]{:S(2)}) %collective-permute-start) | collective-permute-done | bytes 16416 | tf_op jit(solution)/shard_map/ppermute | solution.py:287
  89.3 0.0 collective-permute-start.1
  89.3 4.2 %all-to-all-start.1 = ((bf16[8,128,256]{2,1,0:T(8,128)(2,1)}), bf16[8,128,256]{2,1,0:T(8,128)(2,1)S(1)}, u32[]{:S(2)}, u32[]{:S(2)}) async-start(bf16[8,128,256]{2,1,0:T(8,128)(2,1)} %bitcast.16), calls=%async_computation.1 | async-start | bytes 1048576 | tf_op jit(solution)/shard_map/all_to_all | solution.py:397
  93.5 0.6 collective-permute-done.1
  94.1 0.6 collective-permute-start.2
  94.7 3.7 %collective-permute-done.2 = bf16[4,32,256]{2,1,0:T(8,128)(2,1)S(1)} collective-permute-done((bf16[4,32,256]{2,1,0:T(8,128)(2,1)S(1)}, bf16[4,32,256]{2,1,0:T(8,128)(2,1)S(1)}, u32[]{:S(2)}, u32[]{:S(2)}) %collective-permute-start.2) | collective-permute-done | bytes 65568 | tf_op jit(solution)/shard_map/ppermute | solution.py:287
  98.5 0.1 collective-permute-start.3
  98.6 4.9 %collective-permute-done.3 = bf16[8,32,256]{2,1,0:T(8,128)(2,1)S(1)} collective-permute-done((bf16[8,32,256]{2,1,0:T(8,128)(2,1)S(1)}, bf16[8,32,256]{2,1,0:T(8,128)(2,1)S(1)}, u32[]{:S(2)}, u32[]{:S(2)}) %collective-permute-start.3) | collective-permute-done | bytes 131104 | tf_op jit(solution)/shard_map/ppermute | solution.py:287
  103.5 0.1 collective-permute-start.4
  103.6 1.5 %collective-permute-done.4 = bf16[16,32,256]{2,1,0:T(8,128)(2,1)S(1)} collective-permute-done((bf16[16,32,256]{2,1,0:T(8,128)(2,1)S(1)}, bf16[16,32,256]{2,1,0:T(8,128)(2,1)S(1)}, u32[]{:S(2)}, u32[]{:S(2)}) %collective-permute-start.4) | collective-permute-done | bytes 262176 | tf_op jit(solution)/shard_map/ppermute | solution.py:287
  105.1 0.0 copy-start
  105.2 0.8 copy-done
  105.9 2.7 %unshuffle_weights.1 = (f32[256,256]{1,0:T(8,128)}, f32[256,256]{1,0:T(8,128)}, f32[256,256]{1,0:T(8,128)}, f32[256,256]{1,0:T(8,128)}) custom-call(s32[1]{0:T(128)} %bitcast.10.me_ref, bf16[32,32,256]{2,1,0:T(8,128)(2,1)} %copy-done), custom_call_target="tpu_custom_call" | custom-call | bytes 3145728 | tf_op jit(solution)/shard_map/unshuffle_weights/pallas_call | solution.py:298
  108.7 0.2 all-to-all-done.1
  108.9 0.7 reduce_sum.24
  (9 shorter events, 0.1 us)
Async XLA Ops:
  85.5 3.8 %collective-permute-start = (bf16[1,32,256]{2,1,0:T(8,128)(2,1)S(1)}, bf16[1,32,256]{2,1,0:T(8,128)(2,1)S(1)}, u32[]{:S(2)}, u32[]{:S(2)}) collective-permute-start(bf16[1,32,256]{2,1,0:T(8,128)(2,1)S(1)} %bitcast.18), channel_id=1, source_target_pairs={{0,2},{1,3},{2,0},{3,1},{4,6},{5,7},{6,4},{7,5},{8,10},{9,11},{10,... | collective-permute-start | bytes 49160 | tf_op jit(solution)/shard_map/ppermute | solution.py:287
  89.3 4.8 %collective-permute-start.1 = (bf16[2,32,256]{2,1,0:T(8,128)(2,1)S(1)}, bf16[2,32,256]{2,1,0:T(8,128)(2,1)S(1)}, u32[]{:S(2)}, u32[]{:S(2)}) collective-permute-start(bf16[2,32,256]{2,1,0:T(8,128)(2,1)S(1)} %pad_maximum_fusion.2), channel_id=1, source_target_pairs={{0,4},{1,5},{2,6},{3,7},{4,0},{5,1},{6,2},{7,3},{8,12},{9,13},{10,... | collective-permute-start | bytes 98312 | tf_op jit(solution)/shard_map/ppermute | solution.py:287
  89.3 19.5 %all-to-all-start.1 = ((bf16[8,128,256]{2,1,0:T(8,128)(2,1)}), bf16[8,128,256]{2,1,0:T(8,128)(2,1)S(1)}, u32[]{:S(2)}, u32[]{:S(2)}) async-start(bf16[8,128,256]{2,1,0:T(8,128)(2,1)} %bitcast.16), calls=%async_computation.1 | async-start | bytes 1048576 | tf_op jit(solution)/shard_map/all_to_all | solution.py:397
  94.1 4.3 %collective-permute-start.2 = (bf16[4,32,256]{2,1,0:T(8,128)(2,1)S(1)}, bf16[4,32,256]{2,1,0:T(8,128)(2,1)S(1)}, u32[]{:S(2)}, u32[]{:S(2)}) collective-permute-start(bf16[4,32,256]{2,1,0:T(8,128)(2,1)S(1)} %pad_maximum_fusion.1), channel_id=1, source_target_pairs={{0,16},{8,24},{16,0},{24,8},{1,17},{9,25},{17,1},{25,9},{2,18},{10... | collective-permute-start | bytes 196616 | tf_op jit(solution)/shard_map/ppermute | solution.py:287
  98.5 5.0 %collective-permute-start.3 = (bf16[8,32,256]{2,1,0:T(8,128)(2,1)S(1)}, bf16[8,32,256]{2,1,0:T(8,128)(2,1)S(1)}, u32[]{:S(2)}, u32[]{:S(2)}) collective-permute-start(bf16[8,32,256]{2,1,0:T(8,128)(2,1)S(1)} %pad_maximum_fusion), channel_id=1, source_target_pairs={{0,8},{8,0},{16,24},{24,16},{1,9},{9,1},{17,25},{25,17},{2,10},{10... | collective-permute-start | bytes 393224 | tf_op jit(solution)/shard_map/ppermute | solution.py:287
  103.5 1.6 %collective-permute-start.4 = (bf16[16,32,256]{2,1,0:T(8,128)(2,1)S(1)}, bf16[16,32,256]{2,1,0:T(8,128)(2,1)S(1)}, u32[]{:S(2)}, u32[]{:S(2)}) collective-permute-start(bf16[16,32,256]{2,1,0:T(8,128)(2,1)S(1)} %get-tuple-element.29), channel_id=1, source_target_pairs={{0,1},{1,0},{2,3},{3,2},{4,5},{5,4},{6,7},{7,6},{8,9},{9,8},{10,11... | collective-permute-start | bytes 786440 | tf_op jit(solution)/shard_map/ppermute | solution.py:287
  105.1 0.8 copy-start

commit v3 on v2

--- a/solution.py
+++ b/solution.py
@@ -114,12 +114,12 @@
     fill_bias(inter_ref, bias_ref, head_dim)
     fill_hot(hot_ref, head_dim)
     for head in range(head_count):
-        peak_at, total_at, dot_at = head, head_count + head, 2 * head_count + head
+        mine = slice(head, head + 1)
         col_peak = fill_scores(
             head, head_count, query_ref, hot_ref, key_ref, bias_ref, grad_ref, value_ref,
             score_ref, prob_ref, part_ref,
         )
-        col_ref[peak_at : peak_at + 1, :] = jnp.maximum(col_peak, FLOOR)
+        col_ref[0, mine, :] = jnp.maximum(col_peak, FLOOR)
         row_ref[head] = spread(part_ref[...].max(axis=1, keepdims=True), part_ref)
 
         def totals(step, col_totals):
@@ -131,7 +131,7 @@
                 lanes = slice(tile * 128, tile * 128 + 128)
                 scores = score_ref[span, lanes]
                 row_exp = jnp.exp(scores - row_peak)
-                col_exp = jnp.exp(scores - col_ref[peak_at : peak_at + 1, lanes])
+                col_exp = jnp.exp(scores - col_ref[0, mine, lanes])
                 row_total = row_total + row_exp
                 prob_ref[span, lanes] = row_exp * col_exp * prob_ref[span, lanes]
                 out.append(col_totals[tile] + fold8(col_exp))
@@ -155,13 +155,13 @@
         col_dots = lax.fori_loop(0, rows // STRIP, dots, zeros)
         for tile in range(tiles):
             lanes = slice(tile * 128, tile * 128 + 128)
-            col_ref[total_at : total_at + 1, lanes] = col_totals[tile].sum(axis=0, keepdims=True)
-            col_ref[dot_at : dot_at + 1, lanes] = col_dots[tile].sum(axis=0, keepdims=True)
+            col_ref[1, mine, lanes] = col_totals[tile].sum(axis=0, keepdims=True)
+            col_ref[2, mine, lanes] = col_dots[tile].sum(axis=0, keepdims=True)
 
 
 def grads_kernel(
-    head_count, inter_ref, ref_ref, gout_ref, src_ref, wq_ref, wk_ref, wv_ref, wo_ref, row_ref, all_ref,
-    matched_ref, gref_ref, gsrc_ref, weight_ref,
+    head_count, inter_ref, ref_ref, gout_ref, src_ref, wq_ref, wk_ref, wv_ref, wo_ref, row_ref, near_ref,
+    far_ref, matched_ref, gref_ref, gsrc_ref, weight_ref,
     query_ref, grad_ref, key_ref, value_ref, bias_ref, hot_ref, score_ref, prob_ref, part_ref,
     match_ref, gscore_ref, query_t_ref, grad_t_ref, gkey_ref, gvalue_ref, att_ref, gquery_ref,
     col_ref,
@@ -182,23 +182,15 @@
     fill_bias(inter_ref, bias_ref, head_dim)
     fill_hot(hot_ref, head_dim)
 
-    devices = all_ref.shape[0]
-    peak = all_ref[0, :head_count, :]
-    for device in range(1, devices):
-        peak = jnp.maximum(peak, all_ref[device, :head_count, :])
-    total = jnp.zeros_like(peak)
-    dots = jnp.zeros_like(peak)
-    for device in range(devices):
-        factor = jnp.exp(all_ref[device, :head_count, :] - peak)
-        total = total + factor * all_ref[device, head_count : 2 * head_count, :]
-        dots = dots + factor * all_ref[device, 2 * head_count : 3 * head_count, :]
-    inverse = 1.0 / total
-    col_ref[:head_count, :] = peak
-    col_ref[head_count : 2 * head_count, :] = inverse
-    col_ref[2 * head_count : 3 * head_count, :] = dots * inverse * 0.5
+    peak = jnp.maximum(near_ref[0], far_ref[0])
+    near, far = jnp.exp(near_ref[0] - peak), jnp.exp(far_ref[0] - peak)
+    inverse = 1.0 / (near * near_ref[1] + far * far_ref[1])
+    col_ref[0] = peak
+    col_ref[1] = inverse
+    col_ref[2] = (near * near_ref[2] + far * far_ref[2]) * inverse * 0.5
 
     for head in range(head_count):
-        peak_at, inverse_at, half_at = head, head_count + head, 2 * head_count + head
+        mine = slice(head, head + 1)
         fill_scores(
             head, head_count, query_ref, hot_ref, key_ref, bias_ref, grad_ref, value_ref,
             score_ref, prob_ref,
@@ -214,15 +206,15 @@
                 scores = score_ref[span, lanes]
                 row_prob = jnp.exp(scores - row_peak) * row_inverse
                 col_prob = (
-                    jnp.exp(scores - col_ref[peak_at : peak_at + 1, lanes])
-                    * col_ref[inverse_at : inverse_at + 1, lanes]
+                    jnp.exp(scores - col_ref[0, mine, lanes])
+                    * col_ref[1, mine, lanes]
                 )
                 match = row_prob * col_prob
                 product = match * prob_ref[span, lanes]
                 row_dot = row_dot + product
                 match_ref[span, lanes] = bf(match)
                 score_ref[span, lanes] = row_prob
-                prob_ref[span, lanes] = product - col_prob * col_ref[half_at : half_at + 1, lanes]
+                prob_ref[span, lanes] = product - col_prob * col_ref[2, mine, lanes]
             part_ref[span, :] = row_dot
             return carry
 
@@ -268,28 +260,40 @@
     weight_ref[3] = bf(mm_general(attended, gout_ref[...], TN))
 
 
-def unshuffle_kernel(bits, me_ref, piece_ref, *out_refs):
-    pieces, piece_rows, _ = piece_ref.shape
-    per_out = pieces // len(out_refs)
-    for chunk in range(pieces):
-        apart = me_ref[0] ^ chunk
-        place = 0
-        for at, bit in enumerate(bits):
-            place = place + ((apart // bit) % 2) * (1 << at)
-        rows = pl.ds((chunk % per_out) * piece_rows, piece_rows)
-        out_refs[chunk // per_out][rows, :] = piece_ref[place].astype(jnp.float32)
-
-
-def gather_by_doubling(chunk, steps):
-    held = chunk[None]
-    for axis, bit in steps:
-        pairs = [(i, i ^ bit) for i in range(lax.axis_size(axis))]
-        held = jnp.concatenate([held, lax.ppermute(held, axis, pairs)], axis=0)
-    return held
-
-
-def axis_bits(axis):
-    return [1 << at for at in range(lax.axis_size(axis).bit_length() - 1)]
+def swap(x, axis, apart):
+    pairs = [(i, i ^ apart) for i in range(lax.axis_size(axis))]
+    return lax.ppermute(x, axis, pairs)
+
+
+def at(x, index, axis=0):
+    return lax.dynamic_index_in_dim(x, index, axis, False)
+
+
+def laid(pieces, places, axis=0):
+    out = jnp.zeros(pieces[0].shape[:axis] + (len(pieces),) + pieces[0].shape[axis:], pieces[0].dtype)
+    for piece, place in zip(pieces, places):
+        out = lax.dynamic_update_index_in_dim(out, piece, place, axis)
+    return out
+
+
+def gather_direct(x, axis, me, count, stride):
+    pieces = [x] + [swap(x, axis, k * stride) for k in range(1, count)]
+    return laid(pieces, [me ^ k for k in range(count)])
+
+
+def scatter_direct(x, axis, me, count, stride):
+    total = at(x, me).astype(jnp.float32)
+    for piece in [swap(at(x, me ^ k), axis, k * stride) for k in range(1, count)]:
+        total = total + piece.astype(jnp.float32)
+    return total.astype(x.dtype)
+
+
+def combine_stats(parts):
+    peak = functools.reduce(jnp.maximum, [part[0] for part in parts])
+    factors = [jnp.exp(part[0] - peak) for part in parts]
+    total = sum(factor * part[1] for factor, part in zip(factors, parts))
+    dots = sum(factor * part[2] for factor, part in zip(factors, parts))
+    return jnp.stack([peak, total, dots])
 
 
 def vmem_call(kernel, name, out_shape, scratch, flops, moved, args):
@@ -313,11 +317,15 @@
     out_grad = grad_out[0]
     listed = intersection[0]
     rows, width = ref_rows.shape
-    blk = lax.axis_size("blk")
-    everyone = lax.axis_size("scan") * blk
+    scans, chips = lax.axis_size("scan"), lax.axis_size("blk") // 2
+    scan, core = lax.axis_index("scan"), lax.axis_index("blk") % 2
+    chip = lax.axis_index("blk") // 2
     key_rows = src_rows.shape[0]
-    key_total = key_rows * blk
-    source_all = lax.all_gather(src_rows, "blk", axis=0, tiled=True)
+    key_total = key_rows * chips * 2
+
+    same_core = gather_direct(src_rows, "blk", chip, chips, 2)
+    source_all = laid([same_core, swap(same_core, "blk", 1)], [core, 1 - core], axis=1)
+    source_all = source_all.reshape(key_total, width)
 
     f32, b16 = jnp.float32, jnp.bfloat16
     shape = jax.ShapeDtypeStruct
@@ -337,13 +345,16 @@
     row_stats, col_stats = vmem_call(
         functools.partial(stats_kernel, HEADS),
         "match_stats",
-        [shape((2 * HEADS, rows, 128), f32), shape((3 * HEADS, key_total), f32)],
+        [shape((2 * HEADS, rows, 128), f32), shape((3, HEADS, key_total), f32)],
         common,
         2 * tile_flops,
         2 << 20,
         base,
     )
-    all_stats = lax.all_gather(col_stats, "blk", axis=0)
+    near_stats = combine_stats(
+        [col_stats] + [swap(col_stats, "blk", 2 * k) for k in range(1, chips)]
+    )
+    far_stats = swap(near_stats, "blk", 1)
     matched, grad_ref, source_part, weight_part = vmem_call(
         functools.partial(grads_kernel, HEADS),
         "match_grads",
@@ -363,42 +374,34 @@
             pltpu.VMEM((width, key_total), b16),
             pltpu.VMEM((rows, width), f32),
             pltpu.VMEM((rows, width), f32),
-            pltpu.VMEM((3 * HEADS, key_total), f32),
+            pltpu.VMEM((3, HEADS, key_total), f32),
         ],
         6 * tile_flops,
         4 << 20,
-        base + (row_stats, all_stats),
-    )
-
-    weight_rows = 4 * width // everyone
-    weight_parts = lax.all_to_all(
-        weight_part.reshape(everyone, weight_rows, width), ("scan", "blk"), split_axis=0, concat_axis=0
-    )
-    weight_sum = weight_parts.astype(f32).sum(axis=0).astype(b16)
-    blk_bits, scan_bits = axis_bits("blk"), axis_bits("scan")
-    steps = [("blk", bit) for bit in blk_bits[1:]]
-    steps += [("scan", bit) for bit in reversed(scan_bits)]
-    steps += [("blk", bit) for bit in blk_bits[:1]]
-    pieces = gather_by_doubling(weight_sum, steps)
-    me = lax.axis_index("scan") * blk + lax.axis_index("blk")
-    weights = vmem_call(
-        functools.partial(
-            unshuffle_kernel, [bit * (blk if axis == "scan" else 1) for axis, bit in steps]
-        ),
-        "unshuffle_weights",
-        [shape((width, width), f32)] * 4,
-        [],
-        0,
-        3 << 20,
-        (me.astype(jnp.int32)[None], pieces),
-    )
-
-    source_part, weight_parts = lax.optimization_barrier((source_part, weight_parts))
-    source_parts = lax.all_to_all(
-        source_part.reshape(blk, key_rows, width), "blk", split_axis=0, concat_axis=0
-    )
-    grad_src = source_parts.astype(f32).sum(axis=0).astype(b16)
-    return (matched[None], grad_ref[None], grad_src[None], *weights)
+        base + (row_stats, near_stats, far_stats),
+    )
+
+    weights = weight_part.reshape(2, scans, chips, -1, width)
+    sources = source_part.reshape(chips, 2, key_rows, width)
+    weights = scatter_direct(weights, "blk", core, 2, 1)
+    near, far = at(sources, core, 1), at(sources, 1 - core, 1)
+    sources = (near.astype(f32) + swap(far, "blk", 1).astype(f32)).astype(b16)
+    weights = scatter_direct(weights, "scan", scan, scans, 1)
+    grad_src = scatter_direct(sources, "blk", chip, chips, 2)
+    weights = scatter_direct(weights, "blk", chip, chips, 2)
+    weights = gather_direct(weights, "blk", chip, chips, 2)
+    weights = gather_direct(weights, "scan", scan, scans, 1)
+    weights = gather_direct(weights, "blk", core, 2, 1)
+    weights = weights.reshape(4, width, width).astype(f32)
+    return (
+        matched[None],
+        grad_ref[None],
+        grad_src[None],
+        weights[0],
+        weights[1],
+        weights[2],
+        weights[3],
+    )
 
 
 def solution(mesh):

time: 110 us -> 101 us (0.918)
  blocking collectives: 56 us -> 0 us
  starting transfers between devices: 5.03 us -> 28.9 us
  waiting for transfers between devices: 14.6 us -> 33.1 us
  local copies, waits for them, and re-layouts: 0.85 us -> 5.63 us
  Pallas kernels: 31.5 us -> 28.8 us
  other arithmetic: 0.82 us -> 3.46 us
    all_gather x2 -> x0, blocking collectives: 34 us -> none  [the longest x1 17.8 us: on_device(): source_all = lax.all_gather(src_rows, 'blk', axis=0, tiled=True)]
    ppermute x5 -> x26, starting transfers between devices: 0.84 us -> 28.9 us  [swap(): return lax.ppermute(x, axis, pairs)]
    all_to_all x1 -> x0, blocking collectives: 22 us -> none  [on_device(): lax.all_to_all(weight_part.reshape(everyone, weight_rows, width), ('scan'...]
    ppermute x5 -> x26, waiting for transfers between devices: 14.5 us -> 33.1 us  [swap(): return lax.ppermute(x, axis, pairs)]
    all_to_all x1 -> x0, starting transfers between devices: 4.19 us -> none  [on_device(): lax.all_to_all(source_part.reshape(blk, key_rows, width), 'blk', split_ax...]
    squeeze x0 -> x6, local copies, waits for them, and re-layouts: none -> 3.04 us  [the longest x5 2.05 us: at(): return lax.dynamic_index_in_dim(x, index, axis, False)]
    pallas_call x3 -> x2, Pallas kernels: 31.5 us -> 28.8 us  [vmem_call(): pl.pallas_call(kernel, name=name, out_shape=out_shape, in_specs=specs, ou...]
    add x0 -> x2, other arithmetic: none -> 1.54 us  [the longest x1 0.77 us: combine_stats(): dots = sum((factor * part[2] for factor, part in zip(factors, parts)))]
  transfers between devices with their start and end apart: 6 -> 26, of which waited for: 6 -> 17; matrix products, arithmetic and copies ran while one was open for 0% -> 3% of each run, Pallas kernels for 2% -> 0%
where the time goes in v3:
time: 101 us
  waiting for transfers between devices  33.1 us (33%)
  starting transfers between devices  28.9 us (29%)
  Pallas kernels  28.8 us (29%)
  local copies, waits for them, and re-layouts  5.63 us (6%)
  other arithmetic  3.46 us (3%)
    ppermute x26, waiting for transfers between devices, swap(): return lax.ppermute(x, axis, pairs)  33.1 us
    ppermute x26, starting transfers between devices, swap(): return lax.ppermute(x, axis, pairs)  28.9 us
    pallas_call x2, Pallas kernels, vmem_call(): pl.pallas_call(kernel, name=name, out_shape=out_shape, in_specs=specs, ou...  28.8 us
    squeeze x5, local copies, waits for them, and re-layouts, at(): return lax.dynamic_index_in_dim(x, index, axis, False)  2.05 us
  transfers between devices with their start and end apart: 26, of which 17 were waited for; matrix products, arithmetic and copies ran while one was open for 3% of the time, Pallas kernels for 0%

profile of v3, /device:TPU:0, one launch (start us, length us, event | category | flops | bytes accessed | tf_op | source)
XLA Modules:
  0.0 100.8 jit_solution(2913386752134628943)
XLA Ops:
  0.6 3.1 %collective-permute-start = (bf16[128,256]{1,0:T(8,128)(2,1)}, bf16[128,256]{1,0:T(8,128)(2,1)S(1)}, u32[]{:S(2)}, u32[]{:S(2)}) collective-permute-start(bf16[128,256]{1,0:T(8,128)(2,1)} %bitcast.100), channel_id=1, source_target_pairs={{0,2},{1,3},{2,0},{3,1},{4,6},{5,7},{6,4},{7,5},{8,10},{9,11},{10,... | collective-permute-start | bytes 196616 | tf_op jit(solution)/shard_map/ppermute | solution.py:265
  3.7 2.6 %collective-permute-start.1 = (bf16[128,256]{1,0:T(8,128)(2,1)}, bf16[128,256]{1,0:T(8,128)(2,1)S(1)}, u32[]{:S(2)}, u32[]{:S(2)}) collective-permute-start(bf16[128,256]{1,0:T(8,128)(2,1)} %bitcast.101), channel_id=1, source_target_pairs={{0,4},{1,5},{2,6},{3,7},{4,0},{5,1},{6,2},{7,3},{8,12},{9,13},{10,... | collective-permute-start | bytes 196616 | tf_op jit(solution)/shard_map/ppermute | solution.py:265
  7.2 4.0 %collective-permute-done.1 = bf16[128,256]{1,0:T(8,128)(2,1)S(1)} collective-permute-done((bf16[128,256]{1,0:T(8,128)(2,1)}, bf16[128,256]{1,0:T(8,128)(2,1)S(1)}, u32[]{:S(2)}, u32[]{:S(2)}) %collective-permute-start.1) | collective-permute-done | bytes 65568 | tf_op jit(solution)/shard_map/ppermute | solution.py:265
  11.2 1.4 %collective-permute-done.2 = bf16[128,256]{1,0:T(8,128)(2,1)S(1)} collective-permute-done((bf16[128,256]{1,0:T(8,128)(2,1)}, bf16[128,256]{1,0:T(8,128)(2,1)S(1)}, u32[]{:S(2)}, u32[]{:S(2)}) %collective-permute-start.2) | collective-permute-done | bytes 65568 | tf_op jit(solution)/shard_map/ppermute | solution.py:265
  12.8 1.4 %collective-permute-done.3 = bf16[4,128,256]{2,1,0:T(8,128)(2,1)S(1)} collective-permute-done((bf16[4,128,256]{2,1,0:T(8,128)(2,1)S(1)}, bf16[4,128,256]{2,1,0:T(8,128)(2,1)S(1)}, u32[]{:S(2)}, u32[]{:S(2)}) %collective-permute-start.3) | collective-permute-done | bytes 262176 | tf_op jit(solution)/shard_map/ppermute | solution.py:265
  15.1 11.3 %match_stats.1 = (f32[8,512,128]{2,1,0:T(8,128)}, f32[3,4,1024]{2,1,0:T(4,128)}) custom-call(s32[4,8]{1,0:T(4,128)} %bitcast.107, bf16[512,256]{1,0:T(8,128)(2,1)} %bitcast.103, bf16[512,256]{1,0:T(8,128)(2,1)} %bitcast.105, bf16[1024,256]{1,0:T(8,128)(2,1)} %bitcast.94, bf16[256,256]{1,0:T(8,128)(2,1)} %wq_ref.3, bf16[256,256]{1,0:T(8,128)(2,1)} %wk_ref.3, ...), custom_call_target="tpu_custom_call" | custom-call | flops 536870912 | bytes 2097152 | tf_op jit(solution)/shard_map/match_stats/pallas_call | solution.py:302
  26.4 2.3 %collective-permute-start.5 = (f32[3,4,1024]{2,1,0:T(4,128)}, f32[3,4,1024]{2,1,0:T(4,128)S(1)}, u32[]{:S(2)}, u32[]{:S(2)}) collective-permute-start(f32[3,4,1024]{2,1,0:T(4,128)} %get-tuple-element.14), channel_id=1, source_target_pairs={{0,4},{1,5},{2,6},{3,7},{4,0},{5,1},{6,2},{7,3},{8,12},{9,13},{10,... | collective-permute-start | bytes 147464 | tf_op jit(solution)/shard_map/ppermute | solution.py:265
  28.7 2.0 %collective-permute-start.6 = (f32[3,4,1024]{2,1,0:T(4,128)}, f32[3,4,1024]{2,1,0:T(4,128)S(1)}, u32[]{:S(2)}, u32[]{:S(2)}) collective-permute-start(f32[3,4,1024]{2,1,0:T(4,128)} %get-tuple-element.14), channel_id=1, source_target_pairs={{0,6},{1,7},{2,4},{3,5},{4,2},{5,3},{6,0},{7,1},{8,14},{9,15},{10,... | collective-permute-start | bytes 147464 | tf_op jit(solution)/shard_map/ppermute | solution.py:265
  31.7 3.1 %collective-permute-done.6 = f32[3,4,1024]{2,1,0:T(4,128)S(1)} collective-permute-done((f32[3,4,1024]{2,1,0:T(4,128)}, f32[3,4,1024]{2,1,0:T(4,128)S(1)}, u32[]{:S(2)}, u32[]{:S(2)}) %collective-permute-start.6) | collective-permute-done | bytes 49184 | tf_op jit(solution)/shard_map/ppermute | solution.py:265
  38.3 17.5 %match_grads.1 = (bf16[512,256]{1,0:T(8,128)(2,1)}, bf16[512,256]{1,0:T(8,128)(2,1)}, bf16[1024,256]{1,0:T(8,128)(2,1)}, bf16[4,256,256]{2,1,0:T(8,128)(2,1)}) custom-call(s32[4,8]{1,0:T(4,128)} %bitcast.108, bf16[512,256]{1,0:T(8,128)(2,1)} %bitcast.104, bf16[512,256]{1,0:T(8,128)(2,1)} %bitcast.106, bf16[1024,256]{1,0:T(8,128)(2,1)} %bitcast.95, ...), custom_call_target="tpu_custom_call" | custom-call | flops 1610612736 | bytes 4194304 | tf_op jit(solution)/shard_map/match_grads/pallas_call | solution.py:302
  57.1 1.4 %collective-permute-done.12 = bf16[4,4,32,256]{3,2,1,0:T(8,128)(2,1)S(1)} collective-permute-done((bf16[4,4,32,256]{3,2,1,0:T(8,128)(2,1)S(1)}, bf16[4,4,32,256]{3,2,1,0:T(8,128)(2,1)S(1)}, u32[]{:S(2)}, u32[]{:S(2)}) %collective-permute-start.12) | collective-permute-done | bytes 262176 | tf_op jit(solution)/shard_map/ppermute | solution.py:265
  59.5 1.6 %collective-permute-start.13 = (bf16[4,32,256]{2,1,0:T(8,128)(2,1)S(1)}, bf16[4,32,256]{2,1,0:T(8,128)(2,1)S(1)}, u32[]{:S(2)}, u32[]{:S(2)}) collective-permute-start(bf16[4,32,256]{2,1,0:T(8,128)(2,1)S(1)} %get-tuple-element.27), channel_id=1, source_target_pairs={{0,8},{8,0},{16,24},{24,16},{1,9},{9,1},{17,25},{25,17},{2,10},{10... | collective-permute-start | bytes 196616 | tf_op jit(solution)/shard_map/ppermute | solution.py:265
  61.1 1.5 %collective-permute-start.14 = (bf16[4,32,256]{2,1,0:T(8,128)(2,1)S(1)}, bf16[4,32,256]{2,1,0:T(8,128)(2,1)S(1)}, u32[]{:S(2)}, u32[]{:S(2)}) collective-permute-start(bf16[4,32,256]{2,1,0:T(8,128)(2,1)S(1)} %get-tuple-element.29), channel_id=1, source_target_pairs={{0,16},{8,24},{16,0},{24,8},{1,17},{9,25},{17,1},{25,9},{2,18},{10... | collective-permute-start | bytes 196616 | tf_op jit(solution)/shard_map/ppermute | solution.py:265
  65.3 2.4 %collective-permute-done.15 = bf16[4,32,256]{2,1,0:T(8,128)(2,1)S(1)} collective-permute-done((bf16[4,32,256]{2,1,0:T(8,128)(2,1)S(1)}, bf16[4,32,256]{2,1,0:T(8,128)(2,1)S(1)}, u32[]{:S(2)}, u32[]{:S(2)}) %collective-permute-start.15) | collective-permute-done | bytes 65568 | tf_op jit(solution)/shard_map/ppermute | solution.py:265
  67.9 2.7 %collective-permute-start.17 = (bf16[32,256]{1,0:T(8,128)(2,1)S(1)}, bf16[32,256]{1,0:T(8,128)(2,1)S(1)}, u32[]{:S(2)}, u32[]{:S(2)}) collective-permute-start(bf16[32,256]{1,0:T(8,128)(2,1)S(1)} %get-tuple-element.35), channel_id=1, source_target_pairs={{0,4},{1,5},{2,6},{3,7},{4,0},{5,1},{6,2},{7,3},{8,12},{9,13},{10,... | collective-permute-start | bytes 49160 | tf_op jit(solution)/shard_map/ppermute | solution.py:265
  70.6 1.7 %collective-permute-start.18 = (bf16[32,256]{1,0:T(8,128)(2,1)S(1)}, bf16[32,256]{1,0:T(8,128)(2,1)S(1)}, u32[]{:S(2)}, u32[]{:S(2)}) collective-permute-start(bf16[32,256]{1,0:T(8,128)(2,1)S(1)} %get-tuple-element.34), channel_id=1, source_target_pairs={{0,6},{1,7},{2,4},{3,5},{4,2},{5,3},{6,0},{7,1},{8,14},{9,15},{10,... | collective-permute-start | bytes 49160 | tf_op jit(solution)/shard_map/ppermute | solution.py:265
  72.6 3.5 %collective-permute-done.18 = bf16[32,256]{1,0:T(8,128)(2,1)S(1)} collective-permute-done((bf16[32,256]{1,0:T(8,128)(2,1)S(1)}, bf16[32,256]{1,0:T(8,128)(2,1)S(1)}, u32[]{:S(2)}, u32[]{:S(2)}) %collective-permute-start.18) | collective-permute-done | bytes 16416 | tf_op jit(solution)/shard_map/ppermute | solution.py:265
  76.3 2.4 %collective-permute-start.10 = (bf16[128,256]{1,0:T(8,128)(2,1)S(1)}, bf16[128,256]{1,0:T(8,128)(2,1)S(1)}, u32[]{:S(2)}, u32[]{:S(2)}) collective-permute-start(bf16[128,256]{1,0:T(8,128)(2,1)S(1)} %get-tuple-element.32), channel_id=1, source_target_pairs={{0,4},{1,5},{2,6},{3,7},{4,0},{5,1},{6,2},{7,3},{8,12},{9,13},{10,... | collective-permute-start | bytes 196616 | tf_op jit(solution)/shard_map/ppermute | solution.py:265
  78.7 2.0 %collective-permute-start.11 = (bf16[128,256]{1,0:T(8,128)(2,1)S(1)}, bf16[128,256]{1,0:T(8,128)(2,1)S(1)}, u32[]{:S(2)}, u32[]{:S(2)}) collective-permute-start(bf16[128,256]{1,0:T(8,128)(2,1)S(1)} %get-tuple-element.31), channel_id=1, source_target_pairs={{0,6},{1,7},{2,4},{3,5},{4,2},{5,3},{6,0},{7,1},{8,14},{9,15},{10,... | collective-permute-start | bytes 196616 | tf_op jit(solution)/shard_map/ppermute | solution.py:265
  80.7 2.4 %collective-permute-start.20 = (bf16[32,256]{1,0:T(8,128)(2,1)S(1)}, bf16[32,256]{1,0:T(8,128)(2,1)S(1)}, u32[]{:S(2)}, u32[]{:S(2)}) collective-permute-start(bf16[32,256]{1,0:T(8,128)(2,1)S(1)} %get-tuple-element.20), channel_id=1, source_target_pairs={{0,4},{1,5},{2,6},{3,7},{4,0},{5,1},{6,2},{7,3},{8,12},{9,13},{10,... | collective-permute-start | bytes 49160 | tf_op jit(solution)/shard_map/ppermute | solution.py:265
  83.1 2.0 %collective-permute-start.21 = (bf16[32,256]{1,0:T(8,128)(2,1)S(1)}, bf16[32,256]{1,0:T(8,128)(2,1)S(1)}, u32[]{:S(2)}, u32[]{:S(2)}) collective-permute-start(bf16[32,256]{1,0:T(8,128)(2,1)S(1)} %get-tuple-element.20), channel_id=1, source_target_pairs={{0,6},{1,7},{2,4},{3,5},{4,2},{5,3},{6,0},{7,1},{8,14},{9,15},{10,... | collective-permute-start | bytes 49160 | tf_op jit(solution)/shard_map/ppermute | solution.py:265
  85.4 3.3 %collective-permute-done.21 = bf16[32,256]{1,0:T(8,128)(2,1)S(1)} collective-permute-done((bf16[32,256]{1,0:T(8,128)(2,1)S(1)}, bf16[32,256]{1,0:T(8,128)(2,1)S(1)}, u32[]{:S(2)}, u32[]{:S(2)}) %collective-permute-start.21) | collective-permute-done | bytes 16416 | tf_op jit(solution)/shard_map/ppermute | solution.py:265
  89.7 3.2 %collective-permute-done.22 = bf16[4,32,256]{2,1,0:T(8,128)(2,1)S(1)} collective-permute-done((bf16[4,32,256]{2,1,0:T(8,128)(2,1)S(1)}, bf16[4,32,256]{2,1,0:T(8,128)(2,1)S(1)}, u32[]{:S(2)}, u32[]{:S(2)}) %collective-permute-start.22) | collective-permute-done | bytes 65568 | tf_op jit(solution)/shard_map/ppermute | solution.py:265
  93.4 4.7 %collective-permute-done.24 = bf16[4,32,256]{2,1,0:T(8,128)(2,1)S(1)} collective-permute-done((bf16[4,32,256]{2,1,0:T(8,128)(2,1)S(1)}, bf16[4,32,256]{2,1,0:T(8,128)(2,1)S(1)}, u32[]{:S(2)}, u32[]{:S(2)}) %collective-permute-start.24) | collective-permute-done | bytes 65568 | tf_op jit(solution)/shard_map/ppermute | solution.py:265
  (73 shorter events, 16.3 us)
Async XLA Ops:
  0.6 6.6 %collective-permute-start = (bf16[128,256]{1,0:T(8,128)(2,1)}, bf16[128,256]{1,0:T(8,128)(2,1)S(1)}, u32[]{:S(2)}, u32[]{:S(2)}) collective-permute-start(bf16[128,256]{1,0:T(8,128)(2,1)} %bitcast.100), channel_id=1, source_target_pairs={{0,2},{1,3},{2,0},{3,1},{4,6},{5,7},{6,4},{7,5},{8,10},{9,11},{10,... | collective-permute-start | bytes 196616 | tf_op jit(solution)/shard_map/ppermute | solution.py:265
  3.7 7.5 %collective-permute-start.1 = (bf16[128,256]{1,0:T(8,128)(2,1)}, bf16[128,256]{1,0:T(8,128)(2,1)S(1)}, u32[]{:S(2)}, u32[]{:S(2)}) collective-permute-start(bf16[128,256]{1,0:T(8,128)(2,1)} %bitcast.101), channel_id=1, source_target_pairs={{0,4},{1,5},{2,6},{3,7},{4,0},{5,1},{6,2},{7,3},{8,12},{9,13},{10,... | collective-permute-start | bytes 196616 | tf_op jit(solution)/shard_map/ppermute | solution.py:265
  6.3 6.3 %collective-permute-start.2 = (bf16[128,256]{1,0:T(8,128)(2,1)}, bf16[128,256]{1,0:T(8,128)(2,1)S(1)}, u32[]{:S(2)}, u32[]{:S(2)}) collective-permute-start(bf16[128,256]{1,0:T(8,128)(2,1)} %bitcast.102), channel_id=1, source_target_pairs={{0,6},{1,7},{2,4},{3,5},{4,2},{5,3},{6,0},{7,1},{8,14},{9,15},{10,... | collective-permute-start | bytes 196616 | tf_op jit(solution)/shard_map/ppermute | solution.py:265
  12.6 1.6 %collective-permute-start.3 = (bf16[4,128,256]{2,1,0:T(8,128)(2,1)S(1)}, bf16[4,128,256]{2,1,0:T(8,128)(2,1)S(1)}, u32[]{:S(2)}, u32[]{:S(2)}) collective-permute-start(bf16[4,128,256]{2,1,0:T(8,128)(2,1)S(1)} %bitcast_dynamic-update-slice_fusion.8), channel_id=1, source_target_pairs={{0,1},{1,0},{2,3},{3,2},{4,5},{5,4},{6,7},{7,6},{8,9},{9,8},{10,11... | collective-permute-start | bytes 786440 | tf_op jit(solution)/shard_map/ppermute | solution.py:265
  26.4 5.3 %collective-permute-start.4 = (f32[3,4,1024]{2,1,0:T(4,128)}, f32[3,4,1024]{2,1,0:T(4,128)S(1)}, u32[]{:S(2)}, u32[]{:S(2)}) collective-permute-start(f32[3,4,1024]{2,1,0:T(4,128)} %get-tuple-element.14), channel_id=1, source_target_pairs={{0,2},{1,3},{2,0},{3,1},{4,6},{5,7},{6,4},{7,5},{8,10},{9,11},{10,... | collective-permute-start | bytes 147464 | tf_op jit(solution)/shard_map/ppermute | solution.py:265
  26.4 5.4 %collective-permute-start.5 = (f32[3,4,1024]{2,1,0:T(4,128)}, f32[3,4,1024]{2,1,0:T(4,128)S(1)}, u32[]{:S(2)}, u32[]{:S(2)}) collective-permute-start(f32[3,4,1024]{2,1,0:T(4,128)} %get-tuple-element.14), channel_id=1, source_target_pairs={{0,4},{1,5},{2,6},{3,7},{4,0},{5,1},{6,2},{7,3},{8,12},{9,13},{10,... | collective-permute-start | bytes 147464 | tf_op jit(solution)/shard_map/ppermute | solution.py:265
  28.7 6.1 %collective-permute-start.6 = (f32[3,4,1024]{2,1,0:T(4,128)}, f32[3,4,1024]{2,1,0:T(4,128)S(1)}, u32[]{:S(2)}, u32[]{:S(2)}) collective-permute-start(f32[3,4,1024]{2,1,0:T(4,128)} %get-tuple-element.14), channel_id=1, source_target_pairs={{0,6},{1,7},{2,4},{3,5},{4,2},{5,3},{6,0},{7,1},{8,14},{9,15},{10,... | collective-permute-start | bytes 147464 | tf_op jit(solution)/shard_map/ppermute | solution.py:265
  56.8 1.6 %collective-permute-start.12 = (bf16[4,4,32,256]{3,2,1,0:T(8,128)(2,1)S(1)}, bf16[4,4,32,256]{3,2,1,0:T(8,128)(2,1)S(1)}, u32[]{:S(2)}, u32[]{:S(2)}) collective-permute-start(bf16[4,4,32,256]{3,2,1,0:T(8,128)(2,1)S(1)} %dynamic-slice_bitcast_fusion), channel_id=1, source_target_pairs={{0,1},{1,0},{2,3},{3,2},{4,5},{5,4},{6,7},{7,6},{8,9},{9,8},{10,11... | collective-permute-start | bytes 786440 | tf_op jit(solution)/shard_map/ppermute | solution.py:265
  59.5 4.6 %collective-permute-start.13 = (bf16[4,32,256]{2,1,0:T(8,128)(2,1)S(1)}, bf16[4,32,256]{2,1,0:T(8,128)(2,1)S(1)}, u32[]{:S(2)}, u32[]{:S(2)}) collective-permute-start(bf16[4,32,256]{2,1,0:T(8,128)(2,1)S(1)} %get-tuple-element.27), channel_id=1, source_target_pairs={{0,8},{8,0},{16,24},{24,16},{1,9},{9,1},{17,25},{25,17},{2,10},{10... | collective-permute-start | bytes 196616 | tf_op jit(solution)/shard_map/ppermute | solution.py:265
  61.1 4.3 %collective-permute-start.14 = (bf16[4,32,256]{2,1,0:T(8,128)(2,1)S(1)}, bf16[4,32,256]{2,1,0:T(8,128)(2,1)S(1)}, u32[]{:S(2)}, u32[]{:S(2)}) collective-permute-start(bf16[4,32,256]{2,1,0:T(8,128)(2,1)S(1)} %get-tuple-element.29), channel_id=1, source_target_pairs={{0,16},{8,24},{16,0},{24,8},{1,17},{9,25},{17,1},{25,9},{2,18},{10... | collective-permute-start | bytes 196616 | tf_op jit(solution)/shard_map/ppermute | solution.py:265
  62.6 5.2 %collective-permute-start.15 = (bf16[4,32,256]{2,1,0:T(8,128)(2,1)S(1)}, bf16[4,32,256]{2,1,0:T(8,128)(2,1)S(1)}, u32[]{:S(2)}, u32[]{:S(2)}) collective-permute-start(bf16[4,32,256]{2,1,0:T(8,128)(2,1)S(1)} %get-tuple-element.28), channel_id=1, source_target_pairs={{0,24},{8,16},{16,8},{24,0},{1,25},{9,17},{17,9},{25,1},{2,26},{10... | collective-permute-start | bytes 196616 | tf_op jit(solution)/shard_map/ppermute | solution.py:265
  64.0 8.2 %collective-permute-start.8 = (bf16[4,128,256]{2,1,0:T(8,128)(2,1)S(1)}, bf16[4,128,256]{2,1,0:T(8,128)(2,1)S(1)}, u32[]{:S(2)}, u32[]{:S(2)}) collective-permute-start(bf16[4,128,256]{2,1,0:T(8,128)(2,1)S(1)} %dynamic-slice_bitcast_fusion.1), channel_id=1, source_target_pairs={{0,1},{1,0},{2,3},{3,2},{4,5},{5,4},{6,7},{7,6},{8,9},{9,8},{10,11... | collective-permute-start | bytes 786440 | tf_op jit(solution)/shard_map/ppermute | solution.py:265
  67.8 4.5 %collective-permute-start.16 = (bf16[32,256]{1,0:T(8,128)(2,1)S(1)}, bf16[32,256]{1,0:T(8,128)(2,1)S(1)}, u32[]{:S(2)}, u32[]{:S(2)}) collective-permute-start(bf16[32,256]{1,0:T(8,128)(2,1)S(1)} %get-tuple-element.33), channel_id=1, source_target_pairs={{0,2},{1,3},{2,0},{3,1},{4,6},{5,7},{6,4},{7,5},{8,10},{9,11},{10,... | collective-permute-start | bytes 49160 | tf_op jit(solution)/shard_map/ppermute | solution.py:265
  67.9 4.7 %collective-permute-start.17 = (bf16[32,256]{1,0:T(8,128)(2,1)S(1)}, bf16[32,256]{1,0:T(8,128)(2,1)S(1)}, u32[]{:S(2)}, u32[]{:S(2)}) collective-permute-start(bf16[32,256]{1,0:T(8,128)(2,1)S(1)} %get-tuple-element.35), channel_id=1, source_target_pairs={{0,4},{1,5},{2,6},{3,7},{4,0},{5,1},{6,2},{7,3},{8,12},{9,13},{10,... | collective-permute-start | bytes 49160 | tf_op jit(solution)/shard_map/ppermute | solution.py:265
  70.6 5.5 %collective-permute-start.18 = (bf16[32,256]{1,0:T(8,128)(2,1)S(1)}, bf16[32,256]{1,0:T(8,128)(2,1)S(1)}, u32[]{:S(2)}, u32[]{:S(2)}) collective-permute-start(bf16[32,256]{1,0:T(8,128)(2,1)S(1)} %get-tuple-element.34), channel_id=1, source_target_pairs={{0,6},{1,7},{2,4},{3,5},{4,2},{5,3},{6,0},{7,1},{8,14},{9,15},{10,... | collective-permute-start | bytes 49160 | tf_op jit(solution)/shard_map/ppermute | solution.py:265
  76.1 6.9 %collective-permute-start.19 = (bf16[32,256]{1,0:T(8,128)(2,1)S(1)}, bf16[32,256]{1,0:T(8,128)(2,1)S(1)}, u32[]{:S(2)}, u32[]{:S(2)}) collective-permute-start(bf16[32,256]{1,0:T(8,128)(2,1)S(1)} %get-tuple-element.20), channel_id=1, source_target_pairs={{0,2},{1,3},{2,0},{3,1},{4,6},{5,7},{6,4},{7,5},{8,10},{9,11},{10,... | collective-permute-start | bytes 49160 | tf_op jit(solution)/shard_map/ppermute | solution.py:265
  76.3 21.9 %collective-permute-start.10 = (bf16[128,256]{1,0:T(8,128)(2,1)S(1)}, bf16[128,256]{1,0:T(8,128)(2,1)S(1)}, u32[]{:S(2)}, u32[]{:S(2)}) collective-permute-start(bf16[128,256]{1,0:T(8,128)(2,1)S(1)} %get-tuple-element.32), channel_id=1, source_target_pairs={{0,4},{1,5},{2,6},{3,7},{4,0},{5,1},{6,2},{7,3},{8,12},{9,13},{10,... | collective-permute-start | bytes 196616 | tf_op jit(solution)/shard_map/ppermute | solution.py:265
  78.7 19.5 %collective-permute-start.11 = (bf16[128,256]{1,0:T(8,128)(2,1)S(1)}, bf16[128,256]{1,0:T(8,128)(2,1)S(1)}, u32[]{:S(2)}, u32[]{:S(2)}) collective-permute-start(bf16[128,256]{1,0:T(8,128)(2,1)S(1)} %get-tuple-element.31), channel_id=1, source_target_pairs={{0,6},{1,7},{2,4},{3,5},{4,2},{5,3},{6,0},{7,1},{8,14},{9,15},{10,... | collective-permute-start | bytes 196616 | tf_op jit(solution)/shard_map/ppermute | solution.py:265
  80.7 17.5 %collective-permute-start.9 = (bf16[128,256]{1,0:T(8,128)(2,1)S(1)}, bf16[128,256]{1,0:T(8,128)(2,1)S(1)}, u32[]{:S(2)}, u32[]{:S(2)}) collective-permute-start(bf16[128,256]{1,0:T(8,128)(2,1)S(1)} %get-tuple-element.30), channel_id=1, source_target_pairs={{0,2},{1,3},{2,0},{3,1},{4,6},{5,7},{6,4},{7,5},{8,10},{9,11},{10,... | collective-permute-start | bytes 196616 | tf_op jit(solution)/shard_map/ppermute | solution.py:265
  80.7 4.7 %collective-permute-start.20 = (bf16[32,256]{1,0:T(8,128)(2,1)S(1)}, bf16[32,256]{1,0:T(8,128)(2,1)S(1)}, u32[]{:S(2)}, u32[]{:S(2)}) collective-permute-start(bf16[32,256]{1,0:T(8,128)(2,1)S(1)} %get-tuple-element.20), channel_id=1, source_target_pairs={{0,4},{1,5},{2,6},{3,7},{4,0},{5,1},{6,2},{7,3},{8,12},{9,13},{10,... | collective-permute-start | bytes 49160 | tf_op jit(solution)/shard_map/ppermute | solution.py:265
  83.1 5.5 %collective-permute-start.21 = (bf16[32,256]{1,0:T(8,128)(2,1)S(1)}, bf16[32,256]{1,0:T(8,128)(2,1)S(1)}, u32[]{:S(2)}, u32[]{:S(2)}) collective-permute-start(bf16[32,256]{1,0:T(8,128)(2,1)S(1)} %get-tuple-element.20), channel_id=1, source_target_pairs={{0,6},{1,7},{2,4},{3,5},{4,2},{5,3},{6,0},{7,1},{8,14},{9,15},{10,... | collective-permute-start | bytes 49160 | tf_op jit(solution)/shard_map/ppermute | solution.py:265
  88.6 4.3 %collective-permute-start.22 = (bf16[4,32,256]{2,1,0:T(8,128)(2,1)S(1)}, bf16[4,32,256]{2,1,0:T(8,128)(2,1)S(1)}, u32[]{:S(2)}, u32[]{:S(2)}) collective-permute-start(bf16[4,32,256]{2,1,0:T(8,128)(2,1)S(1)} %bitcast_dynamic-update-slice_fusion.11), channel_id=1, source_target_pairs={{0,8},{8,0},{16,24},{24,16},{1,9},{9,1},{17,25},{25,17},{2,10},{10... | collective-permute-start | bytes 196616 | tf_op jit(solution)/shard_map/ppermute | solution.py:265
  89.1 4.3 %collective-permute-start.23 = (bf16[4,32,256]{2,1,0:T(8,128)(2,1)S(1)}, bf16[4,32,256]{2,1,0:T(8,128)(2,1)S(1)}, u32[]{:S(2)}, u32[]{:S(2)}) collective-permute-start(bf16[4,32,256]{2,1,0:T(8,128)(2,1)S(1)} %bitcast_dynamic-update-slice_fusion.11), channel_id=1, source_target_pairs={{0,16},{8,24},{16,0},{24,8},{1,17},{9,25},{17,1},{25,9},{2,18},{10... | collective-permute-start | bytes 196616 | tf_op jit(solution)/shard_map/ppermute | solution.py:265
  92.9 5.2 %collective-permute-start.24 = (bf16[4,32,256]{2,1,0:T(8,128)(2,1)S(1)}, bf16[4,32,256]{2,1,0:T(8,128)(2,1)S(1)}, u32[]{:S(2)}, u32[]{:S(2)}) collective-permute-start(bf16[4,32,256]{2,1,0:T(8,128)(2,1)S(1)} %bitcast_dynamic-update-slice_fusion.11), channel_id=1, source_target_pairs={{0,24},{8,16},{16,8},{24,0},{1,25},{9,17},{17,9},{25,1},{2,26},{10... | collective-permute-start | bytes 196616 | tf_op jit(solution)/shard_map/ppermute | solution.py:265
  (6 other events, 22.1 us)

commit v4 on v3

--- a/solution.py
+++ b/solution.py
@@ -11,7 +11,7 @@
 BLOCK = 128
 NEG = -1e30
 FLOOR = -1e29
-VMEM_LIMIT = 56 * 1024 * 1024
+VMEM_LIMIT = 30 * 1024 * 1024
 
 NT = (((1,), (1,)), ((), ()))
 TN = (((0,), (0,)), ((), ()))
@@ -269,23 +269,33 @@
     return lax.dynamic_index_in_dim(x, index, axis, False)
 
 
-def laid(pieces, places, axis=0):
-    out = jnp.zeros(pieces[0].shape[:axis] + (len(pieces),) + pieces[0].shape[axis:], pieces[0].dtype)
-    for piece, place in zip(pieces, places):
-        out = lax.dynamic_update_index_in_dim(out, piece, place, axis)
-    return out
-
-
-def gather_direct(x, axis, me, count, stride):
-    pieces = [x] + [swap(x, axis, k * stride) for k in range(1, count)]
-    return laid(pieces, [me ^ k for k in range(count)])
-
-
-def scatter_direct(x, axis, me, count, stride):
-    total = at(x, me).astype(jnp.float32)
-    for piece in [swap(at(x, me ^ k), axis, k * stride) for k in range(1, count)]:
-        total = total + piece.astype(jnp.float32)
-    return total.astype(x.dtype)
+def laid(near, far, side, axis=0):
+    shape = near.shape[:axis] + (2,) + near.shape[axis:]
+    out = lax.dynamic_update_index_in_dim(jnp.zeros(shape, near.dtype), near, side, axis)
+    return lax.dynamic_update_index_in_dim(out, far, 1 - side, axis)
+
+
+def add(near, far):
+    return (near.astype(jnp.float32) + far.astype(jnp.float32)).astype(near.dtype)
+
+
+def halve(x, step, axis=0):
+    mesh_axis, bit, side = step
+    return add(at(x, side, axis), swap(at(x, 1 - side, axis), mesh_axis, bit))
+
+
+def double(x, step, axis=0):
+    mesh_axis, bit, side = step
+    return laid(x, swap(x, mesh_axis, bit), side, axis)
+
+
+def bit_steps(mesh_axis, first=1):
+    count, me = lax.axis_size(mesh_axis), lax.axis_index(mesh_axis)
+    steps = []
+    while first < count:
+        steps.append((mesh_axis, first, (me // first) % 2))
+        first *= 2
+    return steps
 
 
 def combine_stats(parts):
@@ -317,15 +327,16 @@
     out_grad = grad_out[0]
     listed = intersection[0]
     rows, width = ref_rows.shape
-    scans, chips = lax.axis_size("scan"), lax.axis_size("blk") // 2
-    scan, core = lax.axis_index("scan"), lax.axis_index("blk") % 2
-    chip = lax.axis_index("blk") // 2
+    core_step = bit_steps("blk")[0]
+    chip_steps = bit_steps("blk", 2)
+    scan_steps = bit_steps("scan")
     key_rows = src_rows.shape[0]
-    key_total = key_rows * chips * 2
-
-    same_core = gather_direct(src_rows, "blk", chip, chips, 2)
-    source_all = laid([same_core, swap(same_core, "blk", 1)], [core, 1 - core], axis=1)
-    source_all = source_all.reshape(key_total, width)
+    key_total = key_rows * lax.axis_size("blk")
+
+    source_all = src_rows
+    for count, step in enumerate(chip_steps[::-1]):
+        source_all = double(source_all, step, count)
+    source_all = double(source_all, core_step, len(chip_steps)).reshape(key_total, width)
 
     f32, b16 = jnp.float32, jnp.bfloat16
     shape = jax.ShapeDtypeStruct
@@ -351,9 +362,9 @@
         2 << 20,
         base,
     )
-    near_stats = combine_stats(
-        [col_stats] + [swap(col_stats, "blk", 2 * k) for k in range(1, chips)]
-    )
+    near_stats = col_stats
+    for mesh_axis, bit, _ in chip_steps:
+        near_stats = combine_stats([near_stats, swap(near_stats, mesh_axis, bit)])
     far_stats = swap(near_stats, "blk", 1)
     matched, grad_ref, source_part, weight_part = vmem_call(
         functools.partial(grads_kernel, HEADS),
@@ -381,17 +392,20 @@
         base + (row_stats, near_stats, far_stats),
     )
 
-    weights = weight_part.reshape(2, scans, chips, -1, width)
-    sources = source_part.reshape(chips, 2, key_rows, width)
-    weights = scatter_direct(weights, "blk", core, 2, 1)
-    near, far = at(sources, core, 1), at(sources, 1 - core, 1)
-    sources = (near.astype(f32) + swap(far, "blk", 1).astype(f32)).astype(b16)
-    weights = scatter_direct(weights, "scan", scan, scans, 1)
-    grad_src = scatter_direct(sources, "blk", chip, chips, 2)
-    weights = scatter_direct(weights, "blk", chip, chips, 2)
-    weights = gather_direct(weights, "blk", chip, chips, 2)
-    weights = gather_direct(weights, "scan", scan, scans, 1)
-    weights = gather_direct(weights, "blk", core, 2, 1)
+    halves = [core_step] + scan_steps
+    weights = weight_part.reshape((2,) * len(halves) + (-1, width))
+    sources = source_part.reshape((2,) * (len(chip_steps) + 1) + (key_rows, width))
+    weights = halve(weights, halves[0])
+    sources = halve(sources, core_step, len(chip_steps))
+    for step in halves[1:]:
+        weights = halve(weights, step)
+    for count in range(len(chip_steps)):
+        sources = halve(sources, chip_steps[count], len(chip_steps) - 1 - count)
+    grad_src = sources
+    for mesh_axis, bit, _ in chip_steps:
+        weights = add(weights, swap(weights, mesh_axis, bit))
+    for step in halves[::-1]:
+        weights = double(weights, step)
     weights = weights.reshape(4, width, width).astype(f32)
     return (
         matched[None],

time: 101 us -> 86.8 us (0.86)
  starting transfers between devices: 28.9 us -> 22.6 us
  Pallas kernels: 28.8 us -> 24.9 us
  local copies, waits for them, and re-layouts: 5.63 us -> 2.29 us
  other arithmetic: 3.46 us -> 1.11 us
  waiting for transfers between devices: 33.1 us -> 34.7 us
    ppermute x26 -> x17, starting transfers between devices: 28.9 us -> 22.6 us  [swap(): return lax.ppermute(x, axis, pairs)]
    pallas_call x2, Pallas kernels: 28.8 us -> 24.9 us  [vmem_call(): pl.pallas_call(kernel, name=name, out_shape=out_shape, in_specs=specs, ou...]
    squeeze x5, local copies, waits for them, and re-layouts: 2.05 us -> 0.06 us  [at(): return lax.dynamic_index_in_dim(x, index, axis, False)]
    ppermute x26 -> x17, waiting for transfers between devices: 33.1 us -> 34.7 us  [swap(): return lax.ppermute(x, axis, pairs)]
    unnamed x8 -> x14, local copies, waits for them, and re-layouts: 1.42 us -> 0.03 us
  transfers between devices with their start and end apart: 26 -> 17, of which waited for: 17 -> 14; matrix products, arithmetic and copies ran while one was open for 3% -> 2% of each run, Pallas kernels for 0% -> 0%
where the time goes in v4:
time: 86.8 us; the launch traced here: 86.6 us
  waiting for transfers between devices  34.7 us (40%)
  Pallas kernels  24.9 us (29%)
  starting transfers between devices  22.6 us (26%)
  local copies, waits for them, and re-layouts  2.29 us (3%)
  other arithmetic  1.11 us (1%)
  between operations  1.01 us (1%)
    ppermute x17, waiting for transfers between devices, swap(): return lax.ppermute(x, axis, pairs)  34.7 us
    pallas_call x2, Pallas kernels, vmem_call(): pl.pallas_call(kernel, name=name, out_shape=out_shape, in_specs=specs, ou...  24.9 us
    ppermute x17, starting transfers between devices, swap(): return lax.ppermute(x, axis, pairs)  22.6 us
  transfers between devices with their start and end apart: 17, of which 14 were waited for; matrix products, arithmetic and copies ran while one was open for 2% of the time, Pallas kernels for 0%

profile of v4, /device:TPU:0, one launch (start us, length us, event | category | flops | bytes accessed | tf_op | source)
XLA Modules:
  0.0 86.6 jit_solution(16775560302831348302)
XLA Ops:
  0.7 4.1 %collective-permute-start = (bf16[128,256]{1,0:T(8,128)(2,1)}, bf16[128,256]{1,0:T(8,128)(2,1)S(1)}, u32[]{:S(2)}, u32[]{:S(2)}) collective-permute-start(bf16[128,256]{1,0:T(8,128)(2,1)} %bitcast.93), channel_id=1, source_target_pairs={{0,4},{1,5},{2,6},{3,7},{4,0},{5,1},{6,2},{7,3},{8,12},{9,13},{10,... | collective-permute-start | bytes 196616 | tf_op jit(solution)/shard_map/ppermute | solution.py:265
  5.7 3.0 %collective-permute-done = bf16[128,256]{1,0:T(8,128)(2,1)S(1)} collective-permute-done((bf16[128,256]{1,0:T(8,128)(2,1)}, bf16[128,256]{1,0:T(8,128)(2,1)S(1)}, u32[]{:S(2)}, u32[]{:S(2)}) %collective-permute-start) | collective-permute-done | bytes 65568 | tf_op jit(solution)/shard_map/ppermute | solution.py:265
  9.5 4.3 %collective-permute-done.1 = bf16[2,128,256]{2,1,0:T(8,128)(2,1)S(1)} collective-permute-done((bf16[2,128,256]{2,1,0:T(8,128)(2,1)S(1)}, bf16[2,128,256]{2,1,0:T(8,128)(2,1)S(1)}, u32[]{:S(2)}, u32[]{:S(2)}) %collective-permute-start.1) | collective-permute-done | bytes 131104 | tf_op jit(solution)/shard_map/ppermute | solution.py:265
  13.9 1.4 %collective-permute-done.2 = bf16[2,2,128,256]{3,2,1,0:T(8,128)(2,1)S(1)} collective-permute-done((bf16[2,2,128,256]{3,2,1,0:T(8,128)(2,1)S(1)}, bf16[2,2,128,256]{3,2,1,0:T(8,128)(2,1)S(1)}, u32[]{:S(2)}, u32[]{:S(2)}) %collective-permute-start.2) | collective-permute-done | bytes 262176 | tf_op jit(solution)/shard_map/ppermute | solution.py:265
  15.4 9.1 %match_stats.1 = (f32[8,512,128]{2,1,0:T(8,128)S(1)}, f32[3,4,1024]{2,1,0:T(4,128)S(1)}) custom-call(s32[4,8]{1,0:T(4,128)S(1)} %bitcast.89, bf16[512,256]{1,0:T(8,128)(2,1)S(1)} %bitcast.85, bf16[512,256]{1,0:T(8,128)(2,1)S(1)} %bitcast.87, bf16[1024,256]{1,0:T(8,128)(2,1)S(1)} %bitcast.81, bf16[256,256]{1,0:T(8,128)(2,1)S(1)} %copy-done.2, ...), custom_call_target="tpu_custom_call" | custom-call | flops 536870912 | bytes 2097152 | tf_op jit(solution)/shard_map/match_stats/pallas_call | solution.py:312
  25.3 3.4 %collective-permute-done.3 = f32[3,4,1024]{2,1,0:T(4,128)S(1)} collective-permute-done((f32[3,4,1024]{2,1,0:T(4,128)S(1)}, f32[3,4,1024]{2,1,0:T(4,128)S(1)}, u32[]{:S(2)}, u32[]{:S(2)}) %collective-permute-start.3) | collective-permute-done | bytes 49184 | tf_op jit(solution)/shard_map/ppermute | solution.py:265
  28.8 2.4 %collective-permute-start.4 = (f32[3,4,1024]{2,1,0:T(4,128)S(1)}, f32[3,4,1024]{2,1,0:T(4,128)S(1)}, u32[]{:S(2)}, u32[]{:S(2)}) collective-permute-start(f32[3,4,1024]{2,1,0:T(4,128)S(1)} %pad_maximum_fusion), channel_id=1, source_target_pairs={{0,4},{1,5},{2,6},{3,7},{4,0},{5,1},{6,2},{7,3},{8,12},{9,13},{10,... | collective-permute-start | bytes 147464 | tf_op jit(solution)/shard_map/ppermute | solution.py:265
  31.1 2.7 %collective-permute-done.4 = f32[3,4,1024]{2,1,0:T(4,128)S(1)} collective-permute-done((f32[3,4,1024]{2,1,0:T(4,128)S(1)}, f32[3,4,1024]{2,1,0:T(4,128)S(1)}, u32[]{:S(2)}, u32[]{:S(2)}) %collective-permute-start.4) | collective-permute-done | bytes 49184 | tf_op jit(solution)/shard_map/ppermute | solution.py:265
  34.0 1.2 %collective-permute-done.5.far_ref = f32[3,4,1024]{2,1,0:T(4,128)S(1)} collective-permute-done((f32[3,4,1024]{2,1,0:T(4,128)S(1)}, f32[3,4,1024]{2,1,0:T(4,128)S(1)}, u32[]{:S(2)}, u32[]{:S(2)}) %collective-permute-start.5) | collective-permute-done | bytes 49184 | tf_op jit(solution)/shard_map/ppermute | solution.py:265
  35.2 15.8 %match_grads.1 = (bf16[512,256]{1,0:T(8,128)(2,1)}, bf16[512,256]{1,0:T(8,128)(2,1)}, bf16[1024,256]{1,0:T(8,128)(2,1)S(1)}, bf16[4,256,256]{2,1,0:T(8,128)(2,1)S(1)}) custom-call(s32[4,8]{1,0:T(4,128)S(1)} %bitcast.90, bf16[512,256]{1,0:T(8,128)(2,1)S(1)} %bitcast.86, bf16[512,256]{1,0:T(8,128)(2,1)S(1)} %bitcast.88, bf16[1024,256]{1,0:T(8,128)(2,1)S(1)} %bitcast.82, ...), custom_call_target="tpu_custom_call" | custom-call | flops 1610612736 | bytes 4194304 | tf_op jit(solution)/shard_map/match_grads/pallas_call | solution.py:312
  51.2 1.4 %collective-permute-done.9 = bf16[2,2,128,256]{3,2,1,0:T(8,128)(2,1)S(1)} collective-permute-done((bf16[2,2,128,256]{3,2,1,0:T(8,128)(2,1)S(1)}, bf16[2,2,128,256]{3,2,1,0:T(8,128)(2,1)S(1)}, u32[]{:S(2)}, u32[]{:S(2)}) %collective-permute-start.9) | collective-permute-done | bytes 262176 | tf_op jit(solution)/shard_map/ppermute | solution.py:265
  52.7 2.3 %collective-permute-start.10 = (bf16[2,128,256]{2,1,0:T(8,128)(2,1)S(1)}, bf16[2,128,256]{2,1,0:T(8,128)(2,1)S(1)}, u32[]{:S(2)}, u32[]{:S(2)}) collective-permute-start(bf16[2,128,256]{2,1,0:T(8,128)(2,1)S(1)} %dynamic-slice_bitcast_fusion.1), channel_id=1, source_target_pairs={{0,8},{8,0},{16,24},{24,16},{1,9},{9,1},{17,25},{25,17},{2,10},{10... | collective-permute-start | bytes 393224 | tf_op jit(solution)/shard_map/ppermute | solution.py:265
  55.1 3.7 %collective-permute-done.10 = bf16[2,128,256]{2,1,0:T(8,128)(2,1)S(1)} collective-permute-done((bf16[2,128,256]{2,1,0:T(8,128)(2,1)S(1)}, bf16[2,128,256]{2,1,0:T(8,128)(2,1)S(1)}, u32[]{:S(2)}, u32[]{:S(2)}) %collective-permute-start.10) | collective-permute-done | bytes 131104 | tf_op jit(solution)/shard_map/ppermute | solution.py:265
  58.8 1.8 %collective-permute-start.11 = (bf16[128,256]{1,0:T(8,128)(2,1)S(1)}, bf16[128,256]{1,0:T(8,128)(2,1)S(1)}, u32[]{:S(2)}, u32[]{:S(2)}) collective-permute-start(bf16[128,256]{1,0:T(8,128)(2,1)S(1)} %dynamic-slice_bitcast_fusion.3), channel_id=1, source_target_pairs={{0,16},{8,24},{16,0},{24,8},{1,17},{9,25},{17,1},{25,9},{2,18},{10... | collective-permute-start | bytes 196616 | tf_op jit(solution)/shard_map/ppermute | solution.py:265
  60.7 2.4 %collective-permute-done.11 = bf16[128,256]{1,0:T(8,128)(2,1)S(1)} collective-permute-done((bf16[128,256]{1,0:T(8,128)(2,1)S(1)}, bf16[128,256]{1,0:T(8,128)(2,1)S(1)}, u32[]{:S(2)}, u32[]{:S(2)}) %collective-permute-start.11) | collective-permute-done | bytes 65568 | tf_op jit(solution)/shard_map/ppermute | solution.py:265
  63.9 1.4 %collective-permute-start.7 = (bf16[2,128,256]{2,1,0:T(8,128)(2,1)S(1)}, bf16[2,128,256]{2,1,0:T(8,128)(2,1)S(1)}, u32[]{:S(2)}, u32[]{:S(2)}) collective-permute-start(bf16[2,128,256]{2,1,0:T(8,128)(2,1)S(1)} %dynamic-slice_bitcast_fusion.2), channel_id=1, source_target_pairs={{0,2},{1,3},{2,0},{3,1},{4,6},{5,7},{6,4},{7,5},{8,10},{9,11},{10,... | collective-permute-start | bytes 393224 | tf_op jit(solution)/shard_map/ppermute | solution.py:265
  65.4 2.2 %collective-permute-done.12 = bf16[128,256]{1,0:T(8,128)(2,1)S(1)} collective-permute-done((bf16[128,256]{1,0:T(8,128)(2,1)S(1)}, bf16[128,256]{1,0:T(8,128)(2,1)S(1)}, u32[]{:S(2)}, u32[]{:S(2)}) %collective-permute-start.12) | collective-permute-done | bytes 65568 | tf_op jit(solution)/shard_map/ppermute | solution.py:265
  67.5 2.6 %collective-permute-start.13 = (bf16[128,256]{1,0:T(8,128)(2,1)S(1)}, bf16[128,256]{1,0:T(8,128)(2,1)S(1)}, u32[]{:S(2)}, u32[]{:S(2)}) collective-permute-start(bf16[128,256]{1,0:T(8,128)(2,1)S(1)} %add_convert_fusion.1), channel_id=1, source_target_pairs={{0,4},{1,5},{2,6},{3,7},{4,0},{5,1},{6,2},{7,3},{8,12},{9,13},{10,... | collective-permute-start | bytes 196616 | tf_op jit(solution)/shard_map/ppermute | solution.py:265
  70.2 3.3 %collective-permute-done.13 = bf16[128,256]{1,0:T(8,128)(2,1)S(1)} collective-permute-done((bf16[128,256]{1,0:T(8,128)(2,1)S(1)}, bf16[128,256]{1,0:T(8,128)(2,1)S(1)}, u32[]{:S(2)}, u32[]{:S(2)}) %collective-permute-start.13) | collective-permute-done | bytes 65568 | tf_op jit(solution)/shard_map/ppermute | solution.py:265
  73.5 3.1 %collective-permute-start.14 = (bf16[128,256]{1,0:T(8,128)(2,1)S(1)}, bf16[128,256]{1,0:T(8,128)(2,1)S(1)}, u32[]{:S(2)}, u32[]{:S(2)}) collective-permute-start(bf16[128,256]{1,0:T(8,128)(2,1)S(1)} %get-tuple-element.20), channel_id=1, source_target_pairs={{0,16},{8,24},{16,0},{24,8},{1,17},{9,25},{17,1},{25,9},{2,18},{10... | collective-permute-start | bytes 196616 | tf_op jit(solution)/shard_map/ppermute | solution.py:265
  77.2 1.6 %collective-permute-done.14 = bf16[128,256]{1,0:T(8,128)(2,1)S(1)} collective-permute-done((bf16[128,256]{1,0:T(8,128)(2,1)S(1)}, bf16[128,256]{1,0:T(8,128)(2,1)S(1)}, u32[]{:S(2)}, u32[]{:S(2)}) %collective-permute-start.14) | collective-permute-done | bytes 65568 | tf_op jit(solution)/shard_map/ppermute | solution.py:265
  78.8 1.6 %collective-permute-start.15 = (bf16[2,128,256]{2,1,0:T(8,128)(2,1)S(1)}, bf16[2,128,256]{2,1,0:T(8,128)(2,1)S(1)}, u32[]{:S(2)}, u32[]{:S(2)}) collective-permute-start(bf16[2,128,256]{2,1,0:T(8,128)(2,1)S(1)} %bitcast_dynamic-update-slice_fusion.8), channel_id=1, source_target_pairs={{0,8},{8,0},{16,24},{24,16},{1,9},{9,1},{17,25},{25,17},{2,10},{10... | collective-permute-start | bytes 393224 | tf_op jit(solution)/shard_map/ppermute | solution.py:265
  80.5 3.4 %collective-permute-done.15 = bf16[2,128,256]{2,1,0:T(8,128)(2,1)S(1)} collective-permute-done((bf16[2,128,256]{2,1,0:T(8,128)(2,1)S(1)}, bf16[2,128,256]{2,1,0:T(8,128)(2,1)S(1)}, u32[]{:S(2)}, u32[]{:S(2)}) %collective-permute-start.15) | collective-permute-done | bytes 131104 | tf_op jit(solution)/shard_map/ppermute | solution.py:265
  85.6 1.0 %slice_bitcast_fusion = (f32[256,256]{1,0:T(8,128)}, f32[256,256]{1,0:T(8,128)}, f32[256,256]{1,0:T(8,128)}, f32[256,256]{1,0:T(8,128)}) fusion(f32[4,256,256]{2,1,0:T(8,128)S(1)} %convert.7), kind=kLoop, calls=%fused_computation.4 | loop fusion | bytes 2097152 | tf_op jit(solution)/shard_map/squeeze | solution.py:417
  (65 shorter events, 6.5 us)
Async XLA Ops:
  0.6 14.7 %copy-start.6 = (s32[1,4,8]{2,1,0:T(4,128)S(1)}, s32[1,4,8]{2,1,0:T(4,128)}, u32[]{:S(2)}) copy-start(s32[1,4,8]{2,1,0:T(4,128)} %param.15) | copy-start | bytes 388
  0.6 14.7 %copy-start = (bf16[1,512,256]{2,1,0:T(8,128)(2,1)S(1)}, bf16[1,512,256]{2,1,0:T(8,128)(2,1)}, u32[]{:S(2)}) copy-start(bf16[1,512,256]{2,1,0:T(8,128)(2,1)} %param.8) | copy-start | bytes 786436
  0.7 14.7 %copy-start.1 = (bf16[1,512,256]{2,1,0:T(8,128)(2,1)S(1)}, bf16[1,512,256]{2,1,0:T(8,128)(2,1)}, u32[]{:S(2)}) copy-start(bf16[1,512,256]{2,1,0:T(8,128)(2,1)} %param.10) | copy-start | bytes 786436
  0.7 14.7 %copy-start.2 = (bf16[256,256]{1,0:T(8,128)(2,1)S(1)}, bf16[256,256]{1,0:T(8,128)(2,1)}, u32[]{:S(2)}) copy-start(bf16[256,256]{1,0:T(8,128)(2,1)} %wq_ref.3) | copy-start | bytes 393220
  0.7 14.7 %copy-start.3 = (bf16[256,256]{1,0:T(8,128)(2,1)S(1)}, bf16[256,256]{1,0:T(8,128)(2,1)}, u32[]{:S(2)}) copy-start(bf16[256,256]{1,0:T(8,128)(2,1)} %wk_ref.3) | copy-start | bytes 393220
  0.7 14.7 %copy-start.4 = (bf16[256,256]{1,0:T(8,128)(2,1)S(1)}, bf16[256,256]{1,0:T(8,128)(2,1)}, u32[]{:S(2)}) copy-start(bf16[256,256]{1,0:T(8,128)(2,1)} %wv_ref.3) | copy-start | bytes 393220
  0.7 14.7 %copy-start.5 = (bf16[256,256]{1,0:T(8,128)(2,1)S(1)}, bf16[256,256]{1,0:T(8,128)(2,1)}, u32[]{:S(2)}) copy-start(bf16[256,256]{1,0:T(8,128)(2,1)} %wo_ref.3) | copy-start | bytes 393220
  0.7 8.0 %collective-permute-start = (bf16[128,256]{1,0:T(8,128)(2,1)}, bf16[128,256]{1,0:T(8,128)(2,1)S(1)}, u32[]{:S(2)}, u32[]{:S(2)}) collective-permute-start(bf16[128,256]{1,0:T(8,128)(2,1)} %bitcast.93), channel_id=1, source_target_pairs={{0,4},{1,5},{2,6},{3,7},{4,0},{5,1},{6,2},{7,3},{8,12},{9,13},{10,... | collective-permute-start | bytes 196616 | tf_op jit(solution)/shard_map/ppermute | solution.py:265
  8.7 5.0 %collective-permute-start.1 = (bf16[2,128,256]{2,1,0:T(8,128)(2,1)S(1)}, bf16[2,128,256]{2,1,0:T(8,128)(2,1)S(1)}, u32[]{:S(2)}, u32[]{:S(2)}) collective-permute-start(bf16[2,128,256]{2,1,0:T(8,128)(2,1)S(1)} %bitcast_dynamic-update-slice_fusion.10), channel_id=1, source_target_pairs={{0,2},{1,3},{2,0},{3,1},{4,6},{5,7},{6,4},{7,5},{8,10},{9,11},{10,... | collective-permute-start | bytes 393224 | tf_op jit(solution)/shard_map/ppermute | solution.py:265
  13.7 1.6 %collective-permute-start.2 = (bf16[2,2,128,256]{3,2,1,0:T(8,128)(2,1)S(1)}, bf16[2,2,128,256]{3,2,1,0:T(8,128)(2,1)S(1)}, u32[]{:S(2)}, u32[]{:S(2)}) collective-permute-start(bf16[2,2,128,256]{3,2,1,0:T(8,128)(2,1)S(1)} %bitcast_dynamic-update-slice_fusion.7), channel_id=1, source_target_pairs={{0,1},{1,0},{2,3},{3,2},{4,5},{5,4},{6,7},{7,6},{8,9},{9,8},{10,11... | collective-permute-start | bytes 786440 | tf_op jit(solution)/shard_map/ppermute | solution.py:265
  24.5 4.2 %collective-permute-start.3 = (f32[3,4,1024]{2,1,0:T(4,128)S(1)}, f32[3,4,1024]{2,1,0:T(4,128)S(1)}, u32[]{:S(2)}, u32[]{:S(2)}) collective-permute-start(f32[3,4,1024]{2,1,0:T(4,128)S(1)} %get-tuple-element.14), channel_id=1, source_target_pairs={{0,2},{1,3},{2,0},{3,1},{4,6},{5,7},{6,4},{7,5},{8,10},{9,11},{10,... | collective-permute-start | bytes 147464 | tf_op jit(solution)/shard_map/ppermute | solution.py:265
  28.8 5.1 %collective-permute-start.4 = (f32[3,4,1024]{2,1,0:T(4,128)S(1)}, f32[3,4,1024]{2,1,0:T(4,128)S(1)}, u32[]{:S(2)}, u32[]{:S(2)}) collective-permute-start(f32[3,4,1024]{2,1,0:T(4,128)S(1)} %pad_maximum_fusion), channel_id=1, source_target_pairs={{0,4},{1,5},{2,6},{3,7},{4,0},{5,1},{6,2},{7,3},{8,12},{9,13},{10,... | collective-permute-start | bytes 147464 | tf_op jit(solution)/shard_map/ppermute | solution.py:265
  33.9 1.3 %collective-permute-start.5 = (f32[3,4,1024]{2,1,0:T(4,128)S(1)}, f32[3,4,1024]{2,1,0:T(4,128)S(1)}, u32[]{:S(2)}, u32[]{:S(2)}) collective-permute-start(f32[3,4,1024]{2,1,0:T(4,128)S(1)} %pad_maximum_fusion.1.near_ref), channel_id=1, source_target_pairs={{0,1},{1,0},{2,3},{3,2},{4,5},{5,4},{6,7},{7,6},{8,9},{9,8},{10,11... | collective-permute-start | bytes 147464 | tf_op jit(solution)/shard_map/ppermute | solution.py:265
  51.0 1.6 %collective-permute-start.9 = (bf16[2,2,128,256]{3,2,1,0:T(8,128)(2,1)S(1)}, bf16[2,2,128,256]{3,2,1,0:T(8,128)(2,1)S(1)}, u32[]{:S(2)}, u32[]{:S(2)}) collective-permute-start(bf16[2,2,128,256]{3,2,1,0:T(8,128)(2,1)S(1)} %dynamic-slice_bitcast_fusion), channel_id=1, source_target_pairs={{0,1},{1,0},{2,3},{3,2},{4,5},{5,4},{6,7},{7,6},{8,9},{9,8},{10,11... | collective-permute-start | bytes 786440 | tf_op jit(solution)/shard_map/ppermute | solution.py:265
  52.7 6.1 %collective-permute-start.10 = (bf16[2,128,256]{2,1,0:T(8,128)(2,1)S(1)}, bf16[2,128,256]{2,1,0:T(8,128)(2,1)S(1)}, u32[]{:S(2)}, u32[]{:S(2)}) collective-permute-start(bf16[2,128,256]{2,1,0:T(8,128)(2,1)S(1)} %dynamic-slice_bitcast_fusion.1), channel_id=1, source_target_pairs={{0,8},{8,0},{16,24},{24,16},{1,9},{9,1},{17,25},{25,17},{2,10},{10... | collective-permute-start | bytes 393224 | tf_op jit(solution)/shard_map/ppermute | solution.py:265
  55.0 5.7 %collective-permute-start.6 = (bf16[2,2,128,256]{3,2,0,1:T(8,128)(2,1)S(1)}, bf16[2,2,128,256]{3,2,0,1:T(8,128)(2,1)S(1)}, u32[]{:S(2)}, u32[]{:S(2)}) collective-permute-start(bf16[2,2,128,256]{3,2,0,1:T(8,128)(2,1)S(1)} %bitcast.92), channel_id=1, source_target_pairs={{0,1},{1,0},{2,3},{3,2},{4,5},{5,4},{6,7},{7,6},{8,9},{9,8},{10,11... | collective-permute-start | bytes 786440 | tf_op jit(solution)/shard_map/ppermute | solution.py:265
  58.8 4.3 %collective-permute-start.11 = (bf16[128,256]{1,0:T(8,128)(2,1)S(1)}, bf16[128,256]{1,0:T(8,128)(2,1)S(1)}, u32[]{:S(2)}, u32[]{:S(2)}) collective-permute-start(bf16[128,256]{1,0:T(8,128)(2,1)S(1)} %dynamic-slice_bitcast_fusion.3), channel_id=1, source_target_pairs={{0,16},{8,24},{16,0},{24,8},{1,17},{9,25},{17,1},{25,9},{2,18},{10... | collective-permute-start | bytes 196616 | tf_op jit(solution)/shard_map/ppermute | solution.py:265
  63.2 4.3 %collective-permute-start.12 = (bf16[128,256]{1,0:T(8,128)(2,1)S(1)}, bf16[128,256]{1,0:T(8,128)(2,1)S(1)}, u32[]{:S(2)}, u32[]{:S(2)}) collective-permute-start(bf16[128,256]{1,0:T(8,128)(2,1)S(1)} %fusion.4), channel_id=1, source_target_pairs={{0,2},{1,3},{2,0},{3,1},{4,6},{5,7},{6,4},{7,5},{8,10},{9,11},{10,... | collective-permute-start | bytes 196616 | tf_op jit(solution)/shard_map/ppermute | solution.py:265
  63.9 6.2 %collective-permute-start.7 = (bf16[2,128,256]{2,1,0:T(8,128)(2,1)S(1)}, bf16[2,128,256]{2,1,0:T(8,128)(2,1)S(1)}, u32[]{:S(2)}, u32[]{:S(2)}) collective-permute-start(bf16[2,128,256]{2,1,0:T(8,128)(2,1)S(1)} %dynamic-slice_bitcast_fusion.2), channel_id=1, source_target_pairs={{0,2},{1,3},{2,0},{3,1},{4,6},{5,7},{6,4},{7,5},{8,10},{9,11},{10,... | collective-permute-start | bytes 393224 | tf_op jit(solution)/shard_map/ppermute | solution.py:265
  67.5 5.9 %collective-permute-start.13 = (bf16[128,256]{1,0:T(8,128)(2,1)S(1)}, bf16[128,256]{1,0:T(8,128)(2,1)S(1)}, u32[]{:S(2)}, u32[]{:S(2)}) collective-permute-start(bf16[128,256]{1,0:T(8,128)(2,1)S(1)} %add_convert_fusion.1), channel_id=1, source_target_pairs={{0,4},{1,5},{2,6},{3,7},{4,0},{5,1},{6,2},{7,3},{8,12},{9,13},{10,... | collective-permute-start | bytes 196616 | tf_op jit(solution)/shard_map/ppermute | solution.py:265
  73.5 5.3 %collective-permute-start.14 = (bf16[128,256]{1,0:T(8,128)(2,1)S(1)}, bf16[128,256]{1,0:T(8,128)(2,1)S(1)}, u32[]{:S(2)}, u32[]{:S(2)}) collective-permute-start(bf16[128,256]{1,0:T(8,128)(2,1)S(1)} %get-tuple-element.20), channel_id=1, source_target_pairs={{0,16},{8,24},{16,0},{24,8},{1,17},{9,25},{17,1},{25,9},{2,18},{10... | collective-permute-start | bytes 196616 | tf_op jit(solution)/shard_map/ppermute | solution.py:265
  76.6 7.4 %collective-permute-start.8 = (bf16[128,256]{1,0:T(8,128)(2,1)S(1)}, bf16[128,256]{1,0:T(8,128)(2,1)S(1)}, u32[]{:S(2)}, u32[]{:S(2)}) collective-permute-start(bf16[128,256]{1,0:T(8,128)(2,1)S(1)} %dynamic-slice_bitcast_fusion.4), channel_id=1, source_target_pairs={{0,4},{1,5},{2,6},{3,7},{4,0},{5,1},{6,2},{7,3},{8,12},{9,13},{10,... | collective-permute-start | bytes 196616 | tf_op jit(solution)/shard_map/ppermute | solution.py:265
  78.8 5.0 %collective-permute-start.15 = (bf16[2,128,256]{2,1,0:T(8,128)(2,1)S(1)}, bf16[2,128,256]{2,1,0:T(8,128)(2,1)S(1)}, u32[]{:S(2)}, u32[]{:S(2)}) collective-permute-start(bf16[2,128,256]{2,1,0:T(8,128)(2,1)S(1)} %bitcast_dynamic-update-slice_fusion.8), channel_id=1, source_target_pairs={{0,8},{8,0},{16,24},{24,16},{1,9},{9,1},{17,25},{25,17},{2,10},{10... | collective-permute-start | bytes 393224 | tf_op jit(solution)/shard_map/ppermute | solution.py:265
  83.9 1.6 %collective-permute-start.16 = (bf16[2,2,128,256]{3,2,1,0:T(8,128)(2,1)S(1)}, bf16[2,2,128,256]{3,2,1,0:T(8,128)(2,1)S(1)}, u32[]{:S(2)}, u32[]{:S(2)}) collective-permute-start(bf16[2,2,128,256]{3,2,1,0:T(8,128)(2,1)S(1)} %bitcast_dynamic-update-slice_fusion.5), channel_id=1, source_target_pairs={{0,1},{1,0},{2,3},{3,2},{4,5},{5,4},{6,7},{7,6},{8,9},{9,8},{10,11... | collective-permute-start | bytes 786440 | tf_op jit(solution)/shard_map/ppermute | solution.py:265

commit v5 on v4

--- a/solution.py
+++ b/solution.py
@@ -329,7 +329,6 @@
     rows, width = ref_rows.shape
     core_step = bit_steps("blk")[0]
     chip_steps = bit_steps("blk", 2)
-    scan_steps = bit_steps("scan")
     key_rows = src_rows.shape[0]
     key_total = key_rows * lax.axis_size("blk")
 
@@ -392,21 +391,20 @@
         base + (row_stats, near_stats, far_stats),
     )
 
-    halves = [core_step] + scan_steps
-    weights = weight_part.reshape((2,) * len(halves) + (-1, width))
+    scans = lax.axis_size("scan")
+    weights = weight_part.reshape((2, scans, -1, width))
     sources = source_part.reshape((2,) * (len(chip_steps) + 1) + (key_rows, width))
-    weights = halve(weights, halves[0])
+    weights = halve(weights, core_step)
     sources = halve(sources, core_step, len(chip_steps))
-    for step in halves[1:]:
-        weights = halve(weights, step)
+    weights, sources = lax.optimization_barrier((weights, sources))
+    weights = lax.all_to_all(weights, "scan", 0, 0).astype(f32).sum(axis=0).astype(b16)
     for count in range(len(chip_steps)):
         sources = halve(sources, chip_steps[count], len(chip_steps) - 1 - count)
-    grad_src = sources
+    weights, grad_src = lax.optimization_barrier((weights, sources))
     for mesh_axis, bit, _ in chip_steps:
         weights = add(weights, swap(weights, mesh_axis, bit))
-    for step in halves[::-1]:
-        weights = double(weights, step)
-    weights = weights.reshape(4, width, width).astype(f32)
+    weights = lax.all_to_all(jnp.broadcast_to(weights, (scans,) + weights.shape), "scan", 0, 0)
+    weights = double(weights, core_step).reshape(4, width, width).astype(f32)
     return (
         matched[None],
         grad_ref[None],

time: 86.8 us -> 91.5 us (1.054)
  blocking collectives: 0 us -> 8.11 us
  starting transfers between devices: 22.6 us -> 19.2 us
    all_to_all x0 -> x1, blocking collectives: none -> 8.11 us  [on_device(): lax.all_to_all(jnp.broadcast_to(weights, (scans,) + weights.shape), 'scan...]
    ppermute x17 -> x13, starting transfers between devices: 22.6 us -> 15.5 us  [swap(): return lax.ppermute(x, axis, pairs)]
    ppermute x17 -> x13, waiting for transfers between devices: 34.7 us -> 29.4 us  [swap(): return lax.ppermute(x, axis, pairs)]
    all_to_all x0 -> x1, waiting for transfers between devices: none -> 4.72 us  [on_device(): lax.all_to_all(weights, 'scan', 0, 0).astype(f32).sum(axis=0).astype(b16)]
    all_to_all x0 -> x1, starting transfers between devices: none -> 3.72 us  [on_device(): lax.all_to_all(weights, 'scan', 0, 0).astype(f32).sum(axis=0).astype(b16)]
    convert_element_type x6, other arithmetic: 0.26 us -> 1.56 us  [add(): (near.astype(jnp.float32) + far.astype(jnp.float32)).astype(near.dtype)]
  transfers between devices with their start and end apart: 17 -> 14, of which waited for: 14 -> 12; matrix products, arithmetic and copies ran while one was open for 2% -> 3% of each run, Pallas kernels for 0% -> 0%
where the time goes in v5:
time: 91.5 us; the launch traced here: 91.2 us
  waiting for transfers between devices  34.1 us (37%)
  Pallas kernels  24.9 us (27%)
  starting transfers between devices  19.2 us (21%)
  blocking collectives  8.11 us (9%)
  local copies, waits for them, and re-layouts  2.23 us (2%)
  other arithmetic  1.77 us (2%)
  between operations  0.95 us (1%)
    ppermute x13, waiting for transfers between devices, swap(): return lax.ppermute(x, axis, pairs)  29.4 us
    pallas_call x2, Pallas kernels, vmem_call(): pl.pallas_call(kernel, name=name, out_shape=out_shape, in_specs=specs, ou...  24.9 us
    ppermute x13, starting transfers between devices, swap(): return lax.ppermute(x, axis, pairs)  15.5 us
    all_to_all x1, blocking collectives, on_device(): lax.all_to_all(jnp.broadcast_to(weights, (scans,) + weights.shape), 'scan...  8.11 us
    all_to_all x1, waiting for transfers between devices, on_device(): lax.all_to_all(weights, 'scan', 0, 0).astype(f32).sum(axis=0).astype(b16)  4.72 us
    all_to_all x1, starting transfers between devices, on_device(): lax.all_to_all(weights, 'scan', 0, 0).astype(f32).sum(axis=0).astype(b16)  3.72 us
  transfers between devices with their start and end apart: 14, of which 12 were waited for; matrix products, arithmetic and copies ran while one was open for 3% of the time, Pallas kernels for 0%

profile of v5, /device:TPU:0, one launch (start us, length us, event | category | flops | bytes accessed | tf_op | source)
XLA Modules:
  0.0 91.2 jit_solution(6100586271207777308)
XLA Ops:
  0.7 4.1 %collective-permute-start = (bf16[128,256]{1,0:T(8,128)(2,1)}, bf16[128,256]{1,0:T(8,128)(2,1)S(1)}, u32[]{:S(2)}, u32[]{:S(2)}) collective-permute-start(bf16[128,256]{1,0:T(8,128)(2,1)} %bitcast.75), channel_id=1, source_target_pairs={{0,4},{1,5},{2,6},{3,7},{4,0},{5,1},{6,2},{7,3},{8,12},{9,13},{10,... | collective-permute-start | bytes 196616 | tf_op jit(solution)/shard_map/ppermute | solution.py:265
  4.8 0.9 constant_dynamic-update-slice_fusion
  5.7 3.0 %collective-permute-done = bf16[128,256]{1,0:T(8,128)(2,1)S(1)} collective-permute-done((bf16[128,256]{1,0:T(8,128)(2,1)}, bf16[128,256]{1,0:T(8,128)(2,1)S(1)}, u32[]{:S(2)}, u32[]{:S(2)}) %collective-permute-start) | collective-permute-done | bytes 65568 | tf_op jit(solution)/shard_map/ppermute | solution.py:265
  9.5 4.3 %collective-permute-done.1 = bf16[2,128,256]{2,1,0:T(8,128)(2,1)S(1)} collective-permute-done((bf16[2,128,256]{2,1,0:T(8,128)(2,1)S(1)}, bf16[2,128,256]{2,1,0:T(8,128)(2,1)S(1)}, u32[]{:S(2)}, u32[]{:S(2)}) %collective-permute-start.1) | collective-permute-done | bytes 131104 | tf_op jit(solution)/shard_map/ppermute | solution.py:265
  13.9 1.4 %collective-permute-done.2 = bf16[2,2,128,256]{3,2,1,0:T(8,128)(2,1)S(1)} collective-permute-done((bf16[2,2,128,256]{3,2,1,0:T(8,128)(2,1)S(1)}, bf16[2,2,128,256]{3,2,1,0:T(8,128)(2,1)S(1)}, u32[]{:S(2)}, u32[]{:S(2)}) %collective-permute-start.2) | collective-permute-done | bytes 262176 | tf_op jit(solution)/shard_map/ppermute | solution.py:265
  15.4 9.1 %match_stats.1 = (f32[8,512,128]{2,1,0:T(8,128)S(1)}, f32[3,4,1024]{2,1,0:T(4,128)S(1)}) custom-call(s32[4,8]{1,0:T(4,128)S(1)} %bitcast.70, bf16[512,256]{1,0:T(8,128)(2,1)S(1)} %bitcast.66, bf16[512,256]{1,0:T(8,128)(2,1)S(1)} %bitcast.68, bf16[1024,256]{1,0:T(8,128)(2,1)S(1)} %bitcast.62, bf16[256,256]{1,0:T(8,128)(2,1)S(1)} %copy-done.2, ...), custom_call_target="tpu_custom_call" | custom-call | flops 536870912 | bytes 2097152 | tf_op jit(solution)/shard_map/match_stats/pallas_call | solution.py:312
  25.3 3.4 %collective-permute-done.3 = f32[3,4,1024]{2,1,0:T(4,128)S(1)} collective-permute-done((f32[3,4,1024]{2,1,0:T(4,128)S(1)}, f32[3,4,1024]{2,1,0:T(4,128)S(1)}, u32[]{:S(2)}, u32[]{:S(2)}) %collective-permute-start.3) | collective-permute-done | bytes 49184 | tf_op jit(solution)/shard_map/ppermute | solution.py:265
  28.8 2.4 %collective-permute-start.4 = (f32[3,4,1024]{2,1,0:T(4,128)S(1)}, f32[3,4,1024]{2,1,0:T(4,128)S(1)}, u32[]{:S(2)}, u32[]{:S(2)}) collective-permute-start(f32[3,4,1024]{2,1,0:T(4,128)S(1)} %pad_maximum_fusion), channel_id=1, source_target_pairs={{0,4},{1,5},{2,6},{3,7},{4,0},{5,1},{6,2},{7,3},{8,12},{9,13},{10,... | collective-permute-start | bytes 147464 | tf_op jit(solution)/shard_map/ppermute | solution.py:265
  31.1 2.7 %collective-permute-done.4 = f32[3,4,1024]{2,1,0:T(4,128)S(1)} collective-permute-done((f32[3,4,1024]{2,1,0:T(4,128)S(1)}, f32[3,4,1024]{2,1,0:T(4,128)S(1)}, u32[]{:S(2)}, u32[]{:S(2)}) %collective-permute-start.4) | collective-permute-done | bytes 49184 | tf_op jit(solution)/shard_map/ppermute | solution.py:265
  34.0 1.2 %collective-permute-done.5.far_ref = f32[3,4,1024]{2,1,0:T(4,128)S(1)} collective-permute-done((f32[3,4,1024]{2,1,0:T(4,128)S(1)}, f32[3,4,1024]{2,1,0:T(4,128)S(1)}, u32[]{:S(2)}, u32[]{:S(2)}) %collective-permute-start.5) | collective-permute-done | bytes 49184 | tf_op jit(solution)/shard_map/ppermute | solution.py:265
  35.2 15.8 %match_grads.1 = (bf16[512,256]{1,0:T(8,128)(2,1)}, bf16[512,256]{1,0:T(8,128)(2,1)}, bf16[1024,256]{1,0:T(8,128)(2,1)S(1)}, bf16[4,256,256]{2,1,0:T(8,128)(2,1)S(1)}) custom-call(s32[4,8]{1,0:T(4,128)S(1)} %bitcast.71, bf16[512,256]{1,0:T(8,128)(2,1)S(1)} %bitcast.67, bf16[512,256]{1,0:T(8,128)(2,1)S(1)} %bitcast.69, bf16[1024,256]{1,0:T(8,128)(2,1)S(1)} %bitcast.63, ...), custom_call_target="tpu_custom_call" | custom-call | flops 1610612736 | bytes 4194304 | tf_op jit(solution)/shard_map/match_grads/pallas_call | solution.py:312
  51.7 0.9 collective-permute-done.6
  53.4 1.2 %collective-permute-start.8 = (bf16[2,128,256]{2,1,0:T(8,128)(2,1)S(1)}, bf16[2,128,256]{2,1,0:T(8,128)(2,1)S(1)}, u32[]{:S(2)}, u32[]{:S(2)}) collective-permute-start(bf16[2,128,256]{2,1,0:T(8,128)(2,1)S(1)} %dynamic-slice_bitcast_fusion.1), channel_id=1, source_target_pairs={{0,2},{1,3},{2,0},{3,1},{4,6},{5,7},{6,4},{7,5},{8,10},{9,11},{10,... | collective-permute-start | bytes 393224 | tf_op jit(solution)/shard_map/ppermute | solution.py:265
  54.6 4.4 %collective-permute-done.8 = bf16[2,128,256]{2,1,0:T(8,128)(2,1)S(1)} collective-permute-done((bf16[2,128,256]{2,1,0:T(8,128)(2,1)S(1)}, bf16[2,128,256]{2,1,0:T(8,128)(2,1)S(1)}, u32[]{:S(2)}, u32[]{:S(2)}) %collective-permute-start.8) | collective-permute-done | bytes 131104 | tf_op jit(solution)/shard_map/ppermute | solution.py:265
  59.1 2.6 %collective-permute-start.9 = (bf16[128,256]{1,0:T(8,128)(2,1)S(1)}, bf16[128,256]{1,0:T(8,128)(2,1)S(1)}, u32[]{:S(2)}, u32[]{:S(2)}) collective-permute-start(bf16[128,256]{1,0:T(8,128)(2,1)S(1)} %dynamic-slice_bitcast_fusion.2), channel_id=1, source_target_pairs={{0,4},{1,5},{2,6},{3,7},{4,0},{5,1},{6,2},{7,3},{8,12},{9,13},{10,... | collective-permute-start | bytes 196616 | tf_op jit(solution)/shard_map/ppermute | solution.py:265
  61.7 3.7 %all-to-all-start = ((bf16[4,128,256]{2,1,0:T(8,128)(2,1)}), bf16[4,128,256]{2,1,0:T(8,128)(2,1)S(1)}, u32[]{:S(2)}, u32[]{:S(2)}) async-start(bf16[4,128,256]{2,1,0:T(8,128)(2,1)} %fusion.1), calls=%async_computation | async-start | bytes 524288 | tf_op jit(solution)/shard_map/all_to_all | solution.py:400
  66.1 4.7 %all-to-all-done = bf16[4,128,256]{2,1,0:T(8,128)(2,1)S(1)} async-done(((bf16[4,128,256]{2,1,0:T(8,128)(2,1)}), bf16[4,128,256]{2,1,0:T(8,128)(2,1)S(1)}, u32[]{:S(2)}, u32[]{:S(2)}) %all-to-all-start) | async-done | bytes 262176 | tf_op jit(solution)/shard_map/all_to_all | solution.py:400
  70.9 1.8 %collective-permute-start.10 = (bf16[128,256]{1,0:T(8,128)(2,1)S(1)}, bf16[128,256]{1,0:T(8,128)(2,1)S(1)}, u32[]{:S(2)}, u32[]{:S(2)}) collective-permute-start(bf16[128,256]{1,0:T(8,128)(2,1)S(1)} %reduce_sum.12), channel_id=1, source_target_pairs={{0,2},{1,3},{2,0},{3,1},{4,6},{5,7},{6,4},{7,5},{8,10},{9,11},{10,... | collective-permute-start | bytes 196616 | tf_op jit(solution)/shard_map/ppermute | solution.py:265
  72.7 2.5 %collective-permute-done.10 = bf16[128,256]{1,0:T(8,128)(2,1)S(1)} collective-permute-done((bf16[128,256]{1,0:T(8,128)(2,1)S(1)}, bf16[128,256]{1,0:T(8,128)(2,1)S(1)}, u32[]{:S(2)}, u32[]{:S(2)}) %collective-permute-start.10) | collective-permute-done | bytes 65568 | tf_op jit(solution)/shard_map/ppermute | solution.py:265
  75.2 1.2 %collective-permute-start.11 = (bf16[128,256]{1,0:T(8,128)(2,1)S(1)}, bf16[128,256]{1,0:T(8,128)(2,1)S(1)}, u32[]{:S(2)}, u32[]{:S(2)}) collective-permute-start(bf16[128,256]{1,0:T(8,128)(2,1)S(1)} %add_convert_fusion.1), channel_id=1, source_target_pairs={{0,4},{1,5},{2,6},{3,7},{4,0},{5,1},{6,2},{7,3},{8,12},{9,13},{10,... | collective-permute-start | bytes 196616 | tf_op jit(solution)/shard_map/ppermute | solution.py:265
  76.4 4.1 %collective-permute-done.11 = bf16[128,256]{1,0:T(8,128)(2,1)S(1)} collective-permute-done((bf16[128,256]{1,0:T(8,128)(2,1)S(1)}, bf16[128,256]{1,0:T(8,128)(2,1)S(1)}, u32[]{:S(2)}, u32[]{:S(2)}) %collective-permute-start.11) | collective-permute-done | bytes 65568 | tf_op jit(solution)/shard_map/ppermute | solution.py:265
  80.5 8.1 %all_to_all.10 = bf16[4,128,256]{2,1,0:T(8,128)(2,1)S(1)} all-to-all(bf16[4,128,256]{2,1,0:T(8,128)(2,1)S(1)} %broadcast_in_dim.62), channel_id=1, replica_groups=mesh['scan'=4,'blk'=8] {'scan'}, dimensions={0} | all-to-all | bytes 524288 | tf_op jit(solution)/shard_map/all_to_all | solution.py:406
  88.7 1.5 %collective-permute-done.12 = bf16[4,128,256]{2,1,0:T(8,128)(2,1)S(1)} collective-permute-done((bf16[4,128,256]{2,1,0:T(8,128)(2,1)S(1)}, bf16[4,128,256]{2,1,0:T(8,128)(2,1)S(1)}, u32[]{:S(2)}, u32[]{:S(2)}) %collective-permute-start.12) | collective-permute-done | bytes 262176 | tf_op jit(solution)/shard_map/ppermute | solution.py:265
  90.3 1.0 %slice_bitcast_fusion = (f32[256,256]{1,0:T(8,128)}, f32[256,256]{1,0:T(8,128)}, f32[256,256]{1,0:T(8,128)}, f32[256,256]{1,0:T(8,128)}) fusion(f32[4,256,256]{2,1,0:T(8,128)S(1)} %convert.6), kind=kLoop, calls=%fused_computation.4 | loop fusion | bytes 2097152 | tf_op jit(solution)/shard_map/squeeze | solution.py:415
  (53 shorter events, 4.4 us)
Async XLA Ops:
  0.6 14.7 %copy-start.6 = (s32[1,4,8]{2,1,0:T(4,128)S(1)}, s32[1,4,8]{2,1,0:T(4,128)}, u32[]{:S(2)}) copy-start(s32[1,4,8]{2,1,0:T(4,128)} %param.15) | copy-start | bytes 388
  0.6 14.7 %copy-start = (bf16[1,512,256]{2,1,0:T(8,128)(2,1)S(1)}, bf16[1,512,256]{2,1,0:T(8,128)(2,1)}, u32[]{:S(2)}) copy-start(bf16[1,512,256]{2,1,0:T(8,128)(2,1)} %param.8) | copy-start | bytes 786436
  0.7 14.7 %copy-start.1 = (bf16[1,512,256]{2,1,0:T(8,128)(2,1)S(1)}, bf16[1,512,256]{2,1,0:T(8,128)(2,1)}, u32[]{:S(2)}) copy-start(bf16[1,512,256]{2,1,0:T(8,128)(2,1)} %param.10) | copy-start | bytes 786436
  0.7 14.7 %copy-start.2 = (bf16[256,256]{1,0:T(8,128)(2,1)S(1)}, bf16[256,256]{1,0:T(8,128)(2,1)}, u32[]{:S(2)}) copy-start(bf16[256,256]{1,0:T(8,128)(2,1)} %wq_ref.3) | copy-start | bytes 393220
  0.7 14.7 %copy-start.3 = (bf16[256,256]{1,0:T(8,128)(2,1)S(1)}, bf16[256,256]{1,0:T(8,128)(2,1)}, u32[]{:S(2)}) copy-start(bf16[256,256]{1,0:T(8,128)(2,1)} %wk_ref.3) | copy-start | bytes 393220
  0.7 14.7 %copy-start.4 = (bf16[256,256]{1,0:T(8,128)(2,1)S(1)}, bf16[256,256]{1,0:T(8,128)(2,1)}, u32[]{:S(2)}) copy-start(bf16[256,256]{1,0:T(8,128)(2,1)} %wv_ref.3) | copy-start | bytes 393220
  0.7 14.7 %copy-start.5 = (bf16[256,256]{1,0:T(8,128)(2,1)S(1)}, bf16[256,256]{1,0:T(8,128)(2,1)}, u32[]{:S(2)}) copy-start(bf16[256,256]{1,0:T(8,128)(2,1)} %wo_ref.3) | copy-start | bytes 393220
  0.7 8.0 %collective-permute-start = (bf16[128,256]{1,0:T(8,128)(2,1)}, bf16[128,256]{1,0:T(8,128)(2,1)S(1)}, u32[]{:S(2)}, u32[]{:S(2)}) collective-permute-start(bf16[128,256]{1,0:T(8,128)(2,1)} %bitcast.75), channel_id=1, source_target_pairs={{0,4},{1,5},{2,6},{3,7},{4,0},{5,1},{6,2},{7,3},{8,12},{9,13},{10,... | collective-permute-start | bytes 196616 | tf_op jit(solution)/shard_map/ppermute | solution.py:265
  8.7 5.0 %collective-permute-start.1 = (bf16[2,128,256]{2,1,0:T(8,128)(2,1)S(1)}, bf16[2,128,256]{2,1,0:T(8,128)(2,1)S(1)}, u32[]{:S(2)}, u32[]{:S(2)}) collective-permute-start(bf16[2,128,256]{2,1,0:T(8,128)(2,1)S(1)} %bitcast_dynamic-update-slice_fusion.6), channel_id=1, source_target_pairs={{0,2},{1,3},{2,0},{3,1},{4,6},{5,7},{6,4},{7,5},{8,10},{9,11},{10,... | collective-permute-start | bytes 393224 | tf_op jit(solution)/shard_map/ppermute | solution.py:265
  13.7 1.6 %collective-permute-start.2 = (bf16[2,2,128,256]{3,2,1,0:T(8,128)(2,1)S(1)}, bf16[2,2,128,256]{3,2,1,0:T(8,128)(2,1)S(1)}, u32[]{:S(2)}, u32[]{:S(2)}) collective-permute-start(bf16[2,2,128,256]{3,2,1,0:T(8,128)(2,1)S(1)} %bitcast_dynamic-update-slice_fusion.5), channel_id=1, source_target_pairs={{0,1},{1,0},{2,3},{3,2},{4,5},{5,4},{6,7},{7,6},{8,9},{9,8},{10,11... | collective-permute-start | bytes 786440 | tf_op jit(solution)/shard_map/ppermute | solution.py:265
  24.5 4.2 %collective-permute-start.3 = (f32[3,4,1024]{2,1,0:T(4,128)S(1)}, f32[3,4,1024]{2,1,0:T(4,128)S(1)}, u32[]{:S(2)}, u32[]{:S(2)}) collective-permute-start(f32[3,4,1024]{2,1,0:T(4,128)S(1)} %get-tuple-element.18), channel_id=1, source_target_pairs={{0,2},{1,3},{2,0},{3,1},{4,6},{5,7},{6,4},{7,5},{8,10},{9,11},{10,... | collective-permute-start | bytes 147464 | tf_op jit(solution)/shard_map/ppermute | solution.py:265
  28.8 5.1 %collective-permute-start.4 = (f32[3,4,1024]{2,1,0:T(4,128)S(1)}, f32[3,4,1024]{2,1,0:T(4,128)S(1)}, u32[]{:S(2)}, u32[]{:S(2)}) collective-permute-start(f32[3,4,1024]{2,1,0:T(4,128)S(1)} %pad_maximum_fusion), channel_id=1, source_target_pairs={{0,4},{1,5},{2,6},{3,7},{4,0},{5,1},{6,2},{7,3},{8,12},{9,13},{10,... | collective-permute-start | bytes 147464 | tf_op jit(solution)/shard_map/ppermute | solution.py:265
  33.9 1.3 %collective-permute-start.5 = (f32[3,4,1024]{2,1,0:T(4,128)S(1)}, f32[3,4,1024]{2,1,0:T(4,128)S(1)}, u32[]{:S(2)}, u32[]{:S(2)}) collective-permute-start(f32[3,4,1024]{2,1,0:T(4,128)S(1)} %pad_maximum_fusion.1.near_ref), channel_id=1, source_target_pairs={{0,1},{1,0},{2,3},{3,2},{4,5},{5,4},{6,7},{7,6},{8,9},{9,8},{10,11... | collective-permute-start | bytes 147464 | tf_op jit(solution)/shard_map/ppermute | solution.py:265
  51.0 1.6 %collective-permute-start.6 = (bf16[4,128,256]{2,1,0:T(8,128)(2,1)S(1)}, bf16[4,128,256]{2,1,0:T(8,128)(2,1)S(1)}, u32[]{:S(2)}, u32[]{:S(2)}) collective-permute-start(bf16[4,128,256]{2,1,0:T(8,128)(2,1)S(1)} %dynamic-slice_bitcast_fusion), channel_id=1, source_target_pairs={{0,1},{1,0},{2,3},{3,2},{4,5},{5,4},{6,7},{7,6},{8,9},{9,8},{10,11... | collective-permute-start | bytes 786440 | tf_op jit(solution)/shard_map/ppermute | solution.py:265
  51.2 2.1 %collective-permute-start.7 = (bf16[2,2,128,256]{3,2,0,1:T(8,128)(2,1)S(1)}, bf16[2,2,128,256]{3,2,0,1:T(8,128)(2,1)S(1)}, u32[]{:S(2)}, u32[]{:S(2)}) collective-permute-start(bf16[2,2,128,256]{3,2,0,1:T(8,128)(2,1)S(1)} %bitcast.73), channel_id=1, source_target_pairs={{0,1},{1,0},{2,3},{3,2},{4,5},{5,4},{6,7},{7,6},{8,9},{9,8},{10,11... | collective-permute-start | bytes 786440 | tf_op jit(solution)/shard_map/ppermute | solution.py:265
  53.4 5.6 %collective-permute-start.8 = (bf16[2,128,256]{2,1,0:T(8,128)(2,1)S(1)}, bf16[2,128,256]{2,1,0:T(8,128)(2,1)S(1)}, u32[]{:S(2)}, u32[]{:S(2)}) collective-permute-start(bf16[2,128,256]{2,1,0:T(8,128)(2,1)S(1)} %dynamic-slice_bitcast_fusion.1), channel_id=1, source_target_pairs={{0,2},{1,3},{2,0},{3,1},{4,6},{5,7},{6,4},{7,5},{8,10},{9,11},{10,... | collective-permute-start | bytes 393224 | tf_op jit(solution)/shard_map/ppermute | solution.py:265
  59.1 6.3 %collective-permute-start.9 = (bf16[128,256]{1,0:T(8,128)(2,1)S(1)}, bf16[128,256]{1,0:T(8,128)(2,1)S(1)}, u32[]{:S(2)}, u32[]{:S(2)}) collective-permute-start(bf16[128,256]{1,0:T(8,128)(2,1)S(1)} %dynamic-slice_bitcast_fusion.2), channel_id=1, source_target_pairs={{0,4},{1,5},{2,6},{3,7},{4,0},{5,1},{6,2},{7,3},{8,12},{9,13},{10,... | collective-permute-start | bytes 196616 | tf_op jit(solution)/shard_map/ppermute | solution.py:265
  61.7 9.1 %all-to-all-start = ((bf16[4,128,256]{2,1,0:T(8,128)(2,1)}), bf16[4,128,256]{2,1,0:T(8,128)(2,1)S(1)}, u32[]{:S(2)}, u32[]{:S(2)}) async-start(bf16[4,128,256]{2,1,0:T(8,128)(2,1)} %fusion.1), calls=%async_computation | async-start | bytes 524288 | tf_op jit(solution)/shard_map/all_to_all | solution.py:400
  70.9 4.3 %collective-permute-start.10 = (bf16[128,256]{1,0:T(8,128)(2,1)S(1)}, bf16[128,256]{1,0:T(8,128)(2,1)S(1)}, u32[]{:S(2)}, u32[]{:S(2)}) collective-permute-start(bf16[128,256]{1,0:T(8,128)(2,1)S(1)} %reduce_sum.12), channel_id=1, source_target_pairs={{0,2},{1,3},{2,0},{3,1},{4,6},{5,7},{6,4},{7,5},{8,10},{9,11},{10,... | collective-permute-start | bytes 196616 | tf_op jit(solution)/shard_map/ppermute | solution.py:265
  75.2 5.2 %collective-permute-start.11 = (bf16[128,256]{1,0:T(8,128)(2,1)S(1)}, bf16[128,256]{1,0:T(8,128)(2,1)S(1)}, u32[]{:S(2)}, u32[]{:S(2)}) collective-permute-start(bf16[128,256]{1,0:T(8,128)(2,1)S(1)} %add_convert_fusion.1), channel_id=1, source_target_pairs={{0,4},{1,5},{2,6},{3,7},{4,0},{5,1},{6,2},{7,3},{8,12},{9,13},{10,... | collective-permute-start | bytes 196616 | tf_op jit(solution)/shard_map/ppermute | solution.py:265
  88.6 1.5 %collective-permute-start.12 = (bf16[4,128,256]{2,1,0:T(8,128)(2,1)S(1)}, bf16[4,128,256]{2,1,0:T(8,128)(2,1)S(1)}, u32[]{:S(2)}, u32[]{:S(2)}) collective-permute-start(bf16[4,128,256]{2,1,0:T(8,128)(2,1)S(1)} %all_to_all.10), channel_id=1, source_target_pairs={{0,1},{1,0},{2,3},{3,2},{4,5},{5,4},{6,7},{7,6},{8,9},{9,8},{10,11... | collective-permute-start | bytes 786440 | tf_op jit(solution)/shard_map/ppermute | solution.py:265

commit v6 on v5

v6 whole, which is shorter than its diff:
```python
import functools

import jax
import jax.numpy as jnp
from jax import lax
from jax.experimental import pallas as pl
from jax.experimental.pallas import tpu as pltpu
from jax.sharding import PartitionSpec as P

HEADS = 4
BLOCK = 128
NEG = -1e30
FLOOR = -1e29

NT = (((1,), (1,)), ((), ()))
TN = (((0,), (0,)), ((), ()))
TT = (((0,), (1,)), ((), ()))


def mm(left, right):
    return jnp.dot(left, right, preferred_element_type=jnp.float32)


def mm_general(left, right, dims):
    return lax.dot_general(left, right, dims, preferred_element_type=jnp.float32)


def bf(x):
    return x.astype(jnp.bfloat16)


def lane_row(width, head, head_dim):
    lanes = lax.broadcasted_iota(jnp.int32, (1, width), 1) // head_dim
    return bf(jnp.where(lanes == head, 1.0, 0.0))


def fill_bias(inter_ref, bias_ref, head_dim):
    query_blocks, key_blocks = inter_ref.shape
    width = bias_ref.shape[1]
    lane = lax.broadcasted_iota(jnp.int32, (1, width), 1) % head_dim
    for key_block in range(key_blocks):
        row = jnp.zeros((1, width), jnp.float32)
        for query_block in range(query_blocks):
            listed = inter_ref[query_block, key_block] == 1
            row = jnp.where(lane == query_block, jnp.where(listed, 0.0, NEG), row)
        bias_ref[pl.ds(key_block * BLOCK, BLOCK), :] = bf(
            jnp.broadcast_to(row, (BLOCK, width))
        )


def fill_hot(hot_ref, head_dim):
    rows, width = hot_ref.shape
    lane = lax.broadcasted_iota(jnp.int32, (1, width), 1) % head_dim
    for block in range(rows // BLOCK):
        row = bf(jnp.where(lane == block, 1.0, 0.0))
        hot_ref[pl.ds(block * BLOCK, BLOCK), :] = jnp.broadcast_to(row, (BLOCK, width))


def spread(reduced, like):
    return jnp.broadcast_to(reduced, like.shape)


STRIP = 32
STEP = 256


def by_eight(x):
    return x.reshape(x.shape[0] // 8, 8, x.shape[1])


def project_kernel(
    head_count, inter_ref, ref_ref, gout_ref, wq_ref, wo_ref,
    left_ref, gleft_ref, query_t_ref, grad_t_ref, bias_ref, hot_ref,
):
    rows, width = ref_ref.shape
    head_dim = width // head_count
    scale = head_dim ** -0.5
    query = bf(bf(mm(ref_ref[...], wq_ref[...])).astype(jnp.float32) * scale)
    grad = bf(mm_general(gout_ref[...], wo_ref[...], NT))
    query_t = bf(mm_general(wq_ref[...], ref_ref[...], TT)).astype(jnp.float32)
    query_t_ref[...] = bf(query_t * (2.0 * scale))
    grad_t_ref[...] = bf(mm_general(wo_ref[...], gout_ref[...], NT))
    fill_bias(inter_ref, bias_ref, head_dim)
    fill_hot(hot_ref, head_dim)
    for head in range(head_count):
        own = lane_row(width, head, head_dim)
        other = lane_row(width, (head + 1) % head_count, head_dim)
        left_ref[head] = query * own + hot_ref[...] * other
        gleft_ref[head] = grad * own


def fill_step(head, step, left_ref, gleft_ref, right_ref, value_ref, score_ref, prob_ref):
    span = pl.ds(pl.multiple_of(step * STEP, STEP), STEP)
    scores = mm_general(left_ref[head], right_ref[head, span, :], NT)
    score_ref[step] = scores
    prob_ref[step] = mm_general(gleft_ref[head], value_ref[span, :], NT)
    return scores


def strips(step, steps, rows):
    chunk = rows // steps
    for first in range(0, chunk, STRIP):
        yield pl.ds(pl.multiple_of(step * chunk + first, STRIP), STRIP)


def lanes_of(tile):
    first = tile * 128 % STEP
    return tile * 128 // STEP, slice(first, first + 128)


def stats_kernel(
    head_count, left_ref, gleft_ref, bias_ref, src_ref, wk_ref, wv_ref,
    row_ref, col_ref, right_ref, key_ref, value_ref,
    score_a, score_b, prob_a, prob_b, prob_c, sum_ref, top_ref, peak_ref,
):
    rows, width = left_ref.shape[1:]
    key_total = src_ref.shape[0]
    tiles, steps = key_total // 128, key_total // STEP
    head_dim = width // head_count
    key_ref[...] = bf(mm(src_ref[...], wk_ref[...]))
    value_ref[...] = bf(mm(src_ref[...], wv_ref[...]))
    for head in range(head_count):
        own = lane_row(width, head, head_dim)
        other = lane_row(width, (head + 1) % head_count, head_dim)
        right_ref[head] = key_ref[...] * own + bias_ref[...] * other
    scores_of, probs_of = (score_a, score_b), (prob_a, prob_b, prob_c)
    zeros = tuple(jnp.zeros((8, 128), jnp.float32) for _ in range(tiles))

    def fill(head, step):
        scores = fill_step(
            head, step, left_ref, gleft_ref, right_ref, value_ref,
            scores_of[head % 2], probs_of[head % 3],
        )
        top = top_ref[...]
        for first in range(0, STEP, 128):
            top = jnp.maximum(top, scores[:, first : first + 128])
        top_ref[...] = top
        peak = jnp.maximum(scores.max(axis=0, keepdims=True), FLOOR)
        peak_ref[head, step] = jnp.broadcast_to(peak, (8, STEP))

    def close_peaks(head):
        row_ref[head] = spread(top_ref[...].max(axis=1, keepdims=True), top_ref)
        top_ref[...] = jnp.full(top_ref.shape, 2.0 * NEG, jnp.float32)

    def totals(head, span, col_totals):
        score_ref, prob_ref = scores_of[head % 2], probs_of[head % 3]
        row_peak = by_eight(row_ref[head, span, :])
        row_total = jnp.zeros_like(row_peak)
        out = []
        for tile in range(tiles):
            at_step, lanes = lanes_of(tile)
            scores = by_eight(score_ref[at_step, span, lanes])
            row_exp = jnp.exp(scores - row_peak)
            col_exp = jnp.exp(scores - peak_ref[head, at_step, :, lanes][None])
            row_total = row_total + row_exp
            product = row_exp * col_exp * by_eight(prob_ref[at_step, span, lanes])
            prob_ref[at_step, span, lanes] = product.reshape(STRIP, 128)
            out.append(col_totals[tile] + col_exp.sum(axis=0))
        sum_ref[span, :] = row_total.reshape(STRIP, 128)
        return tuple(out)

    def dots(head, span, col_dots):
        prob_ref = probs_of[head % 3]
        row_inverse = by_eight(row_ref[head_count + head, span, :])
        out = []
        for tile in range(tiles):
            at_step, lanes = lanes_of(tile)
            product = by_eight(prob_ref[at_step, span, lanes]) * row_inverse
            out.append(col_dots[tile] + product.sum(axis=0))
        return tuple(out)

    top_ref[...] = jnp.full(top_ref.shape, 2.0 * NEG, jnp.float32)
    lax.fori_loop(0, steps, lambda step, carry: (fill(0, step), carry)[1], 0)
    for head in range(head_count + 1):
        if head < head_count:
            close_peaks(head)

        def body(step, carry, head=head):
            col_totals, col_dots = carry
            for span in strips(step, steps, rows):
                if head < head_count:
                    col_totals = totals(head, span, col_totals)
                if head > 0:
                    col_dots = dots(head - 1, span, col_dots)
            if head + 1 < head_count:
                fill(head + 1, step)
            return col_totals, col_dots

        col_totals, col_dots = lax.fori_loop(0, steps, body, (zeros, zeros))
        for tile in range(tiles):
            lanes = slice(tile * 128, tile * 128 + 128)
            at_step, near = lanes_of(tile)
            if head < head_count:
                col_ref[0, head : head + 1, lanes] = peak_ref[head, at_step, 0:1, near]
                col_ref[1, head : head + 1, lanes] = col_totals[tile].sum(axis=0, keepdims=True)
            if head > 0:
                col_ref[2, head - 1 : head, lanes] = col_dots[tile].sum(axis=0, keepdims=True)
        if head < head_count:
            row_total = sum_ref[...].sum(axis=1, keepdims=True)
            row_ref[head_count + head] = spread(1.0 / row_total, sum_ref)


def grads_kernel(
    head_count, left_ref, gleft_ref, right_ref, key_ref, value_ref, query_t_ref, grad_t_ref, row_ref,
    near_ref, far_ref, ref_ref, gout_ref, src_ref,
    attended_ref, gquery_ref, gkey_ref, gvalue_ref, weight_ref,
    score_a, score_b, prob_a, prob_b, match_a, match_b, gscore_a, gscore_b, att_ref, gq_ref, col_ref,
):
    rows, width = ref_ref.shape
    key_total = src_ref.shape[0]
    tiles, steps = key_total // 128, key_total // STEP
    head_dim = width // head_count
    scale = head_dim ** -0.5
    chunk = rows // steps

    peak = jnp.maximum(near_ref[0], far_ref[0])
    near, far = jnp.exp(near_ref[0] - peak), jnp.exp(far_ref[0] - peak)
    inverse = 1.0 / (near * near_ref[1] + far * far_ref[1])
    half = (near * near_ref[2] + far * far_ref[2]) * inverse * 0.5
    for kind, values in enumerate((peak, inverse, half)):
        for head in range(head_count):
            for step in range(steps):
                piece = values[head : head + 1, step * STEP : (step + 1) * STEP]
                col_ref[kind, head, step] = jnp.broadcast_to(piece, (8, STEP))
    att_ref[...] = jnp.zeros(att_ref.shape, jnp.float32)
    gq_ref[...] = jnp.zeros(gq_ref.shape, jnp.float32)
    scores_of, probs_of = (score_a, score_b), (prob_a, prob_b)
    matches_of, gscores_of = (match_a, match_b), (gscore_a, gscore_b)

    def fill(head, step):
        fill_step(
            head, step, left_ref, gleft_ref, right_ref, value_ref,
            scores_of[head % 2], probs_of[head % 2],
        )

    def products(head, span):
        score_ref, prob_ref, match_ref = scores_of[head % 2], probs_of[head % 2], matches_of[head % 2]
        row_peak = by_eight(row_ref[head, span, :])
        row_inverse = by_eight(row_ref[head_count + head, span, :])
        row_dot = jnp.zeros_like(row_peak)
        for tile in range(tiles):
            at_step, lanes = lanes_of(tile)
            scores = by_eight(score_ref[at_step, span, lanes])
            row_prob = jnp.exp(scores - row_peak) * row_inverse
            col_prob = jnp.exp(scores - col_ref[0, head, at_step, :, lanes][None])
            col_prob = col_prob * col_ref[1, head, at_step, :, lanes][None]
            match = row_prob * col_prob
            product = match * by_eight(prob_ref[at_step, span, lanes])
            row_dot = row_dot + product
            rest = product - col_prob * col_ref[2, head, at_step, :, lanes][None]
            match_ref[span, tile * 128 : tile * 128 + 128] = bf(match.reshape(STRIP, 128))
            score_ref[at_step, span, lanes] = row_prob.reshape(STRIP, 128)
            prob_ref[at_step, span, lanes] = rest.reshape(STRIP, 128)
        return row_dot.reshape(STRIP, 128)

    def score_grads(head, span, row_half):
        score_ref, prob_ref, gscore_ref = scores_of[head % 2], probs_of[head % 2], gscores_of[head % 2]
        for tile in range(tiles):
            at_step, lanes = lanes_of(tile)
            grads = prob_ref[at_step, span, lanes] - score_ref[at_step, span, lanes] * row_half
            gscore_ref[span, tile * 128 : tile * 128 + 128] = bf(grads)

    def outputs(head, step):
        match_ref, gscore_ref = matches_of[head % 2], gscores_of[head % 2]
        own = lane_row(width, head, head_dim).astype(jnp.float32)
        span = pl.ds(pl.multiple_of(step * chunk, chunk), chunk)
        att_ref[span, :] += mm(match_ref[span, :], value_ref[...]) * own
        gq_ref[span, :] += mm(gscore_ref[span, :], key_ref[...]) * own
        lanes = pl.ds(pl.multiple_of(step * STEP, STEP), STEP)
        mine = slice(head * head_dim, (head + 1) * head_dim)
        gkey_ref[mine, lanes] = bf(mm(query_t_ref[mine, :], gscore_ref[:, lanes]))
        gvalue_ref[mine, lanes] = bf(mm(grad_t_ref[mine, :], match_ref[:, lanes]))

    lax.fori_loop(0, steps, lambda step, carry: (fill(0, step), carry)[1], 0)
    for head in range(head_count + 1):

        def body(step, carry, head=head):
            if head > 0:
                outputs(head - 1, step)
            if head + 1 < head_count:
                fill(head + 1, step)
            if head < head_count:
                spans = list(strips(step, steps, rows))
                row_dot = jnp.concatenate([products(head, span) for span in spans], axis=0)
                row_half = spread(row_dot.sum(axis=1, keepdims=True) * 0.5, row_dot)
                for at_strip, span in enumerate(spans):
                    first = at_strip * STRIP
                    score_grads(head, span, row_half[first : first + STRIP])
            return carry

        lax.fori_loop(0, steps, body, 0)

    attended = bf(att_ref[...])
    gquery = bf(gq_ref[...] * (2.0 * scale))
    attended_ref[...] = attended
    gquery_ref[...] = gquery
    weight_ref[0] = bf(mm_general(ref_ref[...], gquery, TN))
    weight_ref[1] = bf(mm(gkey_ref[...], src_ref[...]).T)
    weight_ref[2] = bf(mm(gvalue_ref[...], src_ref[...]).T)
    weight_ref[3] = bf(mm_general(attended, gout_ref[...], TN))


def finish_kernel(
    ref_ref, gout_ref, attended_ref, gquery_ref, gkey_ref, gvalue_ref, wq_ref, wk_ref, wv_ref, wo_ref,
    matched_ref, gref_ref, gsrc_ref,
):
    gsrc_t = mm(wk_ref[...], gkey_ref[...]) + mm(wv_ref[...], gvalue_ref[...])
    gsrc_ref[...] = bf(gsrc_t.T)
    matched = ref_ref[...].astype(jnp.float32) + mm(attended_ref[...], wo_ref[...])
    matched_ref[...] = bf(matched)
    gref = gout_ref[...].astype(jnp.float32) + mm_general(gquery_ref[...], wq_ref[...], NT)
    gref_ref[...] = bf(gref)


def swap(x, axis, apart):
    pairs = [(i, i ^ apart) for i in range(lax.axis_size(axis))]
    return lax.ppermute(x, axis, pairs)


def at(x, index, axis=0):
    return lax.dynamic_index_in_dim(x, index, axis, False)


def laid(near, far, side, axis=0):
    shape = near.shape[:axis] + (2,) + near.shape[axis:]
    out = lax.dynamic_update_index_in_dim(jnp.zeros(shape, near.dtype), near, side, axis)
    return lax.dynamic_update_index_in_dim(out, far, 1 - side, axis)


def add(near, far):
    return (near.astype(jnp.float32) + far.astype(jnp.float32)).astype(near.dtype)


def halve(x, step, axis=0):
    mesh_axis, bit, side = step
    return add(at(x, side, axis), swap(at(x, 1 - side, axis), mesh_axis, bit))


def double(x, step, axis=0):
    mesh_axis, bit, side = step
    return laid(x, swap(x, mesh_axis, bit), side, axis)


def bit_steps(mesh_axis, first=1):
    count, me = lax.axis_size(mesh_axis), lax.axis_index(mesh_axis)
    steps = []
    while first < count:
        steps.append((mesh_axis, first, (me // first) % 2))
        first *= 2
    return steps


def combine_stats(parts):
    peak = functools.reduce(jnp.maximum, [part[0] for part in parts])
    factors = [jnp.exp(part[0] - peak) for part in parts]
    total = sum(factor * part[1] for factor, part in zip(factors, parts))
    dots = sum(factor * part[2] for factor, part in zip(factors, parts))
    return jnp.stack([peak, total, dots])


def vmem_call(kernel, name, out_shape, scratch, limit, flops, moved, args, scalars=0):
    specs = [pl.BlockSpec(memory_space=pltpu.SMEM)] * scalars
    specs += [pl.BlockSpec(memory_space=pltpu.VMEM)] * (len(args) - scalars)
    return pl.pallas_call(
        kernel,
        name=name,
        out_shape=out_shape,
        in_specs=specs,
        out_specs=[pl.BlockSpec(memory_space=pltpu.VMEM)] * len(out_shape),
        scratch_shapes=scratch,
        compiler_params=pltpu.CompilerParams(vmem_limit_bytes=limit),
        cost_estimate=pl.CostEstimate(flops=flops, bytes_accessed=moved, transcendentals=0),
    )(*args)


def on_device(ref_feats, src_feats, grad_out, w_query, w_key, w_value, w_out, intersection):
    ref_rows = ref_feats[0]
    src_rows = src_feats[0]
    out_grad = grad_out[0]
    listed = intersection[0]
    rows, width = ref_rows.shape
    core_step = bit_steps("blk")[0]
    chip_steps = bit_steps("blk", 2)
    key_rows = src_rows.shape[0]
    key_total = key_rows * lax.axis_size("blk")

    source_all = src_rows
    for count, step in enumerate(chip_steps[::-1]):
        source_all = double(source_all, step, count)
    source_all = double(source_all, core_step, len(chip_steps)).reshape(key_total, width)

    f32, b16 = jnp.float32, jnp.bfloat16
    shape, vmem = jax.ShapeDtypeStruct, pltpu.VMEM
    unit = 2 * rows * width * width
    limit = (8 << 20) + rows * key_total * 44
    left, grad_left, query_t, grad_t, bias = vmem_call(
        functools.partial(project_kernel, HEADS),
        "project_reference",
        [
            shape((HEADS, rows, width), b16),
            shape((HEADS, rows, width), b16),
            shape((width, rows), b16),
            shape((width, rows), b16),
            shape((key_total, width), b16),
        ],
        [vmem((rows, width), b16)],
        16 << 20,
        16 * unit,
        4 << 20,
        (listed, ref_rows, out_grad, w_query, w_out),
        scalars=1,
    )
    steps = key_total // STEP
    tile = vmem((steps, rows, STEP), f32)
    row_stats, col_stats, right, keys, values = vmem_call(
        functools.partial(stats_kernel, HEADS),
        "match_stats",
        [
            shape((2 * HEADS, rows, 128), f32),
            shape((3, HEADS, key_total), f32),
            shape((HEADS, key_total, width), b16),
            shape((key_total, width), b16),
            shape((key_total, width), b16),
        ],
        [tile] * 5
        + [vmem((rows, 128), f32), vmem((rows, 128), f32), vmem((HEADS, steps, 8, STEP), f32)],
        limit,
        60 * unit,
        8 << 20,
        (left, grad_left, bias, source_all, w_key, w_value),
    )
    near_stats = col_stats
    for mesh_axis, bit, _ in chip_steps:
        near_stats = combine_stats([near_stats, swap(near_stats, mesh_axis, bit)])
    far_stats = swap(near_stats, "blk", 1)
    attended, grad_query, grad_key, grad_value, weight_part = vmem_call(
        functools.partial(grads_kernel, HEADS),
        "match_grads",
        [
            shape((rows, width), b16),
            shape((rows, width), b16),
            shape((width, key_total), b16),
            shape((width, key_total), b16),
            shape((4, width, width), b16),
        ],
        [tile] * 4
        + [vmem((rows, key_total), b16)] * 4
        + [vmem((rows, width), f32)] * 2
        + [vmem((3, HEADS, steps, 8, STEP), f32)],
        limit,
        100 * unit,
        8 << 20,
        (left, grad_left, right, keys, values, query_t, grad_t, row_stats, near_stats, far_stats,
         ref_rows, out_grad, source_all),
    )
    matched, grad_ref, source_part = vmem_call(
        finish_kernel,
        "finish_rows",
        [
            shape((rows, width), b16),
            shape((rows, width), b16),
            shape((key_total, width), b16),
        ],
        [],
        16 << 20,
        16 * unit,
        4 << 20,
        (ref_rows, out_grad, attended, grad_query, grad_key, grad_value,
         w_query, w_key, w_value, w_out),
    )

    scans = lax.axis_size("scan")
    weights = weight_part.reshape((2, scans, -1, width))
    sources = source_part.reshape((2,) * (len(chip_steps) + 1) + (key_rows, width))
    weights = halve(weights, core_step)
    sources = halve(sources, core_step, len(chip_steps))
    weights = lax.all_to_all(weights, "scan", 0, 0).astype(f32).sum(axis=0).astype(b16)
    for mesh_axis, bit, _ in chip_steps:
        weights = add(weights, swap(weights, mesh_axis, bit))
    sources = halve(sources, chip_steps[0], len(chip_steps) - 1)
    weights, sources = lax.optimization_barrier((weights, sources))
    weights = lax.all_to_all(jnp.broadcast_to(weights, (scans,) + weights.shape), "scan", 0, 0)
    for count in range(1, len(chip_steps)):
        sources = halve(sources, chip_steps[count], len(chip_steps) - 1 - count)
    grad_src = sources
    weights = double(weights, core_step).reshape(4, width, width).astype(f32)
    return (
        matched[None],
        grad_ref[None],
        grad_src[None],
        weights[0],
        weights[1],
        weights[2],
        weights[3],
    )


def solution(mesh):
    split = P("scan", "blk", None)
    whole = P()
    return jax.shard_map(
        on_device,
        mesh=mesh,
        in_specs=(split, split, split, whole, whole, whole, whole, split),
        out_specs=(split, split, split, whole, whole, whole, whole),
        check_vma=False,
    )
```

time: 91.5 us -> 91.8 us (level)
  local copies, waits for them, and re-layouts: 2.23 us -> 11.2 us
  blocking collectives: 8.11 us -> 0 us
  waiting for transfers between devices: 34.1 us -> 29.8 us
  starting transfers between devices: 19.2 us -> 22 us
    ppermute x13, waiting for transfers between devices: 29.4 us -> 20.5 us  [swap(): return lax.ppermute(x, axis, pairs)]
    all_to_all x1 -> x0, blocking collectives: 8.11 us -> none  [on_device(): lax.all_to_all(jnp.broadcast_to(weights, (scans,) + weights.shape), 'scan...]
    unnamed x14 -> x22, local copies, waits for them, and re-layouts: 0.03 us -> 4.42 us
    all_to_all x0 -> x1, waiting for transfers between devices: none -> 3.64 us  [on_device(): lax.all_to_all(jnp.broadcast_to(weights, (scans,) + weights.shape), 'scan...]
    all_to_all x0 -> x1, starting transfers between devices: none -> 3.41 us  [on_device(): lax.all_to_all(jnp.broadcast_to(weights, (scans,) + weights.shape), 'scan...]
    dynamic_update_slice x4, local copies, waits for them, and re-layouts: 0.06 us -> 1.67 us  [laid(): return lax.dynamic_update_index_in_dim(out, far, 1 - side, axis)]
    dynamic_update_slice x4, local copies, waits for them, and re-layouts: 0.93 us -> 2.53 us  [laid(): lax.dynamic_update_index_in_dim(jnp.zeros(shape, near.dtype), near, side,...]
    pallas_call x2 -> x4, Pallas kernels: 24.9 us -> 25.6 us  [vmem_call(): pl.pallas_call(kernel, name=name, out_shape=out_shape, in_specs=specs, ou...]
  transfers between devices with their start and end apart: 14 -> 15, of which waited for: 12 -> 11; matrix products, arithmetic and copies ran while one was open for 3% -> 5% of each run, Pallas kernels for 0% -> 3%
where the time goes in v6:
time: 91.8 us; the launch traced here: 91.2 us
  waiting for transfers between devices  29.8 us (32%)
  Pallas kernels  25.6 us (28%)
  starting transfers between devices  22 us (24%)
  local copies, waits for them, and re-layouts  11.2 us (12%)
  other arithmetic  1.77 us (2%)
    pallas_call x4, Pallas kernels, vmem_call(): pl.pallas_call(kernel, name=name, out_shape=out_shape, in_specs=specs, ou...  25.6 us
    ppermute x13, waiting for transfers between devices, swap(): return lax.ppermute(x, axis, pairs)  20.5 us
    ppermute x13, starting transfers between devices, swap(): return lax.ppermute(x, axis, pairs)  14.8 us
    all_to_all x1, waiting for transfers between devices, on_device(): lax.all_to_all(weights, 'scan', 0, 0).astype(f32).sum(axis=0).astype(b16)  5.61 us
    unnamed x22, local copies, waits for them, and re-layouts  4.42 us
    all_to_all x1, starting transfers between devices, on_device(): lax.all_to_all(weights, 'scan', 0, 0).astype(f32).sum(axis=0).astype(b16)  3.79 us
    all_to_all x1, waiting for transfers between devices, on_device(): lax.all_to_all(jnp.broadcast_to(weights, (scans,) + weights.shape), 'scan...  3.64 us
    all_to_all x1, starting transfers between devices, on_device(): lax.all_to_all(jnp.broadcast_to(weights, (scans,) + weights.shape), 'scan...  3.41 us
  transfers between devices with their start and end apart: 15, of which 11 were waited for; matrix products, arithmetic and copies ran while one was open for 5% of the time, Pallas kernels for 3%

profile of v6, /device:TPU:0, one launch (start us, length us, event | category | flops | bytes accessed | tf_op | source)
XLA Modules:
  0.0 91.2 jit_solution(16123778150977027485)
XLA Ops:
  0.6 4.1 %collective-permute-start = (bf16[128,256]{1,0:T(8,128)(2,1)}, bf16[128,256]{1,0:T(8,128)(2,1)S(1)}, u32[]{:S(2)}, u32[]{:S(2)}) collective-permute-start(bf16[128,256]{1,0:T(8,128)(2,1)} %bitcast.76), channel_id=1, source_target_pairs={{0,4},{1,5},{2,6},{3,7},{4,0},{5,1},{6,2},{7,3},{8,12},{9,13},{10,... | collective-permute-start | bytes 196616 | tf_op jit(solution)/shard_map/ppermute | solution.py:317
  5.6 3.0 %collective-permute-done = bf16[128,256]{1,0:T(8,128)(2,1)S(1)} collective-permute-done((bf16[128,256]{1,0:T(8,128)(2,1)}, bf16[128,256]{1,0:T(8,128)(2,1)S(1)}, u32[]{:S(2)}, u32[]{:S(2)}) %collective-permute-start) | collective-permute-done | bytes 65568 | tf_op jit(solution)/shard_map/ppermute | solution.py:317
  10.7 2.9 %collective-permute-done.1 = bf16[2,128,256]{2,1,0:T(8,128)(2,1)S(1)} collective-permute-done((bf16[2,128,256]{2,1,0:T(8,128)(2,1)S(1)}, bf16[2,128,256]{2,1,0:T(8,128)(2,1)S(1)}, u32[]{:S(2)}, u32[]{:S(2)}) %collective-permute-start.1) | collective-permute-done | bytes 131104 | tf_op jit(solution)/shard_map/ppermute | solution.py:317
  14.3 0.9 %copy-done = bf16[1,512,256]{2,1,0:T(8,128)(2,1)S(1)} copy-done((bf16[1,512,256]{2,1,0:T(8,128)(2,1)S(1)}, bf16[1,512,256]{2,1,0:T(8,128)(2,1)}, u32[]{:S(2)}) %copy-start) | copy-done | bytes 262168
  18.7 1.1 %project_reference.1 = (bf16[4,512,256]{2,1,0:T(8,128)(2,1)S(1)}, bf16[4,512,256]{2,1,0:T(8,128)(2,1)S(1)}, bf16[256,512]{1,0:T(8,128)(2,1)S(1)}, bf16[256,512]{1,0:T(8,128)(2,1)S(1)}, bf16[1024,256]{1,0:T(8,128)(2,1)S(1)}) custom-call(s32[4,8]{1,0:T(4,128)S(1)} %bitcast.73, bf16[512,256]{1,0:T(8,128)(2,1)S(1)} %bitcast.67, bf16[512,256]{1,0:T(8,128)(2,1)S(1)} %bitcast.70, ...), custom_call_target="tpu_custom_call" | custom-call | flops 1073741824 | bytes 4194304 | tf_op jit(solution)/shard_map/project_reference/pallas_call | solution.py:364
  19.9 1.0 %bitcast_dynamic-update-slice_fusion = bf16[2,2,2,128,256]{4,3,2,1,0:T(8,128)(2,1)S(1)} fusion(bf16[2,2,2,128,256]{4,3,2,1,0:T(8,128)(2,1)S(1)} %broadcast_in_dim.50, s32[]{:T(128)S(6)} %select_n.68, bf16[2,2,128,256]{3,2,1,0:T(8,128)(2,1)} %bitcast_dynamic-update-slice_fusion.5), kind=kLoop, calls=%fused_computation.11 | loop fusion | bytes 524292 | tf_op jit(solution)/shard_map/jit(dynamic_update_index_in_dim)/dynamic_update_slice | solution.py:326
  20.9 1.0 %bitcast_dynamic-update-slice_fusion.3 = bf16[2,2,2,128,256]{4,3,2,1,0:T(8,128)(2,1)S(1)} fusion(bf16[2,2,2,128,256]{4,3,2,1,0:T(8,128)(2,1)S(1)} %bitcast_dynamic-update-slice_fusion, s32[]{:T(128)S(6)} %select_n.69, bf16[2,2,128,256]{3,2,1,0:T(8,128)(2,1)} %collective-permute-done.2), kind=kLoop, calls=%fused_computation.14 | loop fusion | bytes 524292 | tf_op jit(solution)/shard_map/jit(dynamic_update_index_in_dim)/dynamic_update_slice | solution.py:327
  21.9 9.3 %match_stats.1 = (f32[8,512,128]{2,1,0:T(8,128)S(1)}, f32[3,4,1024]{2,1,0:T(4,128)S(1)}, bf16[4,1024,256]{2,1,0:T(8,128)(2,1)S(1)}, bf16[1024,256]{1,0:T(8,128)(2,1)S(1)}, bf16[1024,256]{1,0:T(8,128)(2,1)S(1)}) custom-call(bf16[4,512,256]{2,1,0:T(8,128)(2,1)S(1)} %get-tuple-element.27.left_ref, bf16[4,512,256]{2,1,0:T(8,128)(2,1)S(1)} %get-tuple-element.28.gleft_ref, ...), custom_call_target="tpu_custom_call" | custom-call | flops 4026531840 | bytes 8388608 | tf_op jit(solution)/shard_map/match_stats/pallas_call | solution.py:364
  32.0 3.5 %collective-permute-done.3 = f32[3,4,1024]{2,1,0:T(4,128)S(1)} collective-permute-done((f32[3,4,1024]{2,1,0:T(4,128)S(1)}, f32[3,4,1024]{2,1,0:T(4,128)S(1)}, u32[]{:S(2)}, u32[]{:S(2)}) %collective-permute-start.3) | collective-permute-done | bytes 49184 | tf_op jit(solution)/shard_map/ppermute | solution.py:317
  35.5 2.4 %collective-permute-start.4 = (f32[3,4,1024]{2,1,0:T(4,128)S(1)}, f32[3,4,1024]{2,1,0:T(4,128)S(1)}, u32[]{:S(2)}, u32[]{:S(2)}) collective-permute-start(f32[3,4,1024]{2,1,0:T(4,128)S(1)} %pad_maximum_fusion), channel_id=1, source_target_pairs={{0,4},{1,5},{2,6},{3,7},{4,0},{5,1},{6,2},{7,3},{8,12},{9,13},{10,... | collective-permute-start | bytes 147464 | tf_op jit(solution)/shard_map/ppermute | solution.py:317
  37.9 3.3 %collective-permute-done.4 = f32[3,4,1024]{2,1,0:T(4,128)S(1)} collective-permute-done((f32[3,4,1024]{2,1,0:T(4,128)S(1)}, f32[3,4,1024]{2,1,0:T(4,128)S(1)}, u32[]{:S(2)}, u32[]{:S(2)}) %collective-permute-start.4) | collective-permute-done | bytes 49184 | tf_op jit(solution)/shard_map/ppermute | solution.py:317
  41.4 1.2 %collective-permute-done.5.far_ref = f32[3,4,1024]{2,1,0:T(4,128)S(1)} collective-permute-done((f32[3,4,1024]{2,1,0:T(4,128)S(1)}, f32[3,4,1024]{2,1,0:T(4,128)S(1)}, u32[]{:S(2)}, u32[]{:S(2)}) %collective-permute-start.5) | collective-permute-done | bytes 49184 | tf_op jit(solution)/shard_map/ppermute | solution.py:317
  42.6 13.8 %match_grads.1 = (bf16[512,256]{1,0:T(8,128)(2,1)S(1)}, bf16[512,256]{1,0:T(8,128)(2,1)S(1)}, bf16[256,1024]{1,0:T(8,128)(2,1)S(1)}, bf16[256,1024]{1,0:T(8,128)(2,1)S(1)}, bf16[4,256,256]{2,1,0:T(8,128)(2,1)S(1)}) custom-call(bf16[4,512,256]{2,1,0:T(8,128)(2,1)S(1)} %get-tuple-element.27.left_ref, bf16[4,512,256]{2,1,0:T(8,128)(2,1)S(1)} %get-tuple-element.28.gleft_ref, ...), custom_call_target="tpu_custom_call" | custom-call | flops 6710886400 | bytes 8388608 | tf_op jit(solution)/shard_map/match_grads/pallas_call | solution.py:364
  56.7 1.4 %finish_rows.1 = (bf16[512,256]{1,0:T(8,128)(2,1)}, bf16[512,256]{1,0:T(8,128)(2,1)}, bf16[1024,256]{1,0:T(8,128)(2,1)S(1)}) custom-call(bf16[512,256]{1,0:T(8,128)(2,1)S(1)} %bitcast.69, bf16[512,256]{1,0:T(8,128)(2,1)S(1)} %bitcast.72, bf16[512,256]{1,0:T(8,128)(2,1)S(1)} %get-tuple-element.37.attended_ref, ...), custom_call_target="tpu_custom_call" | custom-call | flops 1073741824 | bytes 4194304 | tf_op jit(solution)/shard_map/finish_rows/pallas_call | solution.py:364
  59.3 3.8 %all-to-all-start = ((bf16[4,128,256]{2,1,0:T(8,128)(2,1)}), bf16[4,128,256]{2,1,0:T(8,128)(2,1)S(1)}, u32[]{:S(2)}, u32[]{:S(2)}) async-start(bf16[4,128,256]{2,1,0:T(8,128)(2,1)} %fusion.1), calls=%async_computation | async-start | bytes 524288 | tf_op jit(solution)/shard_map/all_to_all | solution.py:477
  63.2 5.6 %all-to-all-done = bf16[4,128,256]{2,1,0:T(8,128)(2,1)S(1)} async-done(((bf16[4,128,256]{2,1,0:T(8,128)(2,1)}), bf16[4,128,256]{2,1,0:T(8,128)(2,1)S(1)}, u32[]{:S(2)}, u32[]{:S(2)}) %all-to-all-start) | async-done | bytes 262176 | tf_op jit(solution)/shard_map/all_to_all | solution.py:477
  69.4 1.6 %collective-permute-start.10 = (bf16[2,128,256]{2,1,0:T(8,128)(2,1)S(1)}, bf16[2,128,256]{2,1,0:T(8,128)(2,1)S(1)}, u32[]{:S(2)}, u32[]{:S(2)}) collective-permute-start(bf16[2,128,256]{2,1,0:T(8,128)(2,1)S(1)} %dynamic-slice_bitcast_fusion.1), channel_id=1, source_target_pairs={{0,2},{1,3},{2,0},{3,1},{4,6},{5,7},{6,4},{7,5},{8,10},{9,11},{10,... | collective-permute-start | bytes 393224 | tf_op jit(solution)/shard_map/ppermute | solution.py:317
  71.0 2.2 %collective-permute-done.7 = bf16[128,256]{1,0:T(8,128)(2,1)S(1)} collective-permute-done((bf16[128,256]{1,0:T(8,128)(2,1)S(1)}, bf16[128,256]{1,0:T(8,128)(2,1)S(1)}, u32[]{:S(2)}, u32[]{:S(2)}) %collective-permute-start.7) | collective-permute-done | bytes 65568 | tf_op jit(solution)/shard_map/ppermute | solution.py:317
  73.2 2.3 %collective-permute-start.8 = (bf16[128,256]{1,0:T(8,128)(2,1)S(1)}, bf16[128,256]{1,0:T(8,128)(2,1)S(1)}, u32[]{:S(2)}, u32[]{:S(2)}) collective-permute-start(bf16[128,256]{1,0:T(8,128)(2,1)S(1)} %add_convert_fusion.1), channel_id=1, source_target_pairs={{0,4},{1,5},{2,6},{3,7},{4,0},{5,1},{6,2},{7,3},{8,12},{9,13},{10,... | collective-permute-start | bytes 196616 | tf_op jit(solution)/shard_map/ppermute | solution.py:317
  75.5 3.6 %collective-permute-done.8 = bf16[128,256]{1,0:T(8,128)(2,1)S(1)} collective-permute-done((bf16[128,256]{1,0:T(8,128)(2,1)S(1)}, bf16[128,256]{1,0:T(8,128)(2,1)S(1)}, u32[]{:S(2)}, u32[]{:S(2)}) %collective-permute-start.8) | collective-permute-done | bytes 65568 | tf_op jit(solution)/shard_map/ppermute | solution.py:317
  79.9 3.4 %all-to-all-start.1 = ((bf16[4,128,256]{2,1,0:T(8,128)(2,1)}), bf16[4,128,256]{2,1,0:T(8,128)(2,1)S(1)}, u32[]{:S(2)}, u32[]{:S(2)}) async-start(bf16[4,128,256]{2,1,0:T(8,128)(2,1)} %broadcast_in_dim.62), calls=%async_computation.1 | async-start | bytes 524288 | tf_op jit(solution)/shard_map/all_to_all | solution.py:482
  83.3 1.7 %collective-permute-start.11 = (bf16[128,256]{1,0:T(8,128)(2,1)S(1)}, bf16[128,256]{1,0:T(8,128)(2,1)S(1)}, u32[]{:S(2)}, u32[]{:S(2)}) collective-permute-start(bf16[128,256]{1,0:T(8,128)(2,1)S(1)} %dynamic-slice_bitcast_fusion.2), channel_id=1, source_target_pairs={{0,4},{1,5},{2,6},{3,7},{4,0},{5,1},{6,2},{7,3},{8,12},{9,13},{10,... | collective-permute-start | bytes 196616 | tf_op jit(solution)/shard_map/ppermute | solution.py:317
  85.0 3.6 %all-to-all-done.1 = bf16[4,128,256]{2,1,0:T(8,128)(2,1)S(1)} async-done(((bf16[4,128,256]{2,1,0:T(8,128)(2,1)}), bf16[4,128,256]{2,1,0:T(8,128)(2,1)S(1)}, u32[]{:S(2)}, u32[]{:S(2)}) %all-to-all-start.1) | async-done | bytes 262176 | tf_op jit(solution)/shard_map/all_to_all | solution.py:482
  90.3 1.0 %slice_bitcast_fusion = (f32[256,256]{1,0:T(8,128)}, f32[256,256]{1,0:T(8,128)}, f32[256,256]{1,0:T(8,128)}, f32[256,256]{1,0:T(8,128)}) fusion(f32[4,256,256]{2,1,0:T(8,128)S(1)} %convert.6), kind=kLoop, calls=%fused_computation.4 | loop fusion | bytes 2097152 | tf_op jit(solution)/shard_map/squeeze | solution.py:494
  (64 shorter events, 12.7 us)
Async XLA Ops:
  0.6 8.0 %collective-permute-start = (bf16[128,256]{1,0:T(8,128)(2,1)}, bf16[128,256]{1,0:T(8,128)(2,1)S(1)}, u32[]{:S(2)}, u32[]{:S(2)}) collective-permute-start(bf16[128,256]{1,0:T(8,128)(2,1)} %bitcast.76), channel_id=1, source_target_pairs={{0,4},{1,5},{2,6},{3,7},{4,0},{5,1},{6,2},{7,3},{8,12},{9,13},{10,... | collective-permute-start | bytes 196616 | tf_op jit(solution)/shard_map/ppermute | solution.py:317
  8.6 5.0 %collective-permute-start.1 = (bf16[2,128,256]{2,1,0:T(8,128)(2,1)S(1)}, bf16[2,128,256]{2,1,0:T(8,128)(2,1)S(1)}, u32[]{:S(2)}, u32[]{:S(2)}) collective-permute-start(bf16[2,128,256]{2,1,0:T(8,128)(2,1)S(1)} %bitcast_dynamic-update-slice_fusion.6), channel_id=1, source_target_pairs={{0,2},{1,3},{2,0},{3,1},{4,6},{5,7},{6,4},{7,5},{8,10},{9,11},{10,... | collective-permute-start | bytes 393224 | tf_op jit(solution)/shard_map/ppermute | solution.py:317
  14.3 6.6 %collective-permute-start.2 = (bf16[2,2,128,256]{3,2,1,0:T(8,128)(2,1)}, bf16[2,2,128,256]{3,2,1,0:T(8,128)(2,1)}, u32[]{:S(2)}, u32[]{:S(2)}) collective-permute-start(bf16[2,2,128,256]{3,2,1,0:T(8,128)(2,1)} %bitcast_dynamic-update-slice_fusion.5), channel_id=1, source_target_pairs={{0,1},{1,0},{2,3},{3,2},{4,5},{5,4},{6,7},{7,6},{8,9},{9,8},{10,11... | collective-permute-start | bytes 786440 | tf_op jit(solution)/shard_map/ppermute | solution.py:317
  14.3 1.0 %copy-start = (bf16[1,512,256]{2,1,0:T(8,128)(2,1)S(1)}, bf16[1,512,256]{2,1,0:T(8,128)(2,1)}, u32[]{:S(2)}) copy-start(bf16[1,512,256]{2,1,0:T(8,128)(2,1)} %param.8) | copy-start | bytes 786436
  15.3 0.9 %copy-start.2 = (bf16[1,512,256]{2,1,0:T(8,128)(2,1)S(1)}, bf16[1,512,256]{2,1,0:T(8,128)(2,1)}, u32[]{:S(2)}) copy-start(bf16[1,512,256]{2,1,0:T(8,128)(2,1)} %param.10) | copy-start | bytes 786436
  16.2 0.9 copy-start.4
  18.7 3.1 %copy-start.8 = (bf16[256,256]{1,0:T(8,128)(2,1)S(1)}, bf16[256,256]{1,0:T(8,128)(2,1)}, u32[]{:S(2)}) copy-start(bf16[256,256]{1,0:T(8,128)(2,1)} %wk_ref.3) | copy-start | bytes 393220
  18.7 3.2 %copy-start.9 = (bf16[256,256]{1,0:T(8,128)(2,1)S(1)}, bf16[256,256]{1,0:T(8,128)(2,1)}, u32[]{:S(2)}) copy-start(bf16[256,256]{1,0:T(8,128)(2,1)} %wv_ref.3) | copy-start | bytes 393220
  21.9 20.7 %copy-start.1 = (bf16[1,512,256]{2,1,0:T(8,128)(2,1)S(1)}, bf16[1,512,256]{2,1,0:T(8,128)(2,1)}, u32[]{:S(2)}) copy-start(bf16[1,512,256]{2,1,0:T(8,128)(2,1)} %param.8) | copy-start | bytes 786436
  21.9 20.7 %copy-start.3 = (bf16[1,512,256]{2,1,0:T(8,128)(2,1)S(1)}, bf16[1,512,256]{2,1,0:T(8,128)(2,1)}, u32[]{:S(2)}) copy-start(bf16[1,512,256]{2,1,0:T(8,128)(2,1)} %param.10) | copy-start | bytes 786436
  31.2 4.2 %collective-permute-start.3 = (f32[3,4,1024]{2,1,0:T(4,128)S(1)}, f32[3,4,1024]{2,1,0:T(4,128)S(1)}, u32[]{:S(2)}, u32[]{:S(2)}) collective-permute-start(f32[3,4,1024]{2,1,0:T(4,128)S(1)} %get-tuple-element.36), channel_id=1, source_target_pairs={{0,2},{1,3},{2,0},{3,1},{4,6},{5,7},{6,4},{7,5},{8,10},{9,11},{10,... | collective-permute-start | bytes 147464 | tf_op jit(solution)/shard_map/ppermute | solution.py:317
  35.5 5.7 %collective-permute-start.4 = (f32[3,4,1024]{2,1,0:T(4,128)S(1)}, f32[3,4,1024]{2,1,0:T(4,128)S(1)}, u32[]{:S(2)}, u32[]{:S(2)}) collective-permute-start(f32[3,4,1024]{2,1,0:T(4,128)S(1)} %pad_maximum_fusion), channel_id=1, source_target_pairs={{0,4},{1,5},{2,6},{3,7},{4,0},{5,1},{6,2},{7,3},{8,12},{9,13},{10,... | collective-permute-start | bytes 147464 | tf_op jit(solution)/shard_map/ppermute | solution.py:317
  41.3 1.3 %collective-permute-start.5 = (f32[3,4,1024]{2,1,0:T(4,128)S(1)}, f32[3,4,1024]{2,1,0:T(4,128)S(1)}, u32[]{:S(2)}, u32[]{:S(2)}) collective-permute-start(f32[3,4,1024]{2,1,0:T(4,128)S(1)} %pad_maximum_fusion.1.near_ref), channel_id=1, source_target_pairs={{0,1},{1,0},{2,3},{3,2},{4,5},{5,4},{6,7},{7,6},{8,9},{9,8},{10,11... | collective-permute-start | bytes 147464 | tf_op jit(solution)/shard_map/ppermute | solution.py:317
  42.6 14.1 %copy-start.5 = (bf16[256,256]{1,0:T(8,128)(2,1)S(1)}, bf16[256,256]{1,0:T(8,128)(2,1)}, u32[]{:S(2)}) copy-start(bf16[256,256]{1,0:T(8,128)(2,1)} %wq_ref.3) | copy-start | bytes 393220
  42.6 14.1 %copy-start.7 = (bf16[256,256]{1,0:T(8,128)(2,1)S(1)}, bf16[256,256]{1,0:T(8,128)(2,1)}, u32[]{:S(2)}) copy-start(bf16[256,256]{1,0:T(8,128)(2,1)} %wo_ref.3) | copy-start | bytes 393220
  56.5 2.1 %collective-permute-start.6 = (bf16[4,128,256]{2,1,0:T(8,128)(2,1)S(1)}, bf16[4,128,256]{2,1,0:T(8,128)(2,1)S(1)}, u32[]{:S(2)}, u32[]{:S(2)}) collective-permute-start(bf16[4,128,256]{2,1,0:T(8,128)(2,1)S(1)} %dynamic-slice_bitcast_fusion), channel_id=1, source_target_pairs={{0,1},{1,0},{2,3},{3,2},{4,5},{5,4},{6,7},{7,6},{8,9},{9,8},{10,11... | collective-permute-start | bytes 786440 | tf_op jit(solution)/shard_map/ppermute | solution.py:317
  58.1 5.0 %collective-permute-start.9 = (bf16[2,2,128,256]{3,2,0,1:T(8,128)(2,1)S(1)}, bf16[2,2,128,256]{3,2,0,1:T(8,128)(2,1)S(1)}, u32[]{:S(2)}, u32[]{:S(2)}) collective-permute-start(bf16[2,2,128,256]{3,2,0,1:T(8,128)(2,1)S(1)} %bitcast.75), channel_id=1, source_target_pairs={{0,1},{1,0},{2,3},{3,2},{4,5},{5,4},{6,7},{7,6},{8,9},{9,8},{10,11... | collective-permute-start | bytes 786440 | tf_op jit(solution)/shard_map/ppermute | solution.py:317
  59.3 9.5 %all-to-all-start = ((bf16[4,128,256]{2,1,0:T(8,128)(2,1)}), bf16[4,128,256]{2,1,0:T(8,128)(2,1)S(1)}, u32[]{:S(2)}, u32[]{:S(2)}) async-start(bf16[4,128,256]{2,1,0:T(8,128)(2,1)} %fusion.1), calls=%async_computation | async-start | bytes 524288 | tf_op jit(solution)/shard_map/all_to_all | solution.py:477
  68.8 4.3 %collective-permute-start.7 = (bf16[128,256]{1,0:T(8,128)(2,1)S(1)}, bf16[128,256]{1,0:T(8,128)(2,1)S(1)}, u32[]{:S(2)}, u32[]{:S(2)}) collective-permute-start(bf16[128,256]{1,0:T(8,128)(2,1)S(1)} %reduce_sum.12), channel_id=1, source_target_pairs={{0,2},{1,3},{2,0},{3,1},{4,6},{5,7},{6,4},{7,5},{8,10},{9,11},{10,... | collective-permute-start | bytes 196616 | tf_op jit(solution)/shard_map/ppermute | solution.py:317
  69.4 6.1 %collective-permute-start.10 = (bf16[2,128,256]{2,1,0:T(8,128)(2,1)S(1)}, bf16[2,128,256]{2,1,0:T(8,128)(2,1)S(1)}, u32[]{:S(2)}, u32[]{:S(2)}) collective-permute-start(bf16[2,128,256]{2,1,0:T(8,128)(2,1)S(1)} %dynamic-slice_bitcast_fusion.1), channel_id=1, source_target_pairs={{0,2},{1,3},{2,0},{3,1},{4,6},{5,7},{6,4},{7,5},{8,10},{9,11},{10,... | collective-permute-start | bytes 393224 | tf_op jit(solution)/shard_map/ppermute | solution.py:317
  73.2 5.9 %collective-permute-start.8 = (bf16[128,256]{1,0:T(8,128)(2,1)S(1)}, bf16[128,256]{1,0:T(8,128)(2,1)S(1)}, u32[]{:S(2)}, u32[]{:S(2)}) collective-permute-start(bf16[128,256]{1,0:T(8,128)(2,1)S(1)} %add_convert_fusion.1), channel_id=1, source_target_pairs={{0,4},{1,5},{2,6},{3,7},{4,0},{5,1},{6,2},{7,3},{8,12},{9,13},{10,... | collective-permute-start | bytes 196616 | tf_op jit(solution)/shard_map/ppermute | solution.py:317
  79.9 8.8 %all-to-all-start.1 = ((bf16[4,128,256]{2,1,0:T(8,128)(2,1)}), bf16[4,128,256]{2,1,0:T(8,128)(2,1)S(1)}, u32[]{:S(2)}, u32[]{:S(2)}) async-start(bf16[4,128,256]{2,1,0:T(8,128)(2,1)} %broadcast_in_dim.62), calls=%async_computation.1 | async-start | bytes 524288 | tf_op jit(solution)/shard_map/all_to_all | solution.py:482
  83.3 5.9 %collective-permute-start.11 = (bf16[128,256]{1,0:T(8,128)(2,1)S(1)}, bf16[128,256]{1,0:T(8,128)(2,1)S(1)}, u32[]{:S(2)}, u32[]{:S(2)}) collective-permute-start(bf16[128,256]{1,0:T(8,128)(2,1)S(1)} %dynamic-slice_bitcast_fusion.2), channel_id=1, source_target_pairs={{0,4},{1,5},{2,6},{3,7},{4,0},{5,1},{6,2},{7,3},{8,12},{9,13},{10,... | collective-permute-start | bytes 196616 | tf_op jit(solution)/shard_map/ppermute | solution.py:317
  88.6 1.5 %collective-permute-start.12 = (bf16[4,128,256]{2,1,0:T(8,128)(2,1)S(1)}, bf16[4,128,256]{2,1,0:T(8,128)(2,1)S(1)}, u32[]{:S(2)}, u32[]{:S(2)}) collective-permute-start(bf16[4,128,256]{2,1,0:T(8,128)(2,1)S(1)} %all-to-all-done.1), channel_id=1, source_target_pairs={{0,1},{1,0},{2,3},{3,2},{4,5},{5,4},{6,7},{7,6},{8,9},{9,8},{10,11... | collective-permute-start | bytes 786440 | tf_op jit(solution)/shard_map/ppermute | solution.py:317
  (2 other events, 1.6 us)

commit v7 on v6

--- a/solution.py
+++ b/solution.py
@@ -1,4 +1,5 @@
 import functools
+import math
 
 import jax
 import jax.numpy as jnp
@@ -11,6 +12,7 @@
 BLOCK = 128
 NEG = -1e30
 FLOOR = -1e29
+LOG2E = math.log2(math.e)
 
 NT = (((1,), (1,)), ((), ()))
 TN = (((0,), (0,)), ((), ()))
@@ -34,18 +36,15 @@
     return bf(jnp.where(lanes == head, 1.0, 0.0))
 
 
-def fill_bias(inter_ref, bias_ref, head_dim):
+def fill_bias(inter_ref, bias_ref):
     query_blocks, key_blocks = inter_ref.shape
-    width = bias_ref.shape[1]
-    lane = lax.broadcasted_iota(jnp.int32, (1, width), 1) % head_dim
+    block_of = lax.broadcasted_iota(jnp.int32, (bias_ref.shape[0], BLOCK), 0)
     for key_block in range(key_blocks):
-        row = jnp.zeros((1, width), jnp.float32)
+        piece = jnp.zeros(block_of.shape, jnp.float32)
         for query_block in range(query_blocks):
             listed = inter_ref[query_block, key_block] == 1
-            row = jnp.where(lane == query_block, jnp.where(listed, 0.0, NEG), row)
-        bias_ref[pl.ds(key_block * BLOCK, BLOCK), :] = bf(
-            jnp.broadcast_to(row, (BLOCK, width))
-        )
+            piece = jnp.where(block_of == query_block, jnp.where(listed, 0.0, NEG), piece)
+        bias_ref[:, key_block * BLOCK : (key_block + 1) * BLOCK] = bf(piece)
 
 
 def fill_hot(hot_ref, head_dim):
@@ -69,18 +68,14 @@
 
 
 def project_kernel(
-    head_count, inter_ref, ref_ref, gout_ref, wq_ref, wo_ref,
-    left_ref, gleft_ref, query_t_ref, grad_t_ref, bias_ref, hot_ref,
+    head_count, inter_ref, ref_ref, gout_ref, wq_ref, wo_ref, left_ref, gleft_ref, bias_ref, hot_ref
 ):
     rows, width = ref_ref.shape
     head_dim = width // head_count
     scale = head_dim ** -0.5
     query = bf(bf(mm(ref_ref[...], wq_ref[...])).astype(jnp.float32) * scale)
     grad = bf(mm_general(gout_ref[...], wo_ref[...], NT))
-    query_t = bf(mm_general(wq_ref[...], ref_ref[...], TT)).astype(jnp.float32)
-    query_t_ref[...] = bf(query_t * (2.0 * scale))
-    grad_t_ref[...] = bf(mm_general(wo_ref[...], gout_ref[...], NT))
-    fill_bias(inter_ref, bias_ref, head_dim)
+    fill_bias(inter_ref, bias_ref)
     fill_hot(hot_ref, head_dim)
     for head in range(head_count):
         own = lane_row(width, head, head_dim)
@@ -89,12 +84,22 @@
         gleft_ref[head] = grad * own
 
 
-def fill_step(head, step, left_ref, gleft_ref, right_ref, value_ref, score_ref, prob_ref):
+def side_kernel(
+    head_count, ref_ref, gout_ref, src_ref, wq_ref, wk_ref, wv_ref, wo_ref,
+    key_ref, value_ref, query_t_ref, grad_t_ref,
+):
+    scale = (ref_ref.shape[1] // head_count) ** -0.5
+    key_ref[...] = bf(mm(src_ref[...], wk_ref[...]))
+    value_ref[...] = bf(mm(src_ref[...], wv_ref[...]))
+    query_t = bf(mm_general(wq_ref[...], ref_ref[...], TT)).astype(jnp.float32)
+    query_t_ref[...] = bf(query_t * (2.0 * scale))
+    grad_t_ref[...] = bf(mm_general(wo_ref[...], gout_ref[...], NT))
+
+
+def fill_step(head, step, left_ref, gleft_ref, right_ref, value_t_ref, score_ref, prob_ref):
     span = pl.ds(pl.multiple_of(step * STEP, STEP), STEP)
-    scores = mm_general(left_ref[head], right_ref[head, span, :], NT)
-    score_ref[step] = scores
-    prob_ref[step] = mm_general(gleft_ref[head], value_ref[span, :], NT)
-    return scores
+    score_ref[step] = mm(left_ref[head], right_ref[head, :, span]) * LOG2E
+    prob_ref[step] = mm(gleft_ref[head], value_t_ref[:, span])
 
 
 def strips(step, steps, rows):
@@ -110,33 +115,41 @@
 
 def stats_kernel(
     head_count, left_ref, gleft_ref, bias_ref, src_ref, wk_ref, wv_ref,
-    row_ref, col_ref, right_ref, key_ref, value_ref,
+    row_ref, col_ref, right_ref, value_t_ref,
     score_a, score_b, prob_a, prob_b, prob_c, sum_ref, top_ref, peak_ref,
 ):
     rows, width = left_ref.shape[1:]
     key_total = src_ref.shape[0]
     tiles, steps = key_total // 128, key_total // STEP
     head_dim = width // head_count
-    key_ref[...] = bf(mm(src_ref[...], wk_ref[...]))
-    value_ref[...] = bf(mm(src_ref[...], wv_ref[...]))
+    key_t = bf(mm_general(wk_ref[...], src_ref[...], TT))
+    value_t_ref[...] = bf(mm_general(wv_ref[...], src_ref[...], TT))
+    right_ref[...] = jnp.zeros(right_ref.shape, jnp.bfloat16)
     for head in range(head_count):
-        own = lane_row(width, head, head_dim)
-        other = lane_row(width, (head + 1) % head_count, head_dim)
-        right_ref[head] = key_ref[...] * own + bias_ref[...] * other
+        own = slice(head * head_dim, (head + 1) * head_dim)
+        other = (head + 1) % head_count * head_dim
+        right_ref[head, own, :] = key_t[own]
+        right_ref[head, other : other + head_dim, :] = bias_ref[...]
     scores_of, probs_of = (score_a, score_b), (prob_a, prob_b, prob_c)
     zeros = tuple(jnp.zeros((8, 128), jnp.float32) for _ in range(tiles))
 
     def fill(head, step):
-        scores = fill_step(
-            head, step, left_ref, gleft_ref, right_ref, value_ref,
-            scores_of[head % 2], probs_of[head % 3],
+        score_ref = scores_of[head % 2]
+        fill_step(
+            head, step, left_ref, gleft_ref, right_ref, value_t_ref, score_ref, probs_of[head % 3]
         )
-        top = top_ref[...]
-        for first in range(0, STEP, 128):
-            top = jnp.maximum(top, scores[:, first : first + 128])
-        top_ref[...] = top
-        peak = jnp.maximum(scores.max(axis=0, keepdims=True), FLOOR)
-        peak_ref[head, step] = jnp.broadcast_to(peak, (8, STEP))
+        peaks = [jnp.full((8, 128), FLOOR, jnp.float32)] * (STEP // 128)
+        for first in range(0, rows, 4 * STRIP):
+            span = slice(first, first + 4 * STRIP)
+            top = top_ref[span, :]
+            for piece in range(STEP // 128):
+                scores = score_ref[step, span, piece * 128 : piece * 128 + 128]
+                top = jnp.maximum(top, scores)
+                peaks[piece] = jnp.maximum(peaks[piece], by_eight(scores).max(axis=0))
+            top_ref[span, :] = top
+        for piece in range(STEP // 128):
+            peak = jnp.broadcast_to(peaks[piece].max(axis=0, keepdims=True), (8, 128))
+            peak_ref[head, step, :, piece * 128 : piece * 128 + 128] = peak
 
     def close_peaks(head):
         row_ref[head] = spread(top_ref[...].max(axis=1, keepdims=True), top_ref)
@@ -150,8 +163,8 @@
         for tile in range(tiles):
             at_step, lanes = lanes_of(tile)
             scores = by_eight(score_ref[at_step, span, lanes])
-            row_exp = jnp.exp(scores - row_peak)
-            col_exp = jnp.exp(scores - peak_ref[head, at_step, :, lanes][None])
+            row_exp = jnp.exp2(scores - row_peak)
+            col_exp = jnp.exp2(scores - peak_ref[head, at_step, :, lanes][None])
             row_total = row_total + row_exp
             product = row_exp * col_exp * by_eight(prob_ref[at_step, span, lanes])
             prob_ref[at_step, span, lanes] = product.reshape(STRIP, 128)
@@ -201,8 +214,8 @@
 
 
 def grads_kernel(
-    head_count, left_ref, gleft_ref, right_ref, key_ref, value_ref, query_t_ref, grad_t_ref, row_ref,
-    near_ref, far_ref, ref_ref, gout_ref, src_ref,
+    head_count, left_ref, gleft_ref, right_ref, value_t_ref, key_ref, value_ref, query_t_ref, grad_t_ref,
+    row_ref, near_ref, far_ref, ref_ref, gout_ref, src_ref,
     attended_ref, gquery_ref, gkey_ref, gvalue_ref, weight_ref,
     score_a, score_b, prob_a, prob_b, match_a, match_b, gscore_a, gscore_b, att_ref, gq_ref, col_ref,
 ):
@@ -214,7 +227,7 @@
     chunk = rows // steps
 
     peak = jnp.maximum(near_ref[0], far_ref[0])
-    near, far = jnp.exp(near_ref[0] - peak), jnp.exp(far_ref[0] - peak)
+    near, far = jnp.exp2(near_ref[0] - peak), jnp.exp2(far_ref[0] - peak)
     inverse = 1.0 / (near * near_ref[1] + far * far_ref[1])
     half = (near * near_ref[2] + far * far_ref[2]) * inverse * 0.5
     for kind, values in enumerate((peak, inverse, half)):
@@ -229,7 +242,7 @@
 
     def fill(head, step):
         fill_step(
-            head, step, left_ref, gleft_ref, right_ref, value_ref,
+            head, step, left_ref, gleft_ref, right_ref, value_t_ref,
             scores_of[head % 2], probs_of[head % 2],
         )
 
@@ -241,8 +254,8 @@
         for tile in range(tiles):
             at_step, lanes = lanes_of(tile)
             scores = by_eight(score_ref[at_step, span, lanes])
-            row_prob = jnp.exp(scores - row_peak) * row_inverse
-            col_prob = jnp.exp(scores - col_ref[0, head, at_step, :, lanes][None])
+            row_prob = jnp.exp2(scores - row_peak) * row_inverse
+            col_prob = jnp.exp2(scores - col_ref[0, head, at_step, :, lanes][None])
             col_prob = col_prob * col_ref[1, head, at_step, :, lanes][None]
             match = row_prob * col_prob
             product = match * by_eight(prob_ref[at_step, span, lanes])
@@ -352,7 +365,7 @@
 
 def combine_stats(parts):
     peak = functools.reduce(jnp.maximum, [part[0] for part in parts])
-    factors = [jnp.exp(part[0] - peak) for part in parts]
+    factors = [jnp.exp2(part[0] - peak) for part in parts]
     total = sum(factor * part[1] for factor, part in zip(factors, parts))
     dots = sum(factor * part[2] for factor, part in zip(factors, parts))
     return jnp.stack([peak, total, dots])
@@ -387,49 +400,63 @@
     source_all = src_rows
     for count, step in enumerate(chip_steps[::-1]):
         source_all = double(source_all, step, count)
+    ref_near, grad_near, source_all = lax.optimization_barrier((ref_rows, out_grad, source_all))
     source_all = double(source_all, core_step, len(chip_steps)).reshape(key_total, width)
 
     f32, b16 = jnp.float32, jnp.bfloat16
     shape, vmem = jax.ShapeDtypeStruct, pltpu.VMEM
     unit = 2 * rows * width * width
-    limit = (8 << 20) + rows * key_total * 44
-    left, grad_left, query_t, grad_t, bias = vmem_call(
+    left, grad_left, bias = vmem_call(
         functools.partial(project_kernel, HEADS),
         "project_reference",
         [
             shape((HEADS, rows, width), b16),
             shape((HEADS, rows, width), b16),
-            shape((width, rows), b16),
-            shape((width, rows), b16),
-            shape((key_total, width), b16),
+            shape((width // HEADS, key_total), b16),
         ],
         [vmem((rows, width), b16)],
-        16 << 20,
-        16 * unit,
-        4 << 20,
-        (listed, ref_rows, out_grad, w_query, w_out),
+        8 << 20,
+        8 * unit,
+        2 << 20,
+        (listed, ref_near, grad_near, w_query, w_out),
         scalars=1,
     )
     steps = key_total // STEP
     tile = vmem((steps, rows, STEP), f32)
-    row_stats, col_stats, right, keys, values = vmem_call(
+    row_stats, col_stats, right, value_t = vmem_call(
         functools.partial(stats_kernel, HEADS),
         "match_stats",
         [
             shape((2 * HEADS, rows, 128), f32),
             shape((3, HEADS, key_total), f32),
-            shape((HEADS, key_total, width), b16),
-            shape((key_total, width), b16),
-            shape((key_total, width), b16),
+            shape((HEADS, width, key_total), b16),
+            shape((width, key_total), b16),
         ],
         [tile] * 5
         + [vmem((rows, 128), f32), vmem((rows, 128), f32), vmem((HEADS, steps, 8, STEP), f32)],
-        limit,
+        (6 << 20) + rows * key_total * 24,
         60 * unit,
         8 << 20,
         (left, grad_left, bias, source_all, w_key, w_value),
     )
-    near_stats = col_stats
+    ref_near, grad_near, source_near, near_stats = lax.optimization_barrier(
+        (ref_rows, out_grad, source_all, col_stats)
+    )
+    keys, values, query_t, grad_t = vmem_call(
+        functools.partial(side_kernel, HEADS),
+        "project_for_grads",
+        [
+            shape((key_total, width), b16),
+            shape((key_total, width), b16),
+            shape((width, rows), b16),
+            shape((width, rows), b16),
+        ],
+        [],
+        8 << 20,
+        8 * unit,
+        2 << 20,
+        (ref_near, grad_near, source_near, w_query, w_key, w_value, w_out),
+    )
     for mesh_axis, bit, _ in chip_steps:
         near_stats = combine_stats([near_stats, swap(near_stats, mesh_axis, bit)])
     far_stats = swap(near_stats, "blk", 1)
@@ -447,10 +474,10 @@
         + [vmem((rows, key_total), b16)] * 4
         + [vmem((rows, width), f32)] * 2
         + [vmem((3, HEADS, steps, 8, STEP), f32)],
-        limit,
+        (6 << 20) + rows * key_total * 32,
         100 * unit,
         8 << 20,
-        (left, grad_left, right, keys, values, query_t, grad_t, row_stats, near_stats, far_stats,
+        (left, grad_left, right, value_t, keys, values, query_t, grad_t, row_stats, near_stats, far_stats,
          ref_rows, out_grad, source_all),
     )
     matched, grad_ref, source_part = vmem_call(
@@ -462,28 +489,30 @@
             shape((key_total, width), b16),
         ],
         [],
-        16 << 20,
-        16 * unit,
-        4 << 20,
+        8 << 20,
+        8 * unit,
+        2 << 20,
         (ref_rows, out_grad, attended, grad_query, grad_key, grad_value,
          w_query, w_key, w_value, w_out),
     )
 
-    scans = lax.axis_size("scan")
-    weights = weight_part.reshape((2, scans, -1, width))
+    scan_steps = bit_steps("scan")
+    weights = weight_part.reshape((2,) * (1 + len(scan_steps)) + (-1, width))
     sources = source_part.reshape((2,) * (len(chip_steps) + 1) + (key_rows, width))
     weights = halve(weights, core_step)
     sources = halve(sources, core_step, len(chip_steps))
-    weights = lax.all_to_all(weights, "scan", 0, 0).astype(f32).sum(axis=0).astype(b16)
+    for count in range(max(len(scan_steps), len(chip_steps))):
+        weights, sources = lax.optimization_barrier((weights, sources))
+        if count < len(scan_steps):
+            weights = halve(weights, scan_steps[count])
+        if count < len(chip_steps):
+            sources = halve(sources, chip_steps[count], len(chip_steps) - 1 - count)
+    weights, grad_src = lax.optimization_barrier((weights, sources))
     for mesh_axis, bit, _ in chip_steps:
         weights = add(weights, swap(weights, mesh_axis, bit))
-    sources = halve(sources, chip_steps[0], len(chip_steps) - 1)
-    weights, sources = lax.optimization_barrier((weights, sources))
-    weights = lax.all_to_all(jnp.broadcast_to(weights, (scans,) + weights.shape), "scan", 0, 0)
-    for count in range(1, len(chip_steps)):
-        sources = halve(sources, chip_steps[count], len(chip_steps) - 1 - count)
-    grad_src = sources
-    weights = double(weights, core_step).reshape(4, width, width).astype(f32)
+    for step in scan_steps[::-1] + [core_step]:
+        weights = double(weights, step)
+    weights = weights.reshape(4, width, width).astype(f32)
     return (
         matched[None],
         grad_ref[None],

time: 91.8 us -> 92.2 us (level)
  waiting for transfers between devices: 29.8 us -> 37 us
  local copies, waits for them, and re-layouts: 11.2 us -> 6.7 us
    ppermute x13 -> x17, waiting for transfers between devices: 20.5 us -> 37 us  [swap(): return lax.ppermute(x, axis, pairs)]
    all_to_all x2 -> x0, waiting for transfers between devices: 9.25 us -> none  [the longest x1 5.61 us: on_device(): lax.all_to_all(weights, 'scan', 0, 0).astype(f32).sum(axis=0).astype(b16)]
    all_to_all x2 -> x0, starting transfers between devices: 7.2 us -> none  [the longest x1 3.79 us: on_device(): lax.all_to_all(weights, 'scan', 0, 0).astype(f32).sum(axis=0).astype(b16)]
    ppermute x13 -> x17, starting transfers between devices: 14.8 us -> 21.3 us  [swap(): return lax.ppermute(x, axis, pairs)]
    dynamic_update_slice x4 -> x5, local copies, waits for them, and re-layouts: 2.53 us -> 0.94 us  [laid(): lax.dynamic_update_index_in_dim(jnp.zeros(shape, near.dtype), near, side,...]
    dynamic_update_slice x4 -> x6, local copies, waits for them, and re-layouts: 1.67 us -> 0.08 us  [laid(): return lax.dynamic_update_index_in_dim(out, far, 1 - side, axis)]
    broadcast_in_dim x5 -> x0, local copies, waits for them, and re-layouts: 1.53 us -> none  [the longest x4 0.81 us: laid(): jnp.zeros(shape, near.dtype)]
    pallas_call x4 -> x5, Pallas kernels: 25.6 us -> 24.9 us  [vmem_call(): pl.pallas_call(kernel, name=name, out_shape=out_shape, in_specs=specs, ou...]
  transfers between devices with their start and end apart: 15 -> 17, of which waited for: 11 -> 15; matrix products, arithmetic and copies ran while one was open for 5% -> 2% of each run, Pallas kernels for 3% -> 3%
where the time goes in v7:
time: 92.2 us; the launch traced here: 91.9 us
  waiting for transfers between devices  37 us (40%)
  Pallas kernels  24.9 us (27%)
  starting transfers between devices  21.3 us (23%)
  local copies, waits for them, and re-layouts  6.7 us (7%)
  other arithmetic  1.11 us (1%)
  between operations  1 us (1%)
    ppermute x17, waiting for transfers between devices, swap(): return lax.ppermute(x, axis, pairs)  37 us
    pallas_call x5, Pallas kernels, vmem_call(): pl.pallas_call(kernel, name=name, out_shape=out_shape, in_specs=specs, ou...  24.9 us
    ppermute x17, starting transfers between devices, swap(): return lax.ppermute(x, axis, pairs)  21.3 us
    unnamed x22, local copies, waits for them, and re-layouts  4.42 us
  transfers between devices with their start and end apart: 17, of which 15 were waited for; matrix products, arithmetic and copies ran while one was open for 2% of the time, Pallas kernels for 3%

profile of v7, /device:TPU:0, one launch (start us, length us, event | category | flops | bytes accessed | tf_op | source)
XLA Modules:
  0.0 91.9 jit_solution(12809152615054006893)
XLA Ops:
  0.6 4.1 %collective-permute-start = (bf16[128,256]{1,0:T(8,128)(2,1)}, bf16[128,256]{1,0:T(8,128)(2,1)S(1)}, u32[]{:S(2)}, u32[]{:S(2)}) collective-permute-start(bf16[128,256]{1,0:T(8,128)(2,1)} %bitcast.97), channel_id=1, source_target_pairs={{0,4},{1,5},{2,6},{3,7},{4,0},{5,1},{6,2},{7,3},{8,12},{9,13},{10,... | collective-permute-start | bytes 196616 | tf_op jit(solution)/shard_map/ppermute | solution.py:330
  5.6 3.0 %collective-permute-done = bf16[128,256]{1,0:T(8,128)(2,1)S(1)} collective-permute-done((bf16[128,256]{1,0:T(8,128)(2,1)}, bf16[128,256]{1,0:T(8,128)(2,1)S(1)}, u32[]{:S(2)}, u32[]{:S(2)}) %collective-permute-start) | collective-permute-done | bytes 65568 | tf_op jit(solution)/shard_map/ppermute | solution.py:330
  9.4 4.2 %collective-permute-done.1 = bf16[2,128,256]{2,1,0:T(8,128)(2,1)S(1)} collective-permute-done((bf16[2,128,256]{2,1,0:T(8,128)(2,1)S(1)}, bf16[2,128,256]{2,1,0:T(8,128)(2,1)S(1)}, u32[]{:S(2)}, u32[]{:S(2)}) %collective-permute-start.1) | collective-permute-done | bytes 131104 | tf_op jit(solution)/shard_map/ppermute | solution.py:330
  19.3 8.6 %match_stats.1 = (f32[8,512,128]{2,1,0:T(8,128)S(1)}, f32[3,4,1024]{2,1,0:T(4,128)S(1)}, bf16[4,256,1024]{2,1,0:T(8,128)(2,1)S(1)}, bf16[256,1024]{1,0:T(8,128)(2,1)S(1)}) custom-call(bf16[4,512,256]{2,1,0:T(8,128)(2,1)S(1)} %get-tuple-element.41.left_ref, bf16[4,512,256]{2,1,0:T(8,128)(2,1)S(1)} %get-tuple-element.42.gleft_ref, ...), custom_call_target="tpu_custom_call" | custom-call | flops 4026531840 | bytes 8388608 | tf_op jit(solution)/shard_map/match_stats/pallas_call | solution.py:377
  28.7 3.5 %collective-permute-done.3 = f32[3,4,1024]{2,1,0:T(4,128)S(1)} collective-permute-done((f32[3,4,1024]{2,1,0:T(4,128)S(1)}, f32[3,4,1024]{2,1,0:T(4,128)S(1)}, u32[]{:S(2)}, u32[]{:S(2)}) %collective-permute-start.3) | collective-permute-done | bytes 49184 | tf_op jit(solution)/shard_map/ppermute | solution.py:330
  32.2 2.4 %collective-permute-start.4 = (f32[3,4,1024]{2,1,0:T(4,128)S(1)}, f32[3,4,1024]{2,1,0:T(4,128)S(1)}, u32[]{:S(2)}, u32[]{:S(2)}) collective-permute-start(f32[3,4,1024]{2,1,0:T(4,128)S(1)} %pad_maximum_fusion), channel_id=1, source_target_pairs={{0,4},{1,5},{2,6},{3,7},{4,0},{5,1},{6,2},{7,3},{8,12},{9,13},{10,... | collective-permute-start | bytes 147464 | tf_op jit(solution)/shard_map/ppermute | solution.py:330
  34.6 3.3 %collective-permute-done.4 = f32[3,4,1024]{2,1,0:T(4,128)S(1)} collective-permute-done((f32[3,4,1024]{2,1,0:T(4,128)S(1)}, f32[3,4,1024]{2,1,0:T(4,128)S(1)}, u32[]{:S(2)}, u32[]{:S(2)}) %collective-permute-start.4) | collective-permute-done | bytes 49184 | tf_op jit(solution)/shard_map/ppermute | solution.py:330
  39.3 13.3 %match_grads.1 = (bf16[512,256]{1,0:T(8,128)(2,1)S(1)}, bf16[512,256]{1,0:T(8,128)(2,1)S(1)}, bf16[256,1024]{1,0:T(8,128)(2,1)S(1)}, bf16[256,1024]{1,0:T(8,128)(2,1)S(1)}, bf16[4,256,256]{2,1,0:T(8,128)(2,1)S(1)}) custom-call(bf16[4,512,256]{2,1,0:T(8,128)(2,1)S(1)} %get-tuple-element.41.left_ref, bf16[4,512,256]{2,1,0:T(8,128)(2,1)S(1)} %get-tuple-element.42.gleft_ref, ...), custom_call_target="tpu_custom_call" | custom-call | flops 6710886400 | bytes 8388608 | tf_op jit(solution)/shard_map/match_grads/pallas_call | solution.py:377
  52.9 1.4 %finish_rows.1 = (bf16[512,256]{1,0:T(8,128)(2,1)}, bf16[512,256]{1,0:T(8,128)(2,1)}, bf16[1024,256]{1,0:T(8,128)(2,1)S(1)}) custom-call(bf16[512,256]{1,0:T(8,128)(2,1)S(1)} %bitcast.88, bf16[512,256]{1,0:T(8,128)(2,1)S(1)} %bitcast.92, bf16[512,256]{1,0:T(8,128)(2,1)S(1)} %get-tuple-element.57.attended_ref, ...), custom_call_target="tpu_custom_call" | custom-call | flops 536870912 | bytes 2097152 | tf_op jit(solution)/shard_map/finish_rows/pallas_call | solution.py:377
  54.8 1.1 %collective-permute-done.7 = bf16[2,2,128,256]{3,2,0,1:T(8,128)(2,1)S(1)} collective-permute-done((bf16[2,2,128,256]{3,2,0,1:T(8,128)(2,1)S(1)}, bf16[2,2,128,256]{3,2,0,1:T(8,128)(2,1)S(1)}, u32[]{:S(2)}, u32[]{:S(2)}) %collective-permute-start.7) | collective-permute-done | bytes 262176 | tf_op jit(solution)/shard_map/ppermute | solution.py:330
  56.6 1.7 %collective-permute-start.8 = (bf16[2,128,256]{2,1,0:T(8,128)(2,1)S(1)}, bf16[2,128,256]{2,1,0:T(8,128)(2,1)S(1)}, u32[]{:S(2)}, u32[]{:S(2)}) collective-permute-start(bf16[2,128,256]{2,1,0:T(8,128)(2,1)S(1)} %dynamic-slice_bitcast_fusion.2), channel_id=1, source_target_pairs={{0,8},{8,0},{16,24},{24,16},{1,9},{9,1},{17,25},{25,17},{2,10},{10... | collective-permute-start | bytes 393224 | tf_op jit(solution)/shard_map/ppermute | solution.py:330
  58.2 3.6 %collective-permute-done.9 = bf16[2,128,256]{2,1,0:T(8,128)(2,1)S(1)} collective-permute-done((bf16[2,128,256]{2,1,0:T(8,128)(2,1)S(1)}, bf16[2,128,256]{2,1,0:T(8,128)(2,1)S(1)}, u32[]{:S(2)}, u32[]{:S(2)}) %collective-permute-start.9) | collective-permute-done | bytes 131104 | tf_op jit(solution)/shard_map/ppermute | solution.py:330
  62.2 3.2 %collective-permute-start.11 = (bf16[128,256]{1,0:T(8,128)(2,1)S(1)}, bf16[128,256]{1,0:T(8,128)(2,1)S(1)}, u32[]{:S(2)}, u32[]{:S(2)}) collective-permute-start(bf16[128,256]{1,0:T(8,128)(2,1)S(1)} %dynamic-slice_bitcast_fusion.3), channel_id=1, source_target_pairs={{0,4},{1,5},{2,6},{3,7},{4,0},{5,1},{6,2},{7,3},{8,12},{9,13},{10,... | collective-permute-start | bytes 196616 | tf_op jit(solution)/shard_map/ppermute | solution.py:330
  65.4 1.5 %collective-permute-start.10 = (bf16[128,256]{1,0:T(8,128)(2,1)S(1)}, bf16[128,256]{1,0:T(8,128)(2,1)S(1)}, u32[]{:S(2)}, u32[]{:S(2)}) collective-permute-start(bf16[128,256]{1,0:T(8,128)(2,1)S(1)} %dynamic-slice_bitcast_fusion.4), channel_id=1, source_target_pairs={{0,16},{8,24},{16,0},{24,8},{1,17},{9,25},{17,1},{25,9},{2,18},{10... | collective-permute-start | bytes 196616 | tf_op jit(solution)/shard_map/ppermute | solution.py:330
  68.3 1.4 %collective-permute-done.10 = bf16[128,256]{1,0:T(8,128)(2,1)S(1)} collective-permute-done((bf16[128,256]{1,0:T(8,128)(2,1)S(1)}, bf16[128,256]{1,0:T(8,128)(2,1)S(1)}, u32[]{:S(2)}, u32[]{:S(2)}) %collective-permute-start.10) | collective-permute-done | bytes 65568 | tf_op jit(solution)/shard_map/ppermute | solution.py:330
  70.1 3.9 %collective-permute-done.12 = bf16[128,256]{1,0:T(8,128)(2,1)S(1)} collective-permute-done((bf16[128,256]{1,0:T(8,128)(2,1)S(1)}, bf16[128,256]{1,0:T(8,128)(2,1)S(1)}, u32[]{:S(2)}, u32[]{:S(2)}) %collective-permute-start.12) | collective-permute-done | bytes 65568 | tf_op jit(solution)/shard_map/ppermute | solution.py:330
  74.0 2.0 %collective-permute-start.13 = (bf16[128,256]{1,0:T(8,128)(2,1)S(1)}, bf16[128,256]{1,0:T(8,128)(2,1)S(1)}, u32[]{:S(2)}, u32[]{:S(2)}) collective-permute-start(bf16[128,256]{1,0:T(8,128)(2,1)S(1)} %add_convert_fusion.1), channel_id=1, source_target_pairs={{0,4},{1,5},{2,6},{3,7},{4,0},{5,1},{6,2},{7,3},{8,12},{9,13},{10,... | collective-permute-start | bytes 196616 | tf_op jit(solution)/shard_map/ppermute | solution.py:330
  76.0 3.8 %collective-permute-done.13 = bf16[128,256]{1,0:T(8,128)(2,1)S(1)} collective-permute-done((bf16[128,256]{1,0:T(8,128)(2,1)S(1)}, bf16[128,256]{1,0:T(8,128)(2,1)S(1)}, u32[]{:S(2)}, u32[]{:S(2)}) %collective-permute-start.13) | collective-permute-done | bytes 65568 | tf_op jit(solution)/shard_map/ppermute | solution.py:330
  79.8 1.6 %collective-permute-start.14 = (bf16[128,256]{1,0:T(8,128)(2,1)S(1)}, bf16[128,256]{1,0:T(8,128)(2,1)S(1)}, u32[]{:S(2)}, u32[]{:S(2)}) collective-permute-start(bf16[128,256]{1,0:T(8,128)(2,1)S(1)} %get-tuple-element.72), channel_id=1, source_target_pairs={{0,16},{8,24},{16,0},{24,8},{1,17},{9,25},{17,1},{25,9},{2,18},{10... | collective-permute-start | bytes 196616 | tf_op jit(solution)/shard_map/ppermute | solution.py:330
  81.4 2.7 %collective-permute-done.14 = bf16[128,256]{1,0:T(8,128)(2,1)S(1)} collective-permute-done((bf16[128,256]{1,0:T(8,128)(2,1)S(1)}, bf16[128,256]{1,0:T(8,128)(2,1)S(1)}, u32[]{:S(2)}, u32[]{:S(2)}) %collective-permute-start.14) | collective-permute-done | bytes 65568 | tf_op jit(solution)/shard_map/ppermute | solution.py:330
  84.2 1.6 %collective-permute-start.15 = (bf16[2,128,256]{2,1,0:T(8,128)(2,1)S(1)}, bf16[2,128,256]{2,1,0:T(8,128)(2,1)S(1)}, u32[]{:S(2)}, u32[]{:S(2)}) collective-permute-start(bf16[2,128,256]{2,1,0:T(8,128)(2,1)S(1)} %bitcast_dynamic-update-slice_fusion.8), channel_id=1, source_target_pairs={{0,8},{8,0},{16,24},{24,16},{1,9},{9,1},{17,25},{25,17},{2,10},{10... | collective-permute-start | bytes 393224 | tf_op jit(solution)/shard_map/ppermute | solution.py:330
  85.8 3.4 %collective-permute-done.15 = bf16[2,128,256]{2,1,0:T(8,128)(2,1)S(1)} collective-permute-done((bf16[2,128,256]{2,1,0:T(8,128)(2,1)S(1)}, bf16[2,128,256]{2,1,0:T(8,128)(2,1)S(1)}, u32[]{:S(2)}, u32[]{:S(2)}) %collective-permute-start.15) | collective-permute-done | bytes 131104 | tf_op jit(solution)/shard_map/ppermute | solution.py:330
  89.4 1.4 %collective-permute-done.16 = bf16[2,2,128,256]{3,2,1,0:T(8,128)(2,1)S(1)} collective-permute-done((bf16[2,2,128,256]{3,2,1,0:T(8,128)(2,1)S(1)}, bf16[2,2,128,256]{3,2,1,0:T(8,128)(2,1)S(1)}, u32[]{:S(2)}, u32[]{:S(2)}) %collective-permute-start.16) | collective-permute-done | bytes 262176 | tf_op jit(solution)/shard_map/ppermute | solution.py:330
  90.9 1.0 %slice_bitcast_fusion = (f32[256,256]{1,0:T(8,128)}, f32[256,256]{1,0:T(8,128)}, f32[256,256]{1,0:T(8,128)}, f32[256,256]{1,0:T(8,128)}) fusion(f32[4,256,256]{2,1,0:T(8,128)S(1)} %convert.7), kind=kLoop, calls=%fused_computation.4 | loop fusion | bytes 2097152 | tf_op jit(solution)/shard_map/squeeze | solution.py:523
  (76 shorter events, 13.2 us)
Async XLA Ops:
  0.6 8.0 %collective-permute-start = (bf16[128,256]{1,0:T(8,128)(2,1)}, bf16[128,256]{1,0:T(8,128)(2,1)S(1)}, u32[]{:S(2)}, u32[]{:S(2)}) collective-permute-start(bf16[128,256]{1,0:T(8,128)(2,1)} %bitcast.97), channel_id=1, source_target_pairs={{0,4},{1,5},{2,6},{3,7},{4,0},{5,1},{6,2},{7,3},{8,12},{9,13},{10,... | collective-permute-start | bytes 196616 | tf_op jit(solution)/shard_map/ppermute | solution.py:330
  8.6 5.0 %collective-permute-start.1 = (bf16[2,128,256]{2,1,0:T(8,128)(2,1)S(1)}, bf16[2,128,256]{2,1,0:T(8,128)(2,1)S(1)}, u32[]{:S(2)}, u32[]{:S(2)}) collective-permute-start(bf16[2,128,256]{2,1,0:T(8,128)(2,1)S(1)} %bitcast_dynamic-update-slice_fusion.10), channel_id=1, source_target_pairs={{0,2},{1,3},{2,0},{3,1},{4,6},{5,7},{6,4},{7,5},{8,10},{9,11},{10,... | collective-permute-start | bytes 393224 | tf_op jit(solution)/shard_map/ppermute | solution.py:330
  9.4 9.9 %copy-start.8 = (bf16[256,256]{1,0:T(8,128)(2,1)S(1)}, bf16[256,256]{1,0:T(8,128)(2,1)}, u32[]{:S(2)}) copy-start(bf16[256,256]{1,0:T(8,128)(2,1)} %wk_ref.5) | copy-start | bytes 393220
  9.4 9.9 %copy-start.9 = (bf16[256,256]{1,0:T(8,128)(2,1)S(1)}, bf16[256,256]{1,0:T(8,128)(2,1)}, u32[]{:S(2)}) copy-start(bf16[256,256]{1,0:T(8,128)(2,1)} %wv_ref.5) | copy-start | bytes 393220
  13.7 5.5 %collective-permute-start.2 = (bf16[2,2,128,256]{3,2,1,0:T(8,128)(2,1)S(1)}, bf16[2,2,128,256]{3,2,1,0:T(8,128)(2,1)S(1)}, u32[]{:S(2)}, u32[]{:S(2)}) collective-permute-start(bf16[2,2,128,256]{3,2,1,0:T(8,128)(2,1)S(1)} %bitcast_dynamic-update-slice_fusion.7), channel_id=1, source_target_pairs={{0,1},{1,0},{2,3},{3,2},{4,5},{5,4},{6,7},{7,6},{8,9},{9,8},{10,11... | collective-permute-start | bytes 786440 | tf_op jit(solution)/shard_map/ppermute | solution.py:330
  13.7 1.0 %copy-start = (bf16[1,512,256]{2,1,0:T(8,128)(2,1)S(1)}, bf16[1,512,256]{2,1,0:T(8,128)(2,1)}, u32[]{:S(2)}) copy-start(bf16[1,512,256]{2,1,0:T(8,128)(2,1)} %param.8) | copy-start | bytes 786436
  19.2 18.8 %copy-start.1 = (bf16[1,512,256]{2,1,0:T(8,128)(2,1)S(1)}, bf16[1,512,256]{2,1,0:T(8,128)(2,1)}, u32[]{:S(2)}) copy-start(bf16[1,512,256]{2,1,0:T(8,128)(2,1)} %param.8) | copy-start | bytes 786436
  19.3 18.8 %copy-start.3 = (bf16[1,512,256]{2,1,0:T(8,128)(2,1)S(1)}, bf16[1,512,256]{2,1,0:T(8,128)(2,1)}, u32[]{:S(2)}) copy-start(bf16[1,512,256]{2,1,0:T(8,128)(2,1)} %param.10) | copy-start | bytes 786436
  19.3 18.8 %copy-start.5 = (bf16[256,256]{1,0:T(8,128)(2,1)S(1)}, bf16[256,256]{1,0:T(8,128)(2,1)}, u32[]{:S(2)}) copy-start(bf16[256,256]{1,0:T(8,128)(2,1)} %wq_ref.5) | copy-start | bytes 393220
  19.3 18.8 %copy-start.7 = (bf16[256,256]{1,0:T(8,128)(2,1)S(1)}, bf16[256,256]{1,0:T(8,128)(2,1)}, u32[]{:S(2)}) copy-start(bf16[256,256]{1,0:T(8,128)(2,1)} %wo_ref.5) | copy-start | bytes 393220
  27.9 4.2 %collective-permute-start.3 = (f32[3,4,1024]{2,1,0:T(4,128)S(1)}, f32[3,4,1024]{2,1,0:T(4,128)S(1)}, u32[]{:S(2)}, u32[]{:S(2)}) collective-permute-start(f32[3,4,1024]{2,1,0:T(4,128)S(1)} %get-tuple-element.56), channel_id=1, source_target_pairs={{0,2},{1,3},{2,0},{3,1},{4,6},{5,7},{6,4},{7,5},{8,10},{9,11},{10,... | collective-permute-start | bytes 147464 | tf_op jit(solution)/shard_map/ppermute | solution.py:330
  32.2 5.7 %collective-permute-start.4 = (f32[3,4,1024]{2,1,0:T(4,128)S(1)}, f32[3,4,1024]{2,1,0:T(4,128)S(1)}, u32[]{:S(2)}, u32[]{:S(2)}) collective-permute-start(f32[3,4,1024]{2,1,0:T(4,128)S(1)} %pad_maximum_fusion), channel_id=1, source_target_pairs={{0,4},{1,5},{2,6},{3,7},{4,0},{5,1},{6,2},{7,3},{8,12},{9,13},{10,... | collective-permute-start | bytes 147464 | tf_op jit(solution)/shard_map/ppermute | solution.py:330
  38.0 1.3 %collective-permute-start.5 = (f32[3,4,1024]{2,1,0:T(4,128)S(1)}, f32[3,4,1024]{2,1,0:T(4,128)S(1)}, u32[]{:S(2)}, u32[]{:S(2)}) collective-permute-start(f32[3,4,1024]{2,1,0:T(4,128)S(1)} %pad_maximum_fusion.1.near_ref), channel_id=1, source_target_pairs={{0,1},{1,0},{2,3},{3,2},{4,5},{5,4},{6,7},{7,6},{8,9},{9,8},{10,11... | collective-permute-start | bytes 147464 | tf_op jit(solution)/shard_map/ppermute | solution.py:330
  52.7 2.1 %collective-permute-start.6 = (bf16[2,2,128,256]{3,2,1,0:T(8,128)(2,1)S(1)}, bf16[2,2,128,256]{3,2,1,0:T(8,128)(2,1)S(1)}, u32[]{:S(2)}, u32[]{:S(2)}) collective-permute-start(bf16[2,2,128,256]{3,2,1,0:T(8,128)(2,1)S(1)} %dynamic-slice_bitcast_fusion), channel_id=1, source_target_pairs={{0,1},{1,0},{2,3},{3,2},{4,5},{5,4},{6,7},{7,6},{8,9},{9,8},{10,11... | collective-permute-start | bytes 786440 | tf_op jit(solution)/shard_map/ppermute | solution.py:330
  54.3 1.6 %collective-permute-start.7 = (bf16[2,2,128,256]{3,2,0,1:T(8,128)(2,1)S(1)}, bf16[2,2,128,256]{3,2,0,1:T(8,128)(2,1)S(1)}, u32[]{:S(2)}, u32[]{:S(2)}) collective-permute-start(bf16[2,2,128,256]{3,2,0,1:T(8,128)(2,1)S(1)} %bitcast.95), channel_id=1, source_target_pairs={{0,1},{1,0},{2,3},{3,2},{4,5},{5,4},{6,7},{7,6},{8,9},{9,8},{10,11... | collective-permute-start | bytes 786440 | tf_op jit(solution)/shard_map/ppermute | solution.py:330
  56.0 5.8 %collective-permute-start.9 = (bf16[2,128,256]{2,1,0:T(8,128)(2,1)S(1)}, bf16[2,128,256]{2,1,0:T(8,128)(2,1)S(1)}, u32[]{:S(2)}, u32[]{:S(2)}) collective-permute-start(bf16[2,128,256]{2,1,0:T(8,128)(2,1)S(1)} %dynamic-slice_bitcast_fusion.1), channel_id=1, source_target_pairs={{0,2},{1,3},{2,0},{3,1},{4,6},{5,7},{6,4},{7,5},{8,10},{9,11},{10,... | collective-permute-start | bytes 393224 | tf_op jit(solution)/shard_map/ppermute | solution.py:330
  56.6 5.5 %collective-permute-start.8 = (bf16[2,128,256]{2,1,0:T(8,128)(2,1)S(1)}, bf16[2,128,256]{2,1,0:T(8,128)(2,1)S(1)}, u32[]{:S(2)}, u32[]{:S(2)}) collective-permute-start(bf16[2,128,256]{2,1,0:T(8,128)(2,1)S(1)} %dynamic-slice_bitcast_fusion.2), channel_id=1, source_target_pairs={{0,8},{8,0},{16,24},{24,16},{1,9},{9,1},{17,25},{25,17},{2,10},{10... | collective-permute-start | bytes 393224 | tf_op jit(solution)/shard_map/ppermute | solution.py:330
  62.2 5.5 %collective-permute-start.11 = (bf16[128,256]{1,0:T(8,128)(2,1)S(1)}, bf16[128,256]{1,0:T(8,128)(2,1)S(1)}, u32[]{:S(2)}, u32[]{:S(2)}) collective-permute-start(bf16[128,256]{1,0:T(8,128)(2,1)S(1)} %dynamic-slice_bitcast_fusion.3), channel_id=1, source_target_pairs={{0,4},{1,5},{2,6},{3,7},{4,0},{5,1},{6,2},{7,3},{8,12},{9,13},{10,... | collective-permute-start | bytes 196616 | tf_op jit(solution)/shard_map/ppermute | solution.py:330
  65.4 4.3 %collective-permute-start.10 = (bf16[128,256]{1,0:T(8,128)(2,1)S(1)}, bf16[128,256]{1,0:T(8,128)(2,1)S(1)}, u32[]{:S(2)}, u32[]{:S(2)}) collective-permute-start(bf16[128,256]{1,0:T(8,128)(2,1)S(1)} %dynamic-slice_bitcast_fusion.4), channel_id=1, source_target_pairs={{0,16},{8,24},{16,0},{24,8},{1,17},{9,25},{17,1},{25,9},{2,18},{10... | collective-permute-start | bytes 196616 | tf_op jit(solution)/shard_map/ppermute | solution.py:330
  69.7 4.3 %collective-permute-start.12 = (bf16[128,256]{1,0:T(8,128)(2,1)S(1)}, bf16[128,256]{1,0:T(8,128)(2,1)S(1)}, u32[]{:S(2)}, u32[]{:S(2)}) collective-permute-start(bf16[128,256]{1,0:T(8,128)(2,1)S(1)} %fusion.5), channel_id=1, source_target_pairs={{0,2},{1,3},{2,0},{3,1},{4,6},{5,7},{6,4},{7,5},{8,10},{9,11},{10,... | collective-permute-start | bytes 196616 | tf_op jit(solution)/shard_map/ppermute | solution.py:330
  74.0 5.7 %collective-permute-start.13 = (bf16[128,256]{1,0:T(8,128)(2,1)S(1)}, bf16[128,256]{1,0:T(8,128)(2,1)S(1)}, u32[]{:S(2)}, u32[]{:S(2)}) collective-permute-start(bf16[128,256]{1,0:T(8,128)(2,1)S(1)} %add_convert_fusion.1), channel_id=1, source_target_pairs={{0,4},{1,5},{2,6},{3,7},{4,0},{5,1},{6,2},{7,3},{8,12},{9,13},{10,... | collective-permute-start | bytes 196616 | tf_op jit(solution)/shard_map/ppermute | solution.py:330
  79.8 4.3 %collective-permute-start.14 = (bf16[128,256]{1,0:T(8,128)(2,1)S(1)}, bf16[128,256]{1,0:T(8,128)(2,1)S(1)}, u32[]{:S(2)}, u32[]{:S(2)}) collective-permute-start(bf16[128,256]{1,0:T(8,128)(2,1)S(1)} %get-tuple-element.72), channel_id=1, source_target_pairs={{0,16},{8,24},{16,0},{24,8},{1,17},{9,25},{17,1},{25,9},{2,18},{10... | collective-permute-start | bytes 196616 | tf_op jit(solution)/shard_map/ppermute | solution.py:330
  84.2 5.0 %collective-permute-start.15 = (bf16[2,128,256]{2,1,0:T(8,128)(2,1)S(1)}, bf16[2,128,256]{2,1,0:T(8,128)(2,1)S(1)}, u32[]{:S(2)}, u32[]{:S(2)}) collective-permute-start(bf16[2,128,256]{2,1,0:T(8,128)(2,1)S(1)} %bitcast_dynamic-update-slice_fusion.8), channel_id=1, source_target_pairs={{0,8},{8,0},{16,24},{24,16},{1,9},{9,1},{17,25},{25,17},{2,10},{10... | collective-permute-start | bytes 393224 | tf_op jit(solution)/shard_map/ppermute | solution.py:330
  89.2 1.6 %collective-permute-start.16 = (bf16[2,2,128,256]{3,2,1,0:T(8,128)(2,1)S(1)}, bf16[2,2,128,256]{3,2,1,0:T(8,128)(2,1)S(1)}, u32[]{:S(2)}, u32[]{:S(2)}) collective-permute-start(bf16[2,2,128,256]{3,2,1,0:T(8,128)(2,1)S(1)} %bitcast_dynamic-update-slice_fusion.5), channel_id=1, source_target_pairs={{0,1},{1,0},{2,3},{3,2},{4,5},{5,4},{6,7},{7,6},{8,9},{9,8},{10,11... | collective-permute-start | bytes 786440 | tf_op jit(solution)/shard_map/ppermute | solution.py:330
  (4 other events, 3.4 us)

commit v8 on v7

v8 whole, which is shorter than its diff:
```python
import functools
import math

import jax
import jax.numpy as jnp
from jax import lax
from jax.experimental import pallas as pl
from jax.experimental.pallas import tpu as pltpu
from jax.sharding import PartitionSpec as P

HEADS = 4
BLOCK = 128
NEG = -1e30
FLOOR = -1e29
LOG2E = math.log2(math.e)

NT = (((1,), (1,)), ((), ()))
TN = (((0,), (0,)), ((), ()))
TT = (((0,), (1,)), ((), ()))


def mm(left, right):
    return jnp.dot(left, right, preferred_element_type=jnp.float32)


def mm_general(left, right, dims):
    return lax.dot_general(left, right, dims, preferred_element_type=jnp.float32)


def bf(x):
    return x.astype(jnp.bfloat16)


def lane_row(width, head, head_dim):
    lanes = lax.broadcasted_iota(jnp.int32, (1, width), 1) // head_dim
    return bf(jnp.where(lanes == head, 1.0, 0.0))


def spread(reduced, like):
    return jnp.broadcast_to(reduced, like.shape)


STRIP = 32
STEP = 256


def by_eight(x):
    return x.reshape(x.shape[0] // 8, 8, x.shape[1])


def listed_steps(inter_ref, query_block, work):
    per_step = STEP // BLOCK

    def visit(step, carry):
        listed = [inter_ref[query_block, step * per_step + k] == 1 for k in range(per_step)]

        @pl.when(functools.reduce(jnp.logical_or, listed))
        def _():
            work(query_block, step, listed)

        return carry

    lax.fori_loop(0, inter_ref.shape[1] // per_step, visit, 0)


def each_listed(inter_ref, work):
    def visit(query_block, carry):
        listed_steps(inter_ref, query_block, work)
        return carry

    lax.fori_loop(0, inter_ref.shape[0], visit, 0)


def head_strips(heads):
    for head in range(heads):
        spans = [slice(first, first + STRIP) for first in range(0, BLOCK, STRIP)]
        yield head, [slice(head * BLOCK + a.start, head * BLOCK + a.stop) for a in spans]


def score_block(query_block, step, listed, left_ref, key_t_ref, score_ref):
    span = pl.ds(pl.multiple_of(step * STEP, STEP), STEP)
    bias = jnp.concatenate(
        [jnp.full((1, BLOCK), jnp.where(flag, 0.0, NEG), jnp.float32) for flag in listed], axis=1
    )
    score_ref[...] = mm(left_ref[query_block], key_t_ref[:, span]) * LOG2E + bias


def stats_kernel(
    heads, inter_ref, ref_ref, gout_ref, src_ref, wq_ref, wk_ref, wv_ref, wo_ref,
    peak_ref, inverse_ref, col_ref, left_ref, gleft_ref, key_t_ref, value_t_ref,
    score_ref, prob_ref, total_ref, col_peak_ref, col_total_ref, col_dot_ref,
):
    rows, width = ref_ref.shape
    key_total = src_ref.shape[0]
    head_dim = width // heads
    query = bf(bf(mm(ref_ref[...], wq_ref[...])).astype(jnp.float32) * head_dim ** -0.5)
    grad = bf(mm_general(gout_ref[...], wo_ref[...], NT))
    for query_block in range(rows // BLOCK):
        span = slice(query_block * BLOCK, (query_block + 1) * BLOCK)
        for head in range(heads):
            own = lane_row(width, head, head_dim)
            left_ref[query_block, head * BLOCK : (head + 1) * BLOCK, :] = query[span] * own
            gleft_ref[query_block, head * BLOCK : (head + 1) * BLOCK, :] = grad[span] * own
    key_t_ref[...] = bf(mm_general(wk_ref[...], src_ref[...], TT))
    value_t_ref[...] = bf(mm_general(wv_ref[...], src_ref[...], TT))
    steps = key_total // STEP
    peak_ref[...] = jnp.full(peak_ref.shape, 2.0 * NEG, jnp.float32)
    total_ref[...] = jnp.zeros(total_ref.shape, jnp.float32)
    col_peak_ref[...] = jnp.full(col_peak_ref.shape, FLOOR, jnp.float32)
    col_total_ref[...] = jnp.zeros(col_total_ref.shape, jnp.float32)
    col_dot_ref[...] = jnp.zeros(col_dot_ref.shape, jnp.float32)
    tiles = [slice(first, first + 128) for first in range(0, STEP, 128)]

    def peaks(query_block, step, listed):
        block_ref = score_ref.at[query_block * steps + step]
        score_block(query_block, step, listed, left_ref, key_t_ref, block_ref)
        for head, spans in head_strips(heads):
            col_peaks = [col_peak_ref[step, head, :, lanes] for lanes in tiles]
            for span in spans:
                row_peak = peak_ref[query_block, span, :]
                for at, lanes in enumerate(tiles):
                    scores = block_ref[span, lanes]
                    row_peak = jnp.maximum(row_peak, scores)
                    col_peaks[at] = jnp.maximum(col_peaks[at], by_eight(scores).max(axis=0))
                peak_ref[query_block, span, :] = row_peak
            for at, lanes in enumerate(tiles):
                col_peak_ref[step, head, :, lanes] = col_peaks[at]

    each_listed(inter_ref, peaks)
    for query_block in range(rows // BLOCK):
        peak = peak_ref[query_block]
        peak_ref[query_block] = spread(peak.max(axis=1, keepdims=True), peak)
    for step in range(steps):
        for head in range(heads):
            peak = col_peak_ref[step, head]
            col_peak_ref[step, head] = spread(peak.max(axis=0, keepdims=True), peak)

    def totals(query_block, step, listed):
        score_now, prob_now = [ref.at[query_block * steps + step] for ref in (score_ref, prob_ref)]
        span = pl.ds(pl.multiple_of(step * STEP, STEP), STEP)
        prob_now[...] = mm(gleft_ref[query_block], value_t_ref[:, span])
        for head, spans in head_strips(heads):
            col_totals = [col_total_ref[step, head, :, lanes] for lanes in tiles]
            for span in spans:
                row_peak = by_eight(peak_ref[query_block, span, :])
                row_total = by_eight(total_ref[query_block, span, :])
                for at, lanes in enumerate(tiles):
                    scores = by_eight(score_now[span, lanes])
                    row_exp = jnp.exp2(scores - row_peak)
                    col_exp = jnp.exp2(scores - col_peak_ref[step, head, :, lanes][None])
                    row_total = row_total + row_exp
                    product = row_exp * col_exp * by_eight(prob_now[span, lanes])
                    prob_now[span, lanes] = product.reshape(STRIP, 128)
                    col_totals[at] = col_totals[at] + col_exp.sum(axis=0)
                total_ref[query_block, span, :] = row_total.reshape(STRIP, 128)
            for at, lanes in enumerate(tiles):
                col_total_ref[step, head, :, lanes] = col_totals[at]

    each_listed(inter_ref, totals)
    for query_block in range(rows // BLOCK):
        total = total_ref[query_block]
        inverse_ref[query_block] = spread(1.0 / total.sum(axis=1, keepdims=True), total)

    def dots(query_block, step, listed):
        prob_now = prob_ref.at[query_block * steps + step]
        for head, spans in head_strips(heads):
            col_dots = [col_dot_ref[step, head, :, lanes] for lanes in tiles]
            for span in spans:
                inverse = inverse_ref[query_block, span, :]
                for at, lanes in enumerate(tiles):
                    product = by_eight(prob_now[span, lanes] * inverse)
                    col_dots[at] = col_dots[at] + product.sum(axis=0)
            for at, lanes in enumerate(tiles):
                col_dot_ref[step, head, :, lanes] = col_dots[at]

    each_listed(inter_ref, dots)
    for step in range(steps):
        lanes = slice(step * STEP, (step + 1) * STEP)
        for head in range(heads):
            mine = slice(head, head + 1)
            col_ref[0, mine, lanes] = col_peak_ref[step, head, 0:1, :]
            col_ref[1, mine, lanes] = col_total_ref[step, head].sum(axis=0, keepdims=True)
            col_ref[2, mine, lanes] = col_dot_ref[step, head].sum(axis=0, keepdims=True)


def side_kernel(
    heads, ref_ref, gout_ref, src_ref, wq_ref, wk_ref, wv_ref, wo_ref,
    key_ref, value_ref, query_t_ref, grad_t_ref,
):
    rows, width = ref_ref.shape
    scale = (width // heads) ** -0.5
    key_ref[...] = bf(mm(src_ref[...], wk_ref[...]))
    value_ref[...] = bf(mm(src_ref[...], wv_ref[...]))
    query_t = bf(mm_general(wq_ref[...], ref_ref[...], TT)).astype(jnp.float32) * (2.0 * scale)
    grad_t = mm_general(wo_ref[...], gout_ref[...], NT)
    for query_block in range(rows // BLOCK):
        span = slice(query_block * BLOCK, (query_block + 1) * BLOCK)
        query_t_ref[query_block] = bf(query_t[:, span])
        grad_t_ref[query_block] = bf(grad_t[:, span])


def grads_kernel(
    heads, inter_ref, left_ref, gleft_ref, key_t_ref, value_t_ref, key_ref, value_ref,
    query_t_ref, grad_t_ref, peak_ref, inverse_ref, near_ref, far_ref, ref_ref, gout_ref, src_ref,
    attended_ref, gquery_ref, gkey_ref, gvalue_ref, weight_ref,
    row_prob_ref, rest_ref, match_ref, gscore_ref, score_ref, prob_ref, dot_ref, col_ref,
    att_ref, gq_ref, gk_ref, gv_ref,
):
    rows, width = ref_ref.shape
    key_total = src_ref.shape[0]
    steps = key_total // STEP
    head_dim = width // heads
    tiles = [slice(first, first + 128) for first in range(0, STEP, 128)]

    peak = jnp.maximum(near_ref[0], far_ref[0])
    near, far = jnp.exp2(near_ref[0] - peak), jnp.exp2(far_ref[0] - peak)
    inverse = 1.0 / (near * near_ref[1] + far * far_ref[1])
    half = (near * near_ref[2] + far * far_ref[2]) * inverse * 0.5
    for kind, values in enumerate((peak, inverse, half)):
        for head in range(heads):
            for step in range(steps):
                piece = values[head : head + 1, step * STEP : (step + 1) * STEP]
                col_ref[kind, step, head] = jnp.broadcast_to(piece, (8, STEP))
    for ref in (att_ref, gq_ref, gk_ref, gv_ref):
        ref[...] = jnp.zeros(ref.shape, jnp.float32)

    def products(query_block, step, listed):
        row_prob_now, rest_now, match_now = [
            ref.at[step] for ref in (row_prob_ref, rest_ref, match_ref)
        ]
        score_block(query_block, step, listed, left_ref, key_t_ref, score_ref)
        span = pl.ds(pl.multiple_of(step * STEP, STEP), STEP)
        prob_ref[...] = mm(gleft_ref[query_block], value_t_ref[:, span])
        for head, spans in head_strips(heads):
            for span in spans:
                row_peak = by_eight(peak_ref[query_block, span, :])
                row_inverse = by_eight(inverse_ref[query_block, span, :])
                row_dot = by_eight(dot_ref[span, :])
                for lanes in tiles:
                    scores = by_eight(score_ref[span, lanes])
                    row_prob = jnp.exp2(scores - row_peak) * row_inverse
                    col_prob = jnp.exp2(scores - col_ref[0, step, head, :, lanes][None])
                    col_prob = col_prob * col_ref[1, step, head, :, lanes][None]
                    match = row_prob * col_prob
                    product = match * by_eight(prob_ref[span, lanes])
                    row_dot = row_dot + product
                    rest = product - col_prob * col_ref[2, step, head, :, lanes][None]
                    match_now[span, lanes] = bf(match.reshape(STRIP, 128))
                    row_prob_now[span, lanes] = row_prob.reshape(STRIP, 128)
                    rest_now[span, lanes] = rest.reshape(STRIP, 128)
                dot_ref[span, :] = row_dot.reshape(STRIP, 128)

    def own_lanes(stacked):
        total = None
        for head in range(heads):
            own = lane_row(width, head, head_dim).astype(jnp.float32)
            piece = stacked[head * BLOCK : (head + 1) * BLOCK] * own
            total = piece if total is None else total + piece
        return total

    def outputs(query_block, step, listed):
        row_prob_now, rest_now, match_now = [
            ref.at[step] for ref in (row_prob_ref, rest_ref, match_ref)
        ]
        for _, spans in head_strips(heads):
            for span in spans:
                row_half = dot_ref[span, :]
                for lanes in tiles:
                    grads = rest_now[span, lanes] - row_prob_now[span, lanes] * row_half
                    gscore_ref[span, lanes] = bf(grads)
        span = pl.ds(pl.multiple_of(step * STEP, STEP), STEP)
        att_ref[query_block] += own_lanes(mm(match_now[...], value_ref[span, :]))
        gq_ref[query_block] += own_lanes(mm(gscore_ref[...], key_ref[span, :]))
        for head in range(heads):
            mine = slice(head * head_dim, (head + 1) * head_dim)
            stacked = slice(head * BLOCK, (head + 1) * BLOCK)
            gk_ref[step, mine, :] += mm(query_t_ref[query_block, mine, :], gscore_ref[stacked, :])
            gv_ref[step, mine, :] += mm(grad_t_ref[query_block, mine, :], match_now[stacked, :])

    def query_rows(query_block, carry):
        dot_ref[...] = jnp.zeros(dot_ref.shape, jnp.float32)
        listed_steps(inter_ref, query_block, products)
        dot = dot_ref[...]
        dot_ref[...] = spread(dot.sum(axis=1, keepdims=True) * 0.5, dot)
        listed_steps(inter_ref, query_block, outputs)
        return carry

    lax.fori_loop(0, rows // BLOCK, query_rows, 0)
    attended = bf(att_ref[...]).reshape(rows, width)
    gquery = bf(gq_ref[...] * (2.0 * head_dim ** -0.5)).reshape(rows, width)
    attended_ref[...] = attended
    gquery_ref[...] = gquery
    for step in range(steps):
        gkey_ref[:, step * STEP : (step + 1) * STEP] = bf(gk_ref[step])
        gvalue_ref[:, step * STEP : (step + 1) * STEP] = bf(gv_ref[step])
    weight_ref[0] = bf(mm_general(ref_ref[...], gquery, TN))
    weight_ref[1] = bf(mm(gkey_ref[...], src_ref[...]).T)
    weight_ref[2] = bf(mm(gvalue_ref[...], src_ref[...]).T)
    weight_ref[3] = bf(mm_general(attended, gout_ref[...], TN))


def finish_kernel(
    ref_ref, gout_ref, attended_ref, gquery_ref, gkey_ref, gvalue_ref, wq_ref, wk_ref, wv_ref, wo_ref,
    matched_ref, gref_ref, gsrc_ref,
):
    gsrc_t = mm(wk_ref[...], gkey_ref[...]) + mm(wv_ref[...], gvalue_ref[...])
    gsrc_ref[...] = bf(gsrc_t.T)
    matched = ref_ref[...].astype(jnp.float32) + mm(attended_ref[...], wo_ref[...])
    matched_ref[...] = bf(matched)
    gref = gout_ref[...].astype(jnp.float32) + mm_general(gquery_ref[...], wq_ref[...], NT)
    gref_ref[...] = bf(gref)


def swap(x, axis, apart):
    pairs = [(i, i ^ apart) for i in range(lax.axis_size(axis))]
    return lax.ppermute(x, axis, pairs)


def at(x, index, axis=0):
    return lax.dynamic_index_in_dim(x, index, axis, False)


def laid(near, far, side, axis=0):
    shape = near.shape[:axis] + (2,) + near.shape[axis:]
    out = lax.dynamic_update_index_in_dim(jnp.zeros(shape, near.dtype), near, side, axis)
    return lax.dynamic_update_index_in_dim(out, far, 1 - side, axis)


def add(near, far):
    return (near.astype(jnp.float32) + far.astype(jnp.float32)).astype(near.dtype)


def halve(x, step, axis=0):
    mesh_axis, bit, side = step
    return add(at(x, side, axis), swap(at(x, 1 - side, axis), mesh_axis, bit))


def double(x, step, axis=0):
    mesh_axis, bit, side = step
    return laid(x, swap(x, mesh_axis, bit), side, axis)


def bit_steps(mesh_axis, first=1):
    count, me = lax.axis_size(mesh_axis), lax.axis_index(mesh_axis)
    steps = []
    while first < count:
        steps.append((mesh_axis, first, (me // first) % 2))
        first *= 2
    return steps


def combine_stats(parts):
    peak = functools.reduce(jnp.maximum, [part[0] for part in parts])
    factors = [jnp.exp2(part[0] - peak) for part in parts]
    total = sum(factor * part[1] for factor, part in zip(factors, parts))
    dots = sum(factor * part[2] for factor, part in zip(factors, parts))
    return jnp.stack([peak, total, dots])


def vmem_call(kernel, name, out_shape, scratch, limit, flops, moved, args, scalars=0):
    specs = [pl.BlockSpec(memory_space=pltpu.SMEM)] * scalars
    specs += [pl.BlockSpec(memory_space=pltpu.VMEM)] * (len(args) - scalars)
    return pl.pallas_call(
        kernel,
        name=name,
        out_shape=out_shape,
        in_specs=specs,
        out_specs=[pl.BlockSpec(memory_space=pltpu.VMEM)] * len(out_shape),
        scratch_shapes=scratch,
        compiler_params=pltpu.CompilerParams(vmem_limit_bytes=limit),
        cost_estimate=pl.CostEstimate(flops=flops, bytes_accessed=moved, transcendentals=0),
    )(*args)


def on_device(ref_feats, src_feats, grad_out, w_query, w_key, w_value, w_out, intersection):
    ref_rows = ref_feats[0]
    src_rows = src_feats[0]
    out_grad = grad_out[0]
    listed = intersection[0]
    rows, width = ref_rows.shape
    core_step = bit_steps("blk")[0]
    chip_steps = bit_steps("blk", 2)
    key_rows = src_rows.shape[0]
    key_total = key_rows * lax.axis_size("blk")

    source_all = src_rows
    for count, step in enumerate(chip_steps[::-1]):
        source_all = double(source_all, step, count)
    source_all = double(source_all, core_step, len(chip_steps)).reshape(key_total, width)

    f32, b16 = jnp.float32, jnp.bfloat16
    shape, vmem = jax.ShapeDtypeStruct, pltpu.VMEM
    unit = 2 * rows * width * width
    query_blocks, steps = rows // BLOCK, key_total // STEP
    stacked = HEADS * BLOCK
    blocks = vmem((query_blocks * steps, stacked, STEP), f32)
    row_like = shape((query_blocks, stacked, 128), f32)
    col_like = vmem((steps, HEADS, 8, STEP), f32)
    row_peak, row_inverse, col_stats, left, grad_left, key_t, value_t = vmem_call(
        functools.partial(stats_kernel, HEADS),
        "match_stats",
        [
            row_like,
            row_like,
            shape((3, HEADS, key_total), f32),
            shape((query_blocks, stacked, width), b16),
            shape((query_blocks, stacked, width), b16),
            shape((width, key_total), b16),
            shape((width, key_total), b16),
        ],
        [blocks, blocks, vmem(row_like.shape, f32), col_like, col_like, col_like],
        (6 << 20) + rows * key_total * HEADS * 9,
        60 * unit,
        8 << 20,
        (listed, ref_rows, out_grad, source_all, w_query, w_key, w_value, w_out),
        scalars=1,
    )
    ref_near, grad_near, source_near, near_stats = lax.optimization_barrier(
        (ref_rows, out_grad, source_all, col_stats)
    )
    keys, values, query_t, grad_t = vmem_call(
        functools.partial(side_kernel, HEADS),
        "project_for_grads",
        [
            shape((key_total, width), b16),
            shape((key_total, width), b16),
            shape((query_blocks, width, BLOCK), b16),
            shape((query_blocks, width, BLOCK), b16),
        ],
        [],
        8 << 20,
        8 * unit,
        2 << 20,
        (ref_near, grad_near, source_near, w_query, w_key, w_value, w_out),
    )
    for mesh_axis, bit, _ in chip_steps:
        near_stats = combine_stats([near_stats, swap(near_stats, mesh_axis, bit)])
    far_stats = swap(near_stats, "blk", 1)
    attended, grad_query, grad_key, grad_value, weight_part = vmem_call(
        functools.partial(grads_kernel, HEADS),
        "match_grads",
        [
            shape((rows, width), b16),
            shape((rows, width), b16),
            shape((width, key_total), b16),
            shape((width, key_total), b16),
            shape((4, width, width), b16),
        ],
        [
            vmem((steps, stacked, STEP), f32),
            vmem((steps, stacked, STEP), f32),
            vmem((steps, stacked, STEP), b16),
            vmem((stacked, STEP), b16),
            vmem((stacked, STEP), f32),
            vmem((stacked, STEP), f32),
            vmem((stacked, 128), f32),
            vmem((3, steps, HEADS, 8, STEP), f32),
            vmem((query_blocks, BLOCK, width), f32),
            vmem((query_blocks, BLOCK, width), f32),
            vmem((steps, width, STEP), f32),
            vmem((steps, width, STEP), f32),
        ],
        (10 << 20) + BLOCK * key_total * HEADS * 20,
        100 * unit,
        8 << 20,
        (listed, left, grad_left, key_t, value_t, keys, values, query_t, grad_t, row_peak, row_inverse,
         near_stats, far_stats, ref_rows, out_grad, source_all),
        scalars=1,
    )
    matched, grad_ref, source_part = vmem_call(
        finish_kernel,
        "finish_rows",
        [
            shape((rows, width), b16),
            shape((rows, width), b16),
            shape((key_total, width), b16),
        ],
        [],
        8 << 20,
        8 * unit,
        2 << 20,
        (ref_rows, out_grad, attended, grad_query, grad_key, grad_value,
         w_query, w_key, w_value, w_out),
    )

    scan_steps = bit_steps("scan")
    weights = weight_part.reshape((2,) * (1 + len(scan_steps)) + (-1, width))
    sources = source_part.reshape((2,) * (len(chip_steps) + 1) + (key_rows, width))
    source_steps = list(zip(chip_steps, range(len(chip_steps) - 1, -1, -1)))
    weights = halve(weights, core_step)
    sources = halve(sources, core_step, len(chip_steps))
    for count, step in enumerate(scan_steps):
        weights, sources = lax.optimization_barrier((weights, sources))
        weights = halve(weights, step)
        if count == 0:
            sources = halve(sources, *source_steps.pop(0))
    for mesh_axis, bit, _ in chip_steps:
        weights = add(weights, swap(weights, mesh_axis, bit))
    for count, step in enumerate(scan_steps[::-1]):
        weights, sources = lax.optimization_barrier((weights, sources))
        weights = double(weights, step)
        if source_steps and count >= len(scan_steps) - len(source_steps):
            sources = halve(sources, *source_steps.pop(0))
    for step in source_steps:
        sources = halve(sources, *step)
    grad_src = sources
    weights = double(weights, core_step)
    weights = weights.reshape(4, width, width).astype(f32)
    return (
        matched[None],
        grad_ref[None],
        grad_src[None],
        weights[0],
        weights[1],
        weights[2],
        weights[3],
    )


def solution(mesh):
    split = P("scan", "blk", None)
    whole = P()
    return jax.shard_map(
        on_device,
        mesh=mesh,
        in_specs=(split, split, split, whole, whole, whole, whole, split),
        out_specs=(split, split, split, whole, whole, whole, whole),
        check_vma=False,
    )
```

time: 92.2 us -> 82.9 us (0.90)
  Pallas kernels: 24.9 us -> 21 us
  local copies, waits for them, and re-layouts: 6.7 us -> 2.95 us
  waiting for transfers between devices: 37 us -> 35.7 us
    pallas_call x5 -> x4, Pallas kernels: 24.9 us -> 21 us  [vmem_call(): pl.pallas_call(kernel, name=name, out_shape=out_shape, in_specs=specs, ou...]
    unnamed x22 -> x16, local copies, waits for them, and re-layouts: 4.42 us -> 1.51 us
    ppermute x17, waiting for transfers between devices: 37 us -> 35.7 us  [swap(): return lax.ppermute(x, axis, pairs)]
  transfers between devices with their start and end apart: 17 -> 17, of which waited for: 15 -> 15; matrix products, arithmetic and copies ran while one was open for 2% -> 1% of each run, Pallas kernels for 3% -> 2%
where the time goes in v8:
time: 82.9 us; the launch traced here: 82.7 us
  waiting for transfers between devices  35.7 us (43%)
  Pallas kernels  21 us (25%)
  starting transfers between devices  20.9 us (25%)
  local copies, waits for them, and re-layouts  2.95 us (4%)
  other arithmetic  1.11 us (1%)
  between operations  1.08 us (1%)
    ppermute x17, waiting for transfers between devices, swap(): return lax.ppermute(x, axis, pairs)  35.7 us
    pallas_call x4, Pallas kernels, vmem_call(): pl.pallas_call(kernel, name=name, out_shape=out_shape, in_specs=specs, ou...  21 us
    ppermute x17, starting transfers between devices, swap(): return lax.ppermute(x, axis, pairs)  20.9 us
  transfers between devices with their start and end apart: 17, of which 15 were waited for; matrix products, arithmetic and copies ran while one was open for 1% of the time, Pallas kernels for 2%

profile of v8, /device:TPU:0, one launch (start us, length us, event | category | flops | bytes accessed | tf_op | source)
XLA Modules:
  0.0 82.7 jit_solution(6882283148001713712)
XLA Ops:
  0.6 4.1 %collective-permute-start = (bf16[128,256]{1,0:T(8,128)(2,1)}, bf16[128,256]{1,0:T(8,128)(2,1)S(1)}, u32[]{:S(2)}, u32[]{:S(2)}) collective-permute-start(bf16[128,256]{1,0:T(8,128)(2,1)} %bitcast.98), channel_id=1, source_target_pairs={{0,4},{1,5},{2,6},{3,7},{4,0},{5,1},{6,2},{7,3},{8,12},{9,13},{10,... | collective-permute-start | bytes 196616 | tf_op jit(solution)/shard_map/ppermute | solution.py:316
  5.6 3.0 %collective-permute-done = bf16[128,256]{1,0:T(8,128)(2,1)S(1)} collective-permute-done((bf16[128,256]{1,0:T(8,128)(2,1)}, bf16[128,256]{1,0:T(8,128)(2,1)S(1)}, u32[]{:S(2)}, u32[]{:S(2)}) %collective-permute-start) | collective-permute-done | bytes 65568 | tf_op jit(solution)/shard_map/ppermute | solution.py:316
  9.4 4.3 %collective-permute-done.1 = bf16[2,128,256]{2,1,0:T(8,128)(2,1)S(1)} collective-permute-done((bf16[2,128,256]{2,1,0:T(8,128)(2,1)S(1)}, bf16[2,128,256]{2,1,0:T(8,128)(2,1)S(1)}, u32[]{:S(2)}, u32[]{:S(2)}) %collective-permute-start.1) | collective-permute-done | bytes 131104 | tf_op jit(solution)/shard_map/ppermute | solution.py:316
  13.9 1.4 %collective-permute-done.2 = bf16[2,2,128,256]{3,2,1,0:T(8,128)(2,1)S(1)} collective-permute-done((bf16[2,2,128,256]{3,2,1,0:T(8,128)(2,1)S(1)}, bf16[2,2,128,256]{3,2,1,0:T(8,128)(2,1)S(1)}, u32[]{:S(2)}, u32[]{:S(2)}) %collective-permute-start.2) | collective-permute-done | bytes 262176 | tf_op jit(solution)/shard_map/ppermute | solution.py:316
  16.0 8.2 %match_stats.1 = (f32[4,512,128]{2,1,0:T(8,128)S(1)}, f32[4,512,128]{2,1,0:T(8,128)S(1)}, f32[3,4,1024]{2,1,0:T(4,128)S(1)}, bf16[4,512,256]{2,1,0:T(8,128)(2,1)...) custom-call(s32[4,8]{1,0:T(4,128)S(1)} %bitcast.94, ...), custom_call_target="tpu_custom_call" | custom-call | flops 4026531840 | bytes 8388608 | tf_op jit(solution)/shard_map/match_stats/pallas_call | solution.py:363
  24.4 3.9 %collective-permute-done.3 = f32[3,4,1024]{2,1,0:T(4,128)S(1)} collective-permute-done((f32[3,4,1024]{2,1,0:T(4,128)S(1)}, f32[3,4,1024]{2,1,0:T(4,128)S(1)}, u32[]{:S(2)}, u32[]{:S(2)}) %collective-permute-start.3) | collective-permute-done | bytes 49184 | tf_op jit(solution)/shard_map/ppermute | solution.py:316
  28.4 1.5 %collective-permute-start.4 = (f32[3,4,1024]{2,1,0:T(4,128)S(1)}, f32[3,4,1024]{2,1,0:T(4,128)S(1)}, u32[]{:S(2)}, u32[]{:S(2)}) collective-permute-start(f32[3,4,1024]{2,1,0:T(4,128)S(1)} %pad_maximum_fusion), channel_id=1, source_target_pairs={{0,4},{1,5},{2,6},{3,7},{4,0},{5,1},{6,2},{7,3},{8,12},{9,13},{10,... | collective-permute-start | bytes 147464 | tf_op jit(solution)/shard_map/ppermute | solution.py:316
  29.9 3.8 %collective-permute-done.4 = f32[3,4,1024]{2,1,0:T(4,128)S(1)} collective-permute-done((f32[3,4,1024]{2,1,0:T(4,128)S(1)}, f32[3,4,1024]{2,1,0:T(4,128)S(1)}, u32[]{:S(2)}, u32[]{:S(2)}) %collective-permute-start.4) | collective-permute-done | bytes 49184 | tf_op jit(solution)/shard_map/ppermute | solution.py:316
  35.1 10.8 %match_grads.1 = (bf16[512,256]{1,0:T(8,128)(2,1)S(1)}, bf16[512,256]{1,0:T(8,128)(2,1)S(1)}, bf16[256,1024]{1,0:T(8,128)(2,1)S(1)}, bf16[256,1024]{1,0:T(8,128)(2,1)S(1)}, bf16[4,256,256]{2,1,0:T(8,128)(2,1)S(1)}) custom-call(s32[4,8]{1,0:T(4,128)S(1)} %bitcast.95, bf16[4,512,256]{2,1,0:T(8,128)(2,1)S(1)} %get-tuple-element.38.left_ref, ...), custom_call_target="tpu_custom_call" | custom-call | flops 6710886400 | bytes 8388608 | tf_op jit(solution)/shard_map/match_grads/pallas_call | solution.py:363
  46.1 1.4 %finish_rows.1 = (bf16[512,256]{1,0:T(8,128)(2,1)}, bf16[512,256]{1,0:T(8,128)(2,1)}, bf16[1024,256]{1,0:T(8,128)(2,1)S(1)}) custom-call(bf16[512,256]{1,0:T(8,128)(2,1)S(1)} %bitcast.89, bf16[512,256]{1,0:T(8,128)(2,1)S(1)} %bitcast.93, bf16[512,256]{1,0:T(8,128)(2,1)S(1)} %get-tuple-element.53.attended_ref, ...), custom_call_target="tpu_custom_call" | custom-call | flops 536870912 | bytes 2097152 | tf_op jit(solution)/shard_map/finish_rows/pallas_call | solution.py:363
  48.1 1.1 %collective-permute-done.7 = bf16[2,2,128,256]{3,2,0,1:T(8,128)(2,1)S(1)} collective-permute-done((bf16[2,2,128,256]{3,2,0,1:T(8,128)(2,1)S(1)}, bf16[2,2,128,256]{3,2,0,1:T(8,128)(2,1)S(1)}, u32[]{:S(2)}, u32[]{:S(2)}) %collective-permute-start.7) | collective-permute-done | bytes 262176 | tf_op jit(solution)/shard_map/ppermute | solution.py:316
  50.2 4.9 %collective-permute-done.9 = bf16[2,128,256]{2,1,0:T(8,128)(2,1)S(1)} collective-permute-done((bf16[2,128,256]{2,1,0:T(8,128)(2,1)S(1)}, bf16[2,128,256]{2,1,0:T(8,128)(2,1)S(1)}, u32[]{:S(2)}, u32[]{:S(2)}) %collective-permute-start.9) | collective-permute-done | bytes 131104 | tf_op jit(solution)/shard_map/ppermute | solution.py:316
  55.4 2.3 %collective-permute-start.10 = (bf16[128,256]{1,0:T(8,128)(2,1)S(1)}, bf16[128,256]{1,0:T(8,128)(2,1)S(1)}, u32[]{:S(2)}, u32[]{:S(2)}) collective-permute-start(bf16[128,256]{1,0:T(8,128)(2,1)S(1)} %dynamic-slice_bitcast_fusion.4), channel_id=1, source_target_pairs={{0,16},{8,24},{16,0},{24,8},{1,17},{9,25},{17,1},{25,9},{2,18},{10... | collective-permute-start | bytes 196616 | tf_op jit(solution)/shard_map/ppermute | solution.py:316
  57.7 2.2 %collective-permute-done.10 = bf16[128,256]{1,0:T(8,128)(2,1)S(1)} collective-permute-done((bf16[128,256]{1,0:T(8,128)(2,1)S(1)}, bf16[128,256]{1,0:T(8,128)(2,1)S(1)}, u32[]{:S(2)}, u32[]{:S(2)}) %collective-permute-start.10) | collective-permute-done | bytes 65568 | tf_op jit(solution)/shard_map/ppermute | solution.py:316
  60.0 1.7 %collective-permute-start.11 = (bf16[128,256]{1,0:T(8,128)(2,1)S(1)}, bf16[128,256]{1,0:T(8,128)(2,1)S(1)}, u32[]{:S(2)}, u32[]{:S(2)}) collective-permute-start(bf16[128,256]{1,0:T(8,128)(2,1)S(1)} %fusion.5), channel_id=1, source_target_pairs={{0,2},{1,3},{2,0},{3,1},{4,6},{5,7},{6,4},{7,5},{8,10},{9,11},{10,... | collective-permute-start | bytes 196616 | tf_op jit(solution)/shard_map/ppermute | solution.py:316
  61.7 2.6 %collective-permute-done.11 = bf16[128,256]{1,0:T(8,128)(2,1)S(1)} collective-permute-done((bf16[128,256]{1,0:T(8,128)(2,1)S(1)}, bf16[128,256]{1,0:T(8,128)(2,1)S(1)}, u32[]{:S(2)}, u32[]{:S(2)}) %collective-permute-start.11) | collective-permute-done | bytes 65568 | tf_op jit(solution)/shard_map/ppermute | solution.py:316
  64.3 2.6 %collective-permute-start.12 = (bf16[128,256]{1,0:T(8,128)(2,1)S(1)}, bf16[128,256]{1,0:T(8,128)(2,1)S(1)}, u32[]{:S(2)}, u32[]{:S(2)}) collective-permute-start(bf16[128,256]{1,0:T(8,128)(2,1)S(1)} %add_convert_fusion.1), channel_id=1, source_target_pairs={{0,4},{1,5},{2,6},{3,7},{4,0},{5,1},{6,2},{7,3},{8,12},{9,13},{10,... | collective-permute-start | bytes 196616 | tf_op jit(solution)/shard_map/ppermute | solution.py:316
  66.9 2.6 %collective-permute-done.12 = bf16[128,256]{1,0:T(8,128)(2,1)S(1)} collective-permute-done((bf16[128,256]{1,0:T(8,128)(2,1)S(1)}, bf16[128,256]{1,0:T(8,128)(2,1)S(1)}, u32[]{:S(2)}, u32[]{:S(2)}) %collective-permute-start.12) | collective-permute-done | bytes 65568 | tf_op jit(solution)/shard_map/ppermute | solution.py:316
  69.6 2.1 %collective-permute-start.13 = (bf16[128,256]{1,0:T(8,128)(2,1)S(1)}, bf16[128,256]{1,0:T(8,128)(2,1)S(1)}, u32[]{:S(2)}, u32[]{:S(2)}) collective-permute-start(bf16[128,256]{1,0:T(8,128)(2,1)S(1)} %add_convert_fusion), channel_id=1, source_target_pairs={{0,16},{8,24},{16,0},{24,8},{1,17},{9,25},{17,1},{25,9},{2,18},{10... | collective-permute-start | bytes 196616 | tf_op jit(solution)/shard_map/ppermute | solution.py:316
  71.7 2.2 %collective-permute-done.13 = bf16[128,256]{1,0:T(8,128)(2,1)S(1)} collective-permute-done((bf16[128,256]{1,0:T(8,128)(2,1)S(1)}, bf16[128,256]{1,0:T(8,128)(2,1)S(1)}, u32[]{:S(2)}, u32[]{:S(2)}) %collective-permute-start.13) | collective-permute-done | bytes 65568 | tf_op jit(solution)/shard_map/ppermute | solution.py:316
  73.9 1.8 %collective-permute-start.15 = (bf16[2,128,256]{2,1,0:T(8,128)(2,1)S(1)}, bf16[2,128,256]{2,1,0:T(8,128)(2,1)S(1)}, u32[]{:S(2)}, u32[]{:S(2)}) collective-permute-start(bf16[2,128,256]{2,1,0:T(8,128)(2,1)S(1)} %bitcast_dynamic-update-slice_fusion.8), channel_id=1, source_target_pairs={{0,8},{8,0},{16,24},{24,16},{1,9},{9,1},{17,25},{25,17},{2,10},{10... | collective-permute-start | bytes 393224 | tf_op jit(solution)/shard_map/ppermute | solution.py:316
  75.7 2.1 %collective-permute-start.14 = (bf16[128,256]{1,0:T(8,128)(2,1)S(1)}, bf16[128,256]{1,0:T(8,128)(2,1)S(1)}, u32[]{:S(2)}, u32[]{:S(2)}) collective-permute-start(bf16[128,256]{1,0:T(8,128)(2,1)S(1)} %dynamic-slice_bitcast_fusion.3), channel_id=1, source_target_pairs={{0,4},{1,5},{2,6},{3,7},{4,0},{5,1},{6,2},{7,3},{8,12},{9,13},{10,... | collective-permute-start | bytes 196616 | tf_op jit(solution)/shard_map/ppermute | solution.py:316
  77.9 1.1 %collective-permute-done.15 = bf16[2,128,256]{2,1,0:T(8,128)(2,1)S(1)} collective-permute-done((bf16[2,128,256]{2,1,0:T(8,128)(2,1)S(1)}, bf16[2,128,256]{2,1,0:T(8,128)(2,1)S(1)}, u32[]{:S(2)}, u32[]{:S(2)}) %collective-permute-start.15) | collective-permute-done | bytes 131104 | tf_op jit(solution)/shard_map/ppermute | solution.py:316
  79.0 1.8 %collective-permute-done.14 = bf16[128,256]{1,0:T(8,128)(2,1)S(1)} collective-permute-done((bf16[128,256]{1,0:T(8,128)(2,1)S(1)}, bf16[128,256]{1,0:T(8,128)(2,1)S(1)}, u32[]{:S(2)}, u32[]{:S(2)}) %collective-permute-start.14) | collective-permute-done | bytes 65568 | tf_op jit(solution)/shard_map/ppermute | solution.py:316
  (70 shorter events, 8.0 us)
Async XLA Ops:
  0.6 8.0 %collective-permute-start = (bf16[128,256]{1,0:T(8,128)(2,1)}, bf16[128,256]{1,0:T(8,128)(2,1)S(1)}, u32[]{:S(2)}, u32[]{:S(2)}) collective-permute-start(bf16[128,256]{1,0:T(8,128)(2,1)} %bitcast.98), channel_id=1, source_target_pairs={{0,4},{1,5},{2,6},{3,7},{4,0},{5,1},{6,2},{7,3},{8,12},{9,13},{10,... | collective-permute-start | bytes 196616 | tf_op jit(solution)/shard_map/ppermute | solution.py:316
  4.7 0.9 %copy-start.7 = (bf16[1,128,256]{2,1,0:T(8,128)(2,1)S(1)}, bf16[1,128,256]{2,1,0:T(8,128)(2,1)}, u32[]{:S(2)}) copy-start(bf16[1,128,256]{2,1,0:T(8,128)(2,1)} %param.9) | copy-start | bytes 196612
  8.6 5.0 %collective-permute-start.1 = (bf16[2,128,256]{2,1,0:T(8,128)(2,1)S(1)}, bf16[2,128,256]{2,1,0:T(8,128)(2,1)S(1)}, u32[]{:S(2)}, u32[]{:S(2)}) collective-permute-start(bf16[2,128,256]{2,1,0:T(8,128)(2,1)S(1)} %bitcast_dynamic-update-slice_fusion.10), channel_id=1, source_target_pairs={{0,2},{1,3},{2,0},{3,1},{4,6},{5,7},{6,4},{7,5},{8,10},{9,11},{10,... | collective-permute-start | bytes 393224 | tf_op jit(solution)/shard_map/ppermute | solution.py:316
  13.7 1.6 %collective-permute-start.2 = (bf16[2,2,128,256]{3,2,1,0:T(8,128)(2,1)S(1)}, bf16[2,2,128,256]{3,2,1,0:T(8,128)(2,1)S(1)}, u32[]{:S(2)}, u32[]{:S(2)}) collective-permute-start(bf16[2,2,128,256]{3,2,1,0:T(8,128)(2,1)S(1)} %bitcast_dynamic-update-slice_fusion.7), channel_id=1, source_target_pairs={{0,1},{1,0},{2,3},{3,2},{4,5},{5,4},{6,7},{7,6},{8,9},{9,8},{10,11... | collective-permute-start | bytes 786440 | tf_op jit(solution)/shard_map/ppermute | solution.py:316
  13.8 1.5 %copy-start.2 = (bf16[256,256]{1,0:T(8,128)(2,1)S(1)}, bf16[256,256]{1,0:T(8,128)(2,1)}, u32[]{:S(2)}) copy-start(bf16[256,256]{1,0:T(8,128)(2,1)} %wq_ref.5) | copy-start | bytes 393220
  13.8 1.5 %copy-start.3 = (bf16[256,256]{1,0:T(8,128)(2,1)S(1)}, bf16[256,256]{1,0:T(8,128)(2,1)}, u32[]{:S(2)}) copy-start(bf16[256,256]{1,0:T(8,128)(2,1)} %wk_ref.5) | copy-start | bytes 393220
  13.8 1.5 %copy-start.4 = (bf16[256,256]{1,0:T(8,128)(2,1)S(1)}, bf16[256,256]{1,0:T(8,128)(2,1)}, u32[]{:S(2)}) copy-start(bf16[256,256]{1,0:T(8,128)(2,1)} %wv_ref.5) | copy-start | bytes 393220
  13.8 1.5 %copy-start.5 = (bf16[256,256]{1,0:T(8,128)(2,1)S(1)}, bf16[256,256]{1,0:T(8,128)(2,1)}, u32[]{:S(2)}) copy-start(bf16[256,256]{1,0:T(8,128)(2,1)} %wo_ref.5) | copy-start | bytes 393220
  13.9 1.5 %copy-start = (bf16[1,512,256]{2,1,0:T(8,128)(2,1)S(1)}, bf16[1,512,256]{2,1,0:T(8,128)(2,1)}, u32[]{:S(2)}) copy-start(bf16[1,512,256]{2,1,0:T(8,128)(2,1)} %param.8) | copy-start | bytes 786436
  13.9 1.5 %copy-start.1 = (bf16[1,512,256]{2,1,0:T(8,128)(2,1)S(1)}, bf16[1,512,256]{2,1,0:T(8,128)(2,1)}, u32[]{:S(2)}) copy-start(bf16[1,512,256]{2,1,0:T(8,128)(2,1)} %param.10) | copy-start | bytes 786436
  24.2 4.2 %collective-permute-start.3 = (f32[3,4,1024]{2,1,0:T(4,128)S(1)}, f32[3,4,1024]{2,1,0:T(4,128)S(1)}, u32[]{:S(2)}, u32[]{:S(2)}) collective-permute-start(f32[3,4,1024]{2,1,0:T(4,128)S(1)} %get-tuple-element.52), channel_id=1, source_target_pairs={{0,2},{1,3},{2,0},{3,1},{4,6},{5,7},{6,4},{7,5},{8,10},{9,11},{10,... | collective-permute-start | bytes 147464 | tf_op jit(solution)/shard_map/ppermute | solution.py:316
  28.4 5.4 %collective-permute-start.4 = (f32[3,4,1024]{2,1,0:T(4,128)S(1)}, f32[3,4,1024]{2,1,0:T(4,128)S(1)}, u32[]{:S(2)}, u32[]{:S(2)}) collective-permute-start(f32[3,4,1024]{2,1,0:T(4,128)S(1)} %pad_maximum_fusion), channel_id=1, source_target_pairs={{0,4},{1,5},{2,6},{3,7},{4,0},{5,1},{6,2},{7,3},{8,12},{9,13},{10,... | collective-permute-start | bytes 147464 | tf_op jit(solution)/shard_map/ppermute | solution.py:316
  33.8 1.3 %collective-permute-start.5 = (f32[3,4,1024]{2,1,0:T(4,128)S(1)}, f32[3,4,1024]{2,1,0:T(4,128)S(1)}, u32[]{:S(2)}, u32[]{:S(2)}) collective-permute-start(f32[3,4,1024]{2,1,0:T(4,128)S(1)} %pad_maximum_fusion.1.near_ref), channel_id=1, source_target_pairs={{0,1},{1,0},{2,3},{3,2},{4,5},{5,4},{6,7},{7,6},{8,9},{9,8},{10,11... | collective-permute-start | bytes 147464 | tf_op jit(solution)/shard_map/ppermute | solution.py:316
  46.0 2.1 %collective-permute-start.6 = (bf16[2,2,128,256]{3,2,1,0:T(8,128)(2,1)S(1)}, bf16[2,2,128,256]{3,2,1,0:T(8,128)(2,1)S(1)}, u32[]{:S(2)}, u32[]{:S(2)}) collective-permute-start(bf16[2,2,128,256]{3,2,1,0:T(8,128)(2,1)S(1)} %dynamic-slice_bitcast_fusion), channel_id=1, source_target_pairs={{0,1},{1,0},{2,3},{3,2},{4,5},{5,4},{6,7},{7,6},{8,9},{9,8},{10,11... | collective-permute-start | bytes 786440 | tf_op jit(solution)/shard_map/ppermute | solution.py:316
  47.5 1.7 %collective-permute-start.7 = (bf16[2,2,128,256]{3,2,0,1:T(8,128)(2,1)S(1)}, bf16[2,2,128,256]{3,2,0,1:T(8,128)(2,1)S(1)}, u32[]{:S(2)}, u32[]{:S(2)}) collective-permute-start(bf16[2,2,128,256]{3,2,0,1:T(8,128)(2,1)S(1)} %bitcast.97), channel_id=1, source_target_pairs={{0,1},{1,0},{2,3},{3,2},{4,5},{5,4},{6,7},{7,6},{8,9},{9,8},{10,11... | collective-permute-start | bytes 786440 | tf_op jit(solution)/shard_map/ppermute | solution.py:316
  49.3 5.8 %collective-permute-start.9 = (bf16[2,128,256]{2,1,0:T(8,128)(2,1)S(1)}, bf16[2,128,256]{2,1,0:T(8,128)(2,1)S(1)}, u32[]{:S(2)}, u32[]{:S(2)}) collective-permute-start(bf16[2,128,256]{2,1,0:T(8,128)(2,1)S(1)} %dynamic-slice_bitcast_fusion.1), channel_id=1, source_target_pairs={{0,2},{1,3},{2,0},{3,1},{4,6},{5,7},{6,4},{7,5},{8,10},{9,11},{10,... | collective-permute-start | bytes 393224 | tf_op jit(solution)/shard_map/ppermute | solution.py:316
  49.5 5.8 %collective-permute-start.8 = (bf16[2,128,256]{2,1,0:T(8,128)(2,1)S(1)}, bf16[2,128,256]{2,1,0:T(8,128)(2,1)S(1)}, u32[]{:S(2)}, u32[]{:S(2)}) collective-permute-start(bf16[2,128,256]{2,1,0:T(8,128)(2,1)S(1)} %dynamic-slice_bitcast_fusion.2), channel_id=1, source_target_pairs={{0,8},{8,0},{16,24},{24,16},{1,9},{9,1},{17,25},{25,17},{2,10},{10... | collective-permute-start | bytes 393224 | tf_op jit(solution)/shard_map/ppermute | solution.py:316
  55.4 4.6 %collective-permute-start.10 = (bf16[128,256]{1,0:T(8,128)(2,1)S(1)}, bf16[128,256]{1,0:T(8,128)(2,1)S(1)}, u32[]{:S(2)}, u32[]{:S(2)}) collective-permute-start(bf16[128,256]{1,0:T(8,128)(2,1)S(1)} %dynamic-slice_bitcast_fusion.4), channel_id=1, source_target_pairs={{0,16},{8,24},{16,0},{24,8},{1,17},{9,25},{17,1},{25,9},{2,18},{10... | collective-permute-start | bytes 196616 | tf_op jit(solution)/shard_map/ppermute | solution.py:316
  60.0 4.3 %collective-permute-start.11 = (bf16[128,256]{1,0:T(8,128)(2,1)S(1)}, bf16[128,256]{1,0:T(8,128)(2,1)S(1)}, u32[]{:S(2)}, u32[]{:S(2)}) collective-permute-start(bf16[128,256]{1,0:T(8,128)(2,1)S(1)} %fusion.5), channel_id=1, source_target_pairs={{0,2},{1,3},{2,0},{3,1},{4,6},{5,7},{6,4},{7,5},{8,10},{9,11},{10,... | collective-permute-start | bytes 196616 | tf_op jit(solution)/shard_map/ppermute | solution.py:316
  64.3 5.2 %collective-permute-start.12 = (bf16[128,256]{1,0:T(8,128)(2,1)S(1)}, bf16[128,256]{1,0:T(8,128)(2,1)S(1)}, u32[]{:S(2)}, u32[]{:S(2)}) collective-permute-start(bf16[128,256]{1,0:T(8,128)(2,1)S(1)} %add_convert_fusion.1), channel_id=1, source_target_pairs={{0,4},{1,5},{2,6},{3,7},{4,0},{5,1},{6,2},{7,3},{8,12},{9,13},{10,... | collective-permute-start | bytes 196616 | tf_op jit(solution)/shard_map/ppermute | solution.py:316
  69.6 4.3 %collective-permute-start.13 = (bf16[128,256]{1,0:T(8,128)(2,1)S(1)}, bf16[128,256]{1,0:T(8,128)(2,1)S(1)}, u32[]{:S(2)}, u32[]{:S(2)}) collective-permute-start(bf16[128,256]{1,0:T(8,128)(2,1)S(1)} %add_convert_fusion), channel_id=1, source_target_pairs={{0,16},{8,24},{16,0},{24,8},{1,17},{9,25},{17,1},{25,9},{2,18},{10... | collective-permute-start | bytes 196616 | tf_op jit(solution)/shard_map/ppermute | solution.py:316
  73.9 5.0 %collective-permute-start.15 = (bf16[2,128,256]{2,1,0:T(8,128)(2,1)S(1)}, bf16[2,128,256]{2,1,0:T(8,128)(2,1)S(1)}, u32[]{:S(2)}, u32[]{:S(2)}) collective-permute-start(bf16[2,128,256]{2,1,0:T(8,128)(2,1)S(1)} %bitcast_dynamic-update-slice_fusion.8), channel_id=1, source_target_pairs={{0,8},{8,0},{16,24},{24,16},{1,9},{9,1},{17,25},{25,17},{2,10},{10... | collective-permute-start | bytes 393224 | tf_op jit(solution)/shard_map/ppermute | solution.py:316
  75.7 5.2 %collective-permute-start.14 = (bf16[128,256]{1,0:T(8,128)(2,1)S(1)}, bf16[128,256]{1,0:T(8,128)(2,1)S(1)}, u32[]{:S(2)}, u32[]{:S(2)}) collective-permute-start(bf16[128,256]{1,0:T(8,128)(2,1)S(1)} %dynamic-slice_bitcast_fusion.3), channel_id=1, source_target_pairs={{0,4},{1,5},{2,6},{3,7},{4,0},{5,1},{6,2},{7,3},{8,12},{9,13},{10,... | collective-permute-start | bytes 196616 | tf_op jit(solution)/shard_map/ppermute | solution.py:316
  79.0 2.6 %collective-permute-start.16 = (bf16[2,2,128,256]{3,2,1,0:T(8,128)(2,1)S(1)}, bf16[2,2,128,256]{3,2,1,0:T(8,128)(2,1)S(1)}, u32[]{:S(2)}, u32[]{:S(2)}) collective-permute-start(bf16[2,2,128,256]{3,2,1,0:T(8,128)(2,1)S(1)} %bitcast_dynamic-update-slice_fusion.5), channel_id=1, source_target_pairs={{0,1},{1,0},{2,3},{3,2},{4,5},{5,4},{6,7},{7,6},{8,9},{9,8},{10,11... | collective-permute-start | bytes 786440 | tf_op jit(solution)/shard_map/ppermute | solution.py:316
  (1 other events, 0.7 us)

commit v9 on v8

--- a/solution.py
+++ b/solution.py
@@ -340,13 +340,10 @@
     return laid(x, swap(x, mesh_axis, bit), side, axis)
 
 
-def bit_steps(mesh_axis, first=1):
-    count, me = lax.axis_size(mesh_axis), lax.axis_index(mesh_axis)
-    steps = []
-    while first < count:
-        steps.append((mesh_axis, first, (me // first) % 2))
-        first *= 2
-    return steps
+def bit_steps(mesh_axis):
+    me = lax.axis_index(mesh_axis)
+    bits = range(lax.axis_size(mesh_axis).bit_length() - 1)
+    return [(mesh_axis, 1 << bit, (me >> bit) % 2) for bit in bits]
 
 
 def combine_stats(parts):
@@ -378,10 +375,10 @@
     out_grad = grad_out[0]
     listed = intersection[0]
     rows, width = ref_rows.shape
-    core_step = bit_steps("blk")[0]
-    chip_steps = bit_steps("blk", 2)
+    core_step = bit_steps("core")[0]
+    chip_steps = bit_steps("chip")
     key_rows = src_rows.shape[0]
-    key_total = key_rows * lax.axis_size("blk")
+    key_total = key_rows * lax.axis_size("chip") * lax.axis_size("core")
 
     source_all = src_rows
     for count, step in enumerate(chip_steps[::-1]):
@@ -435,7 +432,7 @@
     )
     for mesh_axis, bit, _ in chip_steps:
         near_stats = combine_stats([near_stats, swap(near_stats, mesh_axis, bit)])
-    far_stats = swap(near_stats, "blk", 1)
+    far_stats = swap(near_stats, "core", 1)
     attended, grad_query, grad_key, grad_value, weight_part = vmem_call(
         functools.partial(grads_kernel, HEADS),
         "match_grads",
@@ -483,25 +480,19 @@
          w_query, w_key, w_value, w_out),
     )
 
-    scan_steps = bit_steps("scan")
-    weights = weight_part.reshape((2,) * (1 + len(scan_steps)) + (-1, width))
+    peers = ("scan", "chip")
+    count = lax.axis_size("scan") * lax.axis_size("chip")
+    weights = weight_part.reshape((2, count, -1, width))
     sources = source_part.reshape((2,) * (len(chip_steps) + 1) + (key_rows, width))
     source_steps = list(zip(chip_steps, range(len(chip_steps) - 1, -1, -1)))
     weights = halve(weights, core_step)
     sources = halve(sources, core_step, len(chip_steps))
-    for count, step in enumerate(scan_steps):
-        weights, sources = lax.optimization_barrier((weights, sources))
-        weights = halve(weights, step)
-        if count == 0:
-            sources = halve(sources, *source_steps.pop(0))
-    for mesh_axis, bit, _ in chip_steps:
-        weights = add(weights, swap(weights, mesh_axis, bit))
-    for count, step in enumerate(scan_steps[::-1]):
-        weights, sources = lax.optimization_barrier((weights, sources))
-        weights = double(weights, step)
-        if source_steps and count >= len(scan_steps) - len(source_steps):
-            sources = halve(sources, *source_steps.pop(0))
-    for step in source_steps:
+    weights, sources = lax.optimization_barrier((weights, sources))
+    weights = lax.all_to_all(weights, peers, 0, 0).astype(f32).sum(axis=0).astype(b16)
+    sources = halve(sources, *source_steps[0])
+    weights, sources = lax.optimization_barrier((weights, sources))
+    weights = lax.all_to_all(jnp.broadcast_to(weights, (count,) + weights.shape), peers, 0, 0)
+    for step in source_steps[1:]:
         sources = halve(sources, *step)
     grad_src = sources
     weights = double(weights, core_step)
@@ -518,7 +509,11 @@
 
 
 def solution(mesh):
-    split = P("scan", "blk", None)
+    scans, blks = mesh.shape["scan"], mesh.shape["blk"]
+    mesh = jax.sharding.Mesh(
+        mesh.devices.reshape(scans, blks // 2, 2), ("scan", "chip", "core")
+    )
+    split = P("scan", ("chip", "core"), None)
     whole = P()
     return jax.shard_map(
         on_device,

time: 82.9 us -> 87.4 us (1.054); the launches traced: 82.7 us -> 86.1 us
  starting transfers between devices: 20.9 us -> 23.2 us
    ppermute x17 -> x11, waiting for transfers between devices: 35.7 us -> 25.1 us  [swap(): return lax.ppermute(x, axis, pairs)]
    all_to_all x0 -> x2, waiting for transfers between devices: none -> 10.5 us  [the longest x1 9.45 us: on_device(): lax.all_to_all(jnp.broadcast_to(weights, (count,) + weights.shape), peers...]
    all_to_all x0 -> x2, starting transfers between devices: none -> 10.4 us  [the longest x1 5.94 us: on_device(): lax.all_to_all(weights, peers, 0, 0).astype(f32).sum(axis=0).astype(b16)]
    ppermute x17 -> x11, starting transfers between devices: 20.9 us -> 12.8 us  [swap(): return lax.ppermute(x, axis, pairs)]
  transfers between devices with their start and end apart: 17 -> 13, of which waited for: 15 -> 11; matrix products, arithmetic and copies ran while one was open for 1% -> 2% of each run, Pallas kernels for 2% -> 2%
where the time goes in v9:
time: 87.4 us; the launch traced here: 86.1 us
  waiting for transfers between devices  35.6 us (41%)
  starting transfers between devices  23.2 us (27%)
  Pallas kernels  21 us (24%)
  local copies, waits for them, and re-layouts  3.59 us (4%)
  other arithmetic  1.77 us (2%)
  between operations  0.97 us (1%)
    ppermute x11, waiting for transfers between devices, swap(): return lax.ppermute(x, axis, pairs)  25.1 us
    pallas_call x4, Pallas kernels, vmem_call(): pl.pallas_call(kernel, name=name, out_shape=out_shape, in_specs=specs, ou...  21 us
    ppermute x11, starting transfers between devices, swap(): return lax.ppermute(x, axis, pairs)  12.8 us
    all_to_all x1, waiting for transfers between devices, on_device(): lax.all_to_all(jnp.broadcast_to(weights, (count,) + weights.shape), peers...  9.45 us
    all_to_all x1, starting transfers between devices, on_device(): lax.all_to_all(weights, peers, 0, 0).astype(f32).sum(axis=0).astype(b16)  5.94 us
    all_to_all x1, starting transfers between devices, on_device(): lax.all_to_all(jnp.broadcast_to(weights, (count,) + weights.shape), peers...  4.47 us
  transfers between devices with their start and end apart: 13, of which 11 were waited for; matrix products, arithmetic and copies ran while one was open for 2% of the time, Pallas kernels for 2%

profile of v9, /device:TPU:0, one launch (start us, length us, event | category | flops | bytes accessed | tf_op | source)
XLA Modules:
  0.0 86.1 jit_solution(1136544521701898777)
XLA Ops:
  0.6 4.1 %collective-permute-start = (bf16[128,256]{1,0:T(8,128)(2,1)}, bf16[128,256]{1,0:T(8,128)(2,1)S(1)}, u32[]{:S(2)}, u32[]{:S(2)}) collective-permute-start(bf16[128,256]{1,0:T(8,128)(2,1)} %bitcast.80), channel_id=1, source_target_pairs={{0,4},{2,6},{4,0},{6,2},{1,5},{3,7},{5,1},{7,3},{8,12},{10,14},{12... | collective-permute-start | bytes 196616 | tf_op jit(solution)/shard_map/ppermute | solution.py:316
  4.7 0.9 copy-done.7
  5.6 3.0 %collective-permute-done = bf16[128,256]{1,0:T(8,128)(2,1)S(1)} collective-permute-done((bf16[128,256]{1,0:T(8,128)(2,1)}, bf16[128,256]{1,0:T(8,128)(2,1)S(1)}, u32[]{:S(2)}, u32[]{:S(2)}) %collective-permute-start) | collective-permute-done | bytes 65568 | tf_op jit(solution)/shard_map/ppermute | solution.py:316
  8.6 0.7 collective-permute-start.1
  9.4 4.3 %collective-permute-done.1 = bf16[2,128,256]{2,1,0:T(8,128)(2,1)S(1)} collective-permute-done((bf16[2,128,256]{2,1,0:T(8,128)(2,1)S(1)}, bf16[2,128,256]{2,1,0:T(8,128)(2,1)S(1)}, u32[]{:S(2)}, u32[]{:S(2)}) %collective-permute-start.1) | collective-permute-done | bytes 131104 | tf_op jit(solution)/shard_map/ppermute | solution.py:316
  13.9 1.4 %collective-permute-done.2 = bf16[2,2,128,256]{3,2,1,0:T(8,128)(2,1)S(1)} collective-permute-done((bf16[2,2,128,256]{3,2,1,0:T(8,128)(2,1)S(1)}, bf16[2,2,128,256]{3,2,1,0:T(8,128)(2,1)S(1)}, u32[]{:S(2)}, u32[]{:S(2)}) %collective-permute-start.2) | collective-permute-done | bytes 262176 | tf_op jit(solution)/shard_map/ppermute | solution.py:316
  16.0 8.2 %match_stats.1 = (f32[4,512,128]{2,1,0:T(8,128)S(1)}, f32[4,512,128]{2,1,0:T(8,128)S(1)}, f32[3,4,1024]{2,1,0:T(4,128)S(1)}, bf16[4,512,256]{2,1,0:T(8,128)(2,1)...) custom-call(s32[4,8]{1,0:T(4,128)S(1)} %bitcast.76, ...), custom_call_target="tpu_custom_call" | custom-call | flops 4026531840 | bytes 8388608 | tf_op jit(solution)/shard_map/match_stats/pallas_call | solution.py:360
  24.4 4.0 %collective-permute-done.3 = f32[3,4,1024]{2,1,0:T(4,128)S(1)} collective-permute-done((f32[3,4,1024]{2,1,0:T(4,128)S(1)}, f32[3,4,1024]{2,1,0:T(4,128)S(1)}, u32[]{:S(2)}, u32[]{:S(2)}) %collective-permute-start.3) | collective-permute-done | bytes 49184 | tf_op jit(solution)/shard_map/ppermute | solution.py:316
  28.4 2.1 %collective-permute-start.4 = (f32[3,4,1024]{2,1,0:T(4,128)S(1)}, f32[3,4,1024]{2,1,0:T(4,128)S(1)}, u32[]{:S(2)}, u32[]{:S(2)}) collective-permute-start(f32[3,4,1024]{2,1,0:T(4,128)S(1)} %pad_maximum_fusion), channel_id=1, source_target_pairs={{0,4},{2,6},{4,0},{6,2},{1,5},{3,7},{5,1},{7,3},{8,12},{10,14},{12... | collective-permute-start | bytes 147464 | tf_op jit(solution)/shard_map/ppermute | solution.py:316
  30.5 2.9 %collective-permute-done.4 = f32[3,4,1024]{2,1,0:T(4,128)S(1)} collective-permute-done((f32[3,4,1024]{2,1,0:T(4,128)S(1)}, f32[3,4,1024]{2,1,0:T(4,128)S(1)}, u32[]{:S(2)}, u32[]{:S(2)}) %collective-permute-start.4) | collective-permute-done | bytes 49184 | tf_op jit(solution)/shard_map/ppermute | solution.py:316
  34.8 10.8 %match_grads.1 = (bf16[512,256]{1,0:T(8,128)(2,1)S(1)}, bf16[512,256]{1,0:T(8,128)(2,1)S(1)}, bf16[256,1024]{1,0:T(8,128)(2,1)S(1)}, bf16[256,1024]{1,0:T(8,128)(2,1)S(1)}, bf16[4,256,256]{2,1,0:T(8,128)(2,1)S(1)}) custom-call(s32[4,8]{1,0:T(4,128)S(1)} %bitcast.77, bf16[4,512,256]{2,1,0:T(8,128)(2,1)S(1)} %get-tuple-element.34.left_ref, ...), custom_call_target="tpu_custom_call" | custom-call | flops 6710886400 | bytes 8388608 | tf_op jit(solution)/shard_map/match_grads/pallas_call | solution.py:360
  45.8 1.4 %finish_rows.1 = (bf16[512,256]{1,0:T(8,128)(2,1)}, bf16[512,256]{1,0:T(8,128)(2,1)}, bf16[1024,256]{1,0:T(8,128)(2,1)S(1)}) custom-call(bf16[512,256]{1,0:T(8,128)(2,1)S(1)} %bitcast.71, bf16[512,256]{1,0:T(8,128)(2,1)S(1)} %bitcast.75, bf16[512,256]{1,0:T(8,128)(2,1)S(1)} %get-tuple-element.49.attended_ref, ...), custom_call_target="tpu_custom_call" | custom-call | flops 536870912 | bytes 2097152 | tf_op jit(solution)/shard_map/finish_rows/pallas_call | solution.py:360
  47.8 0.8 fusion.1
  49.0 5.9 %all-to-all-start = ((bf16[16,32,256]{2,1,0:T(8,128)(2,1)}), bf16[16,32,256]{2,1,0:T(8,128)(2,1)S(1)}, u32[]{:S(2)}, u32[]{:S(2)}) async-start(bf16[16,32,256]{2,1,0:T(8,128)(2,1)} %fusion.1), calls=%async_computation | async-start | bytes 524288 | tf_op jit(solution)/shard_map/all_to_all | solution.py:491
  55.0 2.0 %collective-permute-start.8 = (bf16[2,128,256]{2,1,0:T(8,128)(2,1)S(1)}, bf16[2,128,256]{2,1,0:T(8,128)(2,1)S(1)}, u32[]{:S(2)}, u32[]{:S(2)}) collective-permute-start(bf16[2,128,256]{2,1,0:T(8,128)(2,1)S(1)} %dynamic-slice_bitcast_fusion.1), channel_id=1, source_target_pairs={{0,2},{2,0},{4,6},{6,4},{1,3},{3,1},{5,7},{7,5},{8,10},{10,8},{12,... | collective-permute-start | bytes 393224 | tf_op jit(solution)/shard_map/ppermute | solution.py:316
  56.9 7.8 %collective-permute-done.8 = bf16[2,128,256]{2,1,0:T(8,128)(2,1)S(1)} collective-permute-done((bf16[2,128,256]{2,1,0:T(8,128)(2,1)S(1)}, bf16[2,128,256]{2,1,0:T(8,128)(2,1)S(1)}, u32[]{:S(2)}, u32[]{:S(2)}) %collective-permute-start.8) | collective-permute-done | bytes 131104 | tf_op jit(solution)/shard_map/ppermute | solution.py:316
  64.8 1.1 %all-to-all-done = bf16[16,32,256]{2,1,0:T(8,128)(2,1)S(1)} async-done(((bf16[16,32,256]{2,1,0:T(8,128)(2,1)}), bf16[16,32,256]{2,1,0:T(8,128)(2,1)S(1)}, u32[]{:S(2)}, u32[]{:S(2)}) %all-to-all-start) | async-done | bytes 262176 | tf_op jit(solution)/shard_map/all_to_all | solution.py:491
  65.9 0.7 broadcast_in_dim.62
  66.7 4.5 %all-to-all-start.1 = ((bf16[16,32,256]{2,1,0:T(8,128)(2,1)}), bf16[16,32,256]{2,1,0:T(8,128)(2,1)S(1)}, u32[]{:S(2)}, u32[]{:S(2)}) async-start(bf16[16,32,256]{2,1,0:T(8,128)(2,1)} %broadcast_in_dim.62), calls=%async_computation.1 | async-start | bytes 524288 | tf_op jit(solution)/shard_map/all_to_all | solution.py:494
  71.2 2.9 %collective-permute-start.9 = (bf16[128,256]{1,0:T(8,128)(2,1)S(1)}, bf16[128,256]{1,0:T(8,128)(2,1)S(1)}, u32[]{:S(2)}, u32[]{:S(2)}) collective-permute-start(bf16[128,256]{1,0:T(8,128)(2,1)S(1)} %dynamic-slice_bitcast_fusion.2), channel_id=1, source_target_pairs={{0,4},{2,6},{4,0},{6,2},{1,5},{3,7},{5,1},{7,3},{8,12},{10,14},{12... | collective-permute-start | bytes 196616 | tf_op jit(solution)/shard_map/ppermute | solution.py:316
  74.0 9.5 %all-to-all-done.1 = bf16[16,32,256]{2,1,0:T(8,128)(2,1)S(1)} async-done(((bf16[16,32,256]{2,1,0:T(8,128)(2,1)}), bf16[16,32,256]{2,1,0:T(8,128)(2,1)S(1)}, u32[]{:S(2)}, u32[]{:S(2)}) %all-to-all-start.1) | async-done | bytes 262176 | tf_op jit(solution)/shard_map/all_to_all | solution.py:494
  83.5 0.6 fusion.4
  84.2 0.8 collective-permute-done.10
  85.2 1.0 %slice_bitcast_fusion = (f32[256,256]{1,0:T(8,128)}, f32[256,256]{1,0:T(8,128)}, f32[256,256]{1,0:T(8,128)}, f32[256,256]{1,0:T(8,128)}) fusion(f32[4,256,256]{2,1,0:T(8,128)S(1)} %convert.6), kind=kLoop, calls=%fused_computation.4 | loop fusion | bytes 2097152 | tf_op jit(solution)/shard_map/squeeze | solution.py:507
  (52 shorter events, 3.9 us)
Async XLA Ops:
  0.6 8.0 %collective-permute-start = (bf16[128,256]{1,0:T(8,128)(2,1)}, bf16[128,256]{1,0:T(8,128)(2,1)S(1)}, u32[]{:S(2)}, u32[]{:S(2)}) collective-permute-start(bf16[128,256]{1,0:T(8,128)(2,1)} %bitcast.80), channel_id=1, source_target_pairs={{0,4},{2,6},{4,0},{6,2},{1,5},{3,7},{5,1},{7,3},{8,12},{10,14},{12... | collective-permute-start | bytes 196616 | tf_op jit(solution)/shard_map/ppermute | solution.py:316
  4.7 0.9 %copy-start.7 = (bf16[1,128,256]{2,1,0:T(8,128)(2,1)S(1)}, bf16[1,128,256]{2,1,0:T(8,128)(2,1)}, u32[]{:S(2)}) copy-start(bf16[1,128,256]{2,1,0:T(8,128)(2,1)} %param.9) | copy-start | bytes 196612
  8.6 5.0 %collective-permute-start.1 = (bf16[2,128,256]{2,1,0:T(8,128)(2,1)S(1)}, bf16[2,128,256]{2,1,0:T(8,128)(2,1)S(1)}, u32[]{:S(2)}, u32[]{:S(2)}) collective-permute-start(bf16[2,128,256]{2,1,0:T(8,128)(2,1)S(1)} %bitcast_dynamic-update-slice_fusion.6), channel_id=1, source_target_pairs={{0,2},{2,0},{4,6},{6,4},{1,3},{3,1},{5,7},{7,5},{8,10},{10,8},{12,... | collective-permute-start | bytes 393224 | tf_op jit(solution)/shard_map/ppermute | solution.py:316
  13.7 1.6 %collective-permute-start.2 = (bf16[2,2,128,256]{3,2,1,0:T(8,128)(2,1)S(1)}, bf16[2,2,128,256]{3,2,1,0:T(8,128)(2,1)S(1)}, u32[]{:S(2)}, u32[]{:S(2)}) collective-permute-start(bf16[2,2,128,256]{3,2,1,0:T(8,128)(2,1)S(1)} %bitcast_dynamic-update-slice_fusion.5), channel_id=1, source_target_pairs={{0,1},{1,0},{2,3},{3,2},{4,5},{5,4},{6,7},{7,6},{8,9},{9,8},{10,11... | collective-permute-start | bytes 786440 | tf_op jit(solution)/shard_map/ppermute | solution.py:316
  13.8 1.5 %copy-start.2 = (bf16[256,256]{1,0:T(8,128)(2,1)S(1)}, bf16[256,256]{1,0:T(8,128)(2,1)}, u32[]{:S(2)}) copy-start(bf16[256,256]{1,0:T(8,128)(2,1)} %wq_ref.5) | copy-start | bytes 393220
  13.8 1.5 %copy-start.3 = (bf16[256,256]{1,0:T(8,128)(2,1)S(1)}, bf16[256,256]{1,0:T(8,128)(2,1)}, u32[]{:S(2)}) copy-start(bf16[256,256]{1,0:T(8,128)(2,1)} %wk_ref.5) | copy-start | bytes 393220
  13.8 1.5 %copy-start.4 = (bf16[256,256]{1,0:T(8,128)(2,1)S(1)}, bf16[256,256]{1,0:T(8,128)(2,1)}, u32[]{:S(2)}) copy-start(bf16[256,256]{1,0:T(8,128)(2,1)} %wv_ref.5) | copy-start | bytes 393220
  13.8 1.5 %copy-start.5 = (bf16[256,256]{1,0:T(8,128)(2,1)S(1)}, bf16[256,256]{1,0:T(8,128)(2,1)}, u32[]{:S(2)}) copy-start(bf16[256,256]{1,0:T(8,128)(2,1)} %wo_ref.5) | copy-start | bytes 393220
  13.9 1.5 %copy-start = (bf16[1,512,256]{2,1,0:T(8,128)(2,1)S(1)}, bf16[1,512,256]{2,1,0:T(8,128)(2,1)}, u32[]{:S(2)}) copy-start(bf16[1,512,256]{2,1,0:T(8,128)(2,1)} %param.8) | copy-start | bytes 786436
  13.9 1.5 %copy-start.1 = (bf16[1,512,256]{2,1,0:T(8,128)(2,1)S(1)}, bf16[1,512,256]{2,1,0:T(8,128)(2,1)}, u32[]{:S(2)}) copy-start(bf16[1,512,256]{2,1,0:T(8,128)(2,1)} %param.10) | copy-start | bytes 786436
  15.3 0.7 copy-start.6
  24.2 4.2 %collective-permute-start.3 = (f32[3,4,1024]{2,1,0:T(4,128)S(1)}, f32[3,4,1024]{2,1,0:T(4,128)S(1)}, u32[]{:S(2)}, u32[]{:S(2)}) collective-permute-start(f32[3,4,1024]{2,1,0:T(4,128)S(1)} %get-tuple-element.48), channel_id=1, source_target_pairs={{0,2},{2,0},{4,6},{6,4},{1,3},{3,1},{5,7},{7,5},{8,10},{10,8},{12,... | collective-permute-start | bytes 147464 | tf_op jit(solution)/shard_map/ppermute | solution.py:316
  28.4 5.1 %collective-permute-start.4 = (f32[3,4,1024]{2,1,0:T(4,128)S(1)}, f32[3,4,1024]{2,1,0:T(4,128)S(1)}, u32[]{:S(2)}, u32[]{:S(2)}) collective-permute-start(f32[3,4,1024]{2,1,0:T(4,128)S(1)} %pad_maximum_fusion), channel_id=1, source_target_pairs={{0,4},{2,6},{4,0},{6,2},{1,5},{3,7},{5,1},{7,3},{8,12},{10,14},{12... | collective-permute-start | bytes 147464 | tf_op jit(solution)/shard_map/ppermute | solution.py:316
  33.5 1.3 %collective-permute-start.5 = (f32[3,4,1024]{2,1,0:T(4,128)S(1)}, f32[3,4,1024]{2,1,0:T(4,128)S(1)}, u32[]{:S(2)}, u32[]{:S(2)}) collective-permute-start(f32[3,4,1024]{2,1,0:T(4,128)S(1)} %pad_maximum_fusion.1.near_ref), channel_id=1, source_target_pairs={{0,1},{1,0},{2,3},{3,2},{4,5},{5,4},{6,7},{7,6},{8,9},{9,8},{10,11... | collective-permute-start | bytes 147464 | tf_op jit(solution)/shard_map/ppermute | solution.py:316
  45.7 2.1 %collective-permute-start.6 = (bf16[16,32,256]{2,1,0:T(8,128)(2,1)S(1)}, bf16[16,32,256]{2,1,0:T(8,128)(2,1)S(1)}, u32[]{:S(2)}, u32[]{:S(2)}) collective-permute-start(bf16[16,32,256]{2,1,0:T(8,128)(2,1)S(1)} %dynamic-slice_bitcast_fusion), channel_id=1, source_target_pairs={{0,1},{1,0},{2,3},{3,2},{4,5},{5,4},{6,7},{7,6},{8,9},{9,8},{10,11... | collective-permute-start | bytes 786440 | tf_op jit(solution)/shard_map/ppermute | solution.py:316
  47.2 1.7 %collective-permute-start.7 = (bf16[2,2,128,256]{3,2,0,1:T(8,128)(2,1)S(1)}, bf16[2,2,128,256]{3,2,0,1:T(8,128)(2,1)S(1)}, u32[]{:S(2)}, u32[]{:S(2)}) collective-permute-start(bf16[2,2,128,256]{3,2,0,1:T(8,128)(2,1)S(1)} %bitcast.79), channel_id=1, source_target_pairs={{0,1},{1,0},{2,3},{3,2},{4,5},{5,4},{6,7},{7,6},{8,9},{9,8},{10,11... | collective-permute-start | bytes 786440 | tf_op jit(solution)/shard_map/ppermute | solution.py:316
  49.0 16.9 %all-to-all-start = ((bf16[16,32,256]{2,1,0:T(8,128)(2,1)}), bf16[16,32,256]{2,1,0:T(8,128)(2,1)S(1)}, u32[]{:S(2)}, u32[]{:S(2)}) async-start(bf16[16,32,256]{2,1,0:T(8,128)(2,1)} %fusion.1), calls=%async_computation | async-start | bytes 524288 | tf_op jit(solution)/shard_map/all_to_all | solution.py:491
  55.0 9.8 %collective-permute-start.8 = (bf16[2,128,256]{2,1,0:T(8,128)(2,1)S(1)}, bf16[2,128,256]{2,1,0:T(8,128)(2,1)S(1)}, u32[]{:S(2)}, u32[]{:S(2)}) collective-permute-start(bf16[2,128,256]{2,1,0:T(8,128)(2,1)S(1)} %dynamic-slice_bitcast_fusion.1), channel_id=1, source_target_pairs={{0,2},{2,0},{4,6},{6,4},{1,3},{3,1},{5,7},{7,5},{8,10},{10,8},{12,... | collective-permute-start | bytes 393224 | tf_op jit(solution)/shard_map/ppermute | solution.py:316
  66.7 16.8 %all-to-all-start.1 = ((bf16[16,32,256]{2,1,0:T(8,128)(2,1)}), bf16[16,32,256]{2,1,0:T(8,128)(2,1)S(1)}, u32[]{:S(2)}, u32[]{:S(2)}) async-start(bf16[16,32,256]{2,1,0:T(8,128)(2,1)} %broadcast_in_dim.62), calls=%async_computation.1 | async-start | bytes 524288 | tf_op jit(solution)/shard_map/all_to_all | solution.py:494
  71.2 12.3 %collective-permute-start.9 = (bf16[128,256]{1,0:T(8,128)(2,1)S(1)}, bf16[128,256]{1,0:T(8,128)(2,1)S(1)}, u32[]{:S(2)}, u32[]{:S(2)}) collective-permute-start(bf16[128,256]{1,0:T(8,128)(2,1)S(1)} %dynamic-slice_bitcast_fusion.2), channel_id=1, source_target_pairs={{0,4},{2,6},{4,0},{6,2},{1,5},{3,7},{5,1},{7,3},{8,12},{10,14},{12... | collective-permute-start | bytes 196616 | tf_op jit(solution)/shard_map/ppermute | solution.py:316
  83.5 1.5 %collective-permute-start.10 = (bf16[16,32,256]{2,1,0:T(8,128)(2,1)S(1)}, bf16[16,32,256]{2,1,0:T(8,128)(2,1)S(1)}, u32[]{:S(2)}, u32[]{:S(2)}) collective-permute-start(bf16[16,32,256]{2,1,0:T(8,128)(2,1)S(1)} %all-to-all-done.1), channel_id=1, source_target_pairs={{0,1},{1,0},{2,3},{3,2},{4,5},{5,4},{6,7},{7,6},{8,9},{9,8},{10,11... | collective-permute-start | bytes 786440 | tf_op jit(solution)/shard_map/ppermute | solution.py:316

commit v10 on v9

--- a/solution.py
+++ b/solution.py
@@ -85,14 +85,24 @@
     score_ref[...] = mm(left_ref[query_block], key_t_ref[:, span]) * LOG2E + bias
 
 
+def unpack(packed_ref):
+    total, width = packed_ref.shape
+    rows = (total - 4 * width) // 2
+    sizes = [rows, rows, width, width, width, width]
+    return [packed_ref.at[pl.ds(sum(sizes[:k]), sizes[k])] for k in range(len(sizes))]
+
+
 def stats_kernel(
-    heads, inter_ref, ref_ref, gout_ref, src_ref, wq_ref, wk_ref, wv_ref, wo_ref,
-    peak_ref, inverse_ref, col_ref, left_ref, gleft_ref, key_t_ref, value_t_ref,
-    score_ref, prob_ref, total_ref, col_peak_ref, col_total_ref, col_dot_ref,
+    heads, inter_ref, packed_ref, src_ref, peak_ref, inverse_ref, col_ref, score_ref, product_ref,
+    left_ref, gleft_ref, key_t_ref, value_t_ref, prob_ref, total_ref,
+    col_peak_ref, col_total_ref, col_dot_ref,
 ):
+    ref_ref, gout_ref, wq_ref, wk_ref, wv_ref, wo_ref = unpack(packed_ref)
     rows, width = ref_ref.shape
     key_total = src_ref.shape[0]
     head_dim = width // heads
+    key_t_ref[...] = bf(mm_general(wk_ref[...], src_ref[...], TT))
+    value_t_ref[...] = bf(mm_general(wv_ref[...], src_ref[...], TT))
     query = bf(bf(mm(ref_ref[...], wq_ref[...])).astype(jnp.float32) * head_dim ** -0.5)
     grad = bf(mm_general(gout_ref[...], wo_ref[...], NT))
     for query_block in range(rows // BLOCK):
@@ -101,8 +111,6 @@
             own = lane_row(width, head, head_dim)
             left_ref[query_block, head * BLOCK : (head + 1) * BLOCK, :] = query[span] * own
             gleft_ref[query_block, head * BLOCK : (head + 1) * BLOCK, :] = grad[span] * own
-    key_t_ref[...] = bf(mm_general(wk_ref[...], src_ref[...], TT))
-    value_t_ref[...] = bf(mm_general(wv_ref[...], src_ref[...], TT))
     steps = key_total // STEP
     peak_ref[...] = jnp.full(peak_ref.shape, 2.0 * NEG, jnp.float32)
     total_ref[...] = jnp.zeros(total_ref.shape, jnp.float32)
@@ -136,9 +144,11 @@
             col_peak_ref[step, head] = spread(peak.max(axis=0, keepdims=True), peak)
 
     def totals(query_block, step, listed):
-        score_now, prob_now = [ref.at[query_block * steps + step] for ref in (score_ref, prob_ref)]
+        score_now, product_now = [
+            ref.at[query_block * steps + step] for ref in (score_ref, product_ref)
+        ]
         span = pl.ds(pl.multiple_of(step * STEP, STEP), STEP)
-        prob_now[...] = mm(gleft_ref[query_block], value_t_ref[:, span])
+        prob_ref[...] = mm(gleft_ref[query_block], value_t_ref[:, span])
         for head, spans in head_strips(heads):
             col_totals = [col_total_ref[step, head, :, lanes] for lanes in tiles]
             for span in spans:
@@ -149,8 +159,8 @@
                     row_exp = jnp.exp2(scores - row_peak)
                     col_exp = jnp.exp2(scores - col_peak_ref[step, head, :, lanes][None])
                     row_total = row_total + row_exp
-                    product = row_exp * col_exp * by_eight(prob_now[span, lanes])
-                    prob_now[span, lanes] = product.reshape(STRIP, 128)
+                    product = row_exp * col_exp * by_eight(prob_ref[span, lanes])
+                    product_now[span, lanes] = bf(product.reshape(STRIP, 128))
                     col_totals[at] = col_totals[at] + col_exp.sum(axis=0)
                 total_ref[query_block, span, :] = row_total.reshape(STRIP, 128)
             for at, lanes in enumerate(tiles):
@@ -162,13 +172,13 @@
         inverse_ref[query_block] = spread(1.0 / total.sum(axis=1, keepdims=True), total)
 
     def dots(query_block, step, listed):
-        prob_now = prob_ref.at[query_block * steps + step]
+        product_now = product_ref.at[query_block * steps + step]
         for head, spans in head_strips(heads):
             col_dots = [col_dot_ref[step, head, :, lanes] for lanes in tiles]
             for span in spans:
                 inverse = inverse_ref[query_block, span, :]
                 for at, lanes in enumerate(tiles):
-                    product = by_eight(prob_now[span, lanes] * inverse)
+                    product = by_eight(product_now[span, lanes].astype(jnp.float32) * inverse)
                     col_dots[at] = col_dots[at] + product.sum(axis=0)
             for at, lanes in enumerate(tiles):
                 col_dot_ref[step, head, :, lanes] = col_dots[at]
@@ -184,9 +194,9 @@
 
 
 def side_kernel(
-    heads, ref_ref, gout_ref, src_ref, wq_ref, wk_ref, wv_ref, wo_ref,
-    key_ref, value_ref, query_t_ref, grad_t_ref,
+    heads, packed_ref, src_ref, key_ref, value_ref, query_t_ref, grad_t_ref
 ):
+    ref_ref, gout_ref, wq_ref, wk_ref, wv_ref, wo_ref = unpack(packed_ref)
     rows, width = ref_ref.shape
     scale = (width // heads) ** -0.5
     key_ref[...] = bf(mm(src_ref[...], wk_ref[...]))
@@ -200,12 +210,13 @@
 
 
 def grads_kernel(
-    heads, inter_ref, left_ref, gleft_ref, key_t_ref, value_t_ref, key_ref, value_ref,
-    query_t_ref, grad_t_ref, peak_ref, inverse_ref, near_ref, far_ref, ref_ref, gout_ref, src_ref,
+    heads, inter_ref, score_ref, product_ref, key_ref, value_ref,
+    query_t_ref, grad_t_ref, peak_ref, inverse_ref, own_ref, near_ref, far_ref, packed_ref, src_ref,
     attended_ref, gquery_ref, gkey_ref, gvalue_ref, weight_ref,
-    row_prob_ref, rest_ref, match_ref, gscore_ref, score_ref, prob_ref, dot_ref, col_ref,
+    rest_ref, match_ref, gscore_ref, dot_ref, col_ref,
     att_ref, gq_ref, gk_ref, gv_ref,
 ):
+    ref_ref, gout_ref = unpack(packed_ref)[:2]
     rows, width = ref_ref.shape
     key_total = src_ref.shape[0]
     steps = key_total // STEP
@@ -216,7 +227,8 @@
     near, far = jnp.exp2(near_ref[0] - peak), jnp.exp2(far_ref[0] - peak)
     inverse = 1.0 / (near * near_ref[1] + far * far_ref[1])
     half = (near * near_ref[2] + far * far_ref[2]) * inverse * 0.5
-    for kind, values in enumerate((peak, inverse, half)):
+    factor = jnp.exp2(own_ref[0] - peak) * inverse
+    for kind, values in enumerate((peak, inverse, factor, half)):
         for head in range(heads):
             for step in range(steps):
                 piece = values[head : head + 1, step * STEP : (step + 1) * STEP]
@@ -225,29 +237,27 @@
         ref[...] = jnp.zeros(ref.shape, jnp.float32)
 
     def products(query_block, step, listed):
-        row_prob_now, rest_now, match_now = [
-            ref.at[step] for ref in (row_prob_ref, rest_ref, match_ref)
+        score_now, product_now = [
+            ref.at[query_block * steps + step] for ref in (score_ref, product_ref)
         ]
-        score_block(query_block, step, listed, left_ref, key_t_ref, score_ref)
-        span = pl.ds(pl.multiple_of(step * STEP, STEP), STEP)
-        prob_ref[...] = mm(gleft_ref[query_block], value_t_ref[:, span])
+        rest_now, match_now = rest_ref.at[step], match_ref.at[step]
         for head, spans in head_strips(heads):
             for span in spans:
                 row_peak = by_eight(peak_ref[query_block, span, :])
                 row_inverse = by_eight(inverse_ref[query_block, span, :])
                 row_dot = by_eight(dot_ref[span, :])
                 for lanes in tiles:
-                    scores = by_eight(score_ref[span, lanes])
+                    col_peak, col_inverse, col_factor, col_half = [
+                        col_ref[kind, step, head, :, lanes][None] for kind in range(4)
+                    ]
+                    scores = by_eight(score_now[span, lanes])
                     row_prob = jnp.exp2(scores - row_peak) * row_inverse
-                    col_prob = jnp.exp2(scores - col_ref[0, step, head, :, lanes][None])
-                    col_prob = col_prob * col_ref[1, step, head, :, lanes][None]
-                    match = row_prob * col_prob
-                    product = match * by_eight(prob_ref[span, lanes])
+                    col_prob = jnp.exp2(scores - col_peak) * col_inverse
+                    product = by_eight(product_now[span, lanes].astype(jnp.float32))
+                    product = product * row_inverse * col_factor
                     row_dot = row_dot + product
-                    rest = product - col_prob * col_ref[2, step, head, :, lanes][None]
-                    match_now[span, lanes] = bf(match.reshape(STRIP, 128))
-                    row_prob_now[span, lanes] = row_prob.reshape(STRIP, 128)
-                    rest_now[span, lanes] = rest.reshape(STRIP, 128)
+                    match_now[span, lanes] = bf((row_prob * col_prob).reshape(STRIP, 128))
+                    rest_now[span, lanes] = (product - col_prob * col_half).reshape(STRIP, 128)
                 dot_ref[span, :] = row_dot.reshape(STRIP, 128)
 
     def own_lanes(stacked):
@@ -259,15 +269,16 @@
         return total
 
     def outputs(query_block, step, listed):
-        row_prob_now, rest_now, match_now = [
-            ref.at[step] for ref in (row_prob_ref, rest_ref, match_ref)
+        score_now, rest_now, match_now = [
+            score_ref.at[query_block * steps + step], rest_ref.at[step], match_ref.at[step]
         ]
         for _, spans in head_strips(heads):
             for span in spans:
-                row_half = dot_ref[span, :]
+                row_peak = peak_ref[query_block, span, :]
+                row_half = dot_ref[span, :] * inverse_ref[query_block, span, :]
                 for lanes in tiles:
-                    grads = rest_now[span, lanes] - row_prob_now[span, lanes] * row_half
-                    gscore_ref[span, lanes] = bf(grads)
+                    row_part = jnp.exp2(score_now[span, lanes] - row_peak) * row_half
+                    gscore_ref[span, lanes] = bf(rest_now[span, lanes] - row_part)
         span = pl.ds(pl.multiple_of(step * STEP, STEP), STEP)
         att_ref[query_block] += own_lanes(mm(match_now[...], value_ref[span, :]))
         gq_ref[query_block] += own_lanes(mm(gscore_ref[...], key_ref[span, :]))
@@ -300,9 +311,9 @@
 
 
 def finish_kernel(
-    ref_ref, gout_ref, attended_ref, gquery_ref, gkey_ref, gvalue_ref, wq_ref, wk_ref, wv_ref, wo_ref,
-    matched_ref, gref_ref, gsrc_ref,
+    packed_ref, attended_ref, gquery_ref, gkey_ref, gvalue_ref, matched_ref, gref_ref, gsrc_ref
 ):
+    ref_ref, gout_ref, wq_ref, wk_ref, wv_ref, wo_ref = unpack(packed_ref)
     gsrc_t = mm(wk_ref[...], gkey_ref[...]) + mm(wv_ref[...], gvalue_ref[...])
     gsrc_ref[...] = bf(gsrc_t.T)
     matched = ref_ref[...].astype(jnp.float32) + mm(attended_ref[...], wo_ref[...])
@@ -344,6 +355,23 @@
     me = lax.axis_index(mesh_axis)
     bits = range(lax.axis_size(mesh_axis).bit_length() - 1)
     return [(mesh_axis, 1 << bit, (me >> bit) % 2) for bit in bits]
+
+
+def scatter_direct(x, mesh_axis):
+    me, count = lax.axis_index(mesh_axis), lax.axis_size(mesh_axis)
+    total = at(x, me).astype(jnp.float32)
+    for piece in [swap(at(x, me ^ apart), mesh_axis, apart) for apart in range(1, count)]:
+        total = total + piece.astype(jnp.float32)
+    return total.astype(x.dtype)
+
+
+def gather_direct(x, mesh_axis):
+    me, count = lax.axis_index(mesh_axis), lax.axis_size(mesh_axis)
+    pieces = [x] + [swap(x, mesh_axis, apart) for apart in range(1, count)]
+    out = jnp.zeros((count,) + x.shape, x.dtype)
+    for apart, piece in enumerate(pieces):
+        out = lax.dynamic_update_index_in_dim(out, piece, me ^ apart, 0)
+    return out
 
 
 def combine_stats(parts):
@@ -380,6 +408,7 @@
     key_rows = src_rows.shape[0]
     key_total = key_rows * lax.axis_size("chip") * lax.axis_size("core")
 
+    packed = jnp.concatenate([ref_rows, out_grad, w_query, w_key, w_value, w_out], axis=0)
     source_all = src_rows
     for count, step in enumerate(chip_steps[::-1]):
         source_all = double(source_all, step, count)
@@ -390,31 +419,38 @@
     unit = 2 * rows * width * width
     query_blocks, steps = rows // BLOCK, key_total // STEP
     stacked = HEADS * BLOCK
-    blocks = vmem((query_blocks * steps, stacked, STEP), f32)
-    row_like = shape((query_blocks, stacked, 128), f32)
+    blocks = (query_blocks * steps, stacked, STEP)
+    row_like = (query_blocks, stacked, 128)
     col_like = vmem((steps, HEADS, 8, STEP), f32)
-    row_peak, row_inverse, col_stats, left, grad_left, key_t, value_t = vmem_call(
+    room = (16 << 20) + max(0, rows * key_total * HEADS * 10 - (20 << 20))
+    row_peak, row_inverse, col_stats, scores, product = vmem_call(
         functools.partial(stats_kernel, HEADS),
         "match_stats",
         [
-            row_like,
-            row_like,
+            shape(row_like, f32),
+            shape(row_like, f32),
             shape((3, HEADS, key_total), f32),
-            shape((query_blocks, stacked, width), b16),
-            shape((query_blocks, stacked, width), b16),
-            shape((width, key_total), b16),
-            shape((width, key_total), b16),
+            shape(blocks, f32),
+            shape(blocks, b16),
         ],
-        [blocks, blocks, vmem(row_like.shape, f32), col_like, col_like, col_like],
-        (6 << 20) + rows * key_total * HEADS * 9,
+        [
+            vmem((query_blocks, stacked, width), b16),
+            vmem((query_blocks, stacked, width), b16),
+            vmem((width, key_total), b16),
+            vmem((width, key_total), b16),
+            vmem((stacked, STEP), f32),
+            vmem(row_like, f32),
+            col_like,
+            col_like,
+            col_like,
+        ],
+        room,
         60 * unit,
         8 << 20,
-        (listed, ref_rows, out_grad, source_all, w_query, w_key, w_value, w_out),
+        (listed, packed, source_all),
         scalars=1,
     )
-    ref_near, grad_near, source_near, near_stats = lax.optimization_barrier(
-        (ref_rows, out_grad, source_all, col_stats)
-    )
+    near_stats = col_stats
     keys, values, query_t, grad_t = vmem_call(
         functools.partial(side_kernel, HEADS),
         "project_for_grads",
@@ -428,7 +464,7 @@
         8 << 20,
         8 * unit,
         2 << 20,
-        (ref_near, grad_near, source_near, w_query, w_key, w_value, w_out),
+        (packed, source_all),
     )
     for mesh_axis, bit, _ in chip_steps:
         near_stats = combine_stats([near_stats, swap(near_stats, mesh_axis, bit)])
@@ -445,23 +481,20 @@
         ],
         [
             vmem((steps, stacked, STEP), f32),
-            vmem((steps, stacked, STEP), f32),
             vmem((steps, stacked, STEP), b16),
             vmem((stacked, STEP), b16),
-            vmem((stacked, STEP), f32),
-            vmem((stacked, STEP), f32),
             vmem((stacked, 128), f32),
-            vmem((3, steps, HEADS, 8, STEP), f32),
+            vmem((4, steps, HEADS, 8, STEP), f32),
             vmem((query_blocks, BLOCK, width), f32),
             vmem((query_blocks, BLOCK, width), f32),
             vmem((steps, width, STEP), f32),
             vmem((steps, width, STEP), f32),
         ],
-        (10 << 20) + BLOCK * key_total * HEADS * 20,
+        room,
         100 * unit,
         8 << 20,
-        (listed, left, grad_left, key_t, value_t, keys, values, query_t, grad_t, row_peak, row_inverse,
-         near_stats, far_stats, ref_rows, out_grad, source_all),
+        (listed, scores, product, keys, values, query_t, grad_t, row_peak, row_inverse, col_stats,
+         near_stats, far_stats, packed, source_all),
         scalars=1,
     )
     matched, grad_ref, source_part = vmem_call(
@@ -476,22 +509,21 @@
         8 << 20,
         8 * unit,
         2 << 20,
-        (ref_rows, out_grad, attended, grad_query, grad_key, grad_value,
-         w_query, w_key, w_value, w_out),
-    )
-
-    peers = ("scan", "chip")
-    count = lax.axis_size("scan") * lax.axis_size("chip")
-    weights = weight_part.reshape((2, count, -1, width))
+        (packed, attended, grad_query, grad_key, grad_value),
+    )
+
+    weights = weight_part.reshape((2, lax.axis_size("scan"), -1, width))
     sources = source_part.reshape((2,) * (len(chip_steps) + 1) + (key_rows, width))
     source_steps = list(zip(chip_steps, range(len(chip_steps) - 1, -1, -1)))
     weights = halve(weights, core_step)
     sources = halve(sources, core_step, len(chip_steps))
-    weights, sources = lax.optimization_barrier((weights, sources))
-    weights = lax.all_to_all(weights, peers, 0, 0).astype(f32).sum(axis=0).astype(b16)
+    weights = scatter_direct(weights, "scan")
     sources = halve(sources, *source_steps[0])
     weights, sources = lax.optimization_barrier((weights, sources))
-    weights = lax.all_to_all(jnp.broadcast_to(weights, (count,) + weights.shape), peers, 0, 0)
+    for mesh_axis, bit, _ in chip_steps:
+        weights = add(weights, swap(weights, mesh_axis, bit))
+    weights, sources = lax.optimization_barrier((weights, sources))
+    weights = gather_direct(weights, "scan")
     for step in source_steps[1:]:
         sources = halve(sources, *step)
     grad_src = sources

time: 87.4 us -> 79.7 us (0.912); the launches traced: 86.1 us -> 79.4 us
  waiting for transfers between devices: 35.6 us -> 23.4 us
  local copies, waits for them, and re-layouts: 3.59 us -> 8.54 us
  starting transfers between devices: 23.2 us -> 26.9 us
  Pallas kernels: 21 us -> 17.5 us
    ppermute x11 -> x19, starting transfers between devices: 12.8 us -> 26.9 us  [swap(): return lax.ppermute(x, axis, pairs)]
    all_to_all x2 -> x0, waiting for transfers between devices: 10.5 us -> none  [the longest x1 9.45 us: on_device(): lax.all_to_all(jnp.broadcast_to(weights, (count,) + weights.shape), peers...]
    all_to_all x2 -> x0, starting transfers between devices: 10.4 us -> none  [the longest x1 5.94 us: on_device(): lax.all_to_all(weights, peers, 0, 0).astype(f32).sum(axis=0).astype(b16)]
    unnamed x16 -> x7, local copies, waits for them, and re-layouts: 1.51 us -> 5.36 us
    pallas_call x4, Pallas kernels: 21 us -> 17.5 us  [vmem_call(): pl.pallas_call(kernel, name=name, out_shape=out_shape, in_specs=specs, ou...]
    ppermute x11 -> x19, waiting for transfers between devices: 25.1 us -> 23.4 us  [swap(): return lax.ppermute(x, axis, pairs)]
    concatenate x0 -> x1, local copies, waits for them, and re-layouts: none -> 0.92 us  [on_device(): jnp.concatenate([ref_rows, out_grad, w_query, w_key, w_value, w_out], axi...]
  transfers between devices with their start and end apart: 13 -> 19, of which waited for: 11 -> 12; matrix products, arithmetic and copies ran while one was open for 2% -> 11% of each run, Pallas kernels for 2% -> 2%
where the time goes in v10:
time: 79.7 us; the launch traced here: 79.4 us
  starting transfers between devices  26.9 us (34%)
  waiting for transfers between devices  23.4 us (29%)
  Pallas kernels  17.5 us (22%)
  local copies, waits for them, and re-layouts  8.54 us (11%)
  other arithmetic  2.03 us (3%)
  between operations  0.97 us (1%)
    ppermute x19, starting transfers between devices, swap(): return lax.ppermute(x, axis, pairs)  26.9 us
    ppermute x19, waiting for transfers between devices, swap(): return lax.ppermute(x, axis, pairs)  23.4 us
    pallas_call x4, Pallas kernels, vmem_call(): pl.pallas_call(kernel, name=name, out_shape=out_shape, in_specs=specs, ou...  17.5 us
    unnamed x7, local copies, waits for them, and re-layouts  5.36 us
  transfers between devices with their start and end apart: 19, of which 12 were waited for; matrix products, arithmetic and copies ran while one was open for 11% of the time, Pallas kernels for 2%

profile of v10, /device:TPU:0, one launch (start us, length us, event | category | flops | bytes accessed | tf_op | source)
XLA Modules:
  0.0 79.4 jit_solution(9110695614830866345)
XLA Ops:
  0.6 4.1 %collective-permute-start = (bf16[128,256]{1,0:T(8,128)(2,1)}, bf16[128,256]{1,0:T(8,128)(2,1)S(1)}, u32[]{:S(2)}, u32[]{:S(2)}) collective-permute-start(bf16[128,256]{1,0:T(8,128)(2,1)} %bitcast.91), channel_id=1, source_target_pairs={{0,4},{2,6},{4,0},{6,2},{1,5},{3,7},{5,1},{7,3},{8,12},{10,14},{12... | collective-permute-start | bytes 196616 | tf_op jit(solution)/shard_map/ppermute | solution.py:327
  10.3 1.6 %collective-permute-start.1 = (bf16[2,128,256]{2,1,0:T(8,128)(2,1)S(1)}, bf16[2,128,256]{2,1,0:T(8,128)(2,1)S(1)}, u32[]{:S(2)}, u32[]{:S(2)}) collective-permute-start(bf16[2,128,256]{2,1,0:T(8,128)(2,1)S(1)} %bitcast_dynamic-update-slice_fusion.12), channel_id=1, source_target_pairs={{0,2},{2,0},{4,6},{6,4},{1,3},{3,1},{5,7},{7,5},{8,10},{10,8},{12,... | collective-permute-start | bytes 393224 | tf_op jit(solution)/shard_map/ppermute | solution.py:327
  12.0 3.3 %collective-permute-done.1 = bf16[2,128,256]{2,1,0:T(8,128)(2,1)S(1)} collective-permute-done((bf16[2,128,256]{2,1,0:T(8,128)(2,1)S(1)}, bf16[2,128,256]{2,1,0:T(8,128)(2,1)S(1)}, u32[]{:S(2)}, u32[]{:S(2)}) %collective-permute-start.1) | collective-permute-done | bytes 131104 | tf_op jit(solution)/shard_map/ppermute | solution.py:327
  17.7 7.5 %match_stats.1 = (f32[4,512,128]{2,1,0:T(8,128)S(1)}, f32[4,512,128]{2,1,0:T(8,128)S(1)}, f32[3,4,1024]{2,1,0:T(4,128)S(1)}, f32[16,512,256]{2,1,0:T(8,128)S(1)}, bf16[16,512,256]{2,1,0:T(8,128)(2,1)S(1)}) custom-call(s32[4,8]{1,0:T(4,128)S(1)} %bitcast.87, bf16[2048,256]{1,0:T(8,128)(2,1)S(1)} %constant_dynamic-update-slice_fusion.packed_ref, ...), custom_call_target="tpu_custom_call" | custom-call | flops 4026531840 | bytes 8388608 | tf_op jit(solution)/shard_map/match_stats/pallas_call | solution.py:388
  25.3 2.2 %collective-permute-start.3 = (f32[3,4,1024]{2,1,0:T(4,128)S(1)}, f32[3,4,1024]{2,1,0:T(4,128)S(1)}, u32[]{:S(2)}, u32[]{:S(2)}) collective-permute-start(f32[3,4,1024]{2,1,0:T(4,128)S(1)} %get-tuple-element.36.own_ref), channel_id=1, source_target_pairs={{0,2},{2,0},{4,6},{6,4},{1,3},{3,1},{5,7},{7,5},{8,10},{10,8},{12,... | collective-permute-start | bytes 147464 | tf_op jit(solution)/shard_map/ppermute | solution.py:327
  27.5 2.2 %collective-permute-done.3 = f32[3,4,1024]{2,1,0:T(4,128)S(1)} collective-permute-done((f32[3,4,1024]{2,1,0:T(4,128)S(1)}, f32[3,4,1024]{2,1,0:T(4,128)S(1)}, u32[]{:S(2)}, u32[]{:S(2)}) %collective-permute-start.3) | collective-permute-done | bytes 49184 | tf_op jit(solution)/shard_map/ppermute | solution.py:327
  29.8 1.5 %collective-permute-start.4 = (f32[3,4,1024]{2,1,0:T(4,128)S(1)}, f32[3,4,1024]{2,1,0:T(4,128)S(1)}, u32[]{:S(2)}, u32[]{:S(2)}) collective-permute-start(f32[3,4,1024]{2,1,0:T(4,128)S(1)} %pad_maximum_fusion), channel_id=1, source_target_pairs={{0,4},{2,6},{4,0},{6,2},{1,5},{3,7},{5,1},{7,3},{8,12},{10,14},{12... | collective-permute-start | bytes 147464 | tf_op jit(solution)/shard_map/ppermute | solution.py:327
  31.3 3.5 %collective-permute-done.4 = f32[3,4,1024]{2,1,0:T(4,128)S(1)} collective-permute-done((f32[3,4,1024]{2,1,0:T(4,128)S(1)}, f32[3,4,1024]{2,1,0:T(4,128)S(1)}, u32[]{:S(2)}, u32[]{:S(2)}) %collective-permute-start.4) | collective-permute-done | bytes 49184 | tf_op jit(solution)/shard_map/ppermute | solution.py:327
  36.2 8.1 %match_grads.1 = (bf16[512,256]{1,0:T(8,128)(2,1)S(1)}, bf16[512,256]{1,0:T(8,128)(2,1)S(1)}, bf16[256,1024]{1,0:T(8,128)(2,1)S(1)}, bf16[256,1024]{1,0:T(8,128)(2,1)S(1)}, bf16[4,256,256]{2,1,0:T(8,128)(2,1)S(1)}) custom-call(s32[4,8]{1,0:T(4,128)S(1)} %bitcast.88, f32[16,512,256]{2,1,0:T(8,128)S(1)} %get-tuple-element.28.score_ref, ...), custom_call_target="tpu_custom_call" | custom-call | flops 6710886400 | bytes 8388608 | tf_op jit(solution)/shard_map/match_grads/pallas_call | solution.py:388
  45.2 1.4 %finish_rows.1 = (bf16[512,256]{1,0:T(8,128)(2,1)}, bf16[512,256]{1,0:T(8,128)(2,1)}, bf16[1024,256]{1,0:T(8,128)(2,1)S(1)}) custom-call(bf16[2048,256]{1,0:T(8,128)(2,1)S(1)} %constant_dynamic-update-slice_fusion.packed_ref, bf16[512,256]{1,0:T(8,128)(2,1)S(1)} %get-tuple-element.37.attended_ref, bf16[512,256]{1,0:T(8,128)(2,1)S(1)} %get-tuple-element.38.gquery_ref, ...), custom_call_target="tpu_custom_call" | custom-call | flops 536870912 | bytes 2097152 | tf_op jit(solution)/shard_map/finish_rows/pallas_call | solution.py:388
  46.8 1.0 %fusion.1 = bf16[4,128,256]{2,1,0:T(8,128)(2,1)S(1)} fusion(bf16[4,128,256]{2,1,0:T(8,128)(2,1)} %collective-permute-done.6, bf16[2,4,128,256]{3,2,1,0:T(8,128)(2,1)S(1)} %bitcast.86, s32[]{:T(128)S(6)} %select_n.76), kind=kLoop, calls=%fused_computation.3 | loop fusion | flops 524288 | bytes 786436 | tf_op jit(solution)/shard_map/convert_element_type | solution.py:341
  47.8 2.3 %collective-permute-start.7 = (bf16[128,256]{1,0:T(8,128)(2,1)S(1)}, bf16[128,256]{1,0:T(8,128)(2,1)S(1)}, u32[]{:S(2)}, u32[]{:S(2)}) collective-permute-start(bf16[128,256]{1,0:T(8,128)(2,1)S(1)} %get-tuple-element.57), channel_id=1, source_target_pairs={{0,8},{8,0},{16,24},{24,16},{1,9},{9,1},{17,25},{25,17},{2,10},{10... | collective-permute-start | bytes 196616 | tf_op jit(solution)/shard_map/ppermute | solution.py:327
  50.1 3.1 %collective-permute-start.8 = (bf16[128,256]{1,0:T(8,128)(2,1)S(1)}, bf16[128,256]{1,0:T(8,128)(2,1)S(1)}, u32[]{:S(2)}, u32[]{:S(2)}) collective-permute-start(bf16[128,256]{1,0:T(8,128)(2,1)S(1)} %get-tuple-element.59), channel_id=1, source_target_pairs={{0,16},{8,24},{16,0},{24,8},{1,17},{9,25},{17,1},{25,9},{2,18},{10... | collective-permute-start | bytes 196616 | tf_op jit(solution)/shard_map/ppermute | solution.py:327
  53.3 1.2 %collective-permute-start.11 = (bf16[2,128,256]{2,1,0:T(8,128)(2,1)S(1)}, bf16[2,128,256]{2,1,0:T(8,128)(2,1)S(1)}, u32[]{:S(2)}, u32[]{:S(2)}) collective-permute-start(bf16[2,128,256]{2,1,0:T(8,128)(2,1)S(1)} %dynamic-slice_bitcast_fusion.1), channel_id=1, source_target_pairs={{0,2},{2,0},{4,6},{6,4},{1,3},{3,1},{5,7},{7,5},{8,10},{10,8},{12,... | collective-permute-start | bytes 393224 | tf_op jit(solution)/shard_map/ppermute | solution.py:327
  54.5 1.7 %collective-permute-done.8 = bf16[128,256]{1,0:T(8,128)(2,1)S(1)} collective-permute-done((bf16[128,256]{1,0:T(8,128)(2,1)S(1)}, bf16[128,256]{1,0:T(8,128)(2,1)S(1)}, u32[]{:S(2)}, u32[]{:S(2)}) %collective-permute-start.8) | collective-permute-done | bytes 65568 | tf_op jit(solution)/shard_map/ppermute | solution.py:327
  56.2 2.1 %collective-permute-done.9 = bf16[128,256]{1,0:T(8,128)(2,1)S(1)} collective-permute-done((bf16[128,256]{1,0:T(8,128)(2,1)S(1)}, bf16[128,256]{1,0:T(8,128)(2,1)S(1)}, u32[]{:S(2)}, u32[]{:S(2)}) %collective-permute-start.9) | collective-permute-done | bytes 65568 | tf_op jit(solution)/shard_map/ppermute | solution.py:327
  58.5 1.1 %collective-permute-start.12 = (bf16[128,256]{1,0:T(8,128)(2,1)S(1)}, bf16[128,256]{1,0:T(8,128)(2,1)S(1)}, u32[]{:S(2)}, u32[]{:S(2)}) collective-permute-start(bf16[128,256]{1,0:T(8,128)(2,1)S(1)} %fusion.6), channel_id=1, source_target_pairs={{0,2},{2,0},{4,6},{6,4},{1,3},{3,1},{5,7},{7,5},{8,10},{10,8},{12,... | collective-permute-start | bytes 196616 | tf_op jit(solution)/shard_map/ppermute | solution.py:327
  59.6 3.2 %collective-permute-done.12 = bf16[128,256]{1,0:T(8,128)(2,1)S(1)} collective-permute-done((bf16[128,256]{1,0:T(8,128)(2,1)S(1)}, bf16[128,256]{1,0:T(8,128)(2,1)S(1)}, u32[]{:S(2)}, u32[]{:S(2)}) %collective-permute-start.12) | collective-permute-done | bytes 65568 | tf_op jit(solution)/shard_map/ppermute | solution.py:327
  62.8 2.4 %collective-permute-start.13 = (bf16[128,256]{1,0:T(8,128)(2,1)S(1)}, bf16[128,256]{1,0:T(8,128)(2,1)S(1)}, u32[]{:S(2)}, u32[]{:S(2)}) collective-permute-start(bf16[128,256]{1,0:T(8,128)(2,1)S(1)} %add_convert_fusion.1), channel_id=1, source_target_pairs={{0,4},{2,6},{4,0},{6,2},{1,5},{3,7},{5,1},{7,3},{8,12},{10,14},{12... | collective-permute-start | bytes 196616 | tf_op jit(solution)/shard_map/ppermute | solution.py:327
  65.3 2.8 %collective-permute-done.13 = bf16[128,256]{1,0:T(8,128)(2,1)S(1)} collective-permute-done((bf16[128,256]{1,0:T(8,128)(2,1)S(1)}, bf16[128,256]{1,0:T(8,128)(2,1)S(1)}, u32[]{:S(2)}, u32[]{:S(2)}) %collective-permute-start.13) | collective-permute-done | bytes 65568 | tf_op jit(solution)/shard_map/ppermute | solution.py:327
  68.1 1.5 %collective-permute-start.15 = (bf16[128,256]{1,0:T(8,128)(2,1)S(1)}, bf16[128,256]{1,0:T(8,128)(2,1)S(1)}, u32[]{:S(2)}, u32[]{:S(2)}) collective-permute-start(bf16[128,256]{1,0:T(8,128)(2,1)S(1)} %add_convert_fusion), channel_id=1, source_target_pairs={{0,8},{8,0},{16,24},{24,16},{1,9},{9,1},{17,25},{25,17},{2,10},{10... | collective-permute-start | bytes 196616 | tf_op jit(solution)/shard_map/ppermute | solution.py:327
  69.6 2.0 %collective-permute-start.16 = (bf16[128,256]{1,0:T(8,128)(2,1)S(1)}, bf16[128,256]{1,0:T(8,128)(2,1)S(1)}, u32[]{:S(2)}, u32[]{:S(2)}) collective-permute-start(bf16[128,256]{1,0:T(8,128)(2,1)S(1)} %add_convert_fusion), channel_id=1, source_target_pairs={{0,16},{8,24},{16,0},{24,8},{1,17},{9,25},{17,1},{25,9},{2,18},{10... | collective-permute-start | bytes 196616 | tf_op jit(solution)/shard_map/ppermute | solution.py:327
  71.7 2.5 %collective-permute-start.14 = (bf16[128,256]{1,0:T(8,128)(2,1)S(1)}, bf16[128,256]{1,0:T(8,128)(2,1)S(1)}, u32[]{:S(2)}, u32[]{:S(2)}) collective-permute-start(bf16[128,256]{1,0:T(8,128)(2,1)S(1)} %dynamic-slice_bitcast_fusion.2), channel_id=1, source_target_pairs={{0,4},{2,6},{4,0},{6,2},{1,5},{3,7},{5,1},{7,3},{8,12},{10,14},{12... | collective-permute-start | bytes 196616 | tf_op jit(solution)/shard_map/ppermute | solution.py:327
  74.2 2.5 %collective-permute-done.17 = bf16[128,256]{1,0:T(8,128)(2,1)S(1)} collective-permute-done((bf16[128,256]{1,0:T(8,128)(2,1)S(1)}, bf16[128,256]{1,0:T(8,128)(2,1)S(1)}, u32[]{:S(2)}, u32[]{:S(2)}) %collective-permute-start.17) | collective-permute-done | bytes 65568 | tf_op jit(solution)/shard_map/ppermute | solution.py:327
  (63 shorter events, 13.4 us)
Async XLA Ops:
  0.6 9.7 %collective-permute-start = (bf16[128,256]{1,0:T(8,128)(2,1)}, bf16[128,256]{1,0:T(8,128)(2,1)S(1)}, u32[]{:S(2)}, u32[]{:S(2)}) collective-permute-start(bf16[128,256]{1,0:T(8,128)(2,1)} %bitcast.91), channel_id=1, source_target_pairs={{0,4},{2,6},{4,0},{6,2},{1,5},{3,7},{5,1},{7,3},{8,12},{10,14},{12... | collective-permute-start | bytes 196616 | tf_op jit(solution)/shard_map/ppermute | solution.py:327
  10.3 5.0 %collective-permute-start.1 = (bf16[2,128,256]{2,1,0:T(8,128)(2,1)S(1)}, bf16[2,128,256]{2,1,0:T(8,128)(2,1)S(1)}, u32[]{:S(2)}, u32[]{:S(2)}) collective-permute-start(bf16[2,128,256]{2,1,0:T(8,128)(2,1)S(1)} %bitcast_dynamic-update-slice_fusion.12), channel_id=1, source_target_pairs={{0,2},{2,0},{4,6},{6,4},{1,3},{3,1},{5,7},{7,5},{8,10},{10,8},{12,... | collective-permute-start | bytes 393224 | tf_op jit(solution)/shard_map/ppermute | solution.py:327
  15.4 1.6 %collective-permute-start.2 = (bf16[2,2,128,256]{3,2,1,0:T(8,128)(2,1)S(1)}, bf16[2,2,128,256]{3,2,1,0:T(8,128)(2,1)S(1)}, u32[]{:S(2)}, u32[]{:S(2)}) collective-permute-start(bf16[2,2,128,256]{3,2,1,0:T(8,128)(2,1)S(1)} %bitcast_dynamic-update-slice_fusion.7), channel_id=1, source_target_pairs={{0,1},{1,0},{2,3},{3,2},{4,5},{5,4},{6,7},{7,6},{8,9},{9,8},{10,11... | collective-permute-start | bytes 786440 | tf_op jit(solution)/shard_map/ppermute | solution.py:327
  17.0 0.7 copy-start
  25.3 4.5 %collective-permute-start.3 = (f32[3,4,1024]{2,1,0:T(4,128)S(1)}, f32[3,4,1024]{2,1,0:T(4,128)S(1)}, u32[]{:S(2)}, u32[]{:S(2)}) collective-permute-start(f32[3,4,1024]{2,1,0:T(4,128)S(1)} %get-tuple-element.36.own_ref), channel_id=1, source_target_pairs={{0,2},{2,0},{4,6},{6,4},{1,3},{3,1},{5,7},{7,5},{8,10},{10,8},{12,... | collective-permute-start | bytes 147464 | tf_op jit(solution)/shard_map/ppermute | solution.py:327
  29.8 5.1 %collective-permute-start.4 = (f32[3,4,1024]{2,1,0:T(4,128)S(1)}, f32[3,4,1024]{2,1,0:T(4,128)S(1)}, u32[]{:S(2)}, u32[]{:S(2)}) collective-permute-start(f32[3,4,1024]{2,1,0:T(4,128)S(1)} %pad_maximum_fusion), channel_id=1, source_target_pairs={{0,4},{2,6},{4,0},{6,2},{1,5},{3,7},{5,1},{7,3},{8,12},{10,14},{12... | collective-permute-start | bytes 147464 | tf_op jit(solution)/shard_map/ppermute | solution.py:327
  34.9 1.3 %collective-permute-start.5 = (f32[3,4,1024]{2,1,0:T(4,128)S(1)}, f32[3,4,1024]{2,1,0:T(4,128)S(1)}, u32[]{:S(2)}, u32[]{:S(2)}) collective-permute-start(f32[3,4,1024]{2,1,0:T(4,128)S(1)} %pad_maximum_fusion.1.near_ref), channel_id=1, source_target_pairs={{0,1},{1,0},{2,3},{3,2},{4,5},{5,4},{6,7},{7,6},{8,9},{9,8},{10,11... | collective-permute-start | bytes 147464 | tf_op jit(solution)/shard_map/ppermute | solution.py:327
  44.3 2.4 %collective-permute-start.6 = (bf16[4,128,256]{2,1,0:T(8,128)(2,1)S(1)}, bf16[4,128,256]{2,1,0:T(8,128)(2,1)}, u32[]{:S(2)}, u32[]{:S(2)}) collective-permute-start(bf16[4,128,256]{2,1,0:T(8,128)(2,1)S(1)} %dynamic-slice_bitcast_fusion), channel_id=1, source_target_pairs={{0,1},{1,0},{2,3},{3,2},{4,5},{5,4},{6,7},{7,6},{8,9},{9,8},{10,11... | collective-permute-start | bytes 786440 | tf_op jit(solution)/shard_map/ppermute | solution.py:327
  46.6 6.6 %collective-permute-start.10 = (bf16[2,2,128,256]{3,2,0,1:T(8,128)(2,1)S(1)}, bf16[2,2,128,256]{3,2,0,1:T(8,128)(2,1)S(1)}, u32[]{:S(2)}, u32[]{:S(2)}) collective-permute-start(bf16[2,2,128,256]{3,2,0,1:T(8,128)(2,1)S(1)} %bitcast.90), channel_id=1, source_target_pairs={{0,1},{1,0},{2,3},{3,2},{4,5},{5,4},{6,7},{7,6},{8,9},{9,8},{10,11... | collective-permute-start | bytes 786440 | tf_op jit(solution)/shard_map/ppermute | solution.py:327
  47.8 6.7 %collective-permute-start.7 = (bf16[128,256]{1,0:T(8,128)(2,1)S(1)}, bf16[128,256]{1,0:T(8,128)(2,1)S(1)}, u32[]{:S(2)}, u32[]{:S(2)}) collective-permute-start(bf16[128,256]{1,0:T(8,128)(2,1)S(1)} %get-tuple-element.57), channel_id=1, source_target_pairs={{0,8},{8,0},{16,24},{24,16},{1,9},{9,1},{17,25},{25,17},{2,10},{10... | collective-permute-start | bytes 196616 | tf_op jit(solution)/shard_map/ppermute | solution.py:327
  50.1 6.1 %collective-permute-start.8 = (bf16[128,256]{1,0:T(8,128)(2,1)S(1)}, bf16[128,256]{1,0:T(8,128)(2,1)S(1)}, u32[]{:S(2)}, u32[]{:S(2)}) collective-permute-start(bf16[128,256]{1,0:T(8,128)(2,1)S(1)} %get-tuple-element.59), channel_id=1, source_target_pairs={{0,16},{8,24},{16,0},{24,8},{1,17},{9,25},{17,1},{25,9},{2,18},{10... | collective-permute-start | bytes 196616 | tf_op jit(solution)/shard_map/ppermute | solution.py:327
  53.2 5.2 %collective-permute-start.9 = (bf16[128,256]{1,0:T(8,128)(2,1)S(1)}, bf16[128,256]{1,0:T(8,128)(2,1)S(1)}, u32[]{:S(2)}, u32[]{:S(2)}) collective-permute-start(bf16[128,256]{1,0:T(8,128)(2,1)S(1)} %get-tuple-element.58), channel_id=1, source_target_pairs={{0,24},{8,16},{16,8},{24,0},{1,25},{9,17},{17,9},{25,1},{2,26},{10... | collective-permute-start | bytes 196616 | tf_op jit(solution)/shard_map/ppermute | solution.py:327
  53.3 5.1 %collective-permute-start.11 = (bf16[2,128,256]{2,1,0:T(8,128)(2,1)S(1)}, bf16[2,128,256]{2,1,0:T(8,128)(2,1)S(1)}, u32[]{:S(2)}, u32[]{:S(2)}) collective-permute-start(bf16[2,128,256]{2,1,0:T(8,128)(2,1)S(1)} %dynamic-slice_bitcast_fusion.1), channel_id=1, source_target_pairs={{0,2},{2,0},{4,6},{6,4},{1,3},{3,1},{5,7},{7,5},{8,10},{10,8},{12,... | collective-permute-start | bytes 393224 | tf_op jit(solution)/shard_map/ppermute | solution.py:327
  58.5 4.3 %collective-permute-start.12 = (bf16[128,256]{1,0:T(8,128)(2,1)S(1)}, bf16[128,256]{1,0:T(8,128)(2,1)S(1)}, u32[]{:S(2)}, u32[]{:S(2)}) collective-permute-start(bf16[128,256]{1,0:T(8,128)(2,1)S(1)} %fusion.6), channel_id=1, source_target_pairs={{0,2},{2,0},{4,6},{6,4},{1,3},{3,1},{5,7},{7,5},{8,10},{10,8},{12,... | collective-permute-start | bytes 196616 | tf_op jit(solution)/shard_map/ppermute | solution.py:327
  62.8 5.2 %collective-permute-start.13 = (bf16[128,256]{1,0:T(8,128)(2,1)S(1)}, bf16[128,256]{1,0:T(8,128)(2,1)S(1)}, u32[]{:S(2)}, u32[]{:S(2)}) collective-permute-start(bf16[128,256]{1,0:T(8,128)(2,1)S(1)} %add_convert_fusion.1), channel_id=1, source_target_pairs={{0,4},{2,6},{4,0},{6,2},{1,5},{3,7},{5,1},{7,3},{8,12},{10,14},{12... | collective-permute-start | bytes 196616 | tf_op jit(solution)/shard_map/ppermute | solution.py:327
  68.1 6.1 %collective-permute-start.15 = (bf16[128,256]{1,0:T(8,128)(2,1)S(1)}, bf16[128,256]{1,0:T(8,128)(2,1)S(1)}, u32[]{:S(2)}, u32[]{:S(2)}) collective-permute-start(bf16[128,256]{1,0:T(8,128)(2,1)S(1)} %add_convert_fusion), channel_id=1, source_target_pairs={{0,8},{8,0},{16,24},{24,16},{1,9},{9,1},{17,25},{25,17},{2,10},{10... | collective-permute-start | bytes 196616 | tf_op jit(solution)/shard_map/ppermute | solution.py:327
  69.6 4.7 %collective-permute-start.16 = (bf16[128,256]{1,0:T(8,128)(2,1)S(1)}, bf16[128,256]{1,0:T(8,128)(2,1)S(1)}, u32[]{:S(2)}, u32[]{:S(2)}) collective-permute-start(bf16[128,256]{1,0:T(8,128)(2,1)S(1)} %add_convert_fusion), channel_id=1, source_target_pairs={{0,16},{8,24},{16,0},{24,8},{1,17},{9,25},{17,1},{25,9},{2,18},{10... | collective-permute-start | bytes 196616 | tf_op jit(solution)/shard_map/ppermute | solution.py:327
  71.5 5.2 %collective-permute-start.17 = (bf16[128,256]{1,0:T(8,128)(2,1)S(1)}, bf16[128,256]{1,0:T(8,128)(2,1)S(1)}, u32[]{:S(2)}, u32[]{:S(2)}) collective-permute-start(bf16[128,256]{1,0:T(8,128)(2,1)S(1)} %add_convert_fusion), channel_id=1, source_target_pairs={{0,24},{8,16},{16,8},{24,0},{1,25},{9,17},{17,9},{25,1},{2,26},{10... | collective-permute-start | bytes 196616 | tf_op jit(solution)/shard_map/ppermute | solution.py:327
  71.7 5.2 %collective-permute-start.14 = (bf16[128,256]{1,0:T(8,128)(2,1)S(1)}, bf16[128,256]{1,0:T(8,128)(2,1)S(1)}, u32[]{:S(2)}, u32[]{:S(2)}) collective-permute-start(bf16[128,256]{1,0:T(8,128)(2,1)S(1)} %dynamic-slice_bitcast_fusion.2), channel_id=1, source_target_pairs={{0,4},{2,6},{4,0},{6,2},{1,5},{3,7},{5,1},{7,3},{8,12},{10,14},{12... | collective-permute-start | bytes 196616 | tf_op jit(solution)/shard_map/ppermute | solution.py:327
  76.7 1.6 %collective-permute-start.18 = (bf16[4,128,256]{2,1,0:T(8,128)(2,1)S(1)}, bf16[4,128,256]{2,1,0:T(8,128)(2,1)S(1)}, u32[]{:S(2)}, u32[]{:S(2)}) collective-permute-start(bf16[4,128,256]{2,1,0:T(8,128)(2,1)S(1)} %bitcast_dynamic-update-slice_fusion.8), channel_id=1, source_target_pairs={{0,1},{1,0},{2,3},{3,2},{4,5},{5,4},{6,7},{7,6},{8,9},{9,8},{10,11... | collective-permute-start | bytes 786440 | tf_op jit(solution)/shard_map/ppermute | solution.py:327

commit v11 on v10

--- a/solution.py
+++ b/solution.py
@@ -408,10 +408,13 @@
     key_rows = src_rows.shape[0]
     key_total = key_rows * lax.axis_size("chip") * lax.axis_size("core")
 
-    packed = jnp.concatenate([ref_rows, out_grad, w_query, w_key, w_value, w_out], axis=0)
     source_all = src_rows
+    projections = (w_query, w_key, w_value, w_out)
     for count, step in enumerate(chip_steps[::-1]):
         source_all = double(source_all, step, count)
+        if count == 0:
+            source_all, projections = lax.optimization_barrier((source_all, projections))
+    packed = jnp.concatenate([ref_rows, out_grad, *projections], axis=0)
     source_all = double(source_all, core_step, len(chip_steps)).reshape(key_total, width)
 
     f32, b16 = jnp.float32, jnp.bfloat16
@@ -512,21 +515,22 @@
         (packed, attended, grad_query, grad_key, grad_value),
     )
 
-    weights = weight_part.reshape((2, lax.axis_size("scan"), -1, width))
+    scans = lax.axis_size("scan")
+    weights = weight_part.reshape((2, scans // 2, 2, -1, width))
     sources = source_part.reshape((2,) * (len(chip_steps) + 1) + (key_rows, width))
     source_steps = list(zip(chip_steps, range(len(chip_steps) - 1, -1, -1)))
     weights = halve(weights, core_step)
     sources = halve(sources, core_step, len(chip_steps))
-    weights = scatter_direct(weights, "scan")
+    weights, sources = lax.optimization_barrier((weights, sources))
+    weights = scatter_direct(weights.reshape((scans,) + weights.shape[2:]), "scan")
     sources = halve(sources, *source_steps[0])
     weights, sources = lax.optimization_barrier((weights, sources))
+    for step in source_steps[1:]:
+        sources = halve(sources, *step)
     for mesh_axis, bit, _ in chip_steps:
         weights = add(weights, swap(weights, mesh_axis, bit))
-    weights, sources = lax.optimization_barrier((weights, sources))
+    weights, grad_src = lax.optimization_barrier((weights, sources))
     weights = gather_direct(weights, "scan")
-    for step in source_steps[1:]:
-        sources = halve(sources, *step)
-    grad_src = sources
     weights = double(weights, core_step)
     weights = weights.reshape(4, width, width).astype(f32)
     return (

time: 79.7 us -> 78.4 us (0.984)
  waiting for transfers between devices: 23.4 us -> 26.7 us
  starting transfers between devices: 26.9 us -> 24.4 us
  Pallas kernels: 17.5 us -> 16.3 us
  other arithmetic: 2.03 us -> 1.09 us
    ppermute x19, waiting for transfers between devices: 23.4 us -> 26.7 us  [swap(): return lax.ppermute(x, axis, pairs)]
    ppermute x19, starting transfers between devices: 26.9 us -> 24.4 us  [swap(): return lax.ppermute(x, axis, pairs)]
    pallas_call x4, Pallas kernels: 17.5 us -> 16.3 us  [vmem_call(): pl.pallas_call(kernel, name=name, out_shape=out_shape, in_specs=specs, ou...]
  transfers between devices with their start and end apart: 19 -> 19, of which waited for: 12 -> 16; matrix products, arithmetic and copies ran while one was open for 11% -> 10% of each run, Pallas kernels for 2% -> 3%
where the time goes in v11:
time: 78.4 us; the launch traced here: 77.9 us
  waiting for transfers between devices  26.7 us (34%)
  starting transfers between devices  24.4 us (31%)
  Pallas kernels  16.3 us (21%)
  local copies, waits for them, and re-layouts  8.52 us (11%)
  other arithmetic  1.09 us (1%)
  between operations  0.97 us (1%)
    ppermute x19, waiting for transfers between devices, swap(): return lax.ppermute(x, axis, pairs)  26.7 us
    ppermute x19, starting transfers between devices, swap(): return lax.ppermute(x, axis, pairs)  24.4 us
    pallas_call x4, Pallas kernels, vmem_call(): pl.pallas_call(kernel, name=name, out_shape=out_shape, in_specs=specs, ou...  16.3 us
    unnamed x7, local copies, waits for them, and re-layouts  5.36 us
  transfers between devices with their start and end apart: 19, of which 16 were waited for; matrix products, arithmetic and copies ran while one was open for 10% of the time, Pallas kernels for 3%

profile of v11, /device:TPU:0, one launch (start us, length us, event | category | flops | bytes accessed | tf_op | source)
XLA Modules:
  0.0 77.9 jit_solution(17449519598146942322)
XLA Ops:
  0.6 4.1 %collective-permute-start = (bf16[128,256]{1,0:T(8,128)(2,1)}, bf16[128,256]{1,0:T(8,128)(2,1)S(1)}, u32[]{:S(2)}, u32[]{:S(2)}) collective-permute-start(bf16[128,256]{1,0:T(8,128)(2,1)} %bitcast.94), channel_id=1, source_target_pairs={{0,4},{2,6},{4,0},{6,2},{1,5},{3,7},{5,1},{7,3},{8,12},{10,14},{12... | collective-permute-start | bytes 196616 | tf_op jit(solution)/shard_map/ppermute | solution.py:327
  7.6 1.0 %collective-permute-done = bf16[128,256]{1,0:T(8,128)(2,1)S(1)} collective-permute-done((bf16[128,256]{1,0:T(8,128)(2,1)}, bf16[128,256]{1,0:T(8,128)(2,1)S(1)}, u32[]{:S(2)}, u32[]{:S(2)}) %collective-permute-start) | collective-permute-done | bytes 65568 | tf_op jit(solution)/shard_map/ppermute | solution.py:327
  12.1 1.5 %collective-permute-done.1 = bf16[2,128,256]{2,1,0:T(8,128)(2,1)S(1)} collective-permute-done((bf16[2,128,256]{2,1,0:T(8,128)(2,1)S(1)}, bf16[2,128,256]{2,1,0:T(8,128)(2,1)S(1)}, u32[]{:S(2)}, u32[]{:S(2)}) %collective-permute-start.1) | collective-permute-done | bytes 131104 | tf_op jit(solution)/shard_map/ppermute | solution.py:327
  16.0 7.0 %match_stats.1 = (f32[4,512,128]{2,1,0:T(8,128)S(1)}, f32[4,512,128]{2,1,0:T(8,128)S(1)}, f32[3,4,1024]{2,1,0:T(4,128)S(1)}, f32[16,512,256]{2,1,0:T(8,128)S(1)}, bf16[16,512,256]{2,1,0:T(8,128)(2,1)S(1)}) custom-call(s32[4,8]{1,0:T(4,128)S(1)} %bitcast.87, bf16[2048,256]{1,0:T(8,128)(2,1)S(1)} %constant_dynamic-update-slice_fusion.packed_ref, ...), custom_call_target="tpu_custom_call" | custom-call | flops 4026531840 | bytes 8388608 | tf_op jit(solution)/shard_map/match_stats/pallas_call | solution.py:388
  22.9 1.3 %collective-permute-start.3 = (f32[3,4,1024]{2,1,0:T(4,128)S(1)}, f32[3,4,1024]{2,1,0:T(4,128)S(1)}, u32[]{:S(2)}, u32[]{:S(2)}) collective-permute-start(f32[3,4,1024]{2,1,0:T(4,128)S(1)} %get-tuple-element.48.own_ref), channel_id=1, source_target_pairs={{0,2},{2,0},{4,6},{6,4},{1,3},{3,1},{5,7},{7,5},{8,10},{10,8},{12,... | collective-permute-start | bytes 147464 | tf_op jit(solution)/shard_map/ppermute | solution.py:327
  24.3 3.1 %collective-permute-done.3 = f32[3,4,1024]{2,1,0:T(4,128)S(1)} collective-permute-done((f32[3,4,1024]{2,1,0:T(4,128)S(1)}, f32[3,4,1024]{2,1,0:T(4,128)S(1)}, u32[]{:S(2)}, u32[]{:S(2)}) %collective-permute-start.3) | collective-permute-done | bytes 49184 | tf_op jit(solution)/shard_map/ppermute | solution.py:327
  27.5 2.4 %collective-permute-start.4 = (f32[3,4,1024]{2,1,0:T(4,128)S(1)}, f32[3,4,1024]{2,1,0:T(4,128)S(1)}, u32[]{:S(2)}, u32[]{:S(2)}) collective-permute-start(f32[3,4,1024]{2,1,0:T(4,128)S(1)} %pad_maximum_fusion), channel_id=1, source_target_pairs={{0,4},{2,6},{4,0},{6,2},{1,5},{3,7},{5,1},{7,3},{8,12},{10,14},{12... | collective-permute-start | bytes 147464 | tf_op jit(solution)/shard_map/ppermute | solution.py:327
  29.9 2.6 %collective-permute-done.4 = f32[3,4,1024]{2,1,0:T(4,128)S(1)} collective-permute-done((f32[3,4,1024]{2,1,0:T(4,128)S(1)}, f32[3,4,1024]{2,1,0:T(4,128)S(1)}, u32[]{:S(2)}, u32[]{:S(2)}) %collective-permute-start.4) | collective-permute-done | bytes 49184 | tf_op jit(solution)/shard_map/ppermute | solution.py:327
  33.9 7.4 %match_grads.1 = (bf16[512,256]{1,0:T(8,128)(2,1)S(1)}, bf16[512,256]{1,0:T(8,128)(2,1)S(1)}, bf16[256,1024]{1,0:T(8,128)(2,1)S(1)}, bf16[256,1024]{1,0:T(8,128)(2,1)S(1)}, bf16[4,256,256]{2,1,0:T(8,128)(2,1)S(1)}) custom-call(s32[4,8]{1,0:T(4,128)S(1)} %bitcast.88, f32[16,512,256]{2,1,0:T(8,128)S(1)} %get-tuple-element.40.score_ref, ...), custom_call_target="tpu_custom_call" | custom-call | flops 6710886400 | bytes 8388608 | tf_op jit(solution)/shard_map/match_grads/pallas_call | solution.py:388
  42.2 1.4 %finish_rows.1 = (bf16[512,256]{1,0:T(8,128)(2,1)}, bf16[512,256]{1,0:T(8,128)(2,1)}, bf16[1024,256]{1,0:T(8,128)(2,1)S(1)}) custom-call(bf16[2048,256]{1,0:T(8,128)(2,1)S(1)} %constant_dynamic-update-slice_fusion.packed_ref, bf16[512,256]{1,0:T(8,128)(2,1)S(1)} %get-tuple-element.49.attended_ref, bf16[512,256]{1,0:T(8,128)(2,1)S(1)} %get-tuple-element.50.gquery_ref, ...), custom_call_target="tpu_custom_call" | custom-call | flops 536870912 | bytes 2097152 | tf_op jit(solution)/shard_map/finish_rows/pallas_call | solution.py:388
  43.8 1.4 %collective-permute-done.7 = bf16[2,2,128,256]{3,2,0,1:T(8,128)(2,1)S(1)} collective-permute-done((bf16[2,2,128,256]{3,2,0,1:T(8,128)(2,1)S(1)}, bf16[2,2,128,256]{3,2,0,1:T(8,128)(2,1)S(1)}, u32[]{:S(2)}, u32[]{:S(2)}) %collective-permute-start.7) | collective-permute-done | bytes 262176 | tf_op jit(solution)/shard_map/ppermute | solution.py:327
  45.4 5.5 %collective-permute-start.10 = (bf16[128,256]{1,0:T(8,128)(2,1)S(1)}, bf16[128,256]{1,0:T(8,128)(2,1)S(1)}, u32[]{:S(2)}, u32[]{:S(2)}) collective-permute-start(bf16[128,256]{1,0:T(8,128)(2,1)S(1)} %get-tuple-element.72), channel_id=1, source_target_pairs={{0,24},{8,16},{16,8},{24,0},{1,25},{9,17},{17,9},{25,1},{2,26},{10... | collective-permute-start | bytes 196616 | tf_op jit(solution)/shard_map/ppermute | solution.py:327
  51.6 2.2 %collective-permute-done.10 = bf16[128,256]{1,0:T(8,128)(2,1)S(1)} collective-permute-done((bf16[128,256]{1,0:T(8,128)(2,1)S(1)}, bf16[128,256]{1,0:T(8,128)(2,1)S(1)}, u32[]{:S(2)}, u32[]{:S(2)}) %collective-permute-start.10) | collective-permute-done | bytes 65568 | tf_op jit(solution)/shard_map/ppermute | solution.py:327
  53.8 1.3 %collective-permute-done.8 = bf16[128,256]{1,0:T(8,128)(2,1)S(1)} collective-permute-done((bf16[128,256]{1,0:T(8,128)(2,1)S(1)}, bf16[128,256]{1,0:T(8,128)(2,1)S(1)}, u32[]{:S(2)}, u32[]{:S(2)}) %collective-permute-start.8) | collective-permute-done | bytes 65568 | tf_op jit(solution)/shard_map/ppermute | solution.py:327
  55.2 1.6 %collective-permute-done.11 = bf16[2,128,256]{2,1,0:T(8,128)(2,1)S(1)} collective-permute-done((bf16[2,128,256]{2,1,0:T(8,128)(2,1)S(1)}, bf16[2,128,256]{2,1,0:T(8,128)(2,1)S(1)}, u32[]{:S(2)}, u32[]{:S(2)}) %collective-permute-start.11) | collective-permute-done | bytes 131104 | tf_op jit(solution)/shard_map/ppermute | solution.py:327
  57.2 2.9 %collective-permute-start.14 = (bf16[128,256]{1,0:T(8,128)(2,1)S(1)}, bf16[128,256]{1,0:T(8,128)(2,1)S(1)}, u32[]{:S(2)}, u32[]{:S(2)}) collective-permute-start(bf16[128,256]{1,0:T(8,128)(2,1)S(1)} %dynamic-slice_bitcast_fusion.2), channel_id=1, source_target_pairs={{0,4},{2,6},{4,0},{6,2},{1,5},{3,7},{5,1},{7,3},{8,12},{10,14},{12... | collective-permute-start | bytes 196616 | tf_op jit(solution)/shard_map/ppermute | solution.py:327
  60.1 1.1 %collective-permute-done.12 = bf16[128,256]{1,0:T(8,128)(2,1)S(1)} collective-permute-done((bf16[128,256]{1,0:T(8,128)(2,1)S(1)}, bf16[128,256]{1,0:T(8,128)(2,1)S(1)}, u32[]{:S(2)}, u32[]{:S(2)}) %collective-permute-start.12) | collective-permute-done | bytes 65568 | tf_op jit(solution)/shard_map/ppermute | solution.py:327
  61.2 1.6 %collective-permute-start.13 = (bf16[128,256]{1,0:T(8,128)(2,1)S(1)}, bf16[128,256]{1,0:T(8,128)(2,1)S(1)}, u32[]{:S(2)}, u32[]{:S(2)}) collective-permute-start(bf16[128,256]{1,0:T(8,128)(2,1)S(1)} %add_convert_fusion.1), channel_id=1, source_target_pairs={{0,4},{2,6},{4,0},{6,2},{1,5},{3,7},{5,1},{7,3},{8,12},{10,14},{12... | collective-permute-start | bytes 196616 | tf_op jit(solution)/shard_map/ppermute | solution.py:327
  63.5 3.7 %collective-permute-done.13 = bf16[128,256]{1,0:T(8,128)(2,1)S(1)} collective-permute-done((bf16[128,256]{1,0:T(8,128)(2,1)S(1)}, bf16[128,256]{1,0:T(8,128)(2,1)S(1)}, u32[]{:S(2)}, u32[]{:S(2)}) %collective-permute-start.13) | collective-permute-done | bytes 65568 | tf_op jit(solution)/shard_map/ppermute | solution.py:327
  67.2 1.5 %collective-permute-start.15 = (bf16[128,256]{1,0:T(8,128)(2,1)S(1)}, bf16[128,256]{1,0:T(8,128)(2,1)S(1)}, u32[]{:S(2)}, u32[]{:S(2)}) collective-permute-start(bf16[128,256]{1,0:T(8,128)(2,1)S(1)} %add_convert_fusion), channel_id=1, source_target_pairs={{0,8},{8,0},{16,24},{24,16},{1,9},{9,1},{17,25},{25,17},{2,10},{10... | collective-permute-start | bytes 196616 | tf_op jit(solution)/shard_map/ppermute | solution.py:327
  68.6 1.5 %collective-permute-start.16 = (bf16[128,256]{1,0:T(8,128)(2,1)S(1)}, bf16[128,256]{1,0:T(8,128)(2,1)S(1)}, u32[]{:S(2)}, u32[]{:S(2)}) collective-permute-start(bf16[128,256]{1,0:T(8,128)(2,1)S(1)} %add_convert_fusion), channel_id=1, source_target_pairs={{0,16},{8,24},{16,0},{24,8},{1,17},{9,25},{17,1},{25,9},{2,18},{10... | collective-permute-start | bytes 196616 | tf_op jit(solution)/shard_map/ppermute | solution.py:327
  71.5 1.4 %collective-permute-done.16 = bf16[128,256]{1,0:T(8,128)(2,1)S(1)} collective-permute-done((bf16[128,256]{1,0:T(8,128)(2,1)S(1)}, bf16[128,256]{1,0:T(8,128)(2,1)S(1)}, u32[]{:S(2)}, u32[]{:S(2)}) %collective-permute-start.16) | collective-permute-done | bytes 65568 | tf_op jit(solution)/shard_map/ppermute | solution.py:327
  72.9 2.4 %collective-permute-done.17 = bf16[128,256]{1,0:T(8,128)(2,1)S(1)} collective-permute-done((bf16[128,256]{1,0:T(8,128)(2,1)S(1)}, bf16[128,256]{1,0:T(8,128)(2,1)S(1)}, u32[]{:S(2)}, u32[]{:S(2)}) %collective-permute-start.17) | collective-permute-done | bytes 65568 | tf_op jit(solution)/shard_map/ppermute | solution.py:327
  75.4 1.4 %collective-permute-done.18 = bf16[4,128,256]{2,1,0:T(8,128)(2,1)S(1)} collective-permute-done((bf16[4,128,256]{2,1,0:T(8,128)(2,1)S(1)}, bf16[4,128,256]{2,1,0:T(8,128)(2,1)S(1)}, u32[]{:S(2)}, u32[]{:S(2)}) %collective-permute-start.18) | collective-permute-done | bytes 262176 | tf_op jit(solution)/shard_map/ppermute | solution.py:327
  (63 shorter events, 15.7 us)
Async XLA Ops:
  0.6 8.0 %collective-permute-start = (bf16[128,256]{1,0:T(8,128)(2,1)}, bf16[128,256]{1,0:T(8,128)(2,1)S(1)}, u32[]{:S(2)}, u32[]{:S(2)}) collective-permute-start(bf16[128,256]{1,0:T(8,128)(2,1)} %bitcast.94), channel_id=1, source_target_pairs={{0,4},{2,6},{4,0},{6,2},{1,5},{3,7},{5,1},{7,3},{8,12},{10,14},{12... | collective-permute-start | bytes 196616 | tf_op jit(solution)/shard_map/ppermute | solution.py:327
  8.6 5.0 %collective-permute-start.1 = (bf16[2,128,256]{2,1,0:T(8,128)(2,1)S(1)}, bf16[2,128,256]{2,1,0:T(8,128)(2,1)S(1)}, u32[]{:S(2)}, u32[]{:S(2)}) collective-permute-start(bf16[2,128,256]{2,1,0:T(8,128)(2,1)S(1)} %bitcast_dynamic-update-slice_fusion.12), channel_id=1, source_target_pairs={{0,2},{2,0},{4,6},{6,4},{1,3},{3,1},{5,7},{7,5},{8,10},{10,8},{12,... | collective-permute-start | bytes 393224 | tf_op jit(solution)/shard_map/ppermute | solution.py:327
  13.7 1.6 %collective-permute-start.2 = (bf16[2,2,128,256]{3,2,1,0:T(8,128)(2,1)S(1)}, bf16[2,2,128,256]{3,2,1,0:T(8,128)(2,1)S(1)}, u32[]{:S(2)}, u32[]{:S(2)}) collective-permute-start(bf16[2,2,128,256]{3,2,1,0:T(8,128)(2,1)S(1)} %bitcast_dynamic-update-slice_fusion.7), channel_id=1, source_target_pairs={{0,1},{1,0},{2,3},{3,2},{4,5},{5,4},{6,7},{7,6},{8,9},{9,8},{10,11... | collective-permute-start | bytes 786440 | tf_op jit(solution)/shard_map/ppermute | solution.py:327
  15.3 0.7 copy-start
  22.9 4.5 %collective-permute-start.3 = (f32[3,4,1024]{2,1,0:T(4,128)S(1)}, f32[3,4,1024]{2,1,0:T(4,128)S(1)}, u32[]{:S(2)}, u32[]{:S(2)}) collective-permute-start(f32[3,4,1024]{2,1,0:T(4,128)S(1)} %get-tuple-element.48.own_ref), channel_id=1, source_target_pairs={{0,2},{2,0},{4,6},{6,4},{1,3},{3,1},{5,7},{7,5},{8,10},{10,8},{12,... | collective-permute-start | bytes 147464 | tf_op jit(solution)/shard_map/ppermute | solution.py:327
  27.5 5.1 %collective-permute-start.4 = (f32[3,4,1024]{2,1,0:T(4,128)S(1)}, f32[3,4,1024]{2,1,0:T(4,128)S(1)}, u32[]{:S(2)}, u32[]{:S(2)}) collective-permute-start(f32[3,4,1024]{2,1,0:T(4,128)S(1)} %pad_maximum_fusion), channel_id=1, source_target_pairs={{0,4},{2,6},{4,0},{6,2},{1,5},{3,7},{5,1},{7,3},{8,12},{10,14},{12... | collective-permute-start | bytes 147464 | tf_op jit(solution)/shard_map/ppermute | solution.py:327
  32.6 1.3 %collective-permute-start.5 = (f32[3,4,1024]{2,1,0:T(4,128)S(1)}, f32[3,4,1024]{2,1,0:T(4,128)S(1)}, u32[]{:S(2)}, u32[]{:S(2)}) collective-permute-start(f32[3,4,1024]{2,1,0:T(4,128)S(1)} %pad_maximum_fusion.1.near_ref), channel_id=1, source_target_pairs={{0,1},{1,0},{2,3},{3,2},{4,5},{5,4},{6,7},{7,6},{8,9},{9,8},{10,11... | collective-permute-start | bytes 147464 | tf_op jit(solution)/shard_map/ppermute | solution.py:327
  41.3 2.4 %collective-permute-start.6 = (bf16[2,2,128,256]{3,2,1,0:T(8,128)(2,1)S(1)}, bf16[2,2,128,256]{3,2,1,0:T(8,128)(2,1)S(1)}, u32[]{:S(2)}, u32[]{:S(2)}) collective-permute-start(bf16[2,2,128,256]{3,2,1,0:T(8,128)(2,1)S(1)} %dynamic-slice_bitcast_fusion), channel_id=1, source_target_pairs={{0,1},{1,0},{2,3},{3,2},{4,5},{5,4},{6,7},{7,6},{8,9},{9,8},{10,11... | collective-permute-start | bytes 786440 | tf_op jit(solution)/shard_map/ppermute | solution.py:327
  43.7 1.6 %collective-permute-start.7 = (bf16[2,2,128,256]{3,2,0,1:T(8,128)(2,1)S(1)}, bf16[2,2,128,256]{3,2,0,1:T(8,128)(2,1)S(1)}, u32[]{:S(2)}, u32[]{:S(2)}) collective-permute-start(bf16[2,2,128,256]{3,2,0,1:T(8,128)(2,1)S(1)} %bitcast.92), channel_id=1, source_target_pairs={{0,1},{1,0},{2,3},{3,2},{4,5},{5,4},{6,7},{7,6},{8,9},{9,8},{10,11... | collective-permute-start | bytes 786440 | tf_op jit(solution)/shard_map/ppermute | solution.py:327
  45.4 8.4 %collective-permute-start.10 = (bf16[128,256]{1,0:T(8,128)(2,1)S(1)}, bf16[128,256]{1,0:T(8,128)(2,1)S(1)}, u32[]{:S(2)}, u32[]{:S(2)}) collective-permute-start(bf16[128,256]{1,0:T(8,128)(2,1)S(1)} %get-tuple-element.72), channel_id=1, source_target_pairs={{0,24},{8,16},{16,8},{24,0},{1,25},{9,17},{17,9},{25,1},{2,26},{10... | collective-permute-start | bytes 196616 | tf_op jit(solution)/shard_map/ppermute | solution.py:327
  50.9 4.3 %collective-permute-start.8 = (bf16[128,256]{1,0:T(8,128)(2,1)S(1)}, bf16[128,256]{1,0:T(8,128)(2,1)S(1)}, u32[]{:S(2)}, u32[]{:S(2)}) collective-permute-start(bf16[128,256]{1,0:T(8,128)(2,1)S(1)} %get-tuple-element.71), channel_id=1, source_target_pairs={{0,8},{8,0},{16,24},{24,16},{1,9},{9,1},{17,25},{25,17},{2,10},{10... | collective-permute-start | bytes 196616 | tf_op jit(solution)/shard_map/ppermute | solution.py:327
  50.9 4.3 %collective-permute-start.9 = (bf16[128,256]{1,0:T(8,128)(2,1)S(1)}, bf16[128,256]{1,0:T(8,128)(2,1)S(1)}, u32[]{:S(2)}, u32[]{:S(2)}) collective-permute-start(bf16[128,256]{1,0:T(8,128)(2,1)S(1)} %get-tuple-element.73), channel_id=1, source_target_pairs={{0,16},{8,24},{16,0},{24,8},{1,17},{9,25},{17,1},{25,9},{2,18},{10... | collective-permute-start | bytes 196616 | tf_op jit(solution)/shard_map/ppermute | solution.py:327
  51.5 5.3 %collective-permute-start.11 = (bf16[2,128,256]{2,1,0:T(8,128)(2,1)S(1)}, bf16[2,128,256]{2,1,0:T(8,128)(2,1)S(1)}, u32[]{:S(2)}, u32[]{:S(2)}) collective-permute-start(bf16[2,128,256]{2,1,0:T(8,128)(2,1)S(1)} %dynamic-slice_bitcast_fusion.1), channel_id=1, source_target_pairs={{0,2},{2,0},{4,6},{6,4},{1,3},{3,1},{5,7},{7,5},{8,10},{10,8},{12,... | collective-permute-start | bytes 393224 | tf_op jit(solution)/shard_map/ppermute | solution.py:327
  56.8 4.3 %collective-permute-start.12 = (bf16[128,256]{1,0:T(8,128)(2,1)S(1)}, bf16[128,256]{1,0:T(8,128)(2,1)S(1)}, u32[]{:S(2)}, u32[]{:S(2)}) collective-permute-start(bf16[128,256]{1,0:T(8,128)(2,1)S(1)} %fusion.6), channel_id=1, source_target_pairs={{0,2},{2,0},{4,6},{6,4},{1,3},{3,1},{5,7},{7,5},{8,10},{10,8},{12,... | collective-permute-start | bytes 196616 | tf_op jit(solution)/shard_map/ppermute | solution.py:327
  57.2 5.6 %collective-permute-start.14 = (bf16[128,256]{1,0:T(8,128)(2,1)S(1)}, bf16[128,256]{1,0:T(8,128)(2,1)S(1)}, u32[]{:S(2)}, u32[]{:S(2)}) collective-permute-start(bf16[128,256]{1,0:T(8,128)(2,1)S(1)} %dynamic-slice_bitcast_fusion.2), channel_id=1, source_target_pairs={{0,4},{2,6},{4,0},{6,2},{1,5},{3,7},{5,1},{7,3},{8,12},{10,14},{12... | collective-permute-start | bytes 196616 | tf_op jit(solution)/shard_map/ppermute | solution.py:327
  61.2 5.9 %collective-permute-start.13 = (bf16[128,256]{1,0:T(8,128)(2,1)S(1)}, bf16[128,256]{1,0:T(8,128)(2,1)S(1)}, u32[]{:S(2)}, u32[]{:S(2)}) collective-permute-start(bf16[128,256]{1,0:T(8,128)(2,1)S(1)} %add_convert_fusion.1), channel_id=1, source_target_pairs={{0,4},{2,6},{4,0},{6,2},{1,5},{3,7},{5,1},{7,3},{8,12},{10,14},{12... | collective-permute-start | bytes 196616 | tf_op jit(solution)/shard_map/ppermute | solution.py:327
  67.2 4.3 %collective-permute-start.15 = (bf16[128,256]{1,0:T(8,128)(2,1)S(1)}, bf16[128,256]{1,0:T(8,128)(2,1)S(1)}, u32[]{:S(2)}, u32[]{:S(2)}) collective-permute-start(bf16[128,256]{1,0:T(8,128)(2,1)S(1)} %add_convert_fusion), channel_id=1, source_target_pairs={{0,8},{8,0},{16,24},{24,16},{1,9},{9,1},{17,25},{25,17},{2,10},{10... | collective-permute-start | bytes 196616 | tf_op jit(solution)/shard_map/ppermute | solution.py:327
  68.6 4.3 %collective-permute-start.16 = (bf16[128,256]{1,0:T(8,128)(2,1)S(1)}, bf16[128,256]{1,0:T(8,128)(2,1)S(1)}, u32[]{:S(2)}, u32[]{:S(2)}) collective-permute-start(bf16[128,256]{1,0:T(8,128)(2,1)S(1)} %add_convert_fusion), channel_id=1, source_target_pairs={{0,16},{8,24},{16,0},{24,8},{1,17},{9,25},{17,1},{25,9},{2,18},{10... | collective-permute-start | bytes 196616 | tf_op jit(solution)/shard_map/ppermute | solution.py:327
  70.1 5.2 %collective-permute-start.17 = (bf16[128,256]{1,0:T(8,128)(2,1)S(1)}, bf16[128,256]{1,0:T(8,128)(2,1)S(1)}, u32[]{:S(2)}, u32[]{:S(2)}) collective-permute-start(bf16[128,256]{1,0:T(8,128)(2,1)S(1)} %add_convert_fusion), channel_id=1, source_target_pairs={{0,24},{8,16},{16,8},{24,0},{1,25},{9,17},{17,9},{25,1},{2,26},{10... | collective-permute-start | bytes 196616 | tf_op jit(solution)/shard_map/ppermute | solution.py:327
  75.2 1.6 %collective-permute-start.18 = (bf16[4,128,256]{2,1,0:T(8,128)(2,1)S(1)}, bf16[4,128,256]{2,1,0:T(8,128)(2,1)S(1)}, u32[]{:S(2)}, u32[]{:S(2)}) collective-permute-start(bf16[4,128,256]{2,1,0:T(8,128)(2,1)S(1)} %bitcast_dynamic-update-slice_fusion.8), channel_id=1, source_target_pairs={{0,1},{1,0},{2,3},{3,2},{4,5},{5,4},{6,7},{7,6},{8,9},{9,8},{10,11... | collective-permute-start | bytes 786440 | tf_op jit(solution)/shard_map/ppermute | solution.py:327
